TPU v7x, 256 devices: a whole 4x4x8 slice. The times are simulated.
256 devices in a mesh: row: 64 (over y, x, z_hi, core), grp: 4 (over z_lo).
Axes of the slice: x: 4, y: 4, z: 8 (z_hi: 2, z_lo: 4; z = z_hi * 4 + z_lo), core: 2. Of those that a mesh axis runs over, the one named last changes fastest.
Arguments:
- positions: float32 [3, 8192], replicated, may hold values from -0.05 to 9.35, as said below
- detuning: float32 [8192], replicated, may hold values from -1 to 1
- populations: float32 [8192], P('row'), may hold values from 0 to 1
- base: float32 [2, 64, 8192], P(None, 'grp', 'row'), may hold values from -6 to 6
- section: float32 [2, 64, 8192], P(None, 'grp', 'row'), may hold values from -6 to 6
- accum: float32 [2, 64, 8192], P(None, 'grp', 'row'), may hold values from -3 to 3
Outputs:
- next_input: float32 [2, 64, 8192], P(None, 'grp', 'row')
- accum_out: float32 [2, 64, 8192], P(None, 'grp', 'row')
Inputs may be any that keep to these rules, and one draw needn't show every extreme that they name: `positions`: emitter n sits near the lattice point 0.3 * (n % 32, (n // 32) % 32, n // 1024), displaced by at most 0.05 in each coordinate.
All inputs are finite; a program needn't handle non-finite values.
Results may differ from a plain program's by a relative error of at most 0.0003.
Values sent between devices are 32-bit elements; how exact they have to be, the bound alone decides.
No kernel may reach another device: no remote copies, remote signals or barrier semaphores. Data moves between devices by JAX's collectives and lax.ppermute only.
A program may use at most 64 MiB of HBM per device.

v0:
```python
import math

import jax
import jax.numpy as jnp
from jax import lax
from jax.sharding import PartitionSpec as P

WAVE_NUMBER = 2.0 * math.pi
TIME_STEP = 0.2


def rows_first(arrays, axis, dims):
    turned = [jnp.moveaxis(a, dim, 0) for a, dim in zip(arrays, dims)]
    widths = [t[0].size for t in turned]
    both = jnp.concatenate([t.reshape(-1, w) for t, w in zip(turned, widths)], axis=1)
    out = lax.all_gather(both, axis, axis=0, tiled=True)
    blocks = jnp.split(out, [sum(widths[:k]) for k in range(1, len(widths))], axis=1)
    return tuple(
        (
            jnp.moveaxis(b.reshape(-1, *t.shape[1:]), 0, dim)
            for b, t, dim in zip(blocks, turned, dims)
        )
    )


def coupling(pos_rows, pos_cols, row_ids, col_ids):
    offsets = pos_rows[:, :, None] - pos_cols[:, None, :]
    dist_sq = jnp.sum(offsets * offsets, axis=0)
    on_diag = row_ids[:, None] == col_ids[None, :]
    safe_sq = jnp.where(on_diag, 1.0, dist_sq)
    phase = WAVE_NUMBER * jnp.sqrt(safe_sq)
    inverse = 1.0 / phase
    inverse_sq = inverse * inverse
    aligned = offsets[2] * offsets[2] / safe_sq
    quad_real = 1.0 - inverse_sq - aligned * (1.0 - 3.0 * inverse_sq)
    quad_imag = inverse - 3.0 * aligned * inverse
    cosine = jnp.cos(phase)
    sine = jnp.sin(phase)
    h_real = -0.75 * inverse * (cosine * quad_real - sine * quad_imag)
    h_imag = -0.75 * inverse * (sine * quad_real + cosine * quad_imag)
    return (jnp.where(on_diag, 0.0, h_real), jnp.where(on_diag, 0.0, h_imag))


def cross_rows(slab_part, tile):
    return lax.dot_general(
        slab_part,
        tile,
        (((1,), (1,)), ((), ())),
        precision=lax.Precision.HIGHEST,
        preferred_element_type=jnp.float32,
    )


def lead_rows(tile, slab_part):
    return lax.dot_general(
        tile,
        slab_part,
        (((0,), (0,)), ((), ())),
        precision=lax.Precision.HIGHEST,
        preferred_element_type=jnp.float32,
    )


def slab_rate(
    z_real,
    z_imag,
    shift,
    local_slab,
    full_slab,
    local_det,
    slab_pos,
    slab_det,
    col_start,
    col_count,
):
    slab_ids = lax.iota(jnp.int32, slab_pos.shape[1])
    w_real, w_imag = coupling(slab_pos, slab_pos, slab_ids, slab_ids)
    eye_mask = slab_ids[:, None] == slab_ids[None, :]
    w_real = w_real + jnp.where(eye_mask, slab_det[:, None], 0.0)
    w_imag = w_imag + jnp.where(eye_mask, -0.5, 0.0)
    w_real = lax.dynamic_slice_in_dim(w_real, col_start, col_count, 1)
    w_imag = lax.dynamic_slice_in_dim(w_imag, col_start, col_count, 1)
    v_real = lead_rows(w_real, full_slab[0]) + lead_rows(w_imag, full_slab[1])
    v_imag = lead_rows(w_real, full_slab[1]) - lead_rows(w_imag, full_slab[0])
    y_real = local_slab[0]
    y_imag = local_slab[1]
    z_real = z_real + local_det * y_real + 0.5 * y_imag
    z_imag = z_imag + local_det * y_imag - 0.5 * y_real
    f_real = z_imag + shift * y_imag - v_imag
    f_imag = -z_real - shift * y_real + v_real
    return jnp.stack([f_real, f_imag])


def accumulate(totals, pieces, pos_rows, row_ids, positions):
    slab_piece, pop_piece = pieces
    piece_len = slab_piece.shape[2]
    block_len = math.gcd(piece_len, 512)
    signed_pops = 2.0 * pop_piece.reshape(piece_len) - 1.0

    def one_block(step_index, sums):
        offset = step_index * block_len
        slab_block = lax.dynamic_slice_in_dim(slab_piece, offset, block_len, 2)
        pop_block = lax.dynamic_slice_in_dim(signed_pops, offset, block_len, 0)
        pos_block = lax.dynamic_slice_in_dim(positions, offset, block_len, 1)
        col_ids = offset + lax.iota(jnp.int32, block_len)
        h_real, h_imag = coupling(pos_rows, pos_block, row_ids, col_ids)
        z_real = sums[0] + cross_rows(slab_block[0], h_real) - cross_rows(slab_block[1], h_imag)
        z_imag = sums[1] + cross_rows(slab_block[0], h_imag) + cross_rows(slab_block[1], h_real)
        shift = sums[2] + jnp.dot(h_real, pop_block, precision=lax.Precision.HIGHEST)
        return (z_real, z_imag, shift)

    return lax.fori_loop(0, piece_len // block_len, one_block, totals)


def local(positions, detuning, populations, base, section, accum):
    col_count = section.shape[1]
    slab_width = col_count * lax.axis_size("grp")
    row_count = section.shape[2]
    slab_pos = positions[:, :slab_width]
    slab_det = detuning[:slab_width]
    row_start = lax.axis_index("row") * row_count
    pos_rows = lax.dynamic_slice_in_dim(positions, row_start, row_count, 1)
    local_det = lax.dynamic_slice_in_dim(detuning, row_start, row_count, 0)
    row_ids = row_start + lax.iota(jnp.int32, row_count)
    full_slab = lax.all_gather(section, "grp", axis=1, tiled=True)
    pop_piece = populations.reshape(1, 1, row_count)
    zeros_cols = jnp.zeros((col_count, row_count), jnp.float32)
    initial = (zeros_cols, zeros_cols, jnp.zeros((row_count,), jnp.float32))
    z_real, z_imag, shift = accumulate(
        initial, rows_first((section, pop_piece), "row", (2, 2)), pos_rows, row_ids, positions
    )
    col_start = lax.axis_index("grp") * col_count
    rate = slab_rate(
        z_real,
        z_imag,
        shift,
        section,
        full_slab,
        local_det,
        slab_pos,
        slab_det,
        col_start,
        col_count,
    )
    next_input = base + 0.5 * TIME_STEP * rate
    accum_out = accum + TIME_STEP / 3.0 * rate
    return (next_input, accum_out)


def solution(mesh):
    return jax.shard_map(
        local,
        mesh=mesh,
        in_specs=(
            P(),
            P(),
            P("row"),
            P(None, "grp", "row"),
            P(None, "grp", "row"),
            P(None, "grp", "row"),
        ),
        out_specs=(P(None, "grp", "row"), P(None, "grp", "row")),
        check_vma=False,
    )
```

profile of v0, /device:TPU:1, one launch (start us, length us, event | category | flops | bytes accessed | tf_op | source)
XLA Modules:
  0.0 191.0 jit_solution(239833096046484627)
XLA Ops:
  7.2 1.3 pad_maximum_fusion
  9.3 0.8 dynamic_slice.34
  10.7 13.0 %all_gather.7 = f32[2,64,128]{2,1,0:T(8,128)S(1)} all-gather(f32[2,16,128]{2,1,0:T(8,128)} %param.12), channel_id=1, replica_groups=mesh['row'=64,'grp'=4] {'grp'}, dimensions={1}, use_global_device_ids=true | all-gather | bytes 81920 | tf_op jit(solution)/shard_map/all_gather | solution.py:125
  25.2 71.5 %all-gather.2.cloned.1.call-done = f32[8192,33]{0,1:T(8,128)} async-done(((f32[128,33]{0,1:T(8,128)}), f32[8192,33]{0,1:T(8,128)}) %all-gather.2.cloned.1.call-update) | async-done | bytes 1081360 | tf_op jit(solution)/shard_map/all_gather | solution.py:16
  96.8 1.1 fusion.49
  98.1 85.0 %while.18 = (s32[]{:T(128)}, f32[16,128]{1,0:T(8,128)S(1)}, f32[16,128]{1,0:T(8,128)S(1)}, f32[128]{0:T(128)S(1)}, f32[2,16,8192]{2,1,0:T(8,128)S(1)}, /*index=5...) while((s32[]{:T(128)}, f32[16,128]{1,0:T(8,128)S(1)}, ...), condition=%wide.region_2.3_spmd.clone, body=%wide.region_0.2_spmd.clone.sunk | while | flops 54735752 | bytes 3901691 | solution.py:112
  98.2 0.7 constant_dynamic-slice_fusion.3
  99.0 1.6 fusion.84
  100.6 1.5 fusion.83
  103.5 0.7 constant_dynamic-slice_fusion.3
  104.3 1.6 fusion.84
  105.9 1.5 fusion.83
  108.8 0.7 constant_dynamic-slice_fusion.3
  109.6 1.6 fusion.84
  111.2 1.5 fusion.83
  114.1 0.7 constant_dynamic-slice_fusion.3
  115.0 1.6 fusion.84
  116.5 1.5 fusion.83
  119.4 0.7 constant_dynamic-slice_fusion.3
  120.3 1.6 fusion.84
  121.8 1.5 fusion.83
  124.7 0.7 constant_dynamic-slice_fusion.3
  125.6 1.6 fusion.84
  127.2 1.5 fusion.83
  130.0 0.7 constant_dynamic-slice_fusion.3
  130.9 1.6 fusion.84
  132.5 1.5 fusion.83
  136.2 1.6 fusion.84
  137.8 1.5 fusion.83
  141.5 1.6 fusion.84
  143.1 1.5 fusion.83
  146.9 1.6 fusion.84
  148.4 1.5 fusion.83
  151.3 0.7 constant_dynamic-slice_fusion.3
  152.2 1.6 fusion.84
  153.7 1.5 fusion.83
  156.6 0.7 constant_dynamic-slice_fusion.3
  157.5 1.6 fusion.84
  159.0 1.5 fusion.83
  161.9 0.7 constant_dynamic-slice_fusion.3
  162.8 1.6 fusion.84
  164.4 1.5 fusion.83
  168.1 1.6 fusion.84
  169.7 1.5 fusion.83
  173.4 1.6 fusion.84
  175.0 1.5 fusion.83
  178.7 1.6 fusion.84
  180.3 1.5 fusion.83
  (159 shorter events, 32.3 us)
Async XLA Ops:
  7.2 89.6 %all-gather.2.cloned.1.call-start = ((), (), s32[]{:S(2)}) async-start(), calls=%async_computation | async-start | bytes 1331200 | tf_op jit(solution)/shard_map/all_gather | solution.py:16
  96.8 1.3 slice-start
  98.1 85.0 %copy-start = (f32[2,16,128]{2,1,0:T(8,128)S(1)}, f32[2,16,128]{2,1,0:T(8,128)}, u32[]{:S(2)}) copy-start(f32[2,16,128]{2,1,0:T(8,128)} %param.12) | copy-start | bytes 49156
  98.1 85.5 %copy-start.1 = (f32[2,16,128]{2,1,0:T(8,128)S(1)}, f32[2,16,128]{2,1,0:T(8,128)}, u32[]{:S(2)}) copy-start(f32[2,16,128]{2,1,0:T(8,128)} %param.13) | copy-start | bytes 49156
  98.1 85.5 %copy-start.2 = (f32[2,16,128]{2,1,0:T(8,128)S(1)}, f32[2,16,128]{2,1,0:T(8,128)}, u32[]{:S(2)}) copy-start(f32[2,16,128]{2,1,0:T(8,128)} %param.11) | copy-start | bytes 49156
Sparse Core Ops, SparseCore 0:
  11.4 85.3 all-gather.1
where the time goes:
time: 192 us; the launch traced here: 191 us
  waiting for transfers between devices  71.5 us (37%)
  matrix products  45.6 us (24%)
  other arithmetic  29.7 us (15%)
  local copies, waits for them, and re-layouts  15.6 us (8%)
  between operations  14.1 us (7%)
  blocking collectives  13 us (7%)
    all_gather x1, waiting for transfers between devices, rows_first(): out = lax.all_gather(both, axis, axis=0, tiled=True)  71.5 us
    dot_general x16, matrix products, one_block(): jnp.dot(h_real, pop_block, precision=lax.Precision.HIGHEST)  25.1 us
    select_n x16, other arithmetic, coupling(): return (jnp.where(on_diag, 0.0, h_real), jnp.where(on_diag, 0.0, h_imag))  23.5 us
    dot_general x64, matrix products, cross_rows(): lax.dot_general(slab_part, tile, (((1,), (1,)), ((), ())), precision=lax....  19.7 us
    all_gather x1, blocking collectives, local(): full_slab = lax.all_gather(section, 'grp', axis=1, tiled=True)  13 us
    dynamic_slice x16, local copies, waits for them, and re-layouts, one_block(): pos_block = lax.dynamic_slice_in_dim(positions, offset, block_len, 1)  11.2 us
  transfers between devices with their start and end apart: 1, of which 1 were waited for; matrix products, arithmetic and copies ran while one was open for 2% of the time, Pallas kernels for 0%

commit v1 on v0

v1 whole, which is shorter than its diff:
```python
import math

import jax
import jax.numpy as jnp
from jax import lax
from jax.experimental import pallas as pl
from jax.experimental.pallas import tpu as pltpu
from jax.sharding import Mesh
from jax.sharding import PartitionSpec as P

TIME_STEP = 0.2
LANES = 128
COS = (0.9999999892, -19.73920453, 64.93911891, -85.45016433, 60.16782231, -25.96827976, 6.529565646)
SIN = (6.283182817, -41.3414213, 81.59618177, -76.58008122, 41.20531753, -12.27114973)
SCALE = -0.75 / (2.0 * math.pi)
INV_WAVE = 1.0 / (2.0 * math.pi)
ROUNDER = 12582912.0
PART = 40
WIDE = 48


def horner(coefs, scale, arg):
    total = jnp.float32(coefs[-1] * scale)
    for c in coefs[-2::-1]:
        total = total * arg + jnp.float32(c * scale)
    return total


def coupling(dx, dy, dz):
    dz_sq = dz * dz
    dist_sq = dx * dx + dy * dy + dz_sq
    inv = lax.rsqrt(dist_sq)
    dist = dist_sq * inv
    turn = dist - ((dist + ROUNDER) - ROUNDER)
    turn_sq = turn * turn
    cosine = horner(COS, SCALE, turn_sq) * inv
    sine = horner(SIN, SCALE, turn_sq) * turn * inv
    aligned = dz_sq * (inv * inv)
    quad_imag = inv * (INV_WAVE - (3.0 * INV_WAVE) * aligned)
    quad_real = (1.0 - aligned) - (INV_WAVE * inv) * quad_imag
    return cosine * quad_real - sine * quad_imag, sine * quad_real + cosine * quad_imag


def split(value):
    high = value.astype(jnp.bfloat16)
    low = (value - high.astype(jnp.float32)).astype(jnp.bfloat16)
    return high, low


def own_quad():
    return lax.axis_index("zh") * 2 + lax.axis_index("c")


def lanes_at(index):
    return pl.ds(pl.multiple_of(index * LANES, LANES), LANES)


def coupling_kernel(pos_ref, det_ref, high_ref, low_ref, w_ref, row_ref):
    quad = own_quad()
    place = lax.axis_index("yx")
    tiles = pos_ref.shape[1] // (4 * LANES)

    def turned(k, index):
        line = pos_ref[k : k + 1, lanes_at(index)]
        return jnp.broadcast_to(line, (LANES, LANES)).T

    for b in range(4):
        for k in range(3):
            row_ref[k, b * LANES : (b + 1) * LANES, :] = turned(k, place * 4 + b)

    def tile(step, carry):
        at = lanes_at(step * 4 + quad)
        cols = [pos_ref[k : k + 1, at] for k in range(3)]

        def strip(n, carry):
            rows = pl.ds(pl.multiple_of(n * 32, 32), 32)
            dx, dy, dz = [row_ref[k, rows, :] - cols[k] for k in range(3)]
            for part, value in enumerate(coupling(dx, dy, dz)):
                high, low = split(value)
                lanes = lanes_at(step + part * tiles)
                high_ref[rows, lanes] = high
                low_ref[rows, lanes] = low
            return carry

        return lax.fori_loop(0, 16, strip, carry, unroll=2)

    lax.fori_loop(0, tiles, tile, 0)
    rows = pl.ds(pl.multiple_of(quad * LANES, LANES), LANES)
    eye = lax.broadcasted_iota(jnp.int32, (LANES, LANES), 0) == lax.broadcasted_iota(jnp.int32, (LANES, LANES), 1)
    for part in range(2):
        lanes = lanes_at(place + part * tiles)
        for ref in (high_ref, low_ref):
            ref[rows, lanes] = jnp.where(eye, 0.0, ref[rows, lanes].astype(jnp.float32)).astype(jnp.bfloat16)

    start = pl.multiple_of(lax.axis_index("zl") * 16, 16)
    offsets = []
    for k in range(3):
        row_ref[k, 0:LANES, :] = turned(k, 0)
        offsets.append(row_ref[k, pl.ds(start, 16), :] - pos_ref[k : k + 1, 0:LANES])
    w_real, w_imag = coupling(*offsets)
    eye = (lax.broadcasted_iota(jnp.int32, (16, LANES), 0) + start) == lax.broadcasted_iota(jnp.int32, (16, LANES), 1)
    w_ref[0:16, :] = jnp.where(eye, det_ref[:, 0:LANES], w_real)
    w_ref[16:32, :] = jnp.where(eye, -0.5, w_imag)


def product_kernel(high_ref, low_ref, block_ref, out_ref, y_ref):
    tiles = block_ref.shape[0]
    zeros = jnp.zeros((16, LANES), jnp.float32)

    def fill(step, carry):
        block = block_ref[step]
        pops = jnp.concatenate([block[32:40], zeros[0:8]], axis=0)
        first, second = block[0:16], block[16:32]
        for n, value in enumerate((first, second, pops)):
            high, low = split(value)
            y_ref[n * 16 : n * 16 + 16, lanes_at(step)] = high
            y_ref[WIDE + n * 16 : WIDE + n * 16 + 16, lanes_at(step)] = low
        for n, value in enumerate((-second, first, zeros)):
            high, low = split(value)
            y_ref[n * 16 : n * 16 + 16, lanes_at(step + tiles)] = high
            y_ref[WIDE + n * 16 : WIDE + n * 16 + 16, lanes_at(step + tiles)] = low
        y_ref[2 * WIDE :, lanes_at(step)] = jnp.zeros((LANES - 2 * WIDE, LANES), jnp.bfloat16)
        y_ref[2 * WIDE :, lanes_at(step + tiles)] = jnp.zeros((LANES - 2 * WIDE, LANES), jnp.bfloat16)
        return carry

    lax.fori_loop(0, tiles, fill, 0)
    dims = (((1,), (1,)), ((), ()))
    total = lax.dot_general(high_ref[...], y_ref[...], dims, preferred_element_type=jnp.float32)
    total += lax.dot_general(low_ref[...], y_ref[...], dims, preferred_element_type=jnp.float32)
    for b in range(4):
        flat = total[b * LANES : (b + 1) * LANES, :].T
        out_ref[b] = flat[0:PART] + flat[WIDE : WIDE + PART]


def finish_kernel(z_ref, add_ref, w_ref, slab0, slab1, slab2, slab3, base_ref, accum_ref, det_ref, next_ref, acc_ref, y_ref):
    own = lax.axis_index("zl")
    for n, ref in enumerate((slab0, slab1, slab2, slab3)):
        start = pl.multiple_of(lax.rem(own + 4 - n, 4) * 16, 16)
        y_ref[0, pl.ds(start, 16), :] = ref[0]
        y_ref[1, pl.ds(start, 16), :] = ref[1]

    def mul(a, b):
        return jnp.dot(a, b, precision=lax.Precision.HIGHEST, preferred_element_type=jnp.float32)

    w_real, w_imag = w_ref[0:16, 0:64], w_ref[16:32, 0:64]
    v_real = mul(w_real, y_ref[0]) + mul(w_imag, y_ref[1])
    v_imag = mul(w_real, y_ref[1]) - mul(w_imag, y_ref[0])
    z_real = z_ref[0:16] + add_ref[0:16]
    z_imag = z_ref[16:32] + add_ref[16:32]
    shift = z_ref[32:33] + add_ref[32:33]
    y_real, y_imag = slab0[0], slab0[1]
    line = det_ref[:, lanes_at(lax.axis_index("yx") * 4 + own_quad())]
    z_real = z_real + line * y_real + 0.5 * y_imag
    z_imag = z_imag + line * y_imag - 0.5 * y_real
    rate_real = z_imag + shift * y_imag - v_imag
    rate_imag = v_real - z_real - shift * y_real
    for n, rate in enumerate((rate_real, rate_imag)):
        next_ref[n] = base_ref[n] + (0.5 * TIME_STEP) * rate
        acc_ref[n] = accum_ref[n] + (TIME_STEP / 3.0) * rate


def params(mib):
    return pltpu.CompilerParams(vmem_limit_bytes=mib << 20)


def local(positions, detuning, populations, base, section, accum):
    bf16, f32 = jnp.bfloat16, jnp.float32
    count = positions.shape[1]
    tiles = count // (4 * LANES)
    det = detuning.reshape(1, count)
    pops = (2.0 * populations - 1.0).reshape(1, LANES)
    block = jnp.concatenate([section.reshape(32, LANES), pops, jnp.zeros((PART - 33, LANES), f32)], axis=0)
    copies = jnp.broadcast_to(block[None], (tiles, PART, LANES))
    blocks = lax.all_to_all(copies, "yx", 0, 0, tiled=True)
    slabs = [section] + [lax.ppermute(section, "zl", [(i, (i + d) % 4) for i in range(4)]) for d in (1, 2, 3)]

    high, low, w = pl.pallas_call(
        coupling_kernel,
        out_shape=(
            jax.ShapeDtypeStruct((4 * LANES, 2 * tiles * LANES), bf16),
            jax.ShapeDtypeStruct((4 * LANES, 2 * tiles * LANES), bf16),
            jax.ShapeDtypeStruct((32, LANES), f32),
        ),
        in_specs=[pl.BlockSpec(memory_space=pltpu.VMEM), pl.BlockSpec(memory_space=pltpu.VMEM)],
        out_specs=[pl.BlockSpec(memory_space=pltpu.VMEM)] * 3,
        scratch_shapes=[pltpu.VMEM((3, 4 * LANES, LANES), f32)],
        compiler_params=params(24),
        cost_estimate=pl.CostEstimate(flops=60 << 20, bytes_accessed=8 << 20, transcendentals=1 << 20),
        name="coupling_tiles",
    )(positions, det)

    partial = pl.pallas_call(
        product_kernel,
        out_shape=jax.ShapeDtypeStruct((4, PART, LANES), f32),
        scratch_shapes=[pltpu.VMEM((LANES, 2 * tiles * LANES), bf16)],
        compiler_params=params(24),
        cost_estimate=pl.CostEstimate(flops=1 << 30, bytes_accessed=8 << 20, transcendentals=0),
        name="tile_products",
    )(high, low, blocks)

    mine = lax.axis_index("zh")
    other_half = lax.dynamic_slice_in_dim(partial, (1 - mine) * 2, 2, 0)
    own_half = lax.dynamic_slice_in_dim(partial, mine * 2, 2, 0)
    own_half = own_half + lax.ppermute(other_half, "zh", [(0, 1), (1, 0)])
    core = lax.axis_index("c")
    other = lax.dynamic_slice_in_dim(own_half, 1 - core, 1, 0)[0]
    own = lax.dynamic_slice_in_dim(own_half, core, 1, 0)[0]
    added = lax.ppermute(other, "c", [(0, 1), (1, 0)])

    return pl.pallas_call(
        finish_kernel,
        out_shape=(jax.ShapeDtypeStruct(base.shape, f32),) * 2,
        scratch_shapes=[pltpu.VMEM((2, 64, LANES), f32)],
        compiler_params=params(8),
        cost_estimate=pl.CostEstimate(flops=4 << 20, bytes_accessed=1 << 18, transcendentals=0),
        name="finish_rate",
    )(own, added, w, *slabs, base, accum, det)


def solution(mesh):
    fine = Mesh(mesh.devices.reshape(16, 2, 2, 4), ("yx", "zh", "c", "zl"))
    rows = ("yx", "zh", "c")
    slab = P(None, "zl", rows)
    return jax.shard_map(
        local,
        mesh=fine,
        in_specs=(P(), P(), P(rows), slab, slab, slab),
        out_specs=(slab, slab),
        check_vma=False,
    )
```

time: 192 us -> 52.5 us (0.27)
  waiting for transfers between devices: 71.5 us -> 2.52 us
  matrix products: 45.6 us -> 0 us
  other arithmetic: 29.7 us -> 1.46 us
  starting transfers between devices: 0.04 us -> 21.5 us
  Pallas kernels: 0 us -> 14.4 us
  between operations: 14.1 us -> 0.73 us
  blocking collectives: 13 us -> 0 us
  local copies, waits for them, and re-layouts: 15.6 us -> 10.9 us
    all_gather x1 -> x0, waiting for transfers between devices: 71.5 us -> none  [rows_first(): out = lax.all_gather(both, axis, axis=0, tiled=True)]
    dot_general x84 -> x0, matrix products: 45.6 us -> none  [the longest x16 25.1 us: one_block(): jnp.dot(h_real, pop_block, precision=lax.Precision.HIGHEST)]
    select_n x16 -> x0, other arithmetic: 23.5 us -> none  [coupling(): return (jnp.where(on_diag, 0.0, h_real), jnp.where(on_diag, 0.0, h_imag))]
    pallas_call x0 -> x3, Pallas kernels: none -> 14.4 us  [the longest x1 10.9 us: local(): pl.pallas_call(coupling_kernel, out_shape=(jax.ShapeDtypeStruct((4 * LANE...]
    ppermute x0 -> x5, starting transfers between devices: none -> 13.9 us  [the longest x1 6.99 us: local(): own_half = own_half + lax.ppermute(other_half, 'zh', [(0, 1), (1, 0)])]
    dynamic_slice x34 -> x1, local copies, waits for them, and re-layouts: 13.9 us -> 0.01 us  [local(): other_half = lax.dynamic_slice_in_dim(partial, (1 - mine) * 2, 2, 0)]
    all_gather x1 -> x0, blocking collectives: 13 us -> none  [local(): full_slab = lax.all_gather(section, 'grp', axis=1, tiled=True)]
    unnamed x6 -> x20, local copies, waits for them, and re-layouts: 0.05 us -> 9.98 us
  transfers between devices with their start and end apart: 1 -> 6, of which waited for: 1 -> 2; matrix products, arithmetic and copies ran while one was open for 2% -> 0% of each run, Pallas kernels for 0% -> 21%
where the time goes in v1:
time: 52.5 us; the launch traced here: 51.5 us
  starting transfers between devices  21.5 us (41%)
  Pallas kernels  14.4 us (27%)
  local copies, waits for them, and re-layouts  10.9 us (21%)
  waiting for transfers between devices  2.52 us (5%)
  other arithmetic  1.46 us (3%)
  between operations  0.73 us (1%)
    pallas_call x1, Pallas kernels, local(): pl.pallas_call(coupling_kernel, out_shape=(jax.ShapeDtypeStruct((4 * LANE...  10.9 us
    unnamed x20, local copies, waits for them, and re-layouts  9.98 us
    all_to_all x1, starting transfers between devices, local(): blocks = lax.all_to_all(copies, 'yx', 0, 0, tiled=True)  7.58 us
    ppermute x1, starting transfers between devices, local(): own_half = own_half + lax.ppermute(other_half, 'zh', [(0, 1), (1, 0)])  6.99 us
    ppermute x3, starting transfers between devices, local(): lax.ppermute(section, 'zl', [(i, (i + d) % 4) for i in range(4)])  4.94 us
    pallas_call x1, Pallas kernels, local(): pl.pallas_call(product_kernel, out_shape=jax.ShapeDtypeStruct((4, PART, L...  2.66 us
    ppermute x1, starting transfers between devices, local(): added = lax.ppermute(other, 'c', [(0, 1), (1, 0)])  2 us
    ppermute x1, waiting for transfers between devices, local(): own_half = own_half + lax.ppermute(other_half, 'zh', [(0, 1), (1, 0)])  1.39 us
  transfers between devices with their start and end apart: 6, of which 2 were waited for; matrix products, arithmetic and copies ran while one was open for 0% of the time, Pallas kernels for 21%

profile of v1, /device:TPU:1, one launch (start us, length us, event | category | flops | bytes accessed | tf_op | source)
XLA Modules:
  0.0 51.5 jit_solution(2220280317719960612)
XLA Ops:
  0.6 0.7 %add_bitcast_fusion = f32[1,128]{1,0:T(1,128)S(1)} fusion(f32[128]{0:T(128)} %param.8), kind=kLoop, calls=%fused_computation.5 | loop fusion | flops 256 | bytes 1024 | tf_op jit(solution)/shard_map/reshape | solution.py:171
  1.3 0.1 pad.2.clone
  1.4 0.8 %maximum_maximum_fusion = f32[40,128]{1,0:T(8,128)S(1)} fusion(f32[1,128]{1,0:T(1,128)S(1)} %add_bitcast_fusion, f32[32,128]{1,0:T(8,128)} %bitcast.8, f32[40]{0:T(128)S(1)} %pad.2.clone), kind=kLoop, calls=%fused_computation.1 | loop fusion | flops 10240 | bytes 37536 | tf_op jit(solution)/shard_map/concatenate | solution.py:172
  2.2 0.8 %broadcast_in_dim.10 = f32[16,40,128]{2,1,0:T(8,128)} broadcast(f32[40,128]{1,0:T(8,128)S(1)} %maximum_maximum_fusion), dimensions={1,2} | broadcast | bytes 348160 | tf_op jit(solution)/shard_map/broadcast_in_dim | solution.py:173
  2.9 7.6 %all-to-all-start = ((f32[16,40,128]{2,1,0:T(8,128)}), f32[16,40,128]{2,1,0:T(8,128)S(1)}, u32[]{:S(2)}, u32[]{:S(2)}) async-start(f32[16,40,128]{2,1,0:T(8,128)} %broadcast_in_dim.10), calls=%async_computation | async-start | bytes 655360 | tf_op jit(solution)/shard_map/all_to_all | solution.py:174
  10.5 0.0 copy-start.5
  10.5 0.7 %copy-done.5 = f32[8192]{0:T(1024)S(1)} copy-done((f32[8192]{0:T(1024)S(1)}, f32[8192]{0:T(1024)}, u32[]{:S(2)}) %copy-start.5) | copy-done | bytes 32792
  11.3 0.0 copy-start.9
  11.3 0.9 %copy-done.9 = f32[3,8192]{1,0:T(4,128)S(1)} copy-done((f32[3,8192]{1,0:T(4,128)S(1)}, f32[3,8192]{1,0:T(4,128)}, u32[]{:S(2)}) %copy-start.9) | copy-done | bytes 98328
  12.2 10.9 %coupling_tiles.1 = (bf16[512,4096]{1,0:T(8,128)(2,1)S(1)}, bf16[512,4096]{1,0:T(8,128)(2,1)S(1)}, f32[32,128]{1,0:T(8,128)S(1)}) custom-call(f32[3,8192]{1,0:T(4,128)S(1)} %copy-done.9, f32[1,8192]{1,0:T(1,128)S(1)} %bitcast.9), custom_call_target="tpu_custom_call" | custom-call | flops 62914560 | bytes 8388608 | tf_op jit(solution)/shard_map/coupling_tiles/pallas_call | solution.py:177
  23.1 0.0 copy-start
  23.1 1.9 %copy-done = bf16[512,4096]{1,0:T(8,128)(2,1)} copy-done((bf16[512,4096]{1,0:T(8,128)(2,1)}, bf16[512,4096]{1,0:T(8,128)(2,1)S(1)}, u32[]{:S(2)}) %copy-start) | copy-done | bytes 4194328
  25.1 0.0 copy-start.2
  25.1 2.0 %copy-done.2 = bf16[512,4096]{1,0:T(8,128)(2,1)} copy-done((bf16[512,4096]{1,0:T(8,128)(2,1)}, bf16[512,4096]{1,0:T(8,128)(2,1)S(1)}, u32[]{:S(2)}) %copy-start.2) | copy-done | bytes 4194328
  27.1 0.0 all-to-all-done.block_ref
  27.1 0.0 copy-start.1
  27.1 2.2 %copy-done.1 = bf16[512,4096]{1,0:T(8,128)(2,1)S(1)} copy-done((bf16[512,4096]{1,0:T(8,128)(2,1)S(1)}, bf16[512,4096]{1,0:T(8,128)(2,1)}, u32[]{:S(2)}) %copy-start.1) | copy-done | bytes 4194328
  29.2 0.0 copy-start.3
  29.2 2.2 %copy-done.3 = bf16[512,4096]{1,0:T(8,128)(2,1)S(1)} copy-done((bf16[512,4096]{1,0:T(8,128)(2,1)S(1)}, bf16[512,4096]{1,0:T(8,128)(2,1)}, u32[]{:S(2)}) %copy-start.3) | copy-done | bytes 4194328
  31.4 0.0 copy-start.4
  31.4 0.0 copy-start.6
  31.4 0.0 copy-start.7
  31.4 0.0 copy-start.8
  31.4 2.7 %tile_products.1 = f32[4,40,128]{2,1,0:T(8,128)S(1)} custom-call(bf16[512,4096]{1,0:T(8,128)(2,1)S(1)} %copy-done.1, bf16[512,4096]{1,0:T(8,128)(2,1)S(1)} %copy-done.3, f32[16,40,128]{2,1,0:T(8,128)S(1)} %all-to-all-done.block_ref), custom_call_target="tpu_custom_call" | custom-call | flops 1073741824 | bytes 8388608 | tf_op jit(solution)/shard_map/tile_products/pallas_call | solution.py:192
  34.1 7.0 %collective-permute-start = (f32[2,40,128]{2,1,0:T(8,128)S(1)}, f32[2,40,128]{2,1,0:T(8,128)S(1)}, u32[]{:S(2)}, u32[]{:S(2)}) collective-permute-start(f32[2,40,128]{2,1,0:T(8,128)S(1)} %constant_dynamic-slice_fusion), channel_id=1, source_target_pairs={{0,8},{8,0},{1,9},{9,1},{2,10},{10,2},{3,11},{11,3},{4,12},{12,4},... | collective-permute-start | bytes 122888 | tf_op jit(solution)/shard_map/ppermute | solution.py:204
  41.1 1.4 %collective-permute-done = f32[2,40,128]{2,1,0:T(8,128)S(1)} collective-permute-done((f32[2,40,128]{2,1,0:T(8,128)S(1)}, f32[2,40,128]{2,1,0:T(8,128)S(1)}, u32[]{:S(2)}, u32[]{:S(2)}) %collective-permute-start) | collective-permute-done | bytes 40992 | tf_op jit(solution)/shard_map/ppermute | solution.py:204
  42.5 2.0 %collective-permute-start.1 = (f32[40,128]{1,0:T(8,128)S(1)}, f32[40,128]{1,0:T(8,128)S(1)}, u32[]{:S(2)}, u32[]{:S(2)}) collective-permute-start(f32[40,128]{1,0:T(8,128)S(1)} %get-tuple-element.8), channel_id=1, source_target_pairs={{0,4},{4,0},{1,5},{5,1},{2,6},{6,2},{3,7},{7,3},{8,12},{12,8},{9,1... | collective-permute-start | bytes 61448 | tf_op jit(solution)/shard_map/ppermute | solution.py:208
  44.5 0.0 copy-done.4
  44.5 1.7 %collective-permute-start.3 = (f32[2,16,128]{2,1,0:T(8,128)S(1)}, f32[2,16,128]{2,1,0:T(8,128)S(1)}, u32[]{:S(2)}, u32[]{:S(2)}) collective-permute-start(f32[2,16,128]{2,1,0:T(8,128)S(1)} %copy-done.4), channel_id=1, source_target_pairs={{0,2},{1,3},{2,0},{3,1},{4,6},{5,7},{6,4},{7,5},{8,10},{9,11},{10,... | collective-permute-start | bytes 49160 | tf_op jit(solution)/shard_map/ppermute | solution.py:175
  46.2 1.6 %collective-permute-start.2 = (f32[2,16,128]{2,1,0:T(8,128)S(1)}, f32[2,16,128]{2,1,0:T(8,128)S(1)}, u32[]{:S(2)}, u32[]{:S(2)}) collective-permute-start(f32[2,16,128]{2,1,0:T(8,128)S(1)} %copy-done.4), channel_id=1, source_target_pairs={{0,1},{1,2},{2,3},{3,0},{4,5},{5,6},{6,7},{7,4},{8,9},{9,10},{10,1... | collective-permute-start | bytes 49160 | tf_op jit(solution)/shard_map/ppermute | solution.py:175
  47.8 1.6 %collective-permute-start.4 = (f32[2,16,128]{2,1,0:T(8,128)S(1)}, f32[2,16,128]{2,1,0:T(8,128)S(1)}, u32[]{:S(2)}, u32[]{:S(2)}) collective-permute-start(f32[2,16,128]{2,1,0:T(8,128)S(1)} %copy-done.4), channel_id=1, source_target_pairs={{0,3},{1,0},{2,1},{3,2},{4,7},{5,4},{6,5},{7,6},{8,11},{9,8},{10,9... | collective-permute-start | bytes 49160 | tf_op jit(solution)/shard_map/ppermute | solution.py:175
  49.5 0.0 collective-permute-done.3.slab2
  49.5 1.1 %collective-permute-done.2.slab1 = f32[2,16,128]{2,1,0:T(8,128)S(1)} collective-permute-done((f32[2,16,128]{2,1,0:T(8,128)S(1)}, f32[2,16,128]{2,1,0:T(8,128)S(1)}, u32[]{:S(2)}, u32[]{:S(2)}) %collective-permute-start.2) | collective-permute-done | bytes 16416 | tf_op jit(solution)/shard_map/ppermute | solution.py:175
  50.6 0.0 collective-permute-done.4.slab3
  50.6 0.0 collective-permute-done.1.add_ref
  50.6 0.0 copy-done.6
  50.6 0.0 copy-done.7
  50.6 0.0 copy-done.8
  50.6 0.9 %finish_rate.1 = (f32[2,16,128]{2,1,0:T(8,128)}, f32[2,16,128]{2,1,0:T(8,128)}) custom-call(f32[40,128]{1,0:T(8,128)S(1)} %get-tuple-element.9.z_ref, f32[40,128]{1,0:T(8,128)S(1)} %collective-permute-done.1.add_ref, f32[32,128]{1,0:T(8,128)S(1)} %get-tuple-element.7.w_ref, f32[2,16,128]{2,1,0:T(8,128)S(1)} %copy-done.4, ...), custom_call_target="tpu_custom_call" | custom-call | flops 4194304 | bytes 262144 | tf_op jit(solution)/shard_map/finish_rate/pallas_call | solution.py:210
  (4 shorter events, 0.0 us)
Async XLA Ops:
  2.9 24.1 %all-to-all-start = ((f32[16,40,128]{2,1,0:T(8,128)}), f32[16,40,128]{2,1,0:T(8,128)S(1)}, u32[]{:S(2)}, u32[]{:S(2)}) async-start(f32[16,40,128]{2,1,0:T(8,128)} %broadcast_in_dim.10), calls=%async_computation | async-start | bytes 655360 | tf_op jit(solution)/shard_map/all_to_all | solution.py:174
  10.5 0.8 %copy-start.5 = (f32[8192]{0:T(1024)S(1)}, f32[8192]{0:T(1024)}, u32[]{:S(2)}) copy-start(f32[8192]{0:T(1024)} %param.7) | copy-start | bytes 98308
  11.3 0.9 %copy-start.9 = (f32[3,8192]{1,0:T(4,128)S(1)}, f32[3,8192]{1,0:T(4,128)}, u32[]{:S(2)}) copy-start(f32[3,8192]{1,0:T(4,128)} %pos_ref.1) | copy-start | bytes 294916
  23.1 2.0 %copy-start = (bf16[512,4096]{1,0:T(8,128)(2,1)}, bf16[512,4096]{1,0:T(8,128)(2,1)S(1)}, u32[]{:S(2)}) copy-start(bf16[512,4096]{1,0:T(8,128)(2,1)S(1)} %get-tuple-element.5.high_ref) | copy-start | bytes 12582916
  25.1 2.0 %copy-start.2 = (bf16[512,4096]{1,0:T(8,128)(2,1)}, bf16[512,4096]{1,0:T(8,128)(2,1)S(1)}, u32[]{:S(2)}) copy-start(bf16[512,4096]{1,0:T(8,128)(2,1)S(1)} %get-tuple-element.6.low_ref) | copy-start | bytes 12582916
  27.1 2.2 %copy-start.1 = (bf16[512,4096]{1,0:T(8,128)(2,1)S(1)}, bf16[512,4096]{1,0:T(8,128)(2,1)}, u32[]{:S(2)}) copy-start(bf16[512,4096]{1,0:T(8,128)(2,1)} %copy-done) | copy-start | bytes 12582916
  29.2 2.2 %copy-start.3 = (bf16[512,4096]{1,0:T(8,128)(2,1)S(1)}, bf16[512,4096]{1,0:T(8,128)(2,1)}, u32[]{:S(2)}) copy-start(bf16[512,4096]{1,0:T(8,128)(2,1)} %copy-done.2) | copy-start | bytes 12582916
  31.4 13.1 %copy-start.4 = (f32[2,16,128]{2,1,0:T(8,128)S(1)}, f32[2,16,128]{2,1,0:T(8,128)}, u32[]{:S(2)}) copy-start(f32[2,16,128]{2,1,0:T(8,128)} %slab0.1) | copy-start | bytes 49156
  31.4 19.2 %copy-start.6 = (f32[8192]{0:T(1024)S(1)}, f32[8192]{0:T(1024)}, u32[]{:S(2)}) copy-start(f32[8192]{0:T(1024)} %param.7) | copy-start | bytes 98308
  31.4 19.2 %copy-start.7 = (f32[2,16,128]{2,1,0:T(8,128)S(1)}, f32[2,16,128]{2,1,0:T(8,128)}, u32[]{:S(2)}) copy-start(f32[2,16,128]{2,1,0:T(8,128)} %base_ref.1) | copy-start | bytes 49156
  31.4 19.2 %copy-start.8 = (f32[2,16,128]{2,1,0:T(8,128)S(1)}, f32[2,16,128]{2,1,0:T(8,128)}, u32[]{:S(2)}) copy-start(f32[2,16,128]{2,1,0:T(8,128)} %accum_ref.1) | copy-start | bytes 49156
  34.1 8.4 %collective-permute-start = (f32[2,40,128]{2,1,0:T(8,128)S(1)}, f32[2,40,128]{2,1,0:T(8,128)S(1)}, u32[]{:S(2)}, u32[]{:S(2)}) collective-permute-start(f32[2,40,128]{2,1,0:T(8,128)S(1)} %constant_dynamic-slice_fusion), channel_id=1, source_target_pairs={{0,8},{8,0},{1,9},{9,1},{2,10},{10,2},{3,11},{11,3},{4,12},{12,4},... | collective-permute-start | bytes 122888 | tf_op jit(solution)/shard_map/ppermute | solution.py:204
  42.5 8.1 %collective-permute-start.1 = (f32[40,128]{1,0:T(8,128)S(1)}, f32[40,128]{1,0:T(8,128)S(1)}, u32[]{:S(2)}, u32[]{:S(2)}) collective-permute-start(f32[40,128]{1,0:T(8,128)S(1)} %get-tuple-element.8), channel_id=1, source_target_pairs={{0,4},{4,0},{1,5},{5,1},{2,6},{6,2},{3,7},{7,3},{8,12},{12,8},{9,1... | collective-permute-start | bytes 61448 | tf_op jit(solution)/shard_map/ppermute | solution.py:208
  44.5 4.9 %collective-permute-start.3 = (f32[2,16,128]{2,1,0:T(8,128)S(1)}, f32[2,16,128]{2,1,0:T(8,128)S(1)}, u32[]{:S(2)}, u32[]{:S(2)}) collective-permute-start(f32[2,16,128]{2,1,0:T(8,128)S(1)} %copy-done.4), channel_id=1, source_target_pairs={{0,2},{1,3},{2,0},{3,1},{4,6},{5,7},{6,4},{7,5},{8,10},{9,11},{10,... | collective-permute-start | bytes 49160 | tf_op jit(solution)/shard_map/ppermute | solution.py:175
  46.2 4.4 %collective-permute-start.2 = (f32[2,16,128]{2,1,0:T(8,128)S(1)}, f32[2,16,128]{2,1,0:T(8,128)S(1)}, u32[]{:S(2)}, u32[]{:S(2)}) collective-permute-start(f32[2,16,128]{2,1,0:T(8,128)S(1)} %copy-done.4), channel_id=1, source_target_pairs={{0,1},{1,2},{2,3},{3,0},{4,5},{5,6},{6,7},{7,4},{8,9},{9,10},{10,1... | collective-permute-start | bytes 49160 | tf_op jit(solution)/shard_map/ppermute | solution.py:175
  47.8 2.8 %collective-permute-start.4 = (f32[2,16,128]{2,1,0:T(8,128)S(1)}, f32[2,16,128]{2,1,0:T(8,128)S(1)}, u32[]{:S(2)}, u32[]{:S(2)}) collective-permute-start(f32[2,16,128]{2,1,0:T(8,128)S(1)} %copy-done.4), channel_id=1, source_target_pairs={{0,3},{1,0},{2,1},{3,2},{4,7},{5,4},{6,5},{7,6},{8,11},{9,8},{10,9... | collective-permute-start | bytes 49160 | tf_op jit(solution)/shard_map/ppermute | solution.py:175

commit v2 on v1

v2 whole, which is shorter than its diff:
```python
import math

import jax
import jax.numpy as jnp
from jax import lax
from jax.experimental import pallas as pl
from jax.experimental.pallas import tpu as pltpu
from jax.sharding import Mesh
from jax.sharding import PartitionSpec as P

TIME_STEP = 0.2
LANES = 128
COS = (0.9999999892, -19.73920453, 64.93911891, -85.45016433, 60.16782231, -25.96827976, 6.529565646)
SIN = (6.283182817, -41.3414213, 81.59618177, -76.58008122, 41.20531753, -12.27114973)
SCALE = -0.75 / (2.0 * math.pi)
INV_WAVE = 1.0 / (2.0 * math.pi)
ROUNDER = 12582912.0
PART = 40
WIDE = 48


def horner(coefs, scale, arg):
    total = jnp.float32(coefs[-1] * scale)
    for c in coefs[-2::-1]:
        total = total * arg + jnp.float32(c * scale)
    return total


def coupling(dx, dy, dz):
    dz_sq = dz * dz
    dist_sq = dx * dx + dy * dy + dz_sq
    inv = lax.rsqrt(dist_sq)
    dist = dist_sq * inv
    turn = dist - ((dist + ROUNDER) - ROUNDER)
    turn_sq = turn * turn
    cosine = horner(COS, SCALE, turn_sq) * inv
    sine = horner(SIN, SCALE, turn_sq) * turn * inv
    aligned = dz_sq * (inv * inv)
    quad_imag = inv * (INV_WAVE - (3.0 * INV_WAVE) * aligned)
    quad_real = (1.0 - aligned) - (INV_WAVE * inv) * quad_imag
    return cosine * quad_real - sine * quad_imag, sine * quad_real + cosine * quad_imag


def split(value):
    high = value.astype(jnp.bfloat16)
    low = (value - high.astype(jnp.float32)).astype(jnp.bfloat16)
    return high, low


def lanes_at(index):
    return pl.ds(pl.multiple_of(index * LANES, LANES), LANES)


def pack_kernel(section_ref, pops_ref, pos_ref, det_ref, copies_ref, pos_out, det_out, block_ref, sems):
    own = lax.axis_index("yx") * 4 + lax.axis_index("zh") * 2 + lax.axis_index("c")
    moves = [
        pltpu.make_async_copy(section_ref.at[0], block_ref.at[pl.ds(0, 16)], sems.at[0]),
        pltpu.make_async_copy(section_ref.at[1], block_ref.at[pl.ds(16, 16)], sems.at[1]),
        pltpu.make_async_copy(pops_ref, block_ref.at[pl.ds(32, 1)], sems.at[2]),
        pltpu.make_async_copy(pos_ref, pos_out, sems.at[3]),
        pltpu.make_async_copy(det_ref.at[:, lanes_at(own)], det_out.at[pl.ds(0, 1)], sems.at[4]),
        pltpu.make_async_copy(det_ref.at[:, pl.ds(0, LANES)], det_out.at[pl.ds(1, 1)], sems.at[5]),
    ]
    for move in moves:
        move.start()
    for move in moves[:3]:
        move.wait()
    block = block_ref[0:32, :]
    top = lax.broadcasted_iota(jnp.int32, (8, LANES), 0) == 0
    pops = jnp.where(top, 2.0 * block_ref[32:40, :] - 1.0, 0.0)
    for n in range(copies_ref.shape[0]):
        copies_ref[n, 0:32, :] = block
        copies_ref[n, 32:40, :] = pops
    for move in moves[3:]:
        move.wait()


def turned(pos_ref, k, index):
    line = pos_ref[k : k + 1, lanes_at(index)]
    return jnp.broadcast_to(line, (LANES, LANES)).T


def fill_tiles(pos_ref, row_ref, high_ref, low_ref, quads, unroll, after=None):
    quad = lax.axis_index("zh") * 2 + lax.axis_index("c")
    place = lax.axis_index("yx")
    for n, other in enumerate(quads):
        for k in range(3):
            row_ref[k, n * LANES : (n + 1) * LANES, :] = turned(pos_ref, k, place * 4 + other)

    def tile(step, carry):
        at = lanes_at(step * 4 + quad)
        cols = [pos_ref[k : k + 1, at] for k in range(3)]

        def strip(n, carry):
            rows = pl.ds(pl.multiple_of(n * 32, 32), 32)
            dx, dy, dz = [row_ref[k, rows, :] - cols[k] for k in range(3)]
            for part, value in enumerate(coupling(dx, dy, dz)):
                high, low = split(value)
                lanes = lanes_at(step * 2 + part)
                high_ref[rows, lanes] = high
                low_ref[rows, lanes] = low
            return carry

        lax.fori_loop(0, 4 * len(quads), strip, carry, unroll=unroll)
        if after is not None:
            after(step)
        return carry

    lax.fori_loop(0, pos_ref.shape[1] // (4 * LANES), tile, 0)


def far_kernel(pos_ref, near_ref, low_ref, last_ref, row_ref, high_all, low_all, sems):
    half, core = lax.axis_index("zh"), lax.axis_index("c")
    quads = ((1 - half) * 2 + 1 - core, (1 - half) * 2 + core, half * 2 + 1 - core)
    send = 2 * LANES

    def moves(step):
        lanes = pl.ds(pl.multiple_of(step * 2 * LANES, 2 * LANES), 2 * LANES)
        return (
            pltpu.make_async_copy(high_all.at[pl.ds(0, send), lanes], near_ref.at[:, lanes], sems.at[step, 0]),
            pltpu.make_async_copy(low_all.at[pl.ds(0, send), lanes], low_ref.at[:, lanes], sems.at[step, 1]),
            pltpu.make_async_copy(high_all.at[pl.ds(send, LANES), lanes], last_ref.at[0, :, lanes], sems.at[step, 2]),
            pltpu.make_async_copy(low_all.at[pl.ds(send, LANES), lanes], last_ref.at[1, :, lanes], sems.at[step, 3]),
        )

    def start(step):
        for move in moves(step):
            move.start()

    fill_tiles(pos_ref, row_ref, high_all, low_all, quads, 6, start)

    def finish(step, carry):
        for move in moves(step):
            move.wait()
        return carry

    lax.fori_loop(0, pos_ref.shape[1] // (4 * LANES), finish, 0)


def fill_slab(block_ref, y_ref):
    tiles = block_ref.shape[0]
    zeros = jnp.zeros((16, LANES), jnp.float32)

    def fill(step, carry):
        block = block_ref[step]
        pops = jnp.concatenate([block[32:40], zeros[0:8]], axis=0)
        first, second = block[0:16], block[16:32]
        for part, rows in enumerate(((first, second, pops), (-second, first, zeros))):
            lanes = lanes_at(step * 2 + part)
            for n, value in enumerate(rows):
                high, low = split(value)
                y_ref[n * 16 : n * 16 + 16, lanes] = high
                y_ref[WIDE + n * 16 : WIDE + n * 16 + 16, lanes] = low
            y_ref[2 * WIDE :, lanes] = jnp.zeros((LANES - 2 * WIDE, LANES), jnp.bfloat16)
        return carry

    lax.fori_loop(0, tiles, fill, 0, unroll=4)


def store_products(total, out_ref, at):
    for n in range(total.shape[0] // LANES):
        flat = total[n * LANES : (n + 1) * LANES, :].T
        out_ref[at + n] = flat[0:PART] + flat[WIDE : WIDE + PART]


def send_kernel(near_ref, low_ref, block_ref, out_ref, y_ref, low, sem):
    move = pltpu.make_async_copy(low_ref, low, sem)
    move.start()
    fill_slab(block_ref, y_ref)
    dims = (((1,), (1,)), ((), ()))
    total = lax.dot_general(near_ref[...], y_ref[...], dims, preferred_element_type=jnp.float32)
    move.wait()
    total += lax.dot_general(low[...], y_ref[...], dims, preferred_element_type=jnp.float32)
    store_products(total, out_ref, 0)


def keep_kernel(pos_ref, last_ref, y_ref, slab0, slab1, slab2, slab3, det_ref, out_ref, rest_ref, row_ref, high_ref, low_ref, full_ref, last, sem):
    move = pltpu.make_async_copy(last_ref, last, sem)
    move.start()
    own, place = lax.axis_index("zl"), lax.axis_index("yx")
    quad = lax.axis_index("zh") * 2 + lax.axis_index("c")
    fill_tiles(pos_ref, row_ref, high_ref, low_ref, (quad,), 4)
    eye = lax.broadcasted_iota(jnp.int32, (LANES, LANES), 0) == lax.broadcasted_iota(jnp.int32, (LANES, LANES), 1)
    for part in range(2):
        lanes = lanes_at(place * 2 + part)
        for ref in (high_ref, low_ref):
            ref[:, lanes] = jnp.where(eye, 0.0, ref[:, lanes].astype(jnp.float32)).astype(jnp.bfloat16)
    move.wait()
    dims = (((1,), (1,)), ((), ()))
    for n, (high, low) in enumerate(((last[0], last[1]), (high_ref[...], low_ref[...]))):
        total = lax.dot_general(high, y_ref[...], dims, preferred_element_type=jnp.float32)
        total += lax.dot_general(low, y_ref[...], dims, preferred_element_type=jnp.float32)
        store_products(total, out_ref, n)

    start = pl.multiple_of(own * 16, 16)
    offsets = []
    for k in range(3):
        row_ref[k] = turned(pos_ref, k, 0)
        offsets.append(row_ref[k, pl.ds(start, 16), :] - pos_ref[k : k + 1, 0:LANES])
    w_real, w_imag = coupling(*offsets)
    eye = (lax.broadcasted_iota(jnp.int32, (16, LANES), 0) + start) == lax.broadcasted_iota(jnp.int32, (16, LANES), 1)
    w_real = jnp.where(eye, det_ref[1:2, :], w_real)[:, 0:64]
    w_imag = jnp.where(eye, -0.5, w_imag)[:, 0:64]
    for n, ref in enumerate((slab0, slab1, slab2, slab3)):
        there = pl.ds(pl.multiple_of(lax.rem(own + 4 - n, 4) * 16, 16), 16)
        full_ref[0, there, :] = ref[0]
        full_ref[1, there, :] = ref[1]

    def mul(a, b):
        return jnp.dot(a, b, precision=lax.Precision.HIGHEST, preferred_element_type=jnp.float32)

    v_real = mul(w_real, full_ref[0]) + mul(w_imag, full_ref[1])
    v_imag = mul(w_real, full_ref[1]) - mul(w_imag, full_ref[0])
    y_real, y_imag = slab0[0], slab0[1]
    line = det_ref[0:1, :]
    rest_ref[0] = line * y_imag - 0.5 * y_real - v_imag
    rest_ref[1] = v_real - line * y_real - 0.5 * y_imag


def finish_kernel(keep_ref, half_ref, core_ref, rest_ref, slab_ref, base_ref, accum_ref, next_ref, acc_ref):
    z = keep_ref[1] + half_ref[1] + core_ref[...]
    shift = z[32:33]
    rate_real = z[16:32] + shift * slab_ref[1] + rest_ref[0]
    rate_imag = rest_ref[1] - z[0:16] - shift * slab_ref[0]
    for n, rate in enumerate((rate_real, rate_imag)):
        next_ref[n] = base_ref[n] + (0.5 * TIME_STEP) * rate
        acc_ref[n] = accum_ref[n] + (TIME_STEP / 3.0) * rate


def params(mib):
    return pltpu.CompilerParams(vmem_limit_bytes=mib << 20)


def in_hbm(array):
    return pltpu.with_memory_space_constraint(array, pltpu.HBM)


def local(positions, detuning, populations, base, section, accum):
    bf16, f32 = jnp.bfloat16, jnp.float32
    count = positions.shape[1]
    tiles = count // (4 * LANES)
    deep = 2 * tiles * LANES
    hbm, vmem = pl.BlockSpec(memory_space=pltpu.HBM), pl.BlockSpec(memory_space=pltpu.VMEM)

    copies, pos, det = pl.pallas_call(
        pack_kernel,
        out_shape=(
            jax.ShapeDtypeStruct((tiles, PART, LANES), f32),
            pltpu.VMEM(positions.shape, f32),
            pltpu.VMEM((8, LANES), f32),
        ),
        in_specs=[hbm] * 4,
        out_specs=[vmem] * 3,
        scratch_shapes=[pltpu.VMEM((PART, LANES), f32), pltpu.SemaphoreType.DMA((6,))],
        compiler_params=params(4),
        cost_estimate=pl.CostEstimate(flops=1 << 16, bytes_accessed=1 << 19, transcendentals=0),
        name="pack_block",
    )(in_hbm(section), in_hbm(populations.reshape(1, LANES)), in_hbm(positions), in_hbm(detuning.reshape(1, count)))
    blocks = lax.all_to_all(copies, "yx", 0, 0, tiled=True)
    slabs = [section] + [lax.ppermute(section, "zl", [(i, (i + d) % 4) for i in range(4)]) for d in (1, 2, 3)]

    near, low, last = pl.pallas_call(
        far_kernel,
        out_shape=(
            pltpu.VMEM((2 * LANES, deep), bf16),
            pltpu.HBM((2 * LANES, deep), bf16),
            pltpu.HBM((2, LANES, deep), bf16),
        ),
        in_specs=[vmem],
        out_specs=[vmem, hbm, hbm],
        scratch_shapes=[
            pltpu.VMEM((3, 3 * LANES, LANES), f32),
            pltpu.VMEM((3 * LANES, deep), bf16),
            pltpu.VMEM((3 * LANES, deep), bf16),
            pltpu.SemaphoreType.DMA((tiles, 4)),
        ],
        compiler_params=params(12),
        cost_estimate=pl.CostEstimate(flops=45 << 20, bytes_accessed=6 << 20, transcendentals=1 << 20),
        name="far_tiles",
    )(pos)

    sent, y = pl.pallas_call(
        send_kernel,
        out_shape=(pltpu.VMEM((2, PART, LANES), f32), pltpu.VMEM((LANES, deep), bf16)),
        in_specs=[vmem, hbm, vmem],
        out_specs=[vmem] * 2,
        scratch_shapes=[pltpu.VMEM((2 * LANES, deep), bf16), pltpu.SemaphoreType.DMA],
        compiler_params=params(8),
        cost_estimate=pl.CostEstimate(flops=1 << 29, bytes_accessed=4 << 20, transcendentals=0),
        name="send_products",
    )(near, in_hbm(low), blocks)
    half = lax.ppermute(sent, "zh", [(0, 1), (1, 0)])

    keep, rest = pl.pallas_call(
        keep_kernel,
        out_shape=(pltpu.VMEM((2, PART, LANES), f32), pltpu.VMEM((2, 16, LANES), f32)),
        in_specs=[vmem, hbm] + [vmem] * 6,
        out_specs=[vmem] * 2,
        scratch_shapes=[
            pltpu.VMEM((3, LANES, LANES), f32),
            pltpu.VMEM((LANES, deep), bf16),
            pltpu.VMEM((LANES, deep), bf16),
            pltpu.VMEM((2, 64, LANES), f32),
            pltpu.VMEM((2, LANES, deep), bf16),
            pltpu.SemaphoreType.DMA,
        ],
        compiler_params=params(8),
        cost_estimate=pl.CostEstimate(flops=1 << 29, bytes_accessed=4 << 20, transcendentals=1 << 20),
        name="keep_products",
    )(pos, in_hbm(last), y, *slabs, det)
    core = lax.ppermute(keep[0] + half[0], "c", [(0, 1), (1, 0)])

    return pl.pallas_call(
        finish_kernel,
        out_shape=(jax.ShapeDtypeStruct(base.shape, f32),) * 2,
        compiler_params=params(4),
        cost_estimate=pl.CostEstimate(flops=1 << 16, bytes_accessed=1 << 18, transcendentals=0),
        name="finish_rate",
    )(keep, half, core, rest, section, base, accum)


def solution(mesh):
    fine = Mesh(mesh.devices.reshape(16, 2, 2, 4), ("yx", "zh", "c", "zl"))
    rows = ("yx", "zh", "c")
    slab = P(None, "zl", rows)
    return jax.shard_map(
        local,
        mesh=fine,
        in_specs=(P(), P(), P(rows), slab, slab, slab),
        out_specs=(slab, slab),
        check_vma=False,
    )
```

time: 52.5 us -> 40.5 us (0.77); the launches traced: 51.5 us -> 40.2 us
  local copies, waits for them, and re-layouts: 10.9 us -> 0.02 us
  Pallas kernels: 14.4 us -> 18.3 us
  waiting for transfers between devices: 2.52 us -> 0.86 us
  other arithmetic: 1.46 us -> 0.01 us
  starting transfers between devices: 21.5 us -> 20.4 us
    unnamed x20 -> x6, local copies, waits for them, and re-layouts: 9.98 us -> 0.02 us
    pallas_call x2 -> x4, Pallas kernels: 13.6 us -> 17.6 us  [the longest x1 9.04 us: local(): pl.pallas_call(far_kernel, out_shape=(pltpu.VMEM((2 * LANES, deep), bf16)...]
    ppermute x2, starting transfers between devices: 8.99 us -> 7.34 us  [the longest x1 5.2 us: local(): half = lax.ppermute(sent, 'zh', [(0, 1), (1, 0)])]
    ppermute x3, waiting for transfers between devices: 1.12 us -> 0.01 us  [local(): lax.ppermute(section, 'zl', [(i, (i + d) % 4) for i in range(4)])]
    concatenate x1 -> x0, other arithmetic: 0.79 us -> none  [local(): jnp.concatenate([section.reshape(32, LANES), pops, jnp.zeros((PART - 33,...]
    broadcast_in_dim x2 -> x0, local copies, waits for them, and re-layouts: 0.77 us -> none  [the longest x1 0.77 us: local(): copies = jnp.broadcast_to(block[None], (tiles, PART, LANES))]
    reshape x1 -> x0, other arithmetic: 0.66 us -> none  [local(): pops = (2.0 * populations - 1.0).reshape(1, LANES)]
    ppermute x2, waiting for transfers between devices: 1.39 us -> 0.85 us  [the longest x1 0.84 us: local(): core = lax.ppermute(keep[0] + half[0], 'c', [(0, 1), (1, 0)])]
  transfers between devices with their start and end apart: 6 -> 6, of which waited for: 2 -> 1; matrix products, arithmetic and copies ran while one was open for 0% -> 0% of each run, Pallas kernels for 21% -> 40%
where the time goes in v2:
time: 40.5 us; the launch traced here: 40.2 us
  starting transfers between devices  20.4 us (50%)
  Pallas kernels  18.3 us (45%)
  waiting for transfers between devices  0.86 us (2%)
  between operations  0.73 us (2%)
    pallas_call x1, Pallas kernels, local(): pl.pallas_call(far_kernel, out_shape=(pltpu.VMEM((2 * LANES, deep), bf16)...  9.04 us
    all_to_all x1, starting transfers between devices, local(): blocks = lax.all_to_all(copies, 'yx', 0, 0, tiled=True)  7.6 us
    ppermute x3, starting transfers between devices, local(): lax.ppermute(section, 'zl', [(i, (i + d) % 4) for i in range(4)])  5.43 us
    ppermute x1, starting transfers between devices, local(): half = lax.ppermute(sent, 'zh', [(0, 1), (1, 0)])  5.2 us
    pallas_call x1, Pallas kernels, local(): pl.pallas_call(keep_kernel, out_shape=(pltpu.VMEM((2, PART, LANES), f32),...  3.94 us
    pallas_call x1, Pallas kernels, local(): pl.pallas_call(send_kernel, out_shape=(pltpu.VMEM((2, PART, LANES), f32),...  2.92 us
    ppermute x1, starting transfers between devices, local(): core = lax.ppermute(keep[0] + half[0], 'c', [(0, 1), (1, 0)])  2.14 us
    pallas_call x1, Pallas kernels, local(): pl.pallas_call(pack_kernel, out_shape=(jax.ShapeDtypeStruct((tiles, PART,...  1.74 us
  transfers between devices with their start and end apart: 6, of which 1 were waited for; matrix products, arithmetic and copies ran while one was open for 0% of the time, Pallas kernels for 40%

profile of v2, /device:TPU:1, one launch (start us, length us, event | category | flops | bytes accessed | tf_op | source)
XLA Modules:
  0.0 40.2 jit_solution(6814989896663511613)
XLA Ops:
  0.6 1.7 %pack_block.1 = (f32[16,40,128]{2,1,0:T(8,128)}, f32[3,8192]{1,0:T(4,128)S(1)}, f32[8,128]{1,0:T(8,128)S(1)}) custom-call(f32[2,16,128]{2,1,0:T(8,128)} %slab_ref.1, f32[1,128]{1,0:T(1,128)} %bitcast.5, f32[3,8192]{1,0:T(4,128)} %pos_ref.1, f32[1,8192]{1,0:T(1,128)} %bitcast.4), custom_call_target="tpu_custom_call" | custom-call | flops 65536 | bytes 524288 | tf_op jit(solution)/shard_map/pack_block/pallas_call | solution.py:245
  2.4 7.6 %all-to-all-start = ((f32[16,40,128]{2,1,0:T(8,128)}), f32[16,40,128]{2,1,0:T(8,128)S(1)}, u32[]{:S(2)}, u32[]{:S(2)}) async-start(f32[16,40,128]{2,1,0:T(8,128)} %get-tuple-element.16), calls=%async_computation | async-start | bytes 655360 | tf_op jit(solution)/shard_map/all_to_all | solution.py:259
  10.0 1.7 %collective-permute-start = (f32[2,16,128]{2,1,0:T(8,128)}, f32[2,16,128]{2,1,0:T(8,128)S(1)}, u32[]{:S(2)}, u32[]{:S(2)}) collective-permute-start(f32[2,16,128]{2,1,0:T(8,128)} %slab_ref.1), channel_id=1, source_target_pairs={{0,1},{1,2},{2,3},{3,0},{4,5},{5,6},{6,7},{7,4},{8,9},{9,10},{10,1... | collective-permute-start | bytes 49160 | tf_op jit(solution)/shard_map/ppermute | solution.py:260
  11.7 3.0 %collective-permute-start.1 = (f32[2,16,128]{2,1,0:T(8,128)}, f32[2,16,128]{2,1,0:T(8,128)S(1)}, u32[]{:S(2)}, u32[]{:S(2)}) collective-permute-start(f32[2,16,128]{2,1,0:T(8,128)} %slab_ref.1), channel_id=1, source_target_pairs={{0,2},{1,3},{2,0},{3,1},{4,6},{5,7},{6,4},{7,5},{8,10},{9,11},{10,... | collective-permute-start | bytes 49160 | tf_op jit(solution)/shard_map/ppermute | solution.py:260
  14.7 0.7 %collective-permute-start.2 = (f32[2,16,128]{2,1,0:T(8,128)}, f32[2,16,128]{2,1,0:T(8,128)S(1)}, u32[]{:S(2)}, u32[]{:S(2)}) collective-permute-start(f32[2,16,128]{2,1,0:T(8,128)} %slab_ref.1), channel_id=1, source_target_pairs={{0,3},{1,0},{2,1},{3,2},{4,7},{5,4},{6,5},{7,6},{8,11},{9,8},{10,9... | collective-permute-start | bytes 49160 | tf_op jit(solution)/shard_map/ppermute | solution.py:260
  15.4 9.0 %far_tiles.1 = (bf16[256,4096]{1,0:T(8,128)(2,1)S(1)}, bf16[256,4096]{1,0:T(8,128)(2,1)}, bf16[2,128,4096]{2,1,0:T(8,128)(2,1)}) custom-call(f32[3,8192]{1,0:T(4,128)S(1)} %get-tuple-element.12.pos_ref), custom_call_target="tpu_custom_call" | custom-call | flops 47185920 | bytes 6291456 | tf_op jit(solution)/shard_map/far_tiles/pallas_call | solution.py:262
  24.5 0.0 all-to-all-done.block_ref
  24.5 0.0 copy-start
  24.5 2.9 %send_products.1 = (f32[2,40,128]{2,1,0:T(8,128)S(1)}, bf16[128,4096]{1,0:T(8,128)(2,1)S(1)}) custom-call(bf16[256,4096]{1,0:T(8,128)(2,1)S(1)} %get-tuple-element.14.near_ref, bf16[256,4096]{1,0:T(8,128)(2,1)} %get-tuple-element.15.low_ref, f32[16,40,128]{2,1,0:T(8,128)S(1)} %all-to-all-done.block_ref), custom_call_target="tpu_custom_call" | custom-call | flops 536870912 | bytes 4194304 | tf_op jit(solution)/shard_map/send_products/pallas_call | solution.py:282
  27.4 0.0 copy-start.1
  27.4 0.0 copy-start.2
  27.4 5.2 %collective-permute-start.3 = (f32[2,40,128]{2,1,0:T(8,128)S(1)}, f32[2,40,128]{2,1,0:T(8,128)S(1)}, u32[]{:S(2)}, u32[]{:S(2)}) collective-permute-start(f32[2,40,128]{2,1,0:T(8,128)S(1)} %get-tuple-element.20), channel_id=1, source_target_pairs={{0,8},{8,0},{1,9},{9,1},{2,10},{10,2},{3,11},{11,3},{4,12},{12,4},... | collective-permute-start | bytes 122888 | tf_op jit(solution)/shard_map/ppermute | solution.py:292
  32.6 0.0 collective-permute-done.slab1
  32.6 0.0 collective-permute-done.1.slab2
  32.6 0.0 collective-permute-done.2.slab3
  32.6 0.0 copy-done
  32.7 3.9 %keep_products.1 = (f32[2,40,128]{2,1,0:T(8,128)S(1)}, f32[2,16,128]{2,1,0:T(8,128)S(1)}) custom-call(f32[3,8192]{1,0:T(4,128)S(1)} %get-tuple-element.12.pos_ref, bf16[2,128,4096]{2,1,0:T(8,128)(2,1)} %get-tuple-element.13.last_ref, bf16[128,4096]{1,0:T(8,128)(2,1)S(1)} %get-tuple-element.17.y_ref, f32[2,16,128]{2,1,0:T(8,128)S(1)} %copy-done, ...), custom_call_target="tpu_custom_call" | custom-call | flops 536870912 | bytes 4194304 | tf_op jit(solution)/shard_map/keep_products/pallas_call | solution.py:294
  36.6 0.0 collective-permute-done.3.half_ref
  36.6 2.1 %collective-permute-start.4 = (f32[40,128]{1,0:T(8,128)S(1)}, f32[40,128]{1,0:T(8,128)S(1)}, u32[]{:S(2)}, u32[]{:S(2)}) collective-permute-start(f32[40,128]{1,0:T(8,128)S(1)} %fusion), channel_id=1, source_target_pairs={{0,4},{4,0},{1,5},{5,1},{2,6},{6,2},{3,7},{7,3},{8,12},{12,8},{9,1... | collective-permute-start | bytes 61448 | tf_op jit(solution)/shard_map/ppermute | solution.py:311
  38.8 0.8 %collective-permute-done.4.core_ref = f32[40,128]{1,0:T(8,128)S(1)} collective-permute-done((f32[40,128]{1,0:T(8,128)S(1)}, f32[40,128]{1,0:T(8,128)S(1)}, u32[]{:S(2)}, u32[]{:S(2)}) %collective-permute-start.4) | collective-permute-done | bytes 20512 | tf_op jit(solution)/shard_map/ppermute | solution.py:311
  39.6 0.0 copy-done.1
  39.6 0.0 copy-done.2
  39.6 0.6 %finish_rate.1 = (f32[2,16,128]{2,1,0:T(8,128)}, f32[2,16,128]{2,1,0:T(8,128)}) custom-call(f32[2,40,128]{2,1,0:T(8,128)S(1)} %get-tuple-element.19.keep_ref, f32[2,40,128]{2,1,0:T(8,128)S(1)} %collective-permute-done.3.half_ref, f32[40,128]{1,0:T(8,128)S(1)} %collective-permute-done.4.core_ref, f32[2,16,128]{2,1,0:T(8,128)S(1)} %get-tuple-element.21.rest_ref, ...), custom_call_target="tpu_custom_call" | custom-call | flops 65536 | bytes 262144 | tf_op jit(solution)/shard_map/finish_rate/pallas_call | solution.py:313
  (1 shorter events, 0.0 us)
Async XLA Ops:
  2.4 22.1 %all-to-all-start = ((f32[16,40,128]{2,1,0:T(8,128)}), f32[16,40,128]{2,1,0:T(8,128)S(1)}, u32[]{:S(2)}, u32[]{:S(2)}) async-start(f32[16,40,128]{2,1,0:T(8,128)} %get-tuple-element.16), calls=%async_computation | async-start | bytes 655360 | tf_op jit(solution)/shard_map/all_to_all | solution.py:259
  10.0 22.7 %collective-permute-start = (f32[2,16,128]{2,1,0:T(8,128)}, f32[2,16,128]{2,1,0:T(8,128)S(1)}, u32[]{:S(2)}, u32[]{:S(2)}) collective-permute-start(f32[2,16,128]{2,1,0:T(8,128)} %slab_ref.1), channel_id=1, source_target_pairs={{0,1},{1,2},{2,3},{3,0},{4,5},{5,6},{6,7},{7,4},{8,9},{9,10},{10,1... | collective-permute-start | bytes 49160 | tf_op jit(solution)/shard_map/ppermute | solution.py:260
  11.7 20.9 %collective-permute-start.1 = (f32[2,16,128]{2,1,0:T(8,128)}, f32[2,16,128]{2,1,0:T(8,128)S(1)}, u32[]{:S(2)}, u32[]{:S(2)}) collective-permute-start(f32[2,16,128]{2,1,0:T(8,128)} %slab_ref.1), channel_id=1, source_target_pairs={{0,2},{1,3},{2,0},{3,1},{4,6},{5,7},{6,4},{7,5},{8,10},{9,11},{10,... | collective-permute-start | bytes 49160 | tf_op jit(solution)/shard_map/ppermute | solution.py:260
  14.7 18.0 %collective-permute-start.2 = (f32[2,16,128]{2,1,0:T(8,128)}, f32[2,16,128]{2,1,0:T(8,128)S(1)}, u32[]{:S(2)}, u32[]{:S(2)}) collective-permute-start(f32[2,16,128]{2,1,0:T(8,128)} %slab_ref.1), channel_id=1, source_target_pairs={{0,3},{1,0},{2,1},{3,2},{4,7},{5,4},{6,5},{7,6},{8,11},{9,8},{10,9... | collective-permute-start | bytes 49160 | tf_op jit(solution)/shard_map/ppermute | solution.py:260
  24.5 8.2 %copy-start = (f32[2,16,128]{2,1,0:T(8,128)S(1)}, f32[2,16,128]{2,1,0:T(8,128)}, u32[]{:S(2)}) copy-start(f32[2,16,128]{2,1,0:T(8,128)} %slab_ref.1) | copy-start | bytes 49156
  27.4 12.2 %copy-start.1 = (f32[2,16,128]{2,1,0:T(8,128)S(1)}, f32[2,16,128]{2,1,0:T(8,128)}, u32[]{:S(2)}) copy-start(f32[2,16,128]{2,1,0:T(8,128)} %base_ref.1) | copy-start | bytes 49156
  27.4 12.2 %copy-start.2 = (f32[2,16,128]{2,1,0:T(8,128)S(1)}, f32[2,16,128]{2,1,0:T(8,128)}, u32[]{:S(2)}) copy-start(f32[2,16,128]{2,1,0:T(8,128)} %accum_ref.1) | copy-start | bytes 49156
  27.4 9.2 %collective-permute-start.3 = (f32[2,40,128]{2,1,0:T(8,128)S(1)}, f32[2,40,128]{2,1,0:T(8,128)S(1)}, u32[]{:S(2)}, u32[]{:S(2)}) collective-permute-start(f32[2,40,128]{2,1,0:T(8,128)S(1)} %get-tuple-element.20), channel_id=1, source_target_pairs={{0,8},{8,0},{1,9},{9,1},{2,10},{10,2},{3,11},{11,3},{4,12},{12,4},... | collective-permute-start | bytes 122888 | tf_op jit(solution)/shard_map/ppermute | solution.py:292
  36.6 3.0 %collective-permute-start.4 = (f32[40,128]{1,0:T(8,128)S(1)}, f32[40,128]{1,0:T(8,128)S(1)}, u32[]{:S(2)}, u32[]{:S(2)}) collective-permute-start(f32[40,128]{1,0:T(8,128)S(1)} %fusion), channel_id=1, source_target_pairs={{0,4},{4,0},{1,5},{5,1},{2,6},{6,2},{3,7},{7,3},{8,12},{12,8},{9,1... | collective-permute-start | bytes 61448 | tf_op jit(solution)/shard_map/ppermute | solution.py:311

commit v3 on v2

--- a/solution.py
+++ b/solution.py
@@ -17,6 +17,7 @@
 ROUNDER = 12582912.0
 PART = 40
 WIDE = 48
+GROUPS = 2
 
 
 def horner(coefs, scale, arg):
@@ -80,9 +81,11 @@
     return jnp.broadcast_to(line, (LANES, LANES)).T
 
 
-def fill_tiles(pos_ref, row_ref, high_ref, low_ref, quads, unroll, after=None):
+def fill_tiles(pos_ref, row_ref, high_ref, low_ref, quads, after=None):
     quad = lax.axis_index("zh") * 2 + lax.axis_index("c")
     place = lax.axis_index("yx")
+    tiles = pos_ref.shape[1] // (4 * LANES)
+    strips = 4 * len(quads)
     for n, other in enumerate(quads):
         for k in range(3):
             row_ref[k, n * LANES : (n + 1) * LANES, :] = turned(pos_ref, k, place * 4 + other)
@@ -96,82 +99,92 @@
             dx, dy, dz = [row_ref[k, rows, :] - cols[k] for k in range(3)]
             for part, value in enumerate(coupling(dx, dy, dz)):
                 high, low = split(value)
-                lanes = lanes_at(step * 2 + part)
+                lanes = lanes_at(step + part * tiles)
                 high_ref[rows, lanes] = high
                 low_ref[rows, lanes] = low
             return carry
 
-        lax.fori_loop(0, 4 * len(quads), strip, carry, unroll=unroll)
+        return lax.fori_loop(0, strips, strip, carry, unroll=strips)
+
+    group = tiles // GROUPS
+    for g in range(GROUPS):
+        lax.fori_loop(g * group, (g + 1) * group, tile, 0)
         if after is not None:
-            after(step)
-        return carry
-
-    lax.fori_loop(0, pos_ref.shape[1] // (4 * LANES), tile, 0)
-
-
-def far_kernel(pos_ref, near_ref, low_ref, last_ref, row_ref, high_all, low_all, sems):
+            after(g)
+
+
+def far_kernel(pos_ref, near_ref, low_ref, last_ref, row_ref, low_all, last_all, low_sems, last_sems):
     half, core = lax.axis_index("zh"), lax.axis_index("c")
-    quads = ((1 - half) * 2 + 1 - core, (1 - half) * 2 + core, half * 2 + 1 - core)
-    send = 2 * LANES
-
-    def moves(step):
-        lanes = pl.ds(pl.multiple_of(step * 2 * LANES, 2 * LANES), 2 * LANES)
-        return (
-            pltpu.make_async_copy(high_all.at[pl.ds(0, send), lanes], near_ref.at[:, lanes], sems.at[step, 0]),
-            pltpu.make_async_copy(low_all.at[pl.ds(0, send), lanes], low_ref.at[:, lanes], sems.at[step, 1]),
-            pltpu.make_async_copy(high_all.at[pl.ds(send, LANES), lanes], last_ref.at[0, :, lanes], sems.at[step, 2]),
-            pltpu.make_async_copy(low_all.at[pl.ds(send, LANES), lanes], last_ref.at[1, :, lanes], sems.at[step, 3]),
-        )
-
-    def start(step):
-        for move in moves(step):
+    quad = half * 2 + core
+    deep = near_ref.shape[1]
+    wide = deep // 2 // GROUPS
+
+    def moves(source, target, sems, g):
+        for part in range(2):
+            lanes = pl.ds(part * (deep // 2) + g * wide, wide)
+            yield pltpu.make_async_copy(source.at[..., lanes], target.at[..., lanes], sems.at[g, part])
+
+    def start_low(g):
+        for move in moves(low_all, low_ref, low_sems, g):
             move.start()
 
-    fill_tiles(pos_ref, row_ref, high_all, low_all, quads, 6, start)
-
-    def finish(step, carry):
-        for move in moves(step):
+    def start_last(g):
+        for move in moves(last_all, last_ref, last_sems, g):
+            move.start()
+
+    fill_tiles(pos_ref, row_ref, near_ref, low_all, ((1 - half) * 2 + 1 - core, (1 - half) * 2 + core), start_low)
+    fill_tiles(pos_ref, row_ref, last_all.at[0], last_all.at[1], (half * 2 + 1 - core,), start_last)
+    for g in range(GROUPS):
+        for move in moves(low_all, low_ref, low_sems, g):
             move.wait()
-        return carry
-
-    lax.fori_loop(0, pos_ref.shape[1] // (4 * LANES), finish, 0)
+        for move in moves(last_all, last_ref, last_sems, g):
+            move.wait()
 
 
 def fill_slab(block_ref, y_ref):
-    tiles = block_ref.shape[0]
     zeros = jnp.zeros((16, LANES), jnp.float32)
 
     def fill(step, carry):
         block = block_ref[step]
         pops = jnp.concatenate([block[32:40], zeros[0:8]], axis=0)
-        first, second = block[0:16], block[16:32]
-        for part, rows in enumerate(((first, second, pops), (-second, first, zeros))):
-            lanes = lanes_at(step * 2 + part)
-            for n, value in enumerate(rows):
-                high, low = split(value)
-                y_ref[n * 16 : n * 16 + 16, lanes] = high
-                y_ref[WIDE + n * 16 : WIDE + n * 16 + 16, lanes] = low
-            y_ref[2 * WIDE :, lanes] = jnp.zeros((LANES - 2 * WIDE, LANES), jnp.bfloat16)
+        lanes = lanes_at(step)
+        for n, value in enumerate((block[0:16], block[16:32], pops)):
+            high, low = split(value)
+            y_ref[n * 16 : n * 16 + 16, lanes] = high
+            y_ref[WIDE + n * 16 : WIDE + n * 16 + 16, lanes] = low
+        y_ref[2 * WIDE :, lanes] = jnp.zeros((LANES - 2 * WIDE, LANES), jnp.bfloat16)
         return carry
 
-    lax.fori_loop(0, tiles, fill, 0, unroll=4)
-
-
-def store_products(total, out_ref, at):
-    for n in range(total.shape[0] // LANES):
-        flat = total[n * LANES : (n + 1) * LANES, :].T
-        out_ref[at + n] = flat[0:PART] + flat[WIDE : WIDE + PART]
+    lax.fori_loop(0, block_ref.shape[0], fill, 0, unroll=4)
+
+
+def dot_slab(tiles, y):
+    return lax.dot_general(tiles, y, (((1,), (1,)), ((), ())), preferred_element_type=jnp.float32)
+
+
+def store_products(by_real, by_imag, out_ref, at):
+    for n in range(by_real.shape[0] // LANES):
+        rows = slice(n * LANES, (n + 1) * LANES)
+        real, imag = by_real[rows, :].T, by_imag[rows, :].T
+        real = real[0:PART] + real[WIDE : WIDE + PART]
+        imag = imag[0:32] + imag[WIDE : WIDE + 32]
+        out_ref[at + n, 0:16, :] = real[0:16] - imag[16:32]
+        out_ref[at + n, 16:32, :] = real[16:32] + imag[0:16]
+        out_ref[at + n, 32:PART, :] = real[32:PART]
 
 
 def send_kernel(near_ref, low_ref, block_ref, out_ref, y_ref, low, sem):
     move = pltpu.make_async_copy(low_ref, low, sem)
     move.start()
     fill_slab(block_ref, y_ref)
-    dims = (((1,), (1,)), ((), ()))
-    total = lax.dot_general(near_ref[...], y_ref[...], dims, preferred_element_type=jnp.float32)
+    half = near_ref.shape[1] // 2
+    y = y_ref[...]
+    by_real = dot_slab(near_ref[:, 0:half], y)
+    by_imag = dot_slab(near_ref[:, half:], y)
     move.wait()
-    total += lax.dot_general(low[...], y_ref[...], dims, preferred_element_type=jnp.float32)
-    store_products(total, out_ref, 0)
+    by_real += dot_slab(low[:, 0:half], y)
+    by_imag += dot_slab(low[:, half:], y)
+    store_products(by_real, by_imag, out_ref, 0)
 
 
 def keep_kernel(pos_ref, last_ref, y_ref, slab0, slab1, slab2, slab3, det_ref, out_ref, rest_ref, row_ref, high_ref, low_ref, full_ref, last, sem):
@@ -179,18 +192,20 @@
     move.start()
     own, place = lax.axis_index("zl"), lax.axis_index("yx")
     quad = lax.axis_index("zh") * 2 + lax.axis_index("c")
-    fill_tiles(pos_ref, row_ref, high_ref, low_ref, (quad,), 4)
+    tiles = pos_ref.shape[1] // (4 * LANES)
+    half = tiles * LANES
+    fill_tiles(pos_ref, row_ref, high_ref, low_ref, (quad,))
     eye = lax.broadcasted_iota(jnp.int32, (LANES, LANES), 0) == lax.broadcasted_iota(jnp.int32, (LANES, LANES), 1)
     for part in range(2):
-        lanes = lanes_at(place * 2 + part)
+        lanes = lanes_at(place + part * tiles)
         for ref in (high_ref, low_ref):
             ref[:, lanes] = jnp.where(eye, 0.0, ref[:, lanes].astype(jnp.float32)).astype(jnp.bfloat16)
     move.wait()
-    dims = (((1,), (1,)), ((), ()))
-    for n, (high, low) in enumerate(((last[0], last[1]), (high_ref[...], low_ref[...]))):
-        total = lax.dot_general(high, y_ref[...], dims, preferred_element_type=jnp.float32)
-        total += lax.dot_general(low, y_ref[...], dims, preferred_element_type=jnp.float32)
-        store_products(total, out_ref, n)
+    y = y_ref[...]
+    for n, (high, low) in enumerate(((last.at[0], last.at[1]), (high_ref, low_ref))):
+        by_real = dot_slab(high[:, 0:half], y) + dot_slab(low[:, 0:half], y)
+        by_imag = dot_slab(high[:, half:], y) + dot_slab(low[:, half:], y)
+        store_products(by_real, by_imag, out_ref, n)
 
     start = pl.multiple_of(own * 16, 16)
     offsets = []
@@ -256,8 +271,8 @@
         cost_estimate=pl.CostEstimate(flops=1 << 16, bytes_accessed=1 << 19, transcendentals=0),
         name="pack_block",
     )(in_hbm(section), in_hbm(populations.reshape(1, LANES)), in_hbm(positions), in_hbm(detuning.reshape(1, count)))
+    slabs = [section] + [lax.ppermute(section, "zl", [(i, (i + d) % 4) for i in range(4)]) for d in (1, 2, 3)]
     blocks = lax.all_to_all(copies, "yx", 0, 0, tiled=True)
-    slabs = [section] + [lax.ppermute(section, "zl", [(i, (i + d) % 4) for i in range(4)]) for d in (1, 2, 3)]
 
     near, low, last = pl.pallas_call(
         far_kernel,
@@ -269,10 +284,11 @@
         in_specs=[vmem],
         out_specs=[vmem, hbm, hbm],
         scratch_shapes=[
-            pltpu.VMEM((3, 3 * LANES, LANES), f32),
-            pltpu.VMEM((3 * LANES, deep), bf16),
-            pltpu.VMEM((3 * LANES, deep), bf16),
-            pltpu.SemaphoreType.DMA((tiles, 4)),
+            pltpu.VMEM((3, 2 * LANES, LANES), f32),
+            pltpu.VMEM((2 * LANES, deep), bf16),
+            pltpu.VMEM((2, LANES, deep), bf16),
+            pltpu.SemaphoreType.DMA((GROUPS, 2)),
+            pltpu.SemaphoreType.DMA((GROUPS, 2)),
         ],
         compiler_params=params(12),
         cost_estimate=pl.CostEstimate(flops=45 << 20, bytes_accessed=6 << 20, transcendentals=1 << 20),
@@ -281,7 +297,7 @@
 
     sent, y = pl.pallas_call(
         send_kernel,
-        out_shape=(pltpu.VMEM((2, PART, LANES), f32), pltpu.VMEM((LANES, deep), bf16)),
+        out_shape=(pltpu.VMEM((2, PART, LANES), f32), pltpu.VMEM((LANES, deep // 2), bf16)),
         in_specs=[vmem, hbm, vmem],
         out_specs=[vmem] * 2,
         scratch_shapes=[pltpu.VMEM((2 * LANES, deep), bf16), pltpu.SemaphoreType.DMA],

time: 40.5 us -> 40.1 us (level)
  Pallas kernels: 18.3 us -> 17.8 us
    pallas_call x1, Pallas kernels: 9.04 us -> 8.59 us  [local(): pl.pallas_call(far_kernel, out_shape=(pltpu.VMEM((2 * LANES, deep), bf16)...]
  transfers between devices with their start and end apart: 6 -> 6, of which waited for: 1 -> 1; matrix products, arithmetic and copies ran while one was open for 0% -> 0% of each run, Pallas kernels for 40% -> 39%
where the time goes in v3:
time: 40.1 us; the launch traced here: 39.8 us
  starting transfers between devices  20.4 us (51%)
  Pallas kernels  17.8 us (44%)
  waiting for transfers between devices  0.86 us (2%)
  between operations  0.73 us (2%)
    pallas_call x1, Pallas kernels, local(): pl.pallas_call(far_kernel, out_shape=(pltpu.VMEM((2 * LANES, deep), bf16)...  8.59 us
    all_to_all x1, starting transfers between devices, local(): blocks = lax.all_to_all(copies, 'yx', 0, 0, tiled=True)  7.6 us
    ppermute x3, starting transfers between devices, local(): lax.ppermute(section, 'zl', [(i, (i + d) % 4) for i in range(4)])  5.43 us
    ppermute x1, starting transfers between devices, local(): half = lax.ppermute(sent, 'zh', [(0, 1), (1, 0)])  5.2 us
    pallas_call x1, Pallas kernels, local(): pl.pallas_call(keep_kernel, out_shape=(pltpu.VMEM((2, PART, LANES), f32),...  3.98 us
    pallas_call x1, Pallas kernels, local(): pl.pallas_call(send_kernel, out_shape=(pltpu.VMEM((2, PART, LANES), f32),...  2.91 us
    ppermute x1, starting transfers between devices, local(): core = lax.ppermute(keep[0] + half[0], 'c', [(0, 1), (1, 0)])  2.16 us
    pallas_call x1, Pallas kernels, local(): pl.pallas_call(pack_kernel, out_shape=(jax.ShapeDtypeStruct((tiles, PART,...  1.74 us
  transfers between devices with their start and end apart: 6, of which 1 were waited for; matrix products, arithmetic and copies ran while one was open for 0% of the time, Pallas kernels for 39%

profile of v3, /device:TPU:1, one launch (start us, length us, event | category | flops | bytes accessed | tf_op | source)
XLA Modules:
  0.0 39.8 jit_solution(18444204217468412170)
XLA Ops:
  0.6 1.7 %pack_block.1 = (f32[16,40,128]{2,1,0:T(8,128)}, f32[3,8192]{1,0:T(4,128)S(1)}, f32[8,128]{1,0:T(8,128)S(1)}) custom-call(f32[2,16,128]{2,1,0:T(8,128)} %slab_ref.1, f32[1,128]{1,0:T(1,128)} %bitcast.5, f32[3,8192]{1,0:T(4,128)} %pos_ref.1, f32[1,8192]{1,0:T(1,128)} %bitcast.4), custom_call_target="tpu_custom_call" | custom-call | flops 65536 | bytes 524288 | tf_op jit(solution)/shard_map/pack_block/pallas_call | solution.py:260
  2.4 7.6 %all-to-all-start = ((f32[16,40,128]{2,1,0:T(8,128)}), f32[16,40,128]{2,1,0:T(8,128)S(1)}, u32[]{:S(2)}, u32[]{:S(2)}) async-start(f32[16,40,128]{2,1,0:T(8,128)} %get-tuple-element.16), calls=%async_computation | async-start | bytes 655360 | tf_op jit(solution)/shard_map/all_to_all | solution.py:275
  10.0 1.7 %collective-permute-start = (f32[2,16,128]{2,1,0:T(8,128)}, f32[2,16,128]{2,1,0:T(8,128)S(1)}, u32[]{:S(2)}, u32[]{:S(2)}) collective-permute-start(f32[2,16,128]{2,1,0:T(8,128)} %slab_ref.1), channel_id=1, source_target_pairs={{0,1},{1,2},{2,3},{3,0},{4,5},{5,6},{6,7},{7,4},{8,9},{9,10},{10,1... | collective-permute-start | bytes 49160 | tf_op jit(solution)/shard_map/ppermute | solution.py:274
  11.7 3.0 %collective-permute-start.1 = (f32[2,16,128]{2,1,0:T(8,128)}, f32[2,16,128]{2,1,0:T(8,128)S(1)}, u32[]{:S(2)}, u32[]{:S(2)}) collective-permute-start(f32[2,16,128]{2,1,0:T(8,128)} %slab_ref.1), channel_id=1, source_target_pairs={{0,2},{1,3},{2,0},{3,1},{4,6},{5,7},{6,4},{7,5},{8,10},{9,11},{10,... | collective-permute-start | bytes 49160 | tf_op jit(solution)/shard_map/ppermute | solution.py:274
  14.7 0.7 %collective-permute-start.2 = (f32[2,16,128]{2,1,0:T(8,128)}, f32[2,16,128]{2,1,0:T(8,128)S(1)}, u32[]{:S(2)}, u32[]{:S(2)}) collective-permute-start(f32[2,16,128]{2,1,0:T(8,128)} %slab_ref.1), channel_id=1, source_target_pairs={{0,3},{1,0},{2,1},{3,2},{4,7},{5,4},{6,5},{7,6},{8,11},{9,8},{10,9... | collective-permute-start | bytes 49160 | tf_op jit(solution)/shard_map/ppermute | solution.py:274
  15.4 8.6 %far_tiles.1 = (bf16[256,4096]{1,0:T(8,128)(2,1)S(1)}, bf16[256,4096]{1,0:T(8,128)(2,1)}, bf16[2,128,4096]{2,1,0:T(8,128)(2,1)}) custom-call(f32[3,8192]{1,0:T(4,128)S(1)} %get-tuple-element.12.pos_ref), custom_call_target="tpu_custom_call" | custom-call | flops 47185920 | bytes 6291456 | tf_op jit(solution)/shard_map/far_tiles/pallas_call | solution.py:277
  24.0 0.0 all-to-all-done.block_ref
  24.0 0.0 copy-start
  24.0 2.9 %send_products.1 = (f32[2,40,128]{2,1,0:T(8,128)S(1)}, bf16[128,2048]{1,0:T(8,128)(2,1)S(1)}) custom-call(bf16[256,4096]{1,0:T(8,128)(2,1)S(1)} %get-tuple-element.14.near_ref, bf16[256,4096]{1,0:T(8,128)(2,1)} %get-tuple-element.15.low_ref, f32[16,40,128]{2,1,0:T(8,128)S(1)} %all-to-all-done.block_ref), custom_call_target="tpu_custom_call" | custom-call | flops 536870912 | bytes 4194304 | tf_op jit(solution)/shard_map/send_products/pallas_call | solution.py:298
  27.0 0.0 copy-start.1
  27.0 0.0 copy-start.2
  27.0 5.2 %collective-permute-start.3 = (f32[2,40,128]{2,1,0:T(8,128)S(1)}, f32[2,40,128]{2,1,0:T(8,128)S(1)}, u32[]{:S(2)}, u32[]{:S(2)}) collective-permute-start(f32[2,40,128]{2,1,0:T(8,128)S(1)} %get-tuple-element.20), channel_id=1, source_target_pairs={{0,8},{8,0},{1,9},{9,1},{2,10},{10,2},{3,11},{11,3},{4,12},{12,4},... | collective-permute-start | bytes 122888 | tf_op jit(solution)/shard_map/ppermute | solution.py:308
  32.2 0.0 collective-permute-done.slab1
  32.2 0.0 collective-permute-done.1.slab2
  32.2 0.0 collective-permute-done.2.slab3
  32.2 0.0 copy-done
  32.2 4.0 %keep_products.1 = (f32[2,40,128]{2,1,0:T(8,128)S(1)}, f32[2,16,128]{2,1,0:T(8,128)S(1)}) custom-call(f32[3,8192]{1,0:T(4,128)S(1)} %get-tuple-element.12.pos_ref, bf16[2,128,4096]{2,1,0:T(8,128)(2,1)} %get-tuple-element.13.last_ref, bf16[128,2048]{1,0:T(8,128)(2,1)S(1)} %get-tuple-element.17.y_ref, f32[2,16,128]{2,1,0:T(8,128)S(1)} %copy-done, ...), custom_call_target="tpu_custom_call" | custom-call | flops 536870912 | bytes 4194304 | tf_op jit(solution)/shard_map/keep_products/pallas_call | solution.py:310
  36.2 0.0 collective-permute-done.3.half_ref
  36.2 2.2 %collective-permute-start.4 = (f32[40,128]{1,0:T(8,128)S(1)}, f32[40,128]{1,0:T(8,128)S(1)}, u32[]{:S(2)}, u32[]{:S(2)}) collective-permute-start(f32[40,128]{1,0:T(8,128)S(1)} %fusion), channel_id=1, source_target_pairs={{0,4},{4,0},{1,5},{5,1},{2,6},{6,2},{3,7},{7,3},{8,12},{12,8},{9,1... | collective-permute-start | bytes 61448 | tf_op jit(solution)/shard_map/ppermute | solution.py:327
  38.4 0.8 %collective-permute-done.4.core_ref = f32[40,128]{1,0:T(8,128)S(1)} collective-permute-done((f32[40,128]{1,0:T(8,128)S(1)}, f32[40,128]{1,0:T(8,128)S(1)}, u32[]{:S(2)}, u32[]{:S(2)}) %collective-permute-start.4) | collective-permute-done | bytes 20512 | tf_op jit(solution)/shard_map/ppermute | solution.py:327
  39.2 0.0 copy-done.1
  39.2 0.0 copy-done.2
  39.2 0.6 %finish_rate.1 = (f32[2,16,128]{2,1,0:T(8,128)}, f32[2,16,128]{2,1,0:T(8,128)}) custom-call(f32[2,40,128]{2,1,0:T(8,128)S(1)} %get-tuple-element.19.keep_ref, f32[2,40,128]{2,1,0:T(8,128)S(1)} %collective-permute-done.3.half_ref, f32[40,128]{1,0:T(8,128)S(1)} %collective-permute-done.4.core_ref, f32[2,16,128]{2,1,0:T(8,128)S(1)} %get-tuple-element.21.rest_ref, ...), custom_call_target="tpu_custom_call" | custom-call | flops 65536 | bytes 262144 | tf_op jit(solution)/shard_map/finish_rate/pallas_call | solution.py:329
  (1 shorter events, 0.0 us)
Async XLA Ops:
  2.4 21.6 %all-to-all-start = ((f32[16,40,128]{2,1,0:T(8,128)}), f32[16,40,128]{2,1,0:T(8,128)S(1)}, u32[]{:S(2)}, u32[]{:S(2)}) async-start(f32[16,40,128]{2,1,0:T(8,128)} %get-tuple-element.16), calls=%async_computation | async-start | bytes 655360 | tf_op jit(solution)/shard_map/all_to_all | solution.py:275
  10.0 22.2 %collective-permute-start = (f32[2,16,128]{2,1,0:T(8,128)}, f32[2,16,128]{2,1,0:T(8,128)S(1)}, u32[]{:S(2)}, u32[]{:S(2)}) collective-permute-start(f32[2,16,128]{2,1,0:T(8,128)} %slab_ref.1), channel_id=1, source_target_pairs={{0,1},{1,2},{2,3},{3,0},{4,5},{5,6},{6,7},{7,4},{8,9},{9,10},{10,1... | collective-permute-start | bytes 49160 | tf_op jit(solution)/shard_map/ppermute | solution.py:274
  11.7 20.5 %collective-permute-start.1 = (f32[2,16,128]{2,1,0:T(8,128)}, f32[2,16,128]{2,1,0:T(8,128)S(1)}, u32[]{:S(2)}, u32[]{:S(2)}) collective-permute-start(f32[2,16,128]{2,1,0:T(8,128)} %slab_ref.1), channel_id=1, source_target_pairs={{0,2},{1,3},{2,0},{3,1},{4,6},{5,7},{6,4},{7,5},{8,10},{9,11},{10,... | collective-permute-start | bytes 49160 | tf_op jit(solution)/shard_map/ppermute | solution.py:274
  14.7 17.5 %collective-permute-start.2 = (f32[2,16,128]{2,1,0:T(8,128)}, f32[2,16,128]{2,1,0:T(8,128)S(1)}, u32[]{:S(2)}, u32[]{:S(2)}) collective-permute-start(f32[2,16,128]{2,1,0:T(8,128)} %slab_ref.1), channel_id=1, source_target_pairs={{0,3},{1,0},{2,1},{3,2},{4,7},{5,4},{6,5},{7,6},{8,11},{9,8},{10,9... | collective-permute-start | bytes 49160 | tf_op jit(solution)/shard_map/ppermute | solution.py:274
  24.0 8.2 %copy-start = (f32[2,16,128]{2,1,0:T(8,128)S(1)}, f32[2,16,128]{2,1,0:T(8,128)}, u32[]{:S(2)}) copy-start(f32[2,16,128]{2,1,0:T(8,128)} %slab_ref.1) | copy-start | bytes 49156
  27.0 12.3 %copy-start.1 = (f32[2,16,128]{2,1,0:T(8,128)S(1)}, f32[2,16,128]{2,1,0:T(8,128)}, u32[]{:S(2)}) copy-start(f32[2,16,128]{2,1,0:T(8,128)} %base_ref.1) | copy-start | bytes 49156
  27.0 12.3 %copy-start.2 = (f32[2,16,128]{2,1,0:T(8,128)S(1)}, f32[2,16,128]{2,1,0:T(8,128)}, u32[]{:S(2)}) copy-start(f32[2,16,128]{2,1,0:T(8,128)} %accum_ref.1) | copy-start | bytes 49156
  27.0 9.2 %collective-permute-start.3 = (f32[2,40,128]{2,1,0:T(8,128)S(1)}, f32[2,40,128]{2,1,0:T(8,128)S(1)}, u32[]{:S(2)}, u32[]{:S(2)}) collective-permute-start(f32[2,40,128]{2,1,0:T(8,128)S(1)} %get-tuple-element.20), channel_id=1, source_target_pairs={{0,8},{8,0},{1,9},{9,1},{2,10},{10,2},{3,11},{11,3},{4,12},{12,4},... | collective-permute-start | bytes 122888 | tf_op jit(solution)/shard_map/ppermute | solution.py:308
  36.2 3.0 %collective-permute-start.4 = (f32[40,128]{1,0:T(8,128)S(1)}, f32[40,128]{1,0:T(8,128)S(1)}, u32[]{:S(2)}, u32[]{:S(2)}) collective-permute-start(f32[40,128]{1,0:T(8,128)S(1)} %fusion), channel_id=1, source_target_pairs={{0,4},{4,0},{1,5},{5,1},{2,6},{6,2},{3,7},{7,3},{8,12},{12,8},{9,1... | collective-permute-start | bytes 61448 | tf_op jit(solution)/shard_map/ppermute | solution.py:327

commit v4 on v3

v4 whole, which is shorter than its diff:
```python
import math

import jax
import jax.numpy as jnp
from jax import lax
from jax.experimental import pallas as pl
from jax.experimental.pallas import tpu as pltpu
from jax.sharding import Mesh
from jax.sharding import PartitionSpec as P

TIME_STEP = 0.2
LANES = 128
COS = (0.9999999892, -19.73920453, 64.93911891, -85.45016433, 60.16782231, -25.96827976, 6.529565646)
SIN = (6.283182817, -41.3414213, 81.59618177, -76.58008122, 41.20531753, -12.27114973)
SCALE = -0.75 / (2.0 * math.pi)
INV_WAVE = 1.0 / (2.0 * math.pi)
ROUNDER = 12582912.0
PART = 40
WIDE = 48
EARLY = 160


def horner(coefs, scale, arg):
    total = jnp.float32(coefs[-1] * scale)
    for c in coefs[-2::-1]:
        total = total * arg + jnp.float32(c * scale)
    return total


def coupling(dx, dy, dz):
    dz_sq = dz * dz
    dist_sq = dx * dx + dy * dy + dz_sq
    inv = lax.rsqrt(dist_sq)
    dist = dist_sq * inv
    turn = dist - ((dist + ROUNDER) - ROUNDER)
    turn_sq = turn * turn
    cosine = horner(COS, SCALE, turn_sq) * inv
    sine = horner(SIN, SCALE, turn_sq) * turn * inv
    aligned = dz_sq * (inv * inv)
    quad_imag = inv * (INV_WAVE - (3.0 * INV_WAVE) * aligned)
    quad_real = (1.0 - aligned) - (INV_WAVE * inv) * quad_imag
    return cosine * quad_real - sine * quad_imag, sine * quad_real + cosine * quad_imag


def split(value):
    high = value.astype(jnp.bfloat16)
    low = (value - high.astype(jnp.float32)).astype(jnp.bfloat16)
    return high, low


def lanes_at(index):
    return pl.ds(pl.multiple_of(index * LANES, LANES), LANES)


def pack_kernel(section_ref, pops_ref, pos_ref, det_ref, copies_ref, pos_out, det_out, block_ref, sems):
    own = lax.axis_index("yx") * 4 + lax.axis_index("zh") * 2 + lax.axis_index("c")
    moves = [
        pltpu.make_async_copy(section_ref.at[0], block_ref.at[pl.ds(0, 16)], sems.at[0]),
        pltpu.make_async_copy(section_ref.at[1], block_ref.at[pl.ds(16, 16)], sems.at[1]),
        pltpu.make_async_copy(pops_ref, block_ref.at[pl.ds(32, 1)], sems.at[2]),
        pltpu.make_async_copy(pos_ref, pos_out, sems.at[3]),
        pltpu.make_async_copy(det_ref.at[:, lanes_at(own)], det_out.at[pl.ds(0, 1)], sems.at[4]),
        pltpu.make_async_copy(det_ref.at[:, pl.ds(0, LANES)], det_out.at[pl.ds(1, 1)], sems.at[5]),
    ]
    for move in moves:
        move.start()
    for move in moves[:3]:
        move.wait()
    block = block_ref[0:32, :]
    top = lax.broadcasted_iota(jnp.int32, (8, LANES), 0) == 0
    pops = jnp.where(top, 2.0 * block_ref[32:40, :] - 1.0, 0.0)
    for n in range(copies_ref.shape[0]):
        copies_ref[n, 0:32, :] = block
        copies_ref[n, 32:40, :] = pops
    for move in moves[3:]:
        move.wait()


def turned(pos_ref, k, index):
    line = pos_ref[k : k + 1, lanes_at(index)]
    return jnp.broadcast_to(line, (LANES, LANES)).T


def fill_tiles(pos_ref, row_ref, high_ref, low_ref, quads, first, count):
    quad = lax.axis_index("zh") * 2 + lax.axis_index("c")
    place = lax.axis_index("yx")
    tiles = pos_ref.shape[1] // (4 * LANES)
    for n, other in enumerate(quads):
        for k in range(3):
            row_ref[k, n * LANES : (n + 1) * LANES, :] = turned(pos_ref, k, place * 4 + other)

    def tile(step, carry):
        at = lanes_at(step * 4 + quad)
        cols = [pos_ref[k : k + 1, at] for k in range(3)]
        for n in range(0, count, 32):
            dx, dy, dz = [row_ref[k, first + n : first + n + 32, :] - cols[k] for k in range(3)]
            for part, value in enumerate(coupling(dx, dy, dz)):
                high, low = split(value)
                lanes = lanes_at(step + part * tiles)
                high_ref[n : n + 32, lanes] = high
                low_ref[n : n + 32, lanes] = low
        return carry

    lax.fori_loop(0, tiles, tile, 0)


def slab_term(pos_ref, slabs, det_ref, rest_ref, row_ref, full_ref):
    own = lax.axis_index("zl")
    start = pl.multiple_of(own * 16, 16)
    offsets = []
    for k in range(3):
        row_ref[k, 0:LANES, :] = turned(pos_ref, k, 0)
        offsets.append(row_ref[k, pl.ds(start, 16), :] - pos_ref[k : k + 1, 0:LANES])
    w_real, w_imag = coupling(*offsets)
    eye = (lax.broadcasted_iota(jnp.int32, (16, LANES), 0) + start) == lax.broadcasted_iota(jnp.int32, (16, LANES), 1)
    w_real = jnp.where(eye, det_ref[1:2, :], w_real)[:, 0:64]
    w_imag = jnp.where(eye, -0.5, w_imag)[:, 0:64]
    for n, ref in enumerate(slabs):
        there = pl.ds(pl.multiple_of(lax.rem(own + 4 - n, 4) * 16, 16), 16)
        full_ref[0, there, :] = ref[0]
        full_ref[1, there, :] = ref[1]

    def mul(a, b):
        return jnp.dot(a, b, precision=lax.Precision.HIGHEST, preferred_element_type=jnp.float32)

    v_real = mul(w_real, full_ref[0]) + mul(w_imag, full_ref[1])
    v_imag = mul(w_real, full_ref[1]) - mul(w_imag, full_ref[0])
    y_real, y_imag = slabs[0][0], slabs[0][1]
    line = det_ref[0:1, :]
    rest_ref[0] = line * y_imag - 0.5 * y_real - v_imag
    rest_ref[1] = v_real - line * y_real - 0.5 * y_imag


def far_quads():
    half, core = lax.axis_index("zh"), lax.axis_index("c")
    return (1 - half) * 2 + 1 - core, (1 - half) * 2 + core


def far_kernel(pos_ref, slab0, slab1, slab2, slab3, det_ref, high_ref, low_ref, rest_ref, row_ref, full_ref):
    slab_term(pos_ref, (slab0, slab1, slab2, slab3), det_ref, rest_ref, row_ref, full_ref)
    fill_tiles(pos_ref, row_ref, high_ref, low_ref, far_quads(), 0, EARLY)


def fill_slab(block_ref, y_ref):
    zeros = jnp.zeros((16, LANES), jnp.float32)

    def fill(step, carry):
        block = block_ref[step]
        pops = jnp.concatenate([block[32:40], zeros[0:8]], axis=0)
        lanes = lanes_at(step)
        for n, value in enumerate((block[0:16], block[16:32], pops)):
            high, low = split(value)
            y_ref[n * 16 : n * 16 + 16, lanes] = high
            y_ref[WIDE + n * 16 : WIDE + n * 16 + 16, lanes] = low
        y_ref[2 * WIDE :, lanes] = jnp.zeros((LANES - 2 * WIDE, LANES), jnp.bfloat16)
        return carry

    lax.fori_loop(0, block_ref.shape[0], fill, 0, unroll=4)


def dot_slab(tiles, y):
    return lax.dot_general(tiles, y, (((1,), (1,)), ((), ())), preferred_element_type=jnp.float32)


def store_products(by_real, by_imag, out_ref, at):
    for n in range(by_real.shape[0] // LANES):
        rows = slice(n * LANES, (n + 1) * LANES)
        real, imag = by_real[rows, :].T, by_imag[rows, :].T
        real = real[0:PART] + real[WIDE : WIDE + PART]
        imag = imag[0:32] + imag[WIDE : WIDE + 32]
        out_ref[at + n, 0:16, :] = real[0:16] - imag[16:32]
        out_ref[at + n, 16:32, :] = real[16:32] + imag[0:16]
        out_ref[at + n, 32:PART, :] = real[32:PART]


def products(high_ref, low_ref, y):
    half = high_ref.shape[1] // 2
    by_real = dot_slab(high_ref[:, 0:half], y) + dot_slab(low_ref[:, 0:half], y)
    by_imag = dot_slab(high_ref[:, half:], y) + dot_slab(low_ref[:, half:], y)
    return by_real, by_imag


def send_kernel(pos_ref, high_ref, low_ref, block_ref, out_ref, y_ref, row_ref, more_high, more_low):
    fill_slab(block_ref, y_ref)
    fill_tiles(pos_ref, row_ref, more_high, more_low, far_quads()[1:], EARLY - LANES, 2 * LANES - EARLY)
    y = y_ref[...]
    pairs = zip(products(high_ref, low_ref, y), products(more_high, more_low, y))
    by_real, by_imag = [jnp.concatenate(pair, axis=0) for pair in pairs]
    store_products(by_real, by_imag, out_ref, 0)


def keep_kernel(pos_ref, y_ref, out_ref, row_ref, high_ref, low_ref):
    place = lax.axis_index("yx")
    half, core = lax.axis_index("zh"), lax.axis_index("c")
    tiles = pos_ref.shape[1] // (4 * LANES)
    fill_tiles(pos_ref, row_ref, high_ref, low_ref, (half * 2 + 1 - core, half * 2 + core), 0, 2 * LANES)
    eye = lax.broadcasted_iota(jnp.int32, (LANES, LANES), 0) == lax.broadcasted_iota(jnp.int32, (LANES, LANES), 1)
    for part in range(2):
        lanes = lanes_at(place + part * tiles)
        for ref in (high_ref, low_ref):
            own = ref[LANES:, lanes].astype(jnp.float32)
            ref[LANES:, lanes] = jnp.where(eye, 0.0, own).astype(jnp.bfloat16)
    by_real, by_imag = products(high_ref, low_ref, y_ref[...])
    store_products(by_real, by_imag, out_ref, 0)


def finish_kernel(keep_ref, half_ref, core_ref, rest_ref, slab_ref, base_ref, accum_ref, next_ref, acc_ref):
    z = keep_ref[1] + half_ref[1] + core_ref[...]
    shift = z[32:33]
    rate_real = z[16:32] + shift * slab_ref[1] + rest_ref[0]
    rate_imag = rest_ref[1] - z[0:16] - shift * slab_ref[0]
    for n, rate in enumerate((rate_real, rate_imag)):
        next_ref[n] = base_ref[n] + (0.5 * TIME_STEP) * rate
        acc_ref[n] = accum_ref[n] + (TIME_STEP / 3.0) * rate


def params(mib):
    return pltpu.CompilerParams(vmem_limit_bytes=mib << 20)


def in_hbm(array):
    return pltpu.with_memory_space_constraint(array, pltpu.HBM)


def local(positions, detuning, populations, base, section, accum):
    bf16, f32 = jnp.bfloat16, jnp.float32
    count = positions.shape[1]
    tiles = count // (4 * LANES)
    deep = 2 * tiles * LANES
    hbm, vmem = pl.BlockSpec(memory_space=pltpu.HBM), pl.BlockSpec(memory_space=pltpu.VMEM)

    copies, pos, det = pl.pallas_call(
        pack_kernel,
        out_shape=(
            jax.ShapeDtypeStruct((tiles, PART, LANES), f32),
            pltpu.VMEM(positions.shape, f32),
            pltpu.VMEM((8, LANES), f32),
        ),
        in_specs=[hbm] * 4,
        out_specs=[vmem] * 3,
        scratch_shapes=[pltpu.VMEM((PART, LANES), f32), pltpu.SemaphoreType.DMA((6,))],
        compiler_params=params(4),
        cost_estimate=pl.CostEstimate(flops=1 << 16, bytes_accessed=1 << 19, transcendentals=0),
        name="pack_block",
    )(in_hbm(section), in_hbm(populations.reshape(1, LANES)), in_hbm(positions), in_hbm(detuning.reshape(1, count)))
    slabs = [section] + [lax.ppermute(section, "zl", [(i, (i + d) % 4) for i in range(4)]) for d in (1, 2, 3)]
    copies, *slabs = lax.optimization_barrier((copies, *slabs))
    blocks = lax.all_to_all(copies, "yx", 0, 0, tiled=True)

    high, low, rest = pl.pallas_call(
        far_kernel,
        out_shape=(
            pltpu.VMEM((EARLY, deep), bf16),
            pltpu.VMEM((EARLY, deep), bf16),
            pltpu.VMEM((2, 16, LANES), f32),
        ),
        in_specs=[vmem] * 6,
        out_specs=[vmem] * 3,
        scratch_shapes=[pltpu.VMEM((3, 2 * LANES, LANES), f32), pltpu.VMEM((2, 64, LANES), f32)],
        compiler_params=params(4),
        cost_estimate=pl.CostEstimate(flops=45 << 20, bytes_accessed=6 << 20, transcendentals=1 << 20),
        name="far_tiles",
    )(pos, *slabs, det)

    sent, y = pl.pallas_call(
        send_kernel,
        out_shape=(pltpu.VMEM((2, PART, LANES), f32), pltpu.VMEM((LANES, deep // 2), bf16)),
        in_specs=[vmem] * 4,
        out_specs=[vmem] * 2,
        scratch_shapes=[
            pltpu.VMEM((3, LANES, LANES), f32),
            pltpu.VMEM((2 * LANES - EARLY, deep), bf16),
            pltpu.VMEM((2 * LANES - EARLY, deep), bf16),
        ],
        compiler_params=params(8),
        cost_estimate=pl.CostEstimate(flops=1 << 29, bytes_accessed=4 << 20, transcendentals=0),
        name="send_products",
    )(pos, high, low, blocks)
    half = lax.ppermute(sent, "zh", [(0, 1), (1, 0)])

    keep = pl.pallas_call(
        keep_kernel,
        out_shape=pltpu.VMEM((2, PART, LANES), f32),
        in_specs=[vmem] * 2,
        out_specs=vmem,
        scratch_shapes=[
            pltpu.VMEM((3, 2 * LANES, LANES), f32),
            pltpu.VMEM((2 * LANES, deep), bf16),
            pltpu.VMEM((2 * LANES, deep), bf16),
        ],
        compiler_params=params(8),
        cost_estimate=pl.CostEstimate(flops=1 << 29, bytes_accessed=4 << 20, transcendentals=1 << 20),
        name="keep_products",
    )(pos, y)
    core = lax.ppermute(keep[0] + half[0], "c", [(0, 1), (1, 0)])

    return pl.pallas_call(
        finish_kernel,
        out_shape=(jax.ShapeDtypeStruct(base.shape, f32),) * 2,
        compiler_params=params(4),
        cost_estimate=pl.CostEstimate(flops=1 << 16, bytes_accessed=1 << 18, transcendentals=0),
        name="finish_rate",
    )(keep, half, core, rest, section, base, accum)


def solution(mesh):
    fine = Mesh(mesh.devices.reshape(16, 2, 2, 4), ("yx", "zh", "c", "zl"))
    rows = ("yx", "zh", "c")
    slab = P(None, "zl", rows)
    return jax.shard_map(
        local,
        mesh=fine,
        in_specs=(P(), P(), P(rows), slab, slab, slab),
        out_specs=(slab, slab),
        check_vma=False,
    )
```

time: 40.1 us -> 45.4 us (1.13)
  waiting for transfers between devices: 0.86 us -> 7.14 us
  Pallas kernels: 17.8 us -> 15.4 us
  local copies, waits for them, and re-layouts: 0.02 us -> 0.73 us
  starting transfers between devices: 20.4 us -> 21.1 us
    all_to_all x1, waiting for transfers between devices: 0.01 us -> 3.82 us  [local(): blocks = lax.all_to_all(copies, 'yx', 0, 0, tiled=True)]
    pallas_call x2, Pallas kernels: 12.6 us -> 9.47 us  [the longest x1 6.12 us: local(): pl.pallas_call(keep_kernel, out_shape=pltpu.VMEM((2, PART, LANES), f32),...]
    ppermute x3, waiting for transfers between devices: 0.01 us -> 2.48 us  [local(): lax.ppermute(section, 'zl', [(i, (i + d) % 4) for i in range(4)])]
    ppermute x1, starting transfers between devices: 2.16 us -> 4.18 us  [local(): core = lax.ppermute(keep[0] + half[0], 'c', [(0, 1), (1, 0)])]
    all_to_all x1, starting transfers between devices: 7.6 us -> 6.76 us  [local(): blocks = lax.all_to_all(copies, 'yx', 0, 0, tiled=True)]
    unnamed x6 -> x8, local copies, waits for them, and re-layouts: 0.02 us -> 0.73 us
    pallas_call x1, Pallas kernels: 2.91 us -> 3.55 us  [local(): pl.pallas_call(send_kernel, out_shape=(pltpu.VMEM((2, PART, LANES), f32),...]
    ppermute x1, starting transfers between devices: 5.2 us -> 4.57 us  [local(): half = lax.ppermute(sent, 'zh', [(0, 1), (1, 0)])]
  transfers between devices with their start and end apart: 6 -> 6, of which waited for: 1 -> 4; matrix products, arithmetic and copies ran while one was open for 0% -> 0% of each run, Pallas kernels for 39% -> 25%
where the time goes in v4:
time: 45.4 us; the launch traced here: 45.1 us
  starting transfers between devices  21.1 us (46%)
  Pallas kernels  15.4 us (34%)
  waiting for transfers between devices  7.14 us (16%)
  local copies, waits for them, and re-layouts  0.73 us (2%)
  between operations  0.73 us (2%)
    all_to_all x1, starting transfers between devices, local(): blocks = lax.all_to_all(copies, 'yx', 0, 0, tiled=True)  6.76 us
    pallas_call x1, Pallas kernels, local(): pl.pallas_call(keep_kernel, out_shape=pltpu.VMEM((2, PART, LANES), f32),...  6.12 us
    ppermute x3, starting transfers between devices, local(): lax.ppermute(section, 'zl', [(i, (i + d) % 4) for i in range(4)])  5.64 us
    ppermute x1, starting transfers between devices, local(): half = lax.ppermute(sent, 'zh', [(0, 1), (1, 0)])  4.57 us
    ppermute x1, starting transfers between devices, local(): core = lax.ppermute(keep[0] + half[0], 'c', [(0, 1), (1, 0)])  4.18 us
    all_to_all x1, waiting for transfers between devices, local(): blocks = lax.all_to_all(copies, 'yx', 0, 0, tiled=True)  3.82 us
    pallas_call x1, Pallas kernels, local(): pl.pallas_call(send_kernel, out_shape=(pltpu.VMEM((2, PART, LANES), f32),...  3.55 us
    pallas_call x1, Pallas kernels, local(): pl.pallas_call(far_kernel, out_shape=(pltpu.VMEM((EARLY, deep), bf16), pl...  3.35 us
  transfers between devices with their start and end apart: 6, of which 4 were waited for; matrix products, arithmetic and copies ran while one was open for 0% of the time, Pallas kernels for 25%

profile of v4, /device:TPU:1, one launch (start us, length us, event | category | flops | bytes accessed | tf_op | source)
XLA Modules:
  0.0 45.1 jit_solution(14189194637479260525)
XLA Ops:
  0.6 5.2 %collective-permute-start.2 = (f32[2,16,128]{2,1,0:T(8,128)}, f32[2,16,128]{2,1,0:T(8,128)S(1)}, u32[]{:S(2)}, u32[]{:S(2)}) collective-permute-start(f32[2,16,128]{2,1,0:T(8,128)} %slab_ref.1), channel_id=1, source_target_pairs={{0,3},{1,0},{2,1},{3,2},{4,7},{5,4},{6,5},{7,6},{8,11},{9,8},{10,9... | collective-permute-start | bytes 49160 | tf_op jit(solution)/shard_map/ppermute | solution.py:246
  5.9 0.0 collective-permute-start.1
  5.9 0.4 collective-permute-start
  6.3 1.7 %pack_block.1 = (f32[16,40,128]{2,1,0:T(8,128)}, f32[3,8192]{1,0:T(4,128)S(1)}, f32[8,128]{1,0:T(8,128)S(1)}) custom-call(f32[2,16,128]{2,1,0:T(8,128)} %slab_ref.1, f32[1,128]{1,0:T(1,128)} %bitcast.5, f32[3,8192]{1,0:T(4,128)} %pos_ref.1, f32[1,8192]{1,0:T(1,128)} %bitcast.4), custom_call_target="tpu_custom_call" | custom-call | flops 65536 | bytes 524288 | tf_op jit(solution)/shard_map/pack_block/pallas_call | solution.py:232
  8.0 0.0 collective-permute-done.2.slab3
  8.0 1.7 %collective-permute-done.1.slab2 = f32[2,16,128]{2,1,0:T(8,128)S(1)} collective-permute-done((f32[2,16,128]{2,1,0:T(8,128)}, f32[2,16,128]{2,1,0:T(8,128)S(1)}, u32[]{:S(2)}, u32[]{:S(2)}) %collective-permute-start.1) | collective-permute-done | bytes 16416 | tf_op jit(solution)/shard_map/ppermute | solution.py:246
  9.7 0.7 %collective-permute-done.slab1 = f32[2,16,128]{2,1,0:T(8,128)S(1)} collective-permute-done((f32[2,16,128]{2,1,0:T(8,128)}, f32[2,16,128]{2,1,0:T(8,128)S(1)}, u32[]{:S(2)}, u32[]{:S(2)}) %collective-permute-start) | collective-permute-done | bytes 16416 | tf_op jit(solution)/shard_map/ppermute | solution.py:246
  10.5 6.8 %all-to-all-start = ((f32[16,40,128]{2,1,0:T(8,128)}), f32[16,40,128]{2,1,0:T(8,128)S(1)}, u32[]{:S(2)}, u32[]{:S(2)}) async-start(f32[16,40,128]{2,1,0:T(8,128)} %get-tuple-element.24), calls=%async_computation | async-start | bytes 655360 | tf_op jit(solution)/shard_map/all_to_all | solution.py:248
  17.2 0.0 copy-start
  17.3 0.7 %copy-done = f32[2,16,128]{2,1,0:T(8,128)S(1)} copy-done((f32[2,16,128]{2,1,0:T(8,128)S(1)}, f32[2,16,128]{2,1,0:T(8,128)}, u32[]{:S(2)}) %copy-start) | copy-done | bytes 16408
  18.0 3.4 %far_tiles.1 = (bf16[160,4096]{1,0:T(8,128)(2,1)S(1)}, bf16[160,4096]{1,0:T(8,128)(2,1)S(1)}, f32[2,16,128]{2,1,0:T(8,128)S(1)}) custom-call(f32[3,8192]{1,0:T(4,128)S(1)} %get-tuple-element.15.pos_ref, f32[2,16,128]{2,1,0:T(8,128)S(1)} %copy-done, f32[2,16,128]{2,1,0:T(8,128)S(1)} %collective-permute-done.slab1, ...), custom_call_target="tpu_custom_call" | custom-call | flops 47185920 | bytes 6291456 | tf_op jit(solution)/shard_map/far_tiles/pallas_call | solution.py:250
  21.3 3.8 %all-to-all-done.block_ref = f32[16,40,128]{2,1,0:T(8,128)S(1)} async-done(((f32[16,40,128]{2,1,0:T(8,128)}), f32[16,40,128]{2,1,0:T(8,128)S(1)}, u32[]{:S(2)}, u32[]{:S(2)}) %all-to-all-start) | async-done | bytes 327712 | tf_op jit(solution)/shard_map/all_to_all | solution.py:248
  25.1 3.6 %send_products.1 = (f32[2,40,128]{2,1,0:T(8,128)S(1)}, bf16[128,2048]{1,0:T(8,128)(2,1)S(1)}) custom-call(f32[3,8192]{1,0:T(4,128)S(1)} %get-tuple-element.15.pos_ref, bf16[160,4096]{1,0:T(8,128)(2,1)S(1)} %get-tuple-element.22.high_ref, bf16[160,4096]{1,0:T(8,128)(2,1)S(1)} %get-tuple-element.23.low_ref, f32[16,40,128]{2,1,0:T(8,128)S(1)} %all-to-all-done.block_ref), custom_call_target="tpu_custom_call" | custom-call | flops 536870912 | bytes 4194304 | tf_op jit(solution)/shard_map/send_products/pallas_call | solution.py:265
  28.7 0.0 copy-start.1
  28.7 0.0 copy-start.2
  28.7 0.0 copy-start.3
  28.7 4.6 %collective-permute-start.3 = (f32[2,40,128]{2,1,0:T(8,128)S(1)}, f32[2,40,128]{2,1,0:T(8,128)S(1)}, u32[]{:S(2)}, u32[]{:S(2)}) collective-permute-start(f32[2,40,128]{2,1,0:T(8,128)S(1)} %get-tuple-element.26), channel_id=1, source_target_pairs={{0,8},{8,0},{1,9},{9,1},{2,10},{10,2},{3,11},{11,3},{4,12},{12,4},... | collective-permute-start | bytes 122888 | tf_op jit(solution)/shard_map/ppermute | solution.py:279
  33.3 6.1 %keep_products.1.keep_ref = f32[2,40,128]{2,1,0:T(8,128)S(1)} custom-call(f32[3,8192]{1,0:T(4,128)S(1)} %get-tuple-element.15.pos_ref, bf16[128,2048]{1,0:T(8,128)(2,1)S(1)} %get-tuple-element.25.y_ref), custom_call_target="tpu_custom_call" | custom-call | flops 536870912 | bytes 4194304 | tf_op jit(solution)/shard_map/keep_products/pallas_call | solution.py:281
  39.4 0.0 collective-permute-done.3.half_ref
  39.5 4.2 %collective-permute-start.4 = (f32[40,128]{1,0:T(8,128)S(1)}, f32[40,128]{1,0:T(8,128)S(1)}, u32[]{:S(2)}, u32[]{:S(2)}) collective-permute-start(f32[40,128]{1,0:T(8,128)S(1)} %fusion), channel_id=1, source_target_pairs={{0,4},{4,0},{1,5},{5,1},{2,6},{6,2},{3,7},{7,3},{8,12},{12,8},{9,1... | collective-permute-start | bytes 61448 | tf_op jit(solution)/shard_map/ppermute | solution.py:295
  43.6 0.8 %collective-permute-done.4.core_ref = f32[40,128]{1,0:T(8,128)S(1)} collective-permute-done((f32[40,128]{1,0:T(8,128)S(1)}, f32[40,128]{1,0:T(8,128)S(1)}, u32[]{:S(2)}, u32[]{:S(2)}) %collective-permute-start.4) | collective-permute-done | bytes 20512 | tf_op jit(solution)/shard_map/ppermute | solution.py:295
  44.5 0.0 copy-done.1
  44.5 0.0 copy-done.2
  44.5 0.0 copy-done.3
  44.5 0.6 %finish_rate.1 = (f32[2,16,128]{2,1,0:T(8,128)}, f32[2,16,128]{2,1,0:T(8,128)}) custom-call(f32[2,40,128]{2,1,0:T(8,128)S(1)} %keep_products.1.keep_ref, f32[2,40,128]{2,1,0:T(8,128)S(1)} %collective-permute-done.3.half_ref, f32[40,128]{1,0:T(8,128)S(1)} %collective-permute-done.4.core_ref, f32[2,16,128]{2,1,0:T(8,128)S(1)} %get-tuple-element.27.rest_ref, ...), custom_call_target="tpu_custom_call" | custom-call | flops 65536 | bytes 262144 | tf_op jit(solution)/shard_map/finish_rate/pallas_call | solution.py:297
  (1 shorter events, 0.0 us)
Async XLA Ops:
  0.6 7.4 %collective-permute-start.2 = (f32[2,16,128]{2,1,0:T(8,128)}, f32[2,16,128]{2,1,0:T(8,128)S(1)}, u32[]{:S(2)}, u32[]{:S(2)}) collective-permute-start(f32[2,16,128]{2,1,0:T(8,128)} %slab_ref.1), channel_id=1, source_target_pairs={{0,3},{1,0},{2,1},{3,2},{4,7},{5,4},{6,5},{7,6},{8,11},{9,8},{10,9... | collective-permute-start | bytes 49160 | tf_op jit(solution)/shard_map/ppermute | solution.py:246
  5.9 3.9 %collective-permute-start.1 = (f32[2,16,128]{2,1,0:T(8,128)}, f32[2,16,128]{2,1,0:T(8,128)S(1)}, u32[]{:S(2)}, u32[]{:S(2)}) collective-permute-start(f32[2,16,128]{2,1,0:T(8,128)} %slab_ref.1), channel_id=1, source_target_pairs={{0,2},{1,3},{2,0},{3,1},{4,6},{5,7},{6,4},{7,5},{8,10},{9,11},{10,... | collective-permute-start | bytes 49160 | tf_op jit(solution)/shard_map/ppermute | solution.py:246
  5.9 4.6 %collective-permute-start = (f32[2,16,128]{2,1,0:T(8,128)}, f32[2,16,128]{2,1,0:T(8,128)S(1)}, u32[]{:S(2)}, u32[]{:S(2)}) collective-permute-start(f32[2,16,128]{2,1,0:T(8,128)} %slab_ref.1), channel_id=1, source_target_pairs={{0,1},{1,2},{2,3},{3,0},{4,5},{5,6},{6,7},{7,4},{8,9},{9,10},{10,1... | collective-permute-start | bytes 49160 | tf_op jit(solution)/shard_map/ppermute | solution.py:246
  10.5 14.7 %all-to-all-start = ((f32[16,40,128]{2,1,0:T(8,128)}), f32[16,40,128]{2,1,0:T(8,128)S(1)}, u32[]{:S(2)}, u32[]{:S(2)}) async-start(f32[16,40,128]{2,1,0:T(8,128)} %get-tuple-element.24), calls=%async_computation | async-start | bytes 655360 | tf_op jit(solution)/shard_map/all_to_all | solution.py:248
  17.2 0.7 %copy-start = (f32[2,16,128]{2,1,0:T(8,128)S(1)}, f32[2,16,128]{2,1,0:T(8,128)}, u32[]{:S(2)}) copy-start(f32[2,16,128]{2,1,0:T(8,128)} %slab_ref.1) | copy-start | bytes 49156
  28.7 15.8 %copy-start.1 = (f32[2,16,128]{2,1,0:T(8,128)S(1)}, f32[2,16,128]{2,1,0:T(8,128)}, u32[]{:S(2)}) copy-start(f32[2,16,128]{2,1,0:T(8,128)} %slab_ref.1) | copy-start | bytes 49156
  28.7 15.8 %copy-start.2 = (f32[2,16,128]{2,1,0:T(8,128)S(1)}, f32[2,16,128]{2,1,0:T(8,128)}, u32[]{:S(2)}) copy-start(f32[2,16,128]{2,1,0:T(8,128)} %base_ref.1) | copy-start | bytes 49156
  28.7 15.8 %copy-start.3 = (f32[2,16,128]{2,1,0:T(8,128)S(1)}, f32[2,16,128]{2,1,0:T(8,128)}, u32[]{:S(2)}) copy-start(f32[2,16,128]{2,1,0:T(8,128)} %accum_ref.1) | copy-start | bytes 49156
  28.7 10.7 %collective-permute-start.3 = (f32[2,40,128]{2,1,0:T(8,128)S(1)}, f32[2,40,128]{2,1,0:T(8,128)S(1)}, u32[]{:S(2)}, u32[]{:S(2)}) collective-permute-start(f32[2,40,128]{2,1,0:T(8,128)S(1)} %get-tuple-element.26), channel_id=1, source_target_pairs={{0,8},{8,0},{1,9},{9,1},{2,10},{10,2},{3,11},{11,3},{4,12},{12,4},... | collective-permute-start | bytes 122888 | tf_op jit(solution)/shard_map/ppermute | solution.py:279
  39.5 5.0 %collective-permute-start.4 = (f32[40,128]{1,0:T(8,128)S(1)}, f32[40,128]{1,0:T(8,128)S(1)}, u32[]{:S(2)}, u32[]{:S(2)}) collective-permute-start(f32[40,128]{1,0:T(8,128)S(1)} %fusion), channel_id=1, source_target_pairs={{0,4},{4,0},{1,5},{5,1},{2,6},{6,2},{3,7},{7,3},{8,12},{12,8},{9,1... | collective-permute-start | bytes 61448 | tf_op jit(solution)/shard_map/ppermute | solution.py:295

commit v5 on v4

--- a/solution.py
+++ b/solution.py
@@ -10,7 +10,7 @@
 
 TIME_STEP = 0.2
 LANES = 128
-COS = (0.9999999892, -19.73920453, 64.93911891, -85.45016433, 60.16782231, -25.96827976, 6.529565646)
+COS = (0.9999992211, -19.73898242, 64.92872338, -85.27236068, 58.79387231, -21.07651549)
 SIN = (6.283182817, -41.3414213, 81.59618177, -76.58008122, 41.20531753, -12.27114973)
 SCALE = -0.75 / (2.0 * math.pi)
 INV_WAVE = 1.0 / (2.0 * math.pi)
@@ -34,11 +34,12 @@
     dist = dist_sq * inv
     turn = dist - ((dist + ROUNDER) - ROUNDER)
     turn_sq = turn * turn
-    cosine = horner(COS, SCALE, turn_sq) * inv
-    sine = horner(SIN, SCALE, turn_sq) * turn * inv
-    aligned = dz_sq * (inv * inv)
-    quad_imag = inv * (INV_WAVE - (3.0 * INV_WAVE) * aligned)
-    quad_real = (1.0 - aligned) - (INV_WAVE * inv) * quad_imag
+    cosine = horner(COS, SCALE, turn_sq)
+    sine = horner(SIN, SCALE, turn_sq) * turn
+    inv_sq = inv * inv
+    aligned = dz_sq * inv_sq
+    quad_imag = inv_sq * (INV_WAVE - (3.0 * INV_WAVE) * aligned)
+    quad_real = inv * ((1.0 - aligned) - INV_WAVE * quad_imag)
     return cosine * quad_real - sine * quad_imag, sine * quad_real + cosine * quad_imag
 
 
@@ -104,19 +105,21 @@
     lax.fori_loop(0, tiles, tile, 0)
 
 
-def slab_term(pos_ref, slabs, det_ref, rest_ref, row_ref, full_ref):
+def term_kernel(pos_ref, slab_ref, near_ref, pair_ref, det_ref, rest_ref, row_ref, full_ref):
     own = lax.axis_index("zl")
     start = pl.multiple_of(own * 16, 16)
     offsets = []
     for k in range(3):
-        row_ref[k, 0:LANES, :] = turned(pos_ref, k, 0)
+        row_ref[k] = turned(pos_ref, k, 0)
         offsets.append(row_ref[k, pl.ds(start, 16), :] - pos_ref[k : k + 1, 0:LANES])
     w_real, w_imag = coupling(*offsets)
     eye = (lax.broadcasted_iota(jnp.int32, (16, LANES), 0) + start) == lax.broadcasted_iota(jnp.int32, (16, LANES), 1)
     w_real = jnp.where(eye, det_ref[1:2, :], w_real)[:, 0:64]
     w_imag = jnp.where(eye, -0.5, w_imag)[:, 0:64]
-    for n, ref in enumerate(slabs):
-        there = pl.ds(pl.multiple_of(lax.rem(own + 4 - n, 4) * 16, 16), 16)
+    for n, ref in enumerate((slab_ref, near_ref, pair_ref.at[0], pair_ref.at[1])):
+        place = own + (n % 2) * (1 - 2 * (own % 2))
+        place = place + (n // 2) * (2 - 4 * (own // 2))
+        there = pl.ds(pl.multiple_of(place * 16, 16), 16)
         full_ref[0, there, :] = ref[0]
         full_ref[1, there, :] = ref[1]
 
@@ -125,19 +128,23 @@
 
     v_real = mul(w_real, full_ref[0]) + mul(w_imag, full_ref[1])
     v_imag = mul(w_real, full_ref[1]) - mul(w_imag, full_ref[0])
-    y_real, y_imag = slabs[0][0], slabs[0][1]
+    y_real, y_imag = slab_ref[0], slab_ref[1]
     line = det_ref[0:1, :]
     rest_ref[0] = line * y_imag - 0.5 * y_real - v_imag
     rest_ref[1] = v_real - line * y_real - 0.5 * y_imag
 
 
+def pair_kernel(slab_ref, near_ref, pair_ref):
+    pair_ref[0] = slab_ref[...]
+    pair_ref[1] = near_ref[...]
+
+
 def far_quads():
     half, core = lax.axis_index("zh"), lax.axis_index("c")
     return (1 - half) * 2 + 1 - core, (1 - half) * 2 + core
 
 
-def far_kernel(pos_ref, slab0, slab1, slab2, slab3, det_ref, high_ref, low_ref, rest_ref, row_ref, full_ref):
-    slab_term(pos_ref, (slab0, slab1, slab2, slab3), det_ref, rest_ref, row_ref, full_ref)
+def far_kernel(pos_ref, high_ref, low_ref, row_ref):
     fill_tiles(pos_ref, row_ref, high_ref, low_ref, far_quads(), 0, EARLY)
 
 
@@ -243,28 +250,37 @@
         cost_estimate=pl.CostEstimate(flops=1 << 16, bytes_accessed=1 << 19, transcendentals=0),
         name="pack_block",
     )(in_hbm(section), in_hbm(populations.reshape(1, LANES)), in_hbm(positions), in_hbm(detuning.reshape(1, count)))
-    slabs = [section] + [lax.ppermute(section, "zl", [(i, (i + d) % 4) for i in range(4)]) for d in (1, 2, 3)]
-    copies, *slabs = lax.optimization_barrier((copies, *slabs))
     blocks = lax.all_to_all(copies, "yx", 0, 0, tiled=True)
-
-    high, low, rest = pl.pallas_call(
+    near = lax.ppermute(section, "zl", [(i, i ^ 1) for i in range(4)])
+
+    pair = pl.pallas_call(
+        pair_kernel,
+        out_shape=pltpu.VMEM((2, 2, 16, LANES), f32),
+        in_specs=[vmem] * 2,
+        out_specs=vmem,
+        compiler_params=params(1),
+        cost_estimate=pl.CostEstimate(flops=1, bytes_accessed=1 << 16, transcendentals=0),
+        name="pair_blocks",
+    )(section, near)
+    pair = lax.ppermute(pair, "zl", [(i, i ^ 2) for i in range(4)])
+
+    high, low = pl.pallas_call(
         far_kernel,
-        out_shape=(
-            pltpu.VMEM((EARLY, deep), bf16),
-            pltpu.VMEM((EARLY, deep), bf16),
-            pltpu.VMEM((2, 16, LANES), f32),
-        ),
-        in_specs=[vmem] * 6,
-        out_specs=[vmem] * 3,
-        scratch_shapes=[pltpu.VMEM((3, 2 * LANES, LANES), f32), pltpu.VMEM((2, 64, LANES), f32)],
+        out_shape=(pltpu.VMEM((EARLY, deep), bf16),) * 2,
+        in_specs=[vmem],
+        out_specs=[vmem] * 2,
+        scratch_shapes=[pltpu.VMEM((3, 2 * LANES, LANES), f32)],
         compiler_params=params(4),
         cost_estimate=pl.CostEstimate(flops=45 << 20, bytes_accessed=6 << 20, transcendentals=1 << 20),
         name="far_tiles",
-    )(pos, *slabs, det)
+    )(pos)
 
     sent, y = pl.pallas_call(
         send_kernel,
-        out_shape=(pltpu.VMEM((2, PART, LANES), f32), pltpu.VMEM((LANES, deep // 2), bf16)),
+        out_shape=(
+            pltpu.VMEM((2, PART, LANES), f32),
+            pltpu.VMEM((LANES, deep // 2), bf16),
+        ),
         in_specs=[vmem] * 4,
         out_specs=[vmem] * 2,
         scratch_shapes=[
@@ -293,6 +309,16 @@
         name="keep_products",
     )(pos, y)
     core = lax.ppermute(keep[0] + half[0], "c", [(0, 1), (1, 0)])
+    rest = pl.pallas_call(
+        term_kernel,
+        out_shape=pltpu.VMEM((2, 16, LANES), f32),
+        in_specs=[vmem] * 5,
+        out_specs=vmem,
+        scratch_shapes=[pltpu.VMEM((3, LANES, LANES), f32), pltpu.VMEM((2, 64, LANES), f32)],
+        compiler_params=params(4),
+        cost_estimate=pl.CostEstimate(flops=1 << 22, bytes_accessed=1 << 18, transcendentals=1 << 11),
+        name="slab_term",
+    )(pos, section, near, pair, det)
 
     return pl.pallas_call(
         finish_kernel,

time: 45.4 us -> 38.8 us (0.85)
  waiting for transfers between devices: 7.14 us -> 1.12 us
  local copies, waits for them, and re-layouts: 0.73 us -> 0.02 us
  starting transfers between devices: 21.1 us -> 21.6 us
    all_to_all x1, waiting for transfers between devices: 3.82 us -> 0.59 us  [local(): blocks = lax.all_to_all(copies, 'yx', 0, 0, tiled=True)]
    ppermute x3 -> x2, waiting for transfers between devices: 2.48 us -> 0.01 us  [the longest x1 0.01 us: local(): near = lax.ppermute(section, 'zl', [(i, i ^ 1) for i in range(4)])]
    ppermute x1, starting transfers between devices: 4.57 us -> 7 us  [local(): half = lax.ppermute(sent, 'zh', [(0, 1), (1, 0)])]
    ppermute x1, starting transfers between devices: 4.18 us -> 2.23 us  [local(): core = lax.ppermute(keep[0] + half[0], 'c', [(0, 1), (1, 0)])]
    all_to_all x1, starting transfers between devices: 6.76 us -> 7.6 us  [local(): blocks = lax.all_to_all(copies, 'yx', 0, 0, tiled=True)]
    ppermute x3 -> x2, starting transfers between devices: 5.64 us -> 4.8 us  [the longest x1 3.08 us: local(): pair = lax.ppermute(pair, 'zl', [(i, i ^ 2) for i in range(4)])]
    unnamed x8 -> x6, local copies, waits for them, and re-layouts: 0.73 us -> 0.02 us
    pallas_call x1 -> x3, Pallas kernels: 3.35 us -> 3.36 us  [the longest x1 3.05 us: local(): pl.pallas_call(far_kernel, out_shape=(pltpu.VMEM((EARLY, deep), bf16),) *...]
  transfers between devices with their start and end apart: 6 -> 5, of which waited for: 4 -> 2; matrix products, arithmetic and copies ran while one was open for 0% -> 0% of each run, Pallas kernels for 25% -> 33%
where the time goes in v5:
time: 38.8 us; the launch traced here: 38.6 us
  starting transfers between devices  21.6 us (56%)
  Pallas kernels  15.1 us (39%)
  waiting for transfers between devices  1.12 us (3%)
  between operations  0.73 us (2%)
    all_to_all x1, starting transfers between devices, local(): blocks = lax.all_to_all(copies, 'yx', 0, 0, tiled=True)  7.6 us
    ppermute x1, starting transfers between devices, local(): half = lax.ppermute(sent, 'zh', [(0, 1), (1, 0)])  7 us
    pallas_call x1, Pallas kernels, local(): pl.pallas_call(keep_kernel, out_shape=pltpu.VMEM((2, PART, LANES), f32),...  5.82 us
    pallas_call x1, Pallas kernels, local(): pl.pallas_call(send_kernel, out_shape=(pltpu.VMEM((2, PART, LANES), f32),...  3.52 us
    ppermute x1, starting transfers between devices, local(): pair = lax.ppermute(pair, 'zl', [(i, i ^ 2) for i in range(4)])  3.08 us
    pallas_call x1, Pallas kernels, local(): pl.pallas_call(far_kernel, out_shape=(pltpu.VMEM((EARLY, deep), bf16),) *...  3.05 us
    ppermute x1, starting transfers between devices, local(): core = lax.ppermute(keep[0] + half[0], 'c', [(0, 1), (1, 0)])  2.23 us
    pallas_call x1, Pallas kernels, local(): pl.pallas_call(pack_kernel, out_shape=(jax.ShapeDtypeStruct((tiles, PART,...  1.74 us
  transfers between devices with their start and end apart: 5, of which 2 were waited for; matrix products, arithmetic and copies ran while one was open for 0% of the time, Pallas kernels for 33%

profile of v5, /device:TPU:1, one launch (start us, length us, event | category | flops | bytes accessed | tf_op | source)
XLA Modules:
  0.0 38.6 jit_solution(7041275277371030140)
XLA Ops:
  0.6 1.7 %pack_block.1 = (f32[16,40,128]{2,1,0:T(8,128)}, f32[3,8192]{1,0:T(4,128)S(1)}, f32[8,128]{1,0:T(8,128)S(1)}) custom-call(f32[2,16,128]{2,1,0:T(8,128)} %slab_ref.5, f32[1,128]{1,0:T(1,128)} %bitcast.5, f32[3,8192]{1,0:T(4,128)} %pos_ref.1, f32[1,8192]{1,0:T(1,128)} %bitcast.4), custom_call_target="tpu_custom_call" | custom-call | flops 65536 | bytes 524288 | tf_op jit(solution)/shard_map/pack_block/pallas_call | solution.py:239
  2.4 0.0 copy-start
  2.4 7.6 %all-to-all-start = ((f32[16,40,128]{2,1,0:T(8,128)}), f32[16,40,128]{2,1,0:T(8,128)S(1)}, u32[]{:S(2)}, u32[]{:S(2)}) async-start(f32[16,40,128]{2,1,0:T(8,128)} %get-tuple-element.12), calls=%async_computation | async-start | bytes 655360 | tf_op jit(solution)/shard_map/all_to_all | solution.py:253
  10.0 1.7 %collective-permute-start.2 = (f32[2,16,128]{2,1,0:T(8,128)}, f32[2,16,128]{2,1,0:T(8,128)S(1)}, u32[]{:S(2)}, u32[]{:S(2)}) collective-permute-start(f32[2,16,128]{2,1,0:T(8,128)} %slab_ref.5), channel_id=1, source_target_pairs={{0,1},{1,0},{2,3},{3,2},{4,5},{5,4},{6,7},{7,6},{8,9},{9,8},{10,11... | collective-permute-start | bytes 49160 | tf_op jit(solution)/shard_map/ppermute | solution.py:254
  11.7 3.0 %far_tiles.1 = (bf16[160,4096]{1,0:T(8,128)(2,1)S(1)}, bf16[160,4096]{1,0:T(8,128)(2,1)S(1)}) custom-call(f32[3,8192]{1,0:T(4,128)S(1)} %get-tuple-element.9.pos_ref), custom_call_target="tpu_custom_call" | custom-call | flops 47185920 | bytes 6291456 | tf_op jit(solution)/shard_map/far_tiles/pallas_call | solution.py:267
  14.8 0.0 collective-permute-done.2.near_ref
  14.8 0.0 copy-done
  14.8 3.1 %collective-permute-start.3 = (f32[2,2,16,128]{3,2,1,0:T(8,128)S(1)}, f32[2,2,16,128]{3,2,1,0:T(8,128)S(1)}, u32[]{:S(2)}, u32[]{:S(2)}) collective-permute-start(f32[2,2,16,128]{3,2,1,0:T(8,128)S(1)} %pair_blocks.1), channel_id=1, source_target_pairs={{0,2},{1,3},{2,0},{3,1},{4,6},{5,7},{6,4},{7,5},{8,10},{9,11},{10,... | collective-permute-start | bytes 98312 | tf_op jit(solution)/shard_map/ppermute | solution.py:265
  17.9 0.6 %all-to-all-done.block_ref = f32[16,40,128]{2,1,0:T(8,128)S(1)} async-done(((f32[16,40,128]{2,1,0:T(8,128)}), f32[16,40,128]{2,1,0:T(8,128)S(1)}, u32[]{:S(2)}, u32[]{:S(2)}) %all-to-all-start) | async-done | bytes 327712 | tf_op jit(solution)/shard_map/all_to_all | solution.py:253
  18.5 3.5 %send_products.1 = (f32[2,40,128]{2,1,0:T(8,128)S(1)}, bf16[128,2048]{1,0:T(8,128)(2,1)S(1)}) custom-call(f32[3,8192]{1,0:T(4,128)S(1)} %get-tuple-element.9.pos_ref, bf16[160,4096]{1,0:T(8,128)(2,1)S(1)} %get-tuple-element.10.high_ref, bf16[160,4096]{1,0:T(8,128)(2,1)S(1)} %get-tuple-element.11.low_ref, f32[16,40,128]{2,1,0:T(8,128)S(1)} %all-to-all-done.block_ref), custom_call_target="tpu_custom_call" | custom-call | flops 536870912 | bytes 4194304 | tf_op jit(solution)/shard_map/send_products/pallas_call | solution.py:278
  22.0 0.0 copy-start.1
  22.0 0.0 copy-start.2
  22.0 7.0 %collective-permute-start = (f32[2,40,128]{2,1,0:T(8,128)S(1)}, f32[2,40,128]{2,1,0:T(8,128)S(1)}, u32[]{:S(2)}, u32[]{:S(2)}) collective-permute-start(f32[2,40,128]{2,1,0:T(8,128)S(1)} %get-tuple-element.14), channel_id=1, source_target_pairs={{0,8},{8,0},{1,9},{9,1},{2,10},{10,2},{3,11},{11,3},{4,12},{12,4},... | collective-permute-start | bytes 122888 | tf_op jit(solution)/shard_map/ppermute | solution.py:295
  29.0 5.8 %keep_products.1.keep_ref = f32[2,40,128]{2,1,0:T(8,128)S(1)} custom-call(f32[3,8192]{1,0:T(4,128)S(1)} %get-tuple-element.9.pos_ref, bf16[128,2048]{1,0:T(8,128)(2,1)S(1)} %get-tuple-element.13.y_ref), custom_call_target="tpu_custom_call" | custom-call | flops 536870912 | bytes 4194304 | tf_op jit(solution)/shard_map/keep_products/pallas_call | solution.py:297
  34.8 0.0 collective-permute-done.half_ref
  34.9 2.2 %collective-permute-start.1 = (f32[40,128]{1,0:T(8,128)S(1)}, f32[40,128]{1,0:T(8,128)S(1)}, u32[]{:S(2)}, u32[]{:S(2)}) collective-permute-start(f32[40,128]{1,0:T(8,128)S(1)} %fusion), channel_id=1, source_target_pairs={{0,4},{4,0},{1,5},{5,1},{2,6},{6,2},{3,7},{7,3},{8,12},{12,8},{9,1... | collective-permute-start | bytes 61448 | tf_op jit(solution)/shard_map/ppermute | solution.py:311
  37.1 0.0 collective-permute-done.3.pair_ref
  37.1 0.3 slab_term.1.rest_ref
  37.4 0.5 %collective-permute-done.1.core_ref = f32[40,128]{1,0:T(8,128)S(1)} collective-permute-done((f32[40,128]{1,0:T(8,128)S(1)}, f32[40,128]{1,0:T(8,128)S(1)}, u32[]{:S(2)}, u32[]{:S(2)}) %collective-permute-start.1) | collective-permute-done | bytes 20512 | tf_op jit(solution)/shard_map/ppermute | solution.py:311
  37.9 0.0 copy-done.1
  37.9 0.0 copy-done.2
  37.9 0.6 %finish_rate.1 = (f32[2,16,128]{2,1,0:T(8,128)}, f32[2,16,128]{2,1,0:T(8,128)}) custom-call(f32[2,40,128]{2,1,0:T(8,128)S(1)} %keep_products.1.keep_ref, f32[2,40,128]{2,1,0:T(8,128)S(1)} %collective-permute-done.half_ref, f32[40,128]{1,0:T(8,128)S(1)} %collective-permute-done.1.core_ref, f32[2,16,128]{2,1,0:T(8,128)S(1)} %slab_term.1.rest_ref, ...), custom_call_target="tpu_custom_call" | custom-call | flops 65536 | bytes 262144 | tf_op jit(solution)/shard_map/finish_rate/pallas_call | solution.py:323
  (2 shorter events, 0.0 us)
Async XLA Ops:
  2.4 12.4 %copy-start = (f32[2,16,128]{2,1,0:T(8,128)S(1)}, f32[2,16,128]{2,1,0:T(8,128)}, u32[]{:S(2)}) copy-start(f32[2,16,128]{2,1,0:T(8,128)} %slab_ref.5) | copy-start | bytes 49156
  2.4 16.1 %all-to-all-start = ((f32[16,40,128]{2,1,0:T(8,128)}), f32[16,40,128]{2,1,0:T(8,128)S(1)}, u32[]{:S(2)}, u32[]{:S(2)}) async-start(f32[16,40,128]{2,1,0:T(8,128)} %get-tuple-element.12), calls=%async_computation | async-start | bytes 655360 | tf_op jit(solution)/shard_map/all_to_all | solution.py:253
  10.0 4.8 %collective-permute-start.2 = (f32[2,16,128]{2,1,0:T(8,128)}, f32[2,16,128]{2,1,0:T(8,128)S(1)}, u32[]{:S(2)}, u32[]{:S(2)}) collective-permute-start(f32[2,16,128]{2,1,0:T(8,128)} %slab_ref.5), channel_id=1, source_target_pairs={{0,1},{1,0},{2,3},{3,2},{4,5},{5,4},{6,7},{7,6},{8,9},{9,8},{10,11... | collective-permute-start | bytes 49160 | tf_op jit(solution)/shard_map/ppermute | solution.py:254
  14.8 22.3 %collective-permute-start.3 = (f32[2,2,16,128]{3,2,1,0:T(8,128)S(1)}, f32[2,2,16,128]{3,2,1,0:T(8,128)S(1)}, u32[]{:S(2)}, u32[]{:S(2)}) collective-permute-start(f32[2,2,16,128]{3,2,1,0:T(8,128)S(1)} %pair_blocks.1), channel_id=1, source_target_pairs={{0,2},{1,3},{2,0},{3,1},{4,6},{5,7},{6,4},{7,5},{8,10},{9,11},{10,... | collective-permute-start | bytes 98312 | tf_op jit(solution)/shard_map/ppermute | solution.py:265
  22.0 16.0 %copy-start.1 = (f32[2,16,128]{2,1,0:T(8,128)S(1)}, f32[2,16,128]{2,1,0:T(8,128)}, u32[]{:S(2)}) copy-start(f32[2,16,128]{2,1,0:T(8,128)} %base_ref.1) | copy-start | bytes 49156
  22.0 15.9 %copy-start.2 = (f32[2,16,128]{2,1,0:T(8,128)S(1)}, f32[2,16,128]{2,1,0:T(8,128)}, u32[]{:S(2)}) copy-start(f32[2,16,128]{2,1,0:T(8,128)} %accum_ref.1) | copy-start | bytes 49156
  22.0 12.8 %collective-permute-start = (f32[2,40,128]{2,1,0:T(8,128)S(1)}, f32[2,40,128]{2,1,0:T(8,128)S(1)}, u32[]{:S(2)}, u32[]{:S(2)}) collective-permute-start(f32[2,40,128]{2,1,0:T(8,128)S(1)} %get-tuple-element.14), channel_id=1, source_target_pairs={{0,8},{8,0},{1,9},{9,1},{2,10},{10,2},{3,11},{11,3},{4,12},{12,4},... | collective-permute-start | bytes 122888 | tf_op jit(solution)/shard_map/ppermute | solution.py:295
  34.9 3.1 %collective-permute-start.1 = (f32[40,128]{1,0:T(8,128)S(1)}, f32[40,128]{1,0:T(8,128)S(1)}, u32[]{:S(2)}, u32[]{:S(2)}) collective-permute-start(f32[40,128]{1,0:T(8,128)S(1)} %fusion), channel_id=1, source_target_pairs={{0,4},{4,0},{1,5},{5,1},{2,6},{6,2},{3,7},{7,3},{8,12},{12,8},{9,1... | collective-permute-start | bytes 61448 | tf_op jit(solution)/shard_map/ppermute | solution.py:311

commit v6 on v5

--- a/solution.py
+++ b/solution.py
@@ -17,7 +17,7 @@
 ROUNDER = 12582912.0
 PART = 40
 WIDE = 48
-EARLY = 160
+EARLY = 176
 
 
 def horner(coefs, scale, arg):
@@ -94,12 +94,13 @@
         at = lanes_at(step * 4 + quad)
         cols = [pos_ref[k : k + 1, at] for k in range(3)]
         for n in range(0, count, 32):
-            dx, dy, dz = [row_ref[k, first + n : first + n + 32, :] - cols[k] for k in range(3)]
+            size = min(32, count - n)
+            dx, dy, dz = [row_ref[k, first + n : first + n + size, :] - cols[k] for k in range(3)]
             for part, value in enumerate(coupling(dx, dy, dz)):
                 high, low = split(value)
                 lanes = lanes_at(step + part * tiles)
-                high_ref[n : n + 32, lanes] = high
-                low_ref[n : n + 32, lanes] = low
+                high_ref[n : n + size, lanes] = high
+                low_ref[n : n + size, lanes] = low
         return carry
 
     lax.fori_loop(0, tiles, tile, 0)
@@ -134,14 +135,22 @@
     rest_ref[1] = v_real - line * y_real - 0.5 * y_imag
 
 
-def pair_kernel(slab_ref, near_ref, pair_ref):
-    pair_ref[0] = slab_ref[...]
-    pair_ref[1] = near_ref[...]
-
-
 def far_quads():
     half, core = lax.axis_index("zh"), lax.axis_index("c")
     return (1 - half) * 2 + 1 - core, (1 - half) * 2 + core
+
+
+def fill_own(pos_ref, row_ref, high_ref, low_ref):
+    place = lax.axis_index("yx")
+    half, core = lax.axis_index("zh"), lax.axis_index("c")
+    tiles = pos_ref.shape[1] // (4 * LANES)
+    fill_tiles(pos_ref, row_ref, high_ref, low_ref, (half * 2 + 1 - core, half * 2 + core), 0, 2 * LANES)
+    eye = lax.broadcasted_iota(jnp.int32, (LANES, LANES), 0) == lax.broadcasted_iota(jnp.int32, (LANES, LANES), 1)
+    for part in range(2):
+        lanes = lanes_at(place + part * tiles)
+        for ref in (high_ref, low_ref):
+            own = ref[LANES:, lanes].astype(jnp.float32)
+            ref[LANES:, lanes] = jnp.where(eye, 0.0, own).astype(jnp.bfloat16)
 
 
 def far_kernel(pos_ref, high_ref, low_ref, row_ref):
@@ -187,7 +196,7 @@
     return by_real, by_imag
 
 
-def send_kernel(pos_ref, high_ref, low_ref, block_ref, out_ref, y_ref, row_ref, more_high, more_low):
+def send_kernel(pos_ref, high_ref, low_ref, block_ref, out_ref, y_ref, own_high, own_low, row_ref, more_high, more_low):
     fill_slab(block_ref, y_ref)
     fill_tiles(pos_ref, row_ref, more_high, more_low, far_quads()[1:], EARLY - LANES, 2 * LANES - EARLY)
     y = y_ref[...]
@@ -195,20 +204,27 @@
     by_real, by_imag = [jnp.concatenate(pair, axis=0) for pair in pairs]
     store_products(by_real, by_imag, out_ref, 0)
 
-
-def keep_kernel(pos_ref, y_ref, out_ref, row_ref, high_ref, low_ref):
-    place = lax.axis_index("yx")
-    half, core = lax.axis_index("zh"), lax.axis_index("c")
-    tiles = pos_ref.shape[1] // (4 * LANES)
-    fill_tiles(pos_ref, row_ref, high_ref, low_ref, (half * 2 + 1 - core, half * 2 + core), 0, 2 * LANES)
-    eye = lax.broadcasted_iota(jnp.int32, (LANES, LANES), 0) == lax.broadcasted_iota(jnp.int32, (LANES, LANES), 1)
-    for part in range(2):
-        lanes = lanes_at(place + part * tiles)
-        for ref in (high_ref, low_ref):
-            own = ref[LANES:, lanes].astype(jnp.float32)
-            ref[LANES:, lanes] = jnp.where(eye, 0.0, own).astype(jnp.bfloat16)
-    by_real, by_imag = products(high_ref, low_ref, y_ref[...])
-    store_products(by_real, by_imag, out_ref, 0)
+    @pl.when(lax.axis_index("zh") == 0)
+    def _():
+        fill_own(pos_ref, row_ref, own_high, own_low)
+
+
+def keep_kernel(pos_ref, y_ref, done_high, done_low, slab_ref, near_ref, out_ref, pair_ref, row_ref, high_ref, low_ref):
+    pair_ref[0] = slab_ref[...]
+    pair_ref[1] = near_ref[...]
+
+    def finish(high, low):
+        by_real, by_imag = products(high, low, y_ref[...])
+        store_products(by_real, by_imag, out_ref, 0)
+
+    @pl.when(lax.axis_index("zh") == 0)
+    def _():
+        finish(done_high, done_low)
+
+    @pl.when(lax.axis_index("zh") == 1)
+    def _():
+        fill_own(pos_ref, row_ref, high_ref, low_ref)
+        finish(high_ref, low_ref)
 
 
 def finish_kernel(keep_ref, half_ref, core_ref, rest_ref, slab_ref, base_ref, accum_ref, next_ref, acc_ref):
@@ -253,17 +269,6 @@
     blocks = lax.all_to_all(copies, "yx", 0, 0, tiled=True)
     near = lax.ppermute(section, "zl", [(i, i ^ 1) for i in range(4)])
 
-    pair = pl.pallas_call(
-        pair_kernel,
-        out_shape=pltpu.VMEM((2, 2, 16, LANES), f32),
-        in_specs=[vmem] * 2,
-        out_specs=vmem,
-        compiler_params=params(1),
-        cost_estimate=pl.CostEstimate(flops=1, bytes_accessed=1 << 16, transcendentals=0),
-        name="pair_blocks",
-    )(section, near)
-    pair = lax.ppermute(pair, "zl", [(i, i ^ 2) for i in range(4)])
-
     high, low = pl.pallas_call(
         far_kernel,
         out_shape=(pltpu.VMEM((EARLY, deep), bf16),) * 2,
@@ -275,16 +280,18 @@
         name="far_tiles",
     )(pos)
 
-    sent, y = pl.pallas_call(
+    sent, y, own_high, own_low = pl.pallas_call(
         send_kernel,
         out_shape=(
             pltpu.VMEM((2, PART, LANES), f32),
             pltpu.VMEM((LANES, deep // 2), bf16),
+            pltpu.VMEM((2 * LANES, deep), bf16),
+            pltpu.VMEM((2 * LANES, deep), bf16),
         ),
         in_specs=[vmem] * 4,
-        out_specs=[vmem] * 2,
+        out_specs=[vmem] * 4,
         scratch_shapes=[
-            pltpu.VMEM((3, LANES, LANES), f32),
+            pltpu.VMEM((3, 2 * LANES, LANES), f32),
             pltpu.VMEM((2 * LANES - EARLY, deep), bf16),
             pltpu.VMEM((2 * LANES - EARLY, deep), bf16),
         ],
@@ -294,11 +301,11 @@
     )(pos, high, low, blocks)
     half = lax.ppermute(sent, "zh", [(0, 1), (1, 0)])
 
-    keep = pl.pallas_call(
+    keep, pair = pl.pallas_call(
         keep_kernel,
-        out_shape=pltpu.VMEM((2, PART, LANES), f32),
-        in_specs=[vmem] * 2,
-        out_specs=vmem,
+        out_shape=(pltpu.VMEM((2, PART, LANES), f32), pltpu.VMEM((2, 2, 16, LANES), f32)),
+        in_specs=[vmem] * 6,
+        out_specs=[vmem] * 2,
         scratch_shapes=[
             pltpu.VMEM((3, 2 * LANES, LANES), f32),
             pltpu.VMEM((2 * LANES, deep), bf16),
@@ -307,7 +314,8 @@
         compiler_params=params(8),
         cost_estimate=pl.CostEstimate(flops=1 << 29, bytes_accessed=4 << 20, transcendentals=1 << 20),
         name="keep_products",
-    )(pos, y)
+    )(pos, y, own_high, own_low, section, near)
+    pair = lax.ppermute(pair, "zl", [(i, i ^ 2) for i in range(4)])
     core = lax.ppermute(keep[0] + half[0], "c", [(0, 1), (1, 0)])
     rest = pl.pallas_call(
         term_kernel,

time: 38.8 us -> 40.2 us (1.036)
  the two profiles are of different devices: /device:TPU:1 before, /device:TPU:224 now
where the time goes in v6:
time: 40.2 us; the launch traced here: 40.1 us
  Pallas kernels  15.1 us (38%)
  starting transfers between devices  14.3 us (36%)
  waiting for transfers between devices  9.81 us (24%)
  between operations  0.74 us (2%)
    all_to_all x1, starting transfers between devices, local(): blocks = lax.all_to_all(copies, 'yx', 0, 0, tiled=True)  7.05 us
    ppermute x1, starting transfers between devices, local(): half = lax.ppermute(sent, 'zh', [(0, 1), (1, 0)])  6.02 us
    pallas_call x1, Pallas kernels, local(): pl.pallas_call(keep_kernel, out_shape=(pltpu.VMEM((2, PART, LANES), f32),...  5.86 us
    all_to_all x1, waiting for transfers between devices, local(): blocks = lax.all_to_all(copies, 'yx', 0, 0, tiled=True)  5.12 us
    ppermute x1, waiting for transfers between devices, local(): pair = lax.ppermute(pair, 'zl', [(i, i ^ 2) for i in range(4)])  4.68 us
    pallas_call x1, Pallas kernels, local(): pl.pallas_call(send_kernel, out_shape=(pltpu.VMEM((2, PART, LANES), f32),...  3.42 us
    pallas_call x1, Pallas kernels, local(): pl.pallas_call(far_kernel, out_shape=(pltpu.VMEM((EARLY, deep), bf16),) *...  3.15 us
    pallas_call x1, Pallas kernels, local(): pl.pallas_call(pack_kernel, out_shape=(jax.ShapeDtypeStruct((tiles, PART,...  1.73 us
  transfers between devices with their start and end apart: 5, of which 2 were waited for; matrix products, arithmetic and copies ran while one was open for 0% of the time, Pallas kernels for 32%

profile of v6, /device:TPU:224, one launch (start us, length us, event | category | flops | bytes accessed | tf_op | source)
XLA Modules:
  0.0 40.1 jit_solution(13518640572507583595)
XLA Ops:
  0.6 1.7 %pack_block.1 = (f32[16,40,128]{2,1,0:T(8,128)}, f32[3,8192]{1,0:T(4,128)S(1)}, f32[8,128]{1,0:T(8,128)S(1)}) custom-call(f32[2,16,128]{2,1,0:T(8,128)} %slab_ref.5, f32[1,128]{1,0:T(1,128)} %bitcast.5, f32[3,8192]{1,0:T(4,128)} %pos_ref.1, f32[1,8192]{1,0:T(1,128)} %bitcast.4), custom_call_target="tpu_custom_call" | custom-call | flops 65536 | bytes 524288 | tf_op jit(solution)/shard_map/pack_block/pallas_call | solution.py:255
  2.4 7.0 %all-to-all-start = ((f32[16,40,128]{2,1,0:T(8,128)}), f32[16,40,128]{2,1,0:T(8,128)S(1)}, u32[]{:S(2)}, u32[]{:S(2)}) async-start(f32[16,40,128]{2,1,0:T(8,128)} %get-tuple-element.16), calls=%async_computation | async-start | bytes 655360 | tf_op jit(solution)/shard_map/all_to_all | solution.py:269
  9.4 1.1 %collective-permute-start = (f32[2,16,128]{2,1,0:T(8,128)}, f32[2,16,128]{2,1,0:T(8,128)S(1)}, u32[]{:S(2)}, u32[]{:S(2)}) collective-permute-start(f32[2,16,128]{2,1,0:T(8,128)} %slab_ref.5), channel_id=1, source_target_pairs={{0,1},{1,0},{2,3},{3,2},{4,5},{5,4},{6,7},{7,6},{8,9},{9,8},{10,11... | collective-permute-start | bytes 49160 | tf_op jit(solution)/shard_map/ppermute | solution.py:270
  10.5 3.1 %far_tiles.1 = (bf16[176,4096]{1,0:T(8,128)(2,1)S(1)}, bf16[176,4096]{1,0:T(8,128)(2,1)S(1)}) custom-call(f32[3,8192]{1,0:T(4,128)S(1)} %get-tuple-element.13.pos_ref), custom_call_target="tpu_custom_call" | custom-call | flops 47185920 | bytes 6291456 | tf_op jit(solution)/shard_map/far_tiles/pallas_call | solution.py:272
  13.7 0.0 copy-start
  13.7 5.1 %all-to-all-done.block_ref = f32[16,40,128]{2,1,0:T(8,128)S(1)} async-done(((f32[16,40,128]{2,1,0:T(8,128)}), f32[16,40,128]{2,1,0:T(8,128)S(1)}, u32[]{:S(2)}, u32[]{:S(2)}) %all-to-all-start) | async-done | bytes 327712 | tf_op jit(solution)/shard_map/all_to_all | solution.py:269
  18.8 3.4 %send_products.1 = (f32[2,40,128]{2,1,0:T(8,128)S(1)}, bf16[128,2048]{1,0:T(8,128)(2,1)S(1)}, bf16[256,4096]{1,0:T(8,128)(2,1)S(1)}, bf16[256,4096]{1,0:T(8,128)(2,1)S(1)}) custom-call(f32[3,8192]{1,0:T(4,128)S(1)} %get-tuple-element.13.pos_ref, bf16[176,4096]{1,0:T(8,128)(2,1)S(1)} %get-tuple-element.14.high_ref, ...), custom_call_target="tpu_custom_call" | custom-call | flops 536870912 | bytes 4194304 | tf_op jit(solution)/shard_map/send_products/pallas_call | solution.py:283
  22.2 6.0 %collective-permute-start.1 = (f32[2,40,128]{2,1,0:T(8,128)S(1)}, f32[2,40,128]{2,1,0:T(8,128)S(1)}, u32[]{:S(2)}, u32[]{:S(2)}) collective-permute-start(f32[2,40,128]{2,1,0:T(8,128)S(1)} %get-tuple-element.21), channel_id=1, source_target_pairs={{0,8},{8,0},{1,9},{9,1},{2,10},{10,2},{3,11},{11,3},{4,12},{12,4},... | collective-permute-start | bytes 122888 | tf_op jit(solution)/shard_map/ppermute | solution.py:302
  28.3 0.0 collective-permute-done.near_ref
  28.3 0.0 copy-done
  28.3 0.0 copy-start.1
  28.3 0.0 copy-start.2
  28.3 5.9 %keep_products.1 = (f32[2,40,128]{2,1,0:T(8,128)S(1)}, f32[2,2,16,128]{3,2,1,0:T(8,128)S(1)}) custom-call(f32[3,8192]{1,0:T(4,128)S(1)} %get-tuple-element.13.pos_ref, bf16[128,2048]{1,0:T(8,128)(2,1)S(1)} %get-tuple-element.17.y_ref, bf16[256,4096]{1,0:T(8,128)(2,1)S(1)} %get-tuple-element.18.done_high, bf16[256,4096]{1,0:T(8,128)(2,1)S(1)} %get-tuple-element.19.done_low, ...), custom_call_target="tpu_custom_call" | custom-call | flops 536870912 | bytes 4194304 | tf_op jit(solution)/shard_map/keep_products/pallas_call | solution.py:304
  34.1 0.1 collective-permute-start.3
  34.2 0.0 collective-permute-done.1.half_ref
  34.3 0.1 collective-permute-start.2
  34.4 4.7 %collective-permute-done.3.pair_ref = f32[2,2,16,128]{3,2,1,0:T(8,128)S(1)} collective-permute-done((f32[2,2,16,128]{3,2,1,0:T(8,128)S(1)}, f32[2,2,16,128]{3,2,1,0:T(8,128)S(1)}, u32[]{:S(2)}, u32[]{:S(2)}) %collective-permute-start.3) | collective-permute-done | bytes 32800 | tf_op jit(solution)/shard_map/ppermute | solution.py:318
  39.0 0.3 slab_term.1.rest_ref
  39.4 0.0 collective-permute-done.2.core_ref
  39.4 0.1 copy-done.1
  39.4 0.0 copy-done.2
  39.4 0.6 %finish_rate.1 = (f32[2,16,128]{2,1,0:T(8,128)}, f32[2,16,128]{2,1,0:T(8,128)}) custom-call(f32[2,40,128]{2,1,0:T(8,128)S(1)} %get-tuple-element.20.keep_ref, f32[2,40,128]{2,1,0:T(8,128)S(1)} %collective-permute-done.1.half_ref, f32[40,128]{1,0:T(8,128)S(1)} %collective-permute-done.2.core_ref, f32[2,16,128]{2,1,0:T(8,128)S(1)} %slab_term.1.rest_ref, ...), custom_call_target="tpu_custom_call" | custom-call | flops 65536 | bytes 262144 | tf_op jit(solution)/shard_map/finish_rate/pallas_call | solution.py:331
  (1 shorter events, 0.0 us)
Async XLA Ops:
  2.4 16.4 %all-to-all-start = ((f32[16,40,128]{2,1,0:T(8,128)}), f32[16,40,128]{2,1,0:T(8,128)S(1)}, u32[]{:S(2)}, u32[]{:S(2)}) async-start(f32[16,40,128]{2,1,0:T(8,128)} %get-tuple-element.16), calls=%async_computation | async-start | bytes 655360 | tf_op jit(solution)/shard_map/all_to_all | solution.py:269
  9.4 18.8 %collective-permute-start = (f32[2,16,128]{2,1,0:T(8,128)}, f32[2,16,128]{2,1,0:T(8,128)S(1)}, u32[]{:S(2)}, u32[]{:S(2)}) collective-permute-start(f32[2,16,128]{2,1,0:T(8,128)} %slab_ref.5), channel_id=1, source_target_pairs={{0,1},{1,0},{2,3},{3,2},{4,5},{5,4},{6,7},{7,6},{8,9},{9,8},{10,11... | collective-permute-start | bytes 49160 | tf_op jit(solution)/shard_map/ppermute | solution.py:270
  13.7 14.6 %copy-start = (f32[2,16,128]{2,1,0:T(8,128)S(1)}, f32[2,16,128]{2,1,0:T(8,128)}, u32[]{:S(2)}) copy-start(f32[2,16,128]{2,1,0:T(8,128)} %slab_ref.5) | copy-start | bytes 49156
  22.2 12.0 %collective-permute-start.1 = (f32[2,40,128]{2,1,0:T(8,128)S(1)}, f32[2,40,128]{2,1,0:T(8,128)S(1)}, u32[]{:S(2)}, u32[]{:S(2)}) collective-permute-start(f32[2,40,128]{2,1,0:T(8,128)S(1)} %get-tuple-element.21), channel_id=1, source_target_pairs={{0,8},{8,0},{1,9},{9,1},{2,10},{10,2},{3,11},{11,3},{4,12},{12,4},... | collective-permute-start | bytes 122888 | tf_op jit(solution)/shard_map/ppermute | solution.py:302
  28.3 11.2 %copy-start.1 = (f32[2,16,128]{2,1,0:T(8,128)S(1)}, f32[2,16,128]{2,1,0:T(8,128)}, u32[]{:S(2)}) copy-start(f32[2,16,128]{2,1,0:T(8,128)} %base_ref.1) | copy-start | bytes 49156
  28.3 11.2 %copy-start.2 = (f32[2,16,128]{2,1,0:T(8,128)S(1)}, f32[2,16,128]{2,1,0:T(8,128)}, u32[]{:S(2)}) copy-start(f32[2,16,128]{2,1,0:T(8,128)} %accum_ref.1) | copy-start | bytes 49156
  34.1 4.9 %collective-permute-start.3 = (f32[2,2,16,128]{3,2,1,0:T(8,128)S(1)}, f32[2,2,16,128]{3,2,1,0:T(8,128)S(1)}, u32[]{:S(2)}, u32[]{:S(2)}) collective-permute-start(f32[2,2,16,128]{3,2,1,0:T(8,128)S(1)} %get-tuple-element.22), channel_id=1, source_target_pairs={{0,2},{1,3},{2,0},{3,1},{4,6},{5,7},{6,4},{7,5},{8,10},{9,11},{10,... | collective-permute-start | bytes 98312 | tf_op jit(solution)/shard_map/ppermute | solution.py:318
  34.3 5.1 %collective-permute-start.2 = (f32[40,128]{1,0:T(8,128)S(1)}, f32[40,128]{1,0:T(8,128)S(1)}, u32[]{:S(2)}, u32[]{:S(2)}) collective-permute-start(f32[40,128]{1,0:T(8,128)S(1)} %fusion), channel_id=1, source_target_pairs={{0,4},{4,0},{1,5},{5,1},{2,6},{6,2},{3,7},{7,3},{8,12},{12,8},{9,1... | collective-permute-start | bytes 61448 | tf_op jit(solution)/shard_map/ppermute | solution.py:319

commit v7 on v6

--- a/solution.py
+++ b/solution.py
@@ -53,7 +53,7 @@
     return pl.ds(pl.multiple_of(index * LANES, LANES), LANES)
 
 
-def pack_kernel(section_ref, pops_ref, pos_ref, det_ref, copies_ref, pos_out, det_out, block_ref, sems):
+def pack_kernel(section_ref, pops_ref, pos_ref, det_ref, copies_ref, pos_out, det_out, block_ref, sems, out_sems):
     own = lax.axis_index("yx") * 4 + lax.axis_index("zh") * 2 + lax.axis_index("c")
     moves = [
         pltpu.make_async_copy(section_ref.at[0], block_ref.at[pl.ds(0, 16)], sems.at[0]),
@@ -67,13 +67,12 @@
         move.start()
     for move in moves[:3]:
         move.wait()
-    block = block_ref[0:32, :]
     top = lax.broadcasted_iota(jnp.int32, (8, LANES), 0) == 0
-    pops = jnp.where(top, 2.0 * block_ref[32:40, :] - 1.0, 0.0)
-    for n in range(copies_ref.shape[0]):
-        copies_ref[n, 0:32, :] = block
-        copies_ref[n, 32:40, :] = pops
-    for move in moves[3:]:
+    block_ref[32:PART, :] = jnp.where(top, 2.0 * block_ref[32:PART, :] - 1.0, 0.0)
+    spread = [pltpu.make_async_copy(block_ref, copies_ref.at[n], out_sems.at[n]) for n in range(copies_ref.shape[0])]
+    for move in spread:
+        move.start()
+    for move in moves[3:] + spread:
         move.wait()
 
 
@@ -140,17 +139,24 @@
     return (1 - half) * 2 + 1 - core, (1 - half) * 2 + core
 
 
-def fill_own(pos_ref, row_ref, high_ref, low_ref):
+def early_blocks():
+    lo = lax.axis_index("zl")
+    return jnp.where(lo == 0, 2, jnp.where(lo == 3, 0, 1)) * (1 - lax.axis_index("zh"))
+
+
+def fill_own(n, pos_ref, row_ref, high_ref, low_ref):
     place = lax.axis_index("yx")
     half, core = lax.axis_index("zh"), lax.axis_index("c")
     tiles = pos_ref.shape[1] // (4 * LANES)
-    fill_tiles(pos_ref, row_ref, high_ref, low_ref, (half * 2 + 1 - core, half * 2 + core), 0, 2 * LANES)
+    quad = half * 2 + (core if n else 1 - core)
+    fill_tiles(pos_ref, row_ref, high_ref, low_ref, (quad,), 0, LANES)
+    if n == 0:
+        return
     eye = lax.broadcasted_iota(jnp.int32, (LANES, LANES), 0) == lax.broadcasted_iota(jnp.int32, (LANES, LANES), 1)
     for part in range(2):
         lanes = lanes_at(place + part * tiles)
         for ref in (high_ref, low_ref):
-            own = ref[LANES:, lanes].astype(jnp.float32)
-            ref[LANES:, lanes] = jnp.where(eye, 0.0, own).astype(jnp.bfloat16)
+            ref[:, lanes] = jnp.where(eye, 0.0, ref[:, lanes].astype(jnp.float32)).astype(jnp.bfloat16)
 
 
 def far_kernel(pos_ref, high_ref, low_ref, row_ref):
@@ -204,27 +210,31 @@
     by_real, by_imag = [jnp.concatenate(pair, axis=0) for pair in pairs]
     store_products(by_real, by_imag, out_ref, 0)
 
-    @pl.when(lax.axis_index("zh") == 0)
-    def _():
-        fill_own(pos_ref, row_ref, own_high, own_low)
+    for n in range(2):
+
+        @pl.when(early_blocks() > n)
+        def _():
+            fill_own(n, pos_ref, row_ref, own_high.at[n], own_low.at[n])
 
 
 def keep_kernel(pos_ref, y_ref, done_high, done_low, slab_ref, near_ref, out_ref, pair_ref, row_ref, high_ref, low_ref):
     pair_ref[0] = slab_ref[...]
     pair_ref[1] = near_ref[...]
 
-    def finish(high, low):
+    def finish(n, high, low):
         by_real, by_imag = products(high, low, y_ref[...])
-        store_products(by_real, by_imag, out_ref, 0)
-
-    @pl.when(lax.axis_index("zh") == 0)
-    def _():
-        finish(done_high, done_low)
-
-    @pl.when(lax.axis_index("zh") == 1)
-    def _():
-        fill_own(pos_ref, row_ref, high_ref, low_ref)
-        finish(high_ref, low_ref)
+        store_products(by_real, by_imag, out_ref, n)
+
+    for n in range(2):
+
+        @pl.when(early_blocks() > n)
+        def _():
+            finish(n, done_high.at[n], done_low.at[n])
+
+        @pl.when(early_blocks() <= n)
+        def _():
+            fill_own(n, pos_ref, row_ref, high_ref, low_ref)
+            finish(n, high_ref, low_ref)
 
 
 def finish_kernel(keep_ref, half_ref, core_ref, rest_ref, slab_ref, base_ref, accum_ref, next_ref, acc_ref):
@@ -255,13 +265,17 @@
     copies, pos, det = pl.pallas_call(
         pack_kernel,
         out_shape=(
-            jax.ShapeDtypeStruct((tiles, PART, LANES), f32),
+            pltpu.HBM((tiles, PART, LANES), f32),
             pltpu.VMEM(positions.shape, f32),
             pltpu.VMEM((8, LANES), f32),
         ),
         in_specs=[hbm] * 4,
-        out_specs=[vmem] * 3,
-        scratch_shapes=[pltpu.VMEM((PART, LANES), f32), pltpu.SemaphoreType.DMA((6,))],
+        out_specs=[hbm, vmem, vmem],
+        scratch_shapes=[
+            pltpu.VMEM((PART, LANES), f32),
+            pltpu.SemaphoreType.DMA((6,)),
+            pltpu.SemaphoreType.DMA((tiles,)),
+        ],
         compiler_params=params(4),
         cost_estimate=pl.CostEstimate(flops=1 << 16, bytes_accessed=1 << 19, transcendentals=0),
         name="pack_block",
@@ -285,8 +299,8 @@
         out_shape=(
             pltpu.VMEM((2, PART, LANES), f32),
             pltpu.VMEM((LANES, deep // 2), bf16),
-            pltpu.VMEM((2 * LANES, deep), bf16),
-            pltpu.VMEM((2 * LANES, deep), bf16),
+            pltpu.VMEM((2, LANES, deep), bf16),
+            pltpu.VMEM((2, LANES, deep), bf16),
         ),
         in_specs=[vmem] * 4,
         out_specs=[vmem] * 4,
@@ -307,9 +321,9 @@
         in_specs=[vmem] * 6,
         out_specs=[vmem] * 2,
         scratch_shapes=[
-            pltpu.VMEM((3, 2 * LANES, LANES), f32),
-            pltpu.VMEM((2 * LANES, deep), bf16),
-            pltpu.VMEM((2 * LANES, deep), bf16),
+            pltpu.VMEM((3, LANES, LANES), f32),
+            pltpu.VMEM((LANES, deep), bf16),
+            pltpu.VMEM((LANES, deep), bf16),
         ],
         compiler_params=params(8),
         cost_estimate=pl.CostEstimate(flops=1 << 29, bytes_accessed=4 << 20, transcendentals=1 << 20),

time: 40.2 us -> 39.7 us (0.988)
  the two profiles are of different devices: /device:TPU:224 before, /device:TPU:32 now
where the time goes in v7:
time: 39.7 us; the launch traced here: 39.5 us
  Pallas kernels  15.5 us (39%)
  starting transfers between devices  15.4 us (39%)
  waiting for transfers between devices  7.83 us (20%)
  between operations  0.71 us (2%)
    all_to_all x1, starting transfers between devices, local(): blocks = lax.all_to_all(copies, 'yx', 0, 0, tiled=True)  7.05 us
    all_to_all x1, waiting for transfers between devices, local(): blocks = lax.all_to_all(copies, 'yx', 0, 0, tiled=True)  6.03 us
    pallas_call x1, Pallas kernels, local(): pl.pallas_call(send_kernel, out_shape=(pltpu.VMEM((2, PART, LANES), f32),...  5.78 us
    pallas_call x1, Pallas kernels, local(): pl.pallas_call(keep_kernel, out_shape=(pltpu.VMEM((2, PART, LANES), f32),...  4.03 us
    ppermute x1, starting transfers between devices, local(): half = lax.ppermute(sent, 'zh', [(0, 1), (1, 0)])  4.02 us
    ppermute x1, starting transfers between devices, local(): pair = lax.ppermute(pair, 'zl', [(i, i ^ 2) for i in range(4)])  4.02 us
    pallas_call x1, Pallas kernels, local(): pl.pallas_call(far_kernel, out_shape=(pltpu.VMEM((EARLY, deep), bf16),) *...  3.14 us
    ppermute x1, waiting for transfers between devices, local(): pair = lax.ppermute(pair, 'zl', [(i, i ^ 2) for i in range(4)])  1.79 us
  transfers between devices with their start and end apart: 5, of which 2 were waited for; matrix products, arithmetic and copies ran while one was open for 0% of the time, Pallas kernels for 34%

profile of v7, /device:TPU:32, one launch (start us, length us, event | category | flops | bytes accessed | tf_op | source)
XLA Modules:
  0.0 39.5 jit_solution(17895036398423836299)
XLA Ops:
  0.6 1.6 %pack_block.1 = (f32[16,40,128]{2,1,0:T(8,128)}, f32[3,8192]{1,0:T(4,128)S(1)}, f32[8,128]{1,0:T(8,128)S(1)}) custom-call(f32[2,16,128]{2,1,0:T(8,128)} %slab_ref.5, f32[1,128]{1,0:T(1,128)} %bitcast.5, f32[3,8192]{1,0:T(4,128)} %pos_ref.1, f32[1,8192]{1,0:T(1,128)} %bitcast.4), custom_call_target="tpu_custom_call" | custom-call | flops 65536 | bytes 524288 | tf_op jit(solution)/shard_map/pack_block/pallas_call | solution.py:265
  2.3 7.0 %all-to-all-start = ((f32[16,40,128]{2,1,0:T(8,128)}), f32[16,40,128]{2,1,0:T(8,128)S(1)}, u32[]{:S(2)}, u32[]{:S(2)}) async-start(f32[16,40,128]{2,1,0:T(8,128)} %get-tuple-element.16), calls=%async_computation | async-start | bytes 655360 | tf_op jit(solution)/shard_map/all_to_all | solution.py:283
  9.3 0.2 collective-permute-start
  9.5 3.1 %far_tiles.1 = (bf16[176,4096]{1,0:T(8,128)(2,1)S(1)}, bf16[176,4096]{1,0:T(8,128)(2,1)S(1)}) custom-call(f32[3,8192]{1,0:T(4,128)S(1)} %get-tuple-element.13.pos_ref), custom_call_target="tpu_custom_call" | custom-call | flops 47185920 | bytes 6291456 | tf_op jit(solution)/shard_map/far_tiles/pallas_call | solution.py:286
  12.7 0.0 copy-start
  12.7 6.0 %all-to-all-done.block_ref = f32[16,40,128]{2,1,0:T(8,128)S(1)} async-done(((f32[16,40,128]{2,1,0:T(8,128)}), f32[16,40,128]{2,1,0:T(8,128)S(1)}, u32[]{:S(2)}, u32[]{:S(2)}) %all-to-all-start) | async-done | bytes 327712 | tf_op jit(solution)/shard_map/all_to_all | solution.py:283
  18.7 5.8 %send_products.1 = (f32[2,40,128]{2,1,0:T(8,128)S(1)}, bf16[128,2048]{1,0:T(8,128)(2,1)S(1)}, bf16[2,128,4096]{2,1,0:T(8,128)(2,1)S(1)}, bf16[2,128,4096]{2,1,0:T(8,128)(2,1)S(1)}) custom-call(f32[3,8192]{1,0:T(4,128)S(1)} %get-tuple-element.13.pos_ref, bf16[176,4096]{1,0:T(8,128)(2,1)S(1)} %get-tuple-element.14.high_ref, ...), custom_call_target="tpu_custom_call" | custom-call | flops 536870912 | bytes 4194304 | tf_op jit(solution)/shard_map/send_products/pallas_call | solution.py:297
  24.5 4.0 %collective-permute-start.1 = (f32[2,40,128]{2,1,0:T(8,128)S(1)}, f32[2,40,128]{2,1,0:T(8,128)S(1)}, u32[]{:S(2)}, u32[]{:S(2)}) collective-permute-start(f32[2,40,128]{2,1,0:T(8,128)S(1)} %get-tuple-element.21), channel_id=1, source_target_pairs={{0,8},{8,0},{1,9},{9,1},{2,10},{10,2},{3,11},{11,3},{4,12},{12,4},... | collective-permute-start | bytes 122888 | tf_op jit(solution)/shard_map/ppermute | solution.py:316
  28.5 0.0 collective-permute-done.near_ref
  28.5 0.0 copy-done
  28.5 0.0 copy-start.1
  28.5 0.0 copy-start.2
  28.5 4.0 %keep_products.1 = (f32[2,40,128]{2,1,0:T(8,128)S(1)}, f32[2,2,16,128]{3,2,1,0:T(8,128)S(1)}) custom-call(f32[3,8192]{1,0:T(4,128)S(1)} %get-tuple-element.13.pos_ref, bf16[128,2048]{1,0:T(8,128)(2,1)S(1)} %get-tuple-element.17.y_ref, bf16[2,128,4096]{2,1,0:T(8,128)(2,1)S(1)} %get-tuple-element.18.done_high, ...), custom_call_target="tpu_custom_call" | custom-call | flops 536870912 | bytes 4194304 | tf_op jit(solution)/shard_map/keep_products/pallas_call | solution.py:318
  32.6 4.0 %collective-permute-start.3 = (f32[2,2,16,128]{3,2,1,0:T(8,128)S(1)}, f32[2,2,16,128]{3,2,1,0:T(8,128)S(1)}, u32[]{:S(2)}, u32[]{:S(2)}) collective-permute-start(f32[2,2,16,128]{3,2,1,0:T(8,128)S(1)} %get-tuple-element.22), channel_id=1, source_target_pairs={{0,2},{1,3},{2,0},{3,1},{4,6},{5,7},{6,4},{7,5},{8,10},{9,11},{10,... | collective-permute-start | bytes 98312 | tf_op jit(solution)/shard_map/ppermute | solution.py:332
  36.6 0.0 collective-permute-done.1.half_ref
  36.6 0.1 collective-permute-start.2
  36.7 1.8 %collective-permute-done.3.pair_ref = f32[2,2,16,128]{3,2,1,0:T(8,128)S(1)} collective-permute-done((f32[2,2,16,128]{3,2,1,0:T(8,128)S(1)}, f32[2,2,16,128]{3,2,1,0:T(8,128)S(1)}, u32[]{:S(2)}, u32[]{:S(2)}) %collective-permute-start.3) | collective-permute-done | bytes 32800 | tf_op jit(solution)/shard_map/ppermute | solution.py:332
  38.5 0.3 slab_term.1.rest_ref
  38.8 0.0 collective-permute-done.2.core_ref
  38.8 0.1 copy-done.1
  38.9 0.0 copy-done.2
  38.9 0.6 %finish_rate.1 = (f32[2,16,128]{2,1,0:T(8,128)}, f32[2,16,128]{2,1,0:T(8,128)}) custom-call(f32[2,40,128]{2,1,0:T(8,128)S(1)} %get-tuple-element.20.keep_ref, f32[2,40,128]{2,1,0:T(8,128)S(1)} %collective-permute-done.1.half_ref, f32[40,128]{1,0:T(8,128)S(1)} %collective-permute-done.2.core_ref, f32[2,16,128]{2,1,0:T(8,128)S(1)} %slab_term.1.rest_ref, ...), custom_call_target="tpu_custom_call" | custom-call | flops 65536 | bytes 262144 | tf_op jit(solution)/shard_map/finish_rate/pallas_call | solution.py:345
  (1 shorter events, 0.0 us)
Async XLA Ops:
  2.3 16.4 %all-to-all-start = ((f32[16,40,128]{2,1,0:T(8,128)}), f32[16,40,128]{2,1,0:T(8,128)S(1)}, u32[]{:S(2)}, u32[]{:S(2)}) async-start(f32[16,40,128]{2,1,0:T(8,128)} %get-tuple-element.16), calls=%async_computation | async-start | bytes 655360 | tf_op jit(solution)/shard_map/all_to_all | solution.py:283
  9.3 19.2 %collective-permute-start = (f32[2,16,128]{2,1,0:T(8,128)}, f32[2,16,128]{2,1,0:T(8,128)S(1)}, u32[]{:S(2)}, u32[]{:S(2)}) collective-permute-start(f32[2,16,128]{2,1,0:T(8,128)} %slab_ref.5), channel_id=1, source_target_pairs={{0,1},{1,0},{2,3},{3,2},{4,5},{5,4},{6,7},{7,6},{8,9},{9,8},{10,11... | collective-permute-start | bytes 49160 | tf_op jit(solution)/shard_map/ppermute | solution.py:284
  12.7 15.9 %copy-start = (f32[2,16,128]{2,1,0:T(8,128)S(1)}, f32[2,16,128]{2,1,0:T(8,128)}, u32[]{:S(2)}) copy-start(f32[2,16,128]{2,1,0:T(8,128)} %slab_ref.5) | copy-start | bytes 49156
  24.5 12.1 %collective-permute-start.1 = (f32[2,40,128]{2,1,0:T(8,128)S(1)}, f32[2,40,128]{2,1,0:T(8,128)S(1)}, u32[]{:S(2)}, u32[]{:S(2)}) collective-permute-start(f32[2,40,128]{2,1,0:T(8,128)S(1)} %get-tuple-element.21), channel_id=1, source_target_pairs={{0,8},{8,0},{1,9},{9,1},{2,10},{10,2},{3,11},{11,3},{4,12},{12,4},... | collective-permute-start | bytes 122888 | tf_op jit(solution)/shard_map/ppermute | solution.py:316
  28.5 10.3 %copy-start.1 = (f32[2,16,128]{2,1,0:T(8,128)S(1)}, f32[2,16,128]{2,1,0:T(8,128)}, u32[]{:S(2)}) copy-start(f32[2,16,128]{2,1,0:T(8,128)} %base_ref.1) | copy-start | bytes 49156
  28.5 10.3 %copy-start.2 = (f32[2,16,128]{2,1,0:T(8,128)S(1)}, f32[2,16,128]{2,1,0:T(8,128)}, u32[]{:S(2)}) copy-start(f32[2,16,128]{2,1,0:T(8,128)} %accum_ref.1) | copy-start | bytes 49156
  32.6 5.9 %collective-permute-start.3 = (f32[2,2,16,128]{3,2,1,0:T(8,128)S(1)}, f32[2,2,16,128]{3,2,1,0:T(8,128)S(1)}, u32[]{:S(2)}, u32[]{:S(2)}) collective-permute-start(f32[2,2,16,128]{3,2,1,0:T(8,128)S(1)} %get-tuple-element.22), channel_id=1, source_target_pairs={{0,2},{1,3},{2,0},{3,1},{4,6},{5,7},{6,4},{7,5},{8,10},{9,11},{10,... | collective-permute-start | bytes 98312 | tf_op jit(solution)/shard_map/ppermute | solution.py:332
  36.6 2.2 %collective-permute-start.2 = (f32[40,128]{1,0:T(8,128)S(1)}, f32[40,128]{1,0:T(8,128)S(1)}, u32[]{:S(2)}, u32[]{:S(2)}) collective-permute-start(f32[40,128]{1,0:T(8,128)S(1)} %fusion), channel_id=1, source_target_pairs={{0,4},{4,0},{1,5},{5,1},{2,6},{6,2},{3,7},{7,3},{8,12},{12,8},{9,1... | collective-permute-start | bytes 61448 | tf_op jit(solution)/shard_map/ppermute | solution.py:333

commit v8 on v6

--- a/solution.py
+++ b/solution.py
@@ -17,7 +17,6 @@
 ROUNDER = 12582912.0
 PART = 40
 WIDE = 48
-EARLY = 176
 
 
 def horner(coefs, scale, arg):
@@ -53,8 +52,18 @@
     return pl.ds(pl.multiple_of(index * LANES, LANES), LANES)
 
 
-def pack_kernel(section_ref, pops_ref, pos_ref, det_ref, copies_ref, pos_out, det_out, block_ref, sems):
-    own = lax.axis_index("yx") * 4 + lax.axis_index("zh") * 2 + lax.axis_index("c")
+def place_of(step):
+    y = lax.rem(lax.axis_index("y") + 4 - lax.rem(step, 4), 4)
+    x = lax.rem(lax.axis_index("x") + 4 - lax.div(step, 4), 4)
+    return y * 4 + x
+
+
+def own_place():
+    return lax.axis_index("y") * 4 + lax.axis_index("x")
+
+
+def pack_kernel(section_ref, pops_ref, pos_ref, det_ref, block_ref, pos_out, det_out, sems):
+    own = own_place() * 4 + lax.axis_index("zh") * 2 + lax.axis_index("c")
     moves = [
         pltpu.make_async_copy(section_ref.at[0], block_ref.at[pl.ds(0, 16)], sems.at[0]),
         pltpu.make_async_copy(section_ref.at[1], block_ref.at[pl.ds(16, 16)], sems.at[1]),
@@ -65,16 +74,16 @@
     ]
     for move in moves:
         move.start()
-    for move in moves[:3]:
+    for move in moves:
         move.wait()
-    block = block_ref[0:32, :]
     top = lax.broadcasted_iota(jnp.int32, (8, LANES), 0) == 0
-    pops = jnp.where(top, 2.0 * block_ref[32:40, :] - 1.0, 0.0)
-    for n in range(copies_ref.shape[0]):
-        copies_ref[n, 0:32, :] = block
-        copies_ref[n, 32:40, :] = pops
-    for move in moves[3:]:
-        move.wait()
+    block_ref[32:PART, :] = jnp.where(top, 2.0 * block_ref[32:PART, :] - 1.0, 0.0)
+
+
+def merge_kernel(block_ref, one_ref, two_ref, three_ref, pos_ref, first_ref, all_ref, pos_out):
+    for n, ref in enumerate((block_ref, one_ref, two_ref, three_ref)):
+        all_ref[n] = ref[...]
+    pos_out[...] = pos_ref[...]
 
 
 def turned(pos_ref, k, index):
@@ -84,14 +93,14 @@
 
 def fill_tiles(pos_ref, row_ref, high_ref, low_ref, quads, first, count):
     quad = lax.axis_index("zh") * 2 + lax.axis_index("c")
-    place = lax.axis_index("yx")
+    place = own_place()
     tiles = pos_ref.shape[1] // (4 * LANES)
     for n, other in enumerate(quads):
         for k in range(3):
             row_ref[k, n * LANES : (n + 1) * LANES, :] = turned(pos_ref, k, place * 4 + other)
 
     def tile(step, carry):
-        at = lanes_at(step * 4 + quad)
+        at = lanes_at(place_of(step) * 4 + quad)
         cols = [pos_ref[k : k + 1, at] for k in range(3)]
         for n in range(0, count, 32):
             size = min(32, count - n)
@@ -135,43 +144,43 @@
     rest_ref[1] = v_real - line * y_real - 0.5 * y_imag
 
 
-def far_quads():
-    half, core = lax.axis_index("zh"), lax.axis_index("c")
-    return (1 - half) * 2 + 1 - core, (1 - half) * 2 + core
+def early_own():
+    return (1 - lax.axis_index("zh")) * (lax.axis_index("zl") < 2).astype(jnp.int32)
 
 
 def fill_own(pos_ref, row_ref, high_ref, low_ref):
-    place = lax.axis_index("yx")
-    half, core = lax.axis_index("zh"), lax.axis_index("c")
     tiles = pos_ref.shape[1] // (4 * LANES)
-    fill_tiles(pos_ref, row_ref, high_ref, low_ref, (half * 2 + 1 - core, half * 2 + core), 0, 2 * LANES)
+    quad = lax.axis_index("zh") * 2 + lax.axis_index("c")
+    fill_tiles(pos_ref, row_ref, high_ref, low_ref, (quad,), 0, LANES)
     eye = lax.broadcasted_iota(jnp.int32, (LANES, LANES), 0) == lax.broadcasted_iota(jnp.int32, (LANES, LANES), 1)
     for part in range(2):
-        lanes = lanes_at(place + part * tiles)
+        lanes = pl.ds(part * tiles * LANES, LANES)
         for ref in (high_ref, low_ref):
-            own = ref[LANES:, lanes].astype(jnp.float32)
-            ref[LANES:, lanes] = jnp.where(eye, 0.0, own).astype(jnp.bfloat16)
-
-
-def far_kernel(pos_ref, high_ref, low_ref, row_ref):
-    fill_tiles(pos_ref, row_ref, high_ref, low_ref, far_quads(), 0, EARLY)
-
-
-def fill_slab(block_ref, y_ref):
+            ref[:, lanes] = jnp.where(eye, 0.0, ref[:, lanes].astype(jnp.float32)).astype(jnp.bfloat16)
+
+
+def first_kernel(pos_ref, high_ref, low_ref, row_ref):
+    half, core = lax.axis_index("zh"), lax.axis_index("c")
+    fill_tiles(pos_ref, row_ref, high_ref, low_ref, ((1 - half) * 2 + 1 - core,), 0, LANES)
+
+
+def second_kernel(pos_ref, high_ref, low_ref, row_ref):
+    half, core = lax.axis_index("zh"), lax.axis_index("c")
+    quads = ((1 - half) * 2 + core, half * 2 + 1 - core)
+    fill_tiles(pos_ref, row_ref, high_ref, low_ref, quads, 0, 2 * LANES)
+
+
+def fill_slab(refs, y_ref):
     zeros = jnp.zeros((16, LANES), jnp.float32)
-
-    def fill(step, carry):
-        block = block_ref[step]
+    for step in range(16):
+        block = refs[step // 4][step % 4]
         pops = jnp.concatenate([block[32:40], zeros[0:8]], axis=0)
-        lanes = lanes_at(step)
+        lanes = slice(step * LANES, (step + 1) * LANES)
         for n, value in enumerate((block[0:16], block[16:32], pops)):
             high, low = split(value)
             y_ref[n * 16 : n * 16 + 16, lanes] = high
             y_ref[WIDE + n * 16 : WIDE + n * 16 + 16, lanes] = low
         y_ref[2 * WIDE :, lanes] = jnp.zeros((LANES - 2 * WIDE, LANES), jnp.bfloat16)
-        return carry
-
-    lax.fori_loop(0, block_ref.shape[0], fill, 0, unroll=4)
 
 
 def dot_slab(tiles, y):
@@ -196,35 +205,31 @@
     return by_real, by_imag
 
 
-def send_kernel(pos_ref, high_ref, low_ref, block_ref, out_ref, y_ref, own_high, own_low, row_ref, more_high, more_low):
-    fill_slab(block_ref, y_ref)
-    fill_tiles(pos_ref, row_ref, more_high, more_low, far_quads()[1:], EARLY - LANES, 2 * LANES - EARLY)
+def send_kernel(pos_ref, high0, low0, high1, low1, all0, all1, all2, all3, out_ref, y_ref, own_high, own_low, row_ref):
+    fill_slab((all0, all1, all2, all3), y_ref)
     y = y_ref[...]
-    pairs = zip(products(high_ref, low_ref, y), products(more_high, more_low, y))
-    by_real, by_imag = [jnp.concatenate(pair, axis=0) for pair in pairs]
-    store_products(by_real, by_imag, out_ref, 0)
-
-    @pl.when(lax.axis_index("zh") == 0)
+    store_products(*products(high0, low0, y), out_ref, 0)
+    store_products(*products(high1.at[pl.ds(0, LANES)], low1.at[pl.ds(0, LANES)], y), out_ref, 1)
+
+    @pl.when(early_own() == 1)
     def _():
         fill_own(pos_ref, row_ref, own_high, own_low)
 
 
-def keep_kernel(pos_ref, y_ref, done_high, done_low, slab_ref, near_ref, out_ref, pair_ref, row_ref, high_ref, low_ref):
+def keep_kernel(pos_ref, y_ref, high1, low1, done_high, done_low, slab_ref, near_ref, out_ref, pair_ref, row_ref, high_ref, low_ref):
     pair_ref[0] = slab_ref[...]
     pair_ref[1] = near_ref[...]
-
-    def finish(high, low):
-        by_real, by_imag = products(high, low, y_ref[...])
-        store_products(by_real, by_imag, out_ref, 0)
-
-    @pl.when(lax.axis_index("zh") == 0)
+    y = y_ref[...]
+    store_products(*products(high1.at[pl.ds(LANES, LANES)], low1.at[pl.ds(LANES, LANES)], y), out_ref, 0)
+
+    @pl.when(early_own() == 1)
     def _():
-        finish(done_high, done_low)
-
-    @pl.when(lax.axis_index("zh") == 1)
+        store_products(*products(done_high, done_low, y), out_ref, 1)
+
+    @pl.when(early_own() == 0)
     def _():
         fill_own(pos_ref, row_ref, high_ref, low_ref)
-        finish(high_ref, low_ref)
+        store_products(*products(high_ref, low_ref, y), out_ref, 1)
 
 
 def finish_kernel(keep_ref, half_ref, core_ref, rest_ref, slab_ref, base_ref, accum_ref, next_ref, acc_ref):
@@ -252,69 +257,83 @@
     deep = 2 * tiles * LANES
     hbm, vmem = pl.BlockSpec(memory_space=pltpu.HBM), pl.BlockSpec(memory_space=pltpu.VMEM)
 
-    copies, pos, det = pl.pallas_call(
+    block, pos, det = pl.pallas_call(
         pack_kernel,
-        out_shape=(
-            jax.ShapeDtypeStruct((tiles, PART, LANES), f32),
-            pltpu.VMEM(positions.shape, f32),
-            pltpu.VMEM((8, LANES), f32),
-        ),
+        out_shape=(pltpu.VMEM((PART, LANES), f32), pltpu.VMEM(positions.shape, f32), pltpu.VMEM((8, LANES), f32)),
         in_specs=[hbm] * 4,
         out_specs=[vmem] * 3,
-        scratch_shapes=[pltpu.VMEM((PART, LANES), f32), pltpu.SemaphoreType.DMA((6,))],
+        scratch_shapes=[pltpu.SemaphoreType.DMA((6,))],
         compiler_params=params(4),
         cost_estimate=pl.CostEstimate(flops=1 << 16, bytes_accessed=1 << 19, transcendentals=0),
         name="pack_block",
     )(in_hbm(section), in_hbm(populations.reshape(1, LANES)), in_hbm(positions), in_hbm(detuning.reshape(1, count)))
-    blocks = lax.all_to_all(copies, "yx", 0, 0, tiled=True)
+    along_y = [lax.ppermute(block, "y", [(i, (i + d) % 4) for i in range(4)]) for d in (1, 2, 3)]
+
+    high0, low0 = pl.pallas_call(
+        first_kernel,
+        out_shape=(pltpu.VMEM((LANES, deep), bf16),) * 2,
+        in_specs=[vmem],
+        out_specs=[vmem] * 2,
+        scratch_shapes=[pltpu.VMEM((3, LANES, LANES), f32)],
+        compiler_params=params(4),
+        cost_estimate=pl.CostEstimate(flops=15 << 20, bytes_accessed=2 << 20, transcendentals=1 << 20),
+        name="first_tiles",
+    )(pos)
+
+    merged, pos_again = pl.pallas_call(
+        merge_kernel,
+        out_shape=(pltpu.VMEM((4, PART, LANES), f32), pltpu.VMEM(positions.shape, f32)),
+        in_specs=[vmem] * 5 + [pl.BlockSpec(memory_space=pl.ANY)],
+        out_specs=[vmem] * 2,
+        compiler_params=params(2),
+        cost_estimate=pl.CostEstimate(flops=1, bytes_accessed=1 << 18, transcendentals=0),
+        name="merge_blocks",
+    )(block, *along_y, pos, high0)
+    along_x = [lax.ppermute(merged, "x", [(i, (i + d) % 4) for i in range(4)]) for d in (1, 2, 3)]
     near = lax.ppermute(section, "zl", [(i, i ^ 1) for i in range(4)])
 
-    high, low = pl.pallas_call(
-        far_kernel,
-        out_shape=(pltpu.VMEM((EARLY, deep), bf16),) * 2,
+    high1, low1 = pl.pallas_call(
+        second_kernel,
+        out_shape=(pltpu.VMEM((2 * LANES, deep), bf16),) * 2,
         in_specs=[vmem],
         out_specs=[vmem] * 2,
         scratch_shapes=[pltpu.VMEM((3, 2 * LANES, LANES), f32)],
         compiler_params=params(4),
-        cost_estimate=pl.CostEstimate(flops=45 << 20, bytes_accessed=6 << 20, transcendentals=1 << 20),
-        name="far_tiles",
-    )(pos)
+        cost_estimate=pl.CostEstimate(flops=30 << 20, bytes_accessed=4 << 20, transcendentals=1 << 20),
+        name="second_tiles",
+    )(pos_again)
 
     sent, y, own_high, own_low = pl.pallas_call(
         send_kernel,
         out_shape=(
             pltpu.VMEM((2, PART, LANES), f32),
             pltpu.VMEM((LANES, deep // 2), bf16),
-            pltpu.VMEM((2 * LANES, deep), bf16),
-            pltpu.VMEM((2 * LANES, deep), bf16),
+            pltpu.VMEM((LANES, deep), bf16),
+            pltpu.VMEM((LANES, deep), bf16),
         ),
-        in_specs=[vmem] * 4,
+        in_specs=[vmem] * 9,
         out_specs=[vmem] * 4,
-        scratch_shapes=[
-            pltpu.VMEM((3, 2 * LANES, LANES), f32),
-            pltpu.VMEM((2 * LANES - EARLY, deep), bf16),
-            pltpu.VMEM((2 * LANES - EARLY, deep), bf16),
-        ],
+        scratch_shapes=[pltpu.VMEM((3, LANES, LANES), f32)],
         compiler_params=params(8),
         cost_estimate=pl.CostEstimate(flops=1 << 29, bytes_accessed=4 << 20, transcendentals=0),
         name="send_products",
-    )(pos, high, low, blocks)
+    )(pos, high0, low0, high1, low1, merged, *along_x)
     half = lax.ppermute(sent, "zh", [(0, 1), (1, 0)])
 
     keep, pair = pl.pallas_call(
         keep_kernel,
         out_shape=(pltpu.VMEM((2, PART, LANES), f32), pltpu.VMEM((2, 2, 16, LANES), f32)),
-        in_specs=[vmem] * 6,
+        in_specs=[vmem] * 8,
         out_specs=[vmem] * 2,
         scratch_shapes=[
-            pltpu.VMEM((3, 2 * LANES, LANES), f32),
-            pltpu.VMEM((2 * LANES, deep), bf16),
-            pltpu.VMEM((2 * LANES, deep), bf16),
+            pltpu.VMEM((3, LANES, LANES), f32),
+            pltpu.VMEM((LANES, deep), bf16),
+            pltpu.VMEM((LANES, deep), bf16),
         ],
         compiler_params=params(8),
         cost_estimate=pl.CostEstimate(flops=1 << 29, bytes_accessed=4 << 20, transcendentals=1 << 20),
         name="keep_products",
-    )(pos, y, own_high, own_low, section, near)
+    )(pos, y, high1, low1, own_high, own_low, section, near)
     pair = lax.ppermute(pair, "zl", [(i, i ^ 2) for i in range(4)])
     core = lax.ppermute(keep[0] + half[0], "c", [(0, 1), (1, 0)])
     rest = pl.pallas_call(
@@ -338,8 +357,8 @@
 
 
 def solution(mesh):
-    fine = Mesh(mesh.devices.reshape(16, 2, 2, 4), ("yx", "zh", "c", "zl"))
-    rows = ("yx", "zh", "c")
+    fine = Mesh(mesh.devices.reshape(4, 4, 2, 2, 4), ("y", "x", "zh", "c", "zl"))
+    rows = ("y", "x", "zh", "c")
     slab = P(None, "zl", rows)
     return jax.shard_map(
         local,

time: 40.2 us -> 38.9 us (0.968)
  the two profiles are of different devices: /device:TPU:224 before, /device:TPU:1 now
where the time goes in v8:
time: 38.9 us; the launch traced here: 38.8 us
  starting transfers between devices  23.1 us (59%)
  Pallas kernels  14.4 us (37%)
  between operations  0.74 us (2%)
  waiting for transfers between devices  0.55 us (1%)
    ppermute x3, starting transfers between devices, local(): lax.ppermute(block, 'y', [(i, (i + d) % 4) for i in range(4)])  5.89 us
    ppermute x3, starting transfers between devices, local(): lax.ppermute(merged, 'x', [(i, (i + d) % 4) for i in range(4)])  4.89 us
    pallas_call x1, Pallas kernels, local(): pl.pallas_call(second_kernel, out_shape=(pltpu.VMEM((2 * LANES, deep), bf...  4.54 us
    pallas_call x1, Pallas kernels, local(): pl.pallas_call(send_kernel, out_shape=(pltpu.VMEM((2, PART, LANES), f32),...  3.91 us
    ppermute x1, starting transfers between devices, local(): pair = lax.ppermute(pair, 'zl', [(i, i ^ 2) for i in range(4)])  3.83 us
    ppermute x1, starting transfers between devices, local(): half = lax.ppermute(sent, 'zh', [(0, 1), (1, 0)])  3.55 us
    ppermute x1, starting transfers between devices, local(): core = lax.ppermute(keep[0] + half[0], 'c', [(0, 1), (1, 0)])  3.28 us
    pallas_call x1, Pallas kernels, local(): pl.pallas_call(first_kernel, out_shape=(pltpu.VMEM((LANES, deep), bf16),)...  2.5 us
  transfers between devices with their start and end apart: 10, of which 1 were waited for; matrix products, arithmetic and copies ran while one was open for 0% of the time, Pallas kernels for 33%

profile of v8, /device:TPU:1, one launch (start us, length us, event | category | flops | bytes accessed | tf_op | source)
XLA Modules:
  0.0 38.8 jit_solution(9596894731292458218)
XLA Ops:
  0.6 0.0 copy-start
  0.6 1.0 %pack_block.1 = (f32[40,128]{1,0:T(8,128)S(1)}, f32[3,8192]{1,0:T(4,128)S(1)}, f32[8,128]{1,0:T(8,128)S(1)}) custom-call(f32[2,16,128]{2,1,0:T(8,128)} %slab_ref.5, f32[1,128]{1,0:T(1,128)} %bitcast.5, f32[3,8192]{1,0:T(4,128)} %pos_ref.1, f32[1,8192]{1,0:T(1,128)} %bitcast.4), custom_call_target="tpu_custom_call" | custom-call | flops 65536 | bytes 524288 | tf_op jit(solution)/shard_map/pack_block/pallas_call | solution.py:260
  1.7 2.2 %collective-permute-start = (f32[40,128]{1,0:T(8,128)S(1)}, f32[40,128]{1,0:T(8,128)S(1)}, u32[]{:S(2)}, u32[]{:S(2)}) collective-permute-start(f32[40,128]{1,0:T(8,128)S(1)} %get-tuple-element.20.block_ref), channel_id=1, source_target_pairs={{0,64},{64,128},{128,192},{192,0},{1,65},{65,129},{129,193},{193,1... | collective-permute-start | bytes 61448 | tf_op jit(solution)/shard_map/ppermute | solution.py:270
  3.9 2.6 %collective-permute-start.1 = (f32[40,128]{1,0:T(8,128)S(1)}, f32[40,128]{1,0:T(8,128)S(1)}, u32[]{:S(2)}, u32[]{:S(2)}) collective-permute-start(f32[40,128]{1,0:T(8,128)S(1)} %get-tuple-element.20.block_ref), channel_id=1, source_target_pairs={{0,128},{64,192},{128,0},{192,64},{1,129},{65,193},{129,1},{193,65... | collective-permute-start | bytes 61448 | tf_op jit(solution)/shard_map/ppermute | solution.py:270
  6.5 1.1 %collective-permute-start.2 = (f32[40,128]{1,0:T(8,128)S(1)}, f32[40,128]{1,0:T(8,128)S(1)}, u32[]{:S(2)}, u32[]{:S(2)}) collective-permute-start(f32[40,128]{1,0:T(8,128)S(1)} %get-tuple-element.20.block_ref), channel_id=1, source_target_pairs={{0,192},{64,0},{128,64},{192,128},{1,193},{65,1},{129,65},{193,129... | collective-permute-start | bytes 61448 | tf_op jit(solution)/shard_map/ppermute | solution.py:270
  7.6 2.5 %first_tiles.1 = (bf16[128,4096]{1,0:T(8,128)(2,1)S(1)}, bf16[128,4096]{1,0:T(8,128)(2,1)S(1)}) custom-call(f32[3,8192]{1,0:T(4,128)S(1)} %get-tuple-element.17.pos_ref), custom_call_target="tpu_custom_call" | custom-call | flops 15728640 | bytes 2097152 | tf_op jit(solution)/shard_map/first_tiles/pallas_call | solution.py:272
  10.1 0.0 collective-permute-done.one_ref
  10.1 0.0 collective-permute-done.1.two_ref
  10.1 0.0 collective-permute-done.2.three_ref
  10.1 1.3 %collective-permute-start.3 = (f32[4,40,128]{2,1,0:T(8,128)S(1)}, f32[4,40,128]{2,1,0:T(8,128)S(1)}, u32[]{:S(2)}, u32[]{:S(2)}) collective-permute-start(f32[4,40,128]{2,1,0:T(8,128)S(1)} %get-tuple-element.24.all0), channel_id=1, source_target_pairs={{0,16},{16,32},{32,48},{48,0},{1,17},{17,33},{33,49},{49,1},{2,18}... | collective-permute-start | bytes 245768 | tf_op jit(solution)/shard_map/ppermute | solution.py:292
  11.4 2.5 %collective-permute-start.4 = (f32[4,40,128]{2,1,0:T(8,128)S(1)}, f32[4,40,128]{2,1,0:T(8,128)S(1)}, u32[]{:S(2)}, u32[]{:S(2)}) collective-permute-start(f32[4,40,128]{2,1,0:T(8,128)S(1)} %get-tuple-element.24.all0), channel_id=1, source_target_pairs={{0,32},{16,48},{32,0},{48,16},{1,33},{17,49},{33,1},{49,17},{2,34}... | collective-permute-start | bytes 245768 | tf_op jit(solution)/shard_map/ppermute | solution.py:292
  13.9 1.2 %collective-permute-start.5 = (f32[4,40,128]{2,1,0:T(8,128)S(1)}, f32[4,40,128]{2,1,0:T(8,128)S(1)}, u32[]{:S(2)}, u32[]{:S(2)}) collective-permute-start(f32[4,40,128]{2,1,0:T(8,128)S(1)} %get-tuple-element.24.all0), channel_id=1, source_target_pairs={{0,48},{16,0},{32,16},{48,32},{1,49},{17,1},{33,17},{49,33},{2,50}... | collective-permute-start | bytes 245768 | tf_op jit(solution)/shard_map/ppermute | solution.py:292
  15.0 0.0 copy-done
  15.0 1.6 %collective-permute-start.6 = (f32[2,16,128]{2,1,0:T(8,128)S(1)}, f32[2,16,128]{2,1,0:T(8,128)S(1)}, u32[]{:S(2)}, u32[]{:S(2)}) collective-permute-start(f32[2,16,128]{2,1,0:T(8,128)S(1)} %copy-done), channel_id=1, source_target_pairs={{0,1},{1,0},{2,3},{3,2},{4,5},{5,4},{6,7},{7,6},{8,9},{9,8},{10,11... | collective-permute-start | bytes 49160 | tf_op jit(solution)/shard_map/ppermute | solution.py:293
  16.7 4.5 %second_tiles.1 = (bf16[256,4096]{1,0:T(8,128)(2,1)S(1)}, bf16[256,4096]{1,0:T(8,128)(2,1)S(1)}) custom-call(f32[3,8192]{1,0:T(4,128)S(1)} %get-tuple-element.21.pos_ref), custom_call_target="tpu_custom_call" | custom-call | flops 31457280 | bytes 4194304 | tf_op jit(solution)/shard_map/second_tiles/pallas_call | solution.py:295
  21.2 0.0 collective-permute-done.3.all1
  21.2 0.0 collective-permute-done.4.all2
  21.2 0.0 collective-permute-done.5.all3
  21.2 3.9 %send_products.1 = (f32[2,40,128]{2,1,0:T(8,128)S(1)}, bf16[128,2048]{1,0:T(8,128)(2,1)S(1)}, bf16[128,4096]{1,0:T(8,128)(2,1)S(1)}, bf16[128,4096]{1,0:T(8,128)(2,1)S(1)}) custom-call(f32[3,8192]{1,0:T(4,128)S(1)} %get-tuple-element.17.pos_ref, bf16[128,4096]{1,0:T(8,128)(2,1)S(1)} %get-tuple-element.18.first_ref.high0, ...), custom_call_target="tpu_custom_call" | custom-call | flops 536870912 | bytes 4194304 | tf_op jit(solution)/shard_map/send_products/pallas_call | solution.py:306
  25.2 3.5 %collective-permute-start.7 = (f32[2,40,128]{2,1,0:T(8,128)S(1)}, f32[2,40,128]{2,1,0:T(8,128)S(1)}, u32[]{:S(2)}, u32[]{:S(2)}) collective-permute-start(f32[2,40,128]{2,1,0:T(8,128)S(1)} %get-tuple-element.29), channel_id=1, source_target_pairs={{0,8},{8,0},{1,9},{9,1},{2,10},{10,2},{3,11},{11,3},{4,12},{12,4},... | collective-permute-start | bytes 122888 | tf_op jit(solution)/shard_map/ppermute | solution.py:321
  28.7 0.0 collective-permute-done.6.near_ref
  28.7 0.0 copy-start.1
  28.7 0.0 copy-start.2
  28.7 1.5 %keep_products.1 = (f32[2,40,128]{2,1,0:T(8,128)S(1)}, f32[2,2,16,128]{3,2,1,0:T(8,128)S(1)}) custom-call(f32[3,8192]{1,0:T(4,128)S(1)} %get-tuple-element.17.pos_ref, bf16[128,2048]{1,0:T(8,128)(2,1)S(1)} %get-tuple-element.25.y_ref, bf16[256,4096]{1,0:T(8,128)(2,1)S(1)} %get-tuple-element.22.high1, bf16[256,4096]{1,0:T(8,128)(2,1)S(1)} %get-tuple-element.23.low1, ...), custom_call_target="tpu_custom_call" | custom-call | flops 536870912 | bytes 4194304 | tf_op jit(solution)/shard_map/keep_products/pallas_call | solution.py:323
  30.2 3.8 %collective-permute-start.9 = (f32[2,2,16,128]{3,2,1,0:T(8,128)S(1)}, f32[2,2,16,128]{3,2,1,0:T(8,128)S(1)}, u32[]{:S(2)}, u32[]{:S(2)}) collective-permute-start(f32[2,2,16,128]{3,2,1,0:T(8,128)S(1)} %get-tuple-element.30), channel_id=1, source_target_pairs={{0,2},{1,3},{2,0},{3,1},{4,6},{5,7},{6,4},{7,5},{8,10},{9,11},{10,... | collective-permute-start | bytes 98312 | tf_op jit(solution)/shard_map/ppermute | solution.py:337
  34.1 0.0 collective-permute-done.7.half_ref
  34.1 3.3 %collective-permute-start.8 = (f32[40,128]{1,0:T(8,128)S(1)}, f32[40,128]{1,0:T(8,128)S(1)}, u32[]{:S(2)}, u32[]{:S(2)}) collective-permute-start(f32[40,128]{1,0:T(8,128)S(1)} %fusion), channel_id=1, source_target_pairs={{0,4},{4,0},{1,5},{5,1},{2,6},{6,2},{3,7},{7,3},{8,12},{12,8},{9,1... | collective-permute-start | bytes 61448 | tf_op jit(solution)/shard_map/ppermute | solution.py:338
  37.3 0.0 collective-permute-done.9.pair_ref
  37.3 0.3 slab_term.1.rest_ref
  37.7 0.5 %collective-permute-done.8.core_ref = f32[40,128]{1,0:T(8,128)S(1)} collective-permute-done((f32[40,128]{1,0:T(8,128)S(1)}, f32[40,128]{1,0:T(8,128)S(1)}, u32[]{:S(2)}, u32[]{:S(2)}) %collective-permute-start.8) | collective-permute-done | bytes 20512 | tf_op jit(solution)/shard_map/ppermute | solution.py:338
  38.2 0.0 copy-done.1
  38.2 0.0 copy-done.2
  38.2 0.6 %finish_rate.1 = (f32[2,16,128]{2,1,0:T(8,128)}, f32[2,16,128]{2,1,0:T(8,128)}) custom-call(f32[2,40,128]{2,1,0:T(8,128)S(1)} %get-tuple-element.28.keep_ref, f32[2,40,128]{2,1,0:T(8,128)S(1)} %collective-permute-done.7.half_ref, f32[40,128]{1,0:T(8,128)S(1)} %collective-permute-done.8.core_ref, f32[2,16,128]{2,1,0:T(8,128)S(1)} %slab_term.1.rest_ref, ...), custom_call_target="tpu_custom_call" | custom-call | flops 65536 | bytes 262144 | tf_op jit(solution)/shard_map/finish_rate/pallas_call | solution.py:350
  (2 shorter events, 0.0 us)
Async XLA Ops:
  0.6 14.4 %copy-start = (f32[2,16,128]{2,1,0:T(8,128)S(1)}, f32[2,16,128]{2,1,0:T(8,128)}, u32[]{:S(2)}) copy-start(f32[2,16,128]{2,1,0:T(8,128)} %slab_ref.5) | copy-start | bytes 49156
  1.7 8.4 %collective-permute-start = (f32[40,128]{1,0:T(8,128)S(1)}, f32[40,128]{1,0:T(8,128)S(1)}, u32[]{:S(2)}, u32[]{:S(2)}) collective-permute-start(f32[40,128]{1,0:T(8,128)S(1)} %get-tuple-element.20.block_ref), channel_id=1, source_target_pairs={{0,64},{64,128},{128,192},{192,0},{1,65},{65,129},{129,193},{193,1... | collective-permute-start | bytes 61448 | tf_op jit(solution)/shard_map/ppermute | solution.py:270
  3.9 6.2 %collective-permute-start.1 = (f32[40,128]{1,0:T(8,128)S(1)}, f32[40,128]{1,0:T(8,128)S(1)}, u32[]{:S(2)}, u32[]{:S(2)}) collective-permute-start(f32[40,128]{1,0:T(8,128)S(1)} %get-tuple-element.20.block_ref), channel_id=1, source_target_pairs={{0,128},{64,192},{128,0},{192,64},{1,129},{65,193},{129,1},{193,65... | collective-permute-start | bytes 61448 | tf_op jit(solution)/shard_map/ppermute | solution.py:270
  6.5 3.6 %collective-permute-start.2 = (f32[40,128]{1,0:T(8,128)S(1)}, f32[40,128]{1,0:T(8,128)S(1)}, u32[]{:S(2)}, u32[]{:S(2)}) collective-permute-start(f32[40,128]{1,0:T(8,128)S(1)} %get-tuple-element.20.block_ref), channel_id=1, source_target_pairs={{0,192},{64,0},{128,64},{192,128},{1,193},{65,1},{129,65},{193,129... | collective-permute-start | bytes 61448 | tf_op jit(solution)/shard_map/ppermute | solution.py:270
  10.1 11.1 %collective-permute-start.3 = (f32[4,40,128]{2,1,0:T(8,128)S(1)}, f32[4,40,128]{2,1,0:T(8,128)S(1)}, u32[]{:S(2)}, u32[]{:S(2)}) collective-permute-start(f32[4,40,128]{2,1,0:T(8,128)S(1)} %get-tuple-element.24.all0), channel_id=1, source_target_pairs={{0,16},{16,32},{32,48},{48,0},{1,17},{17,33},{33,49},{49,1},{2,18}... | collective-permute-start | bytes 245768 | tf_op jit(solution)/shard_map/ppermute | solution.py:292
  11.4 9.8 %collective-permute-start.4 = (f32[4,40,128]{2,1,0:T(8,128)S(1)}, f32[4,40,128]{2,1,0:T(8,128)S(1)}, u32[]{:S(2)}, u32[]{:S(2)}) collective-permute-start(f32[4,40,128]{2,1,0:T(8,128)S(1)} %get-tuple-element.24.all0), channel_id=1, source_target_pairs={{0,32},{16,48},{32,0},{48,16},{1,33},{17,49},{33,1},{49,17},{2,34}... | collective-permute-start | bytes 245768 | tf_op jit(solution)/shard_map/ppermute | solution.py:292
  13.9 7.4 %collective-permute-start.5 = (f32[4,40,128]{2,1,0:T(8,128)S(1)}, f32[4,40,128]{2,1,0:T(8,128)S(1)}, u32[]{:S(2)}, u32[]{:S(2)}) collective-permute-start(f32[4,40,128]{2,1,0:T(8,128)S(1)} %get-tuple-element.24.all0), channel_id=1, source_target_pairs={{0,48},{16,0},{32,16},{48,32},{1,49},{17,1},{33,17},{49,33},{2,50}... | collective-permute-start | bytes 245768 | tf_op jit(solution)/shard_map/ppermute | solution.py:292
  15.0 13.7 %collective-permute-start.6 = (f32[2,16,128]{2,1,0:T(8,128)S(1)}, f32[2,16,128]{2,1,0:T(8,128)S(1)}, u32[]{:S(2)}, u32[]{:S(2)}) collective-permute-start(f32[2,16,128]{2,1,0:T(8,128)S(1)} %copy-done), channel_id=1, source_target_pairs={{0,1},{1,0},{2,3},{3,2},{4,5},{5,4},{6,7},{7,6},{8,9},{9,8},{10,11... | collective-permute-start | bytes 49160 | tf_op jit(solution)/shard_map/ppermute | solution.py:293
  25.2 8.9 %collective-permute-start.7 = (f32[2,40,128]{2,1,0:T(8,128)S(1)}, f32[2,40,128]{2,1,0:T(8,128)S(1)}, u32[]{:S(2)}, u32[]{:S(2)}) collective-permute-start(f32[2,40,128]{2,1,0:T(8,128)S(1)} %get-tuple-element.29), channel_id=1, source_target_pairs={{0,8},{8,0},{1,9},{9,1},{2,10},{10,2},{3,11},{11,3},{4,12},{12,4},... | collective-permute-start | bytes 122888 | tf_op jit(solution)/shard_map/ppermute | solution.py:321
  28.7 9.5 %copy-start.1 = (f32[2,16,128]{2,1,0:T(8,128)S(1)}, f32[2,16,128]{2,1,0:T(8,128)}, u32[]{:S(2)}) copy-start(f32[2,16,128]{2,1,0:T(8,128)} %base_ref.1) | copy-start | bytes 49156
  28.7 9.5 %copy-start.2 = (f32[2,16,128]{2,1,0:T(8,128)S(1)}, f32[2,16,128]{2,1,0:T(8,128)}, u32[]{:S(2)}) copy-start(f32[2,16,128]{2,1,0:T(8,128)} %accum_ref.1) | copy-start | bytes 49156
  30.2 7.1 %collective-permute-start.9 = (f32[2,2,16,128]{3,2,1,0:T(8,128)S(1)}, f32[2,2,16,128]{3,2,1,0:T(8,128)S(1)}, u32[]{:S(2)}, u32[]{:S(2)}) collective-permute-start(f32[2,2,16,128]{3,2,1,0:T(8,128)S(1)} %get-tuple-element.30), channel_id=1, source_target_pairs={{0,2},{1,3},{2,0},{3,1},{4,6},{5,7},{6,4},{7,5},{8,10},{9,11},{10,... | collective-permute-start | bytes 98312 | tf_op jit(solution)/shard_map/ppermute | solution.py:337
  34.1 4.1 %collective-permute-start.8 = (f32[40,128]{1,0:T(8,128)S(1)}, f32[40,128]{1,0:T(8,128)S(1)}, u32[]{:S(2)}, u32[]{:S(2)}) collective-permute-start(f32[40,128]{1,0:T(8,128)S(1)} %fusion), channel_id=1, source_target_pairs={{0,4},{4,0},{1,5},{5,1},{2,6},{6,2},{3,7},{7,3},{8,12},{12,8},{9,1... | collective-permute-start | bytes 61448 | tf_op jit(solution)/shard_map/ppermute | solution.py:338

commit v9 on v8

v9 whole, which is shorter than its diff:
```python
import functools
import math

import jax
import jax.numpy as jnp
from jax import lax
from jax.experimental import pallas as pl
from jax.experimental.pallas import tpu as pltpu
from jax.sharding import Mesh
from jax.sharding import PartitionSpec as P

TIME_STEP = 0.2
LANES = 128
COS = (0.9999992211, -19.73898242, 64.92872338, -85.27236068, 58.79387231, -21.07651549)
SIN = (6.283182817, -41.3414213, 81.59618177, -76.58008122, 41.20531753, -12.27114973)
SCALE = -0.75 / (2.0 * math.pi)
INV_WAVE = 1.0 / (2.0 * math.pi)
ROUNDER = 12582912.0
PART = 40
WIDE = 48


def horner(coefs, scale, arg):
    total = jnp.float32(coefs[-1] * scale)
    for c in coefs[-2::-1]:
        total = total * arg + jnp.float32(c * scale)
    return total


def coupling(dx, dy, dz):
    dz_sq = dz * dz
    dist_sq = dx * dx + dy * dy + dz_sq
    inv = lax.rsqrt(dist_sq)
    dist = dist_sq * inv
    turn = dist - ((dist + ROUNDER) - ROUNDER)
    turn_sq = turn * turn
    cosine = horner(COS, SCALE, turn_sq)
    sine = horner(SIN, SCALE, turn_sq) * turn
    inv_sq = inv * inv
    aligned = dz_sq * inv_sq
    quad_imag = inv_sq * (INV_WAVE - (3.0 * INV_WAVE) * aligned)
    quad_real = inv * ((1.0 - aligned) - INV_WAVE * quad_imag)
    return cosine * quad_real - sine * quad_imag, sine * quad_real + cosine * quad_imag


def split(value):
    high = value.astype(jnp.bfloat16)
    low = (value - high.astype(jnp.float32)).astype(jnp.bfloat16)
    return high, low


def lanes_at(index):
    return pl.ds(pl.multiple_of(index * LANES, LANES), LANES)


def place_of(dx, dy):
    y = lax.rem(lax.axis_index("y") + 4 - dy, 4)
    x = lax.rem(lax.axis_index("x") + 4 - dx, 4)
    return y * 4 + x


def own_place():
    return lax.axis_index("y") * 4 + lax.axis_index("x")


def pack_kernel(section_ref, pops_ref, pos_ref, det_ref, block_ref, pos_out, det_out, high_ref, low_ref, row_ref, sems):
    own = own_place() * 4 + lax.axis_index("zh") * 2 + lax.axis_index("c")
    moves = [
        pltpu.make_async_copy(section_ref.at[0], block_ref.at[pl.ds(0, 16)], sems.at[0]),
        pltpu.make_async_copy(section_ref.at[1], block_ref.at[pl.ds(16, 16)], sems.at[1]),
        pltpu.make_async_copy(pops_ref, block_ref.at[pl.ds(32, 1)], sems.at[2]),
        pltpu.make_async_copy(pos_ref, pos_out, sems.at[3]),
        pltpu.make_async_copy(det_ref.at[:, lanes_at(own)], det_out.at[pl.ds(0, 1)], sems.at[4]),
        pltpu.make_async_copy(det_ref.at[:, pl.ds(0, LANES)], det_out.at[pl.ds(1, 1)], sems.at[5]),
    ]
    for move in moves:
        move.start()
    for move in moves:
        move.wait()
    top = lax.broadcasted_iota(jnp.int32, (8, LANES), 0) == 0
    block_ref[32:PART, :] = jnp.where(top, 2.0 * block_ref[32:PART, :] - 1.0, 0.0)


    @pl.when(ahead() == 1)
    def _():
        fill_rows(pos_out, row_ref)
        fill_unit(0, pos_out, row_ref, high_ref, low_ref)


def halves_kernel(own_ref, other_ref, after_ref, both_ref, token_ref):
    both_ref[0] = own_ref[...]
    both_ref[1] = other_ref[...]
    token_ref[...] = own_ref[0:8, :]


def lines_kernel(zero_ref, one_ref, two_ref, three_ref, slab_ref, near_ref, after_ref, all_ref, pair_ref, token_ref):
    for n, ref in enumerate((zero_ref, one_ref, two_ref, three_ref)):
        all_ref[n] = ref[...]
    pair_ref[0] = slab_ref[...]
    pair_ref[1] = near_ref[...]
    token_ref[...] = zero_ref[0, 0:8, :]


def turned(pos_ref, k, index):
    line = pos_ref[k : k + 1, lanes_at(index)]
    return jnp.broadcast_to(line, (LANES, LANES)).T


def ahead():
    return (1 - lax.axis_index("zh")) * (lax.axis_index("zl") < 2).astype(jnp.int32)


def fill_rows(pos_ref, row_ref):
    half, core = lax.axis_index("zh"), lax.axis_index("c")
    for n, quad in enumerate((half * 2 + 1 - core, half * 2 + core)):
        for k in range(3):
            row_ref[k, n * LANES : (n + 1) * LANES, :] = turned(pos_ref, k, own_place() * 4 + quad)


def fill_unit(unit, pos_ref, row_ref, high_ref, low_ref):
    half, core = lax.axis_index("zh"), lax.axis_index("c")
    quad = (half if unit < 2 else 1 - half) * 2 + core

    def tile(step, carry):
        at = lanes_at(place_of(2 * (unit % 2) + lax.div(step, 4), lax.rem(step, 4)) * 4 + quad)
        cols = [pos_ref[k : k + 1, at] for k in range(3)]
        for n in range(0, 2 * LANES, 32):
            dx, dy, dz = [row_ref[k, n : n + 32, :] - cols[k] for k in range(3)]
            for part, value in enumerate(coupling(dx, dy, dz)):
                high, low = split(value)
                lanes = lanes_at(step + part * 8)
                high_ref[n : n + 32, lanes] = high
                low_ref[n : n + 32, lanes] = low
        return carry

    lax.fori_loop(0, 8, tile, 0)
    if unit > 0:
        return
    eye = lax.broadcasted_iota(jnp.int32, (LANES, LANES), 0) == lax.broadcasted_iota(jnp.int32, (LANES, LANES), 1)
    for part in range(2):
        lanes = slice(part * 8 * LANES, (part * 8 + 1) * LANES)
        for ref in (high_ref, low_ref):
            own = ref[LANES:, lanes].astype(jnp.float32)
            ref[LANES:, lanes] = jnp.where(eye, 0.0, own).astype(jnp.bfloat16)


def near_kernel(pos_ref, high0_ref, low0_ref, high1_ref, low1_ref, row_ref):
    fill_rows(pos_ref, row_ref)
    fill_unit(1, pos_ref, row_ref, high1_ref, low1_ref)

    @pl.when(ahead() == 0)
    def _():
        fill_unit(0, pos_ref, row_ref, high0_ref, low0_ref)


def far_kernel(unit, pos_ref, row_ref, token_ref, high_ref, low_ref):
    fill_unit(unit, pos_ref, row_ref, high_ref, low_ref)


def term_kernel(pos_ref, slab_ref, near_ref, pair_ref, det_ref, rest_ref, row_ref, full_ref):
    own = lax.axis_index("zl")
    start = pl.multiple_of(own * 16, 16)
    offsets = []
    for k in range(3):
        row_ref[k] = turned(pos_ref, k, 0)
        offsets.append(row_ref[k, pl.ds(start, 16), :] - pos_ref[k : k + 1, 0:LANES])
    w_real, w_imag = coupling(*offsets)
    eye = (lax.broadcasted_iota(jnp.int32, (16, LANES), 0) + start) == lax.broadcasted_iota(jnp.int32, (16, LANES), 1)
    w_real = jnp.where(eye, det_ref[1:2, :], w_real)[:, 0:64]
    w_imag = jnp.where(eye, -0.5, w_imag)[:, 0:64]
    for n, ref in enumerate((slab_ref, near_ref, pair_ref.at[0], pair_ref.at[1])):
        place = own + (n % 2) * (1 - 2 * (own % 2))
        place = place + (n // 2) * (2 - 4 * (own // 2))
        there = pl.ds(pl.multiple_of(place * 16, 16), 16)
        full_ref[0, there, :] = ref[0]
        full_ref[1, there, :] = ref[1]

    def mul(a, b):
        return jnp.dot(a, b, precision=lax.Precision.HIGHEST, preferred_element_type=jnp.float32)

    v_real = mul(w_real, full_ref[0]) + mul(w_imag, full_ref[1])
    v_imag = mul(w_real, full_ref[1]) - mul(w_imag, full_ref[0])
    y_real, y_imag = slab_ref[0], slab_ref[1]
    line = det_ref[0:1, :]
    rest_ref[0] = line * y_imag - 0.5 * y_real - v_imag
    rest_ref[1] = v_real - line * y_real - 0.5 * y_imag


def early_own():
    return (1 - lax.axis_index("zh")) * (lax.axis_index("zl") < 2).astype(jnp.int32)


def fill_slab(unit, refs, y_ref):
    zeros = jnp.zeros((16, LANES), jnp.float32)
    for step in range(8):
        block = refs[2 * (unit % 2) + step // 4][step % 4, unit // 2]
        pops = jnp.concatenate([block[32:40], zeros[0:8]], axis=0)
        lanes = slice(step * LANES, (step + 1) * LANES)
        for n, value in enumerate((block[0:16], block[16:32], pops)):
            high, low = split(value)
            y_ref[n * 16 : n * 16 + 16, lanes] = high
            y_ref[WIDE + n * 16 : WIDE + n * 16 + 16, lanes] = low
        y_ref[2 * WIDE :, lanes] = jnp.zeros((LANES - 2 * WIDE, LANES), jnp.bfloat16)


def dot_slab(tiles, y):
    return lax.dot_general(tiles, y, (((1,), (1,)), ((), ())), preferred_element_type=jnp.float32)


def store_products(by_real, by_imag, out_ref, at):
    for n in range(by_real.shape[0] // LANES):
        rows = slice(n * LANES, (n + 1) * LANES)
        real, imag = by_real[rows, :].T, by_imag[rows, :].T
        real = real[0:PART] + real[WIDE : WIDE + PART]
        imag = imag[0:32] + imag[WIDE : WIDE + 32]
        out_ref[at + n, 0:16, :] = real[0:16] - imag[16:32]
        out_ref[at + n, 16:32, :] = real[16:32] + imag[0:16]
        out_ref[at + n, 32:PART, :] = real[32:PART]


def products(high_ref, low_ref, y):
    half = high_ref.shape[1] // 2
    by_real = dot_slab(high_ref[:, 0:half], y) + dot_slab(low_ref[:, 0:half], y)
    by_imag = dot_slab(high_ref[:, half:], y) + dot_slab(low_ref[:, half:], y)
    return by_real, by_imag


def product_kernel(early_high, early_low, high0, low0, high1, low1, high2, low2, high3, low3, all0, all1, all2, all3, out_ref, y_ref, real_ref, imag_ref):
    refs = (all0, all1, all2, all3)
    for unit in range(4):
        fill_slab(unit, refs, y_ref.at[unit])

    @pl.when(ahead() == 1)
    def _():
        real_ref[...], imag_ref[...] = products(early_high, early_low, y_ref[0])

    @pl.when(ahead() == 0)
    def _():
        real_ref[...], imag_ref[...] = products(high0, low0, y_ref[0])

    by_real, by_imag = real_ref[...], imag_ref[...]
    for unit, (high, low) in ((1, (high1, low1)), (2, (high2, low2)), (3, (high3, low3))):
        more_real, more_imag = products(high, low, y_ref[unit])
        by_real, by_imag = by_real + more_real, by_imag + more_imag
    store_products(by_real, by_imag, out_ref, 0)


def finish_kernel(keep_ref, core_ref, rest_ref, slab_ref, base_ref, accum_ref, next_ref, acc_ref):
    z = keep_ref[1] + core_ref[...]
    shift = z[32:33]
    rate_real = z[16:32] + shift * slab_ref[1] + rest_ref[0]
    rate_imag = rest_ref[1] - z[0:16] - shift * slab_ref[0]
    for n, rate in enumerate((rate_real, rate_imag)):
        next_ref[n] = base_ref[n] + (0.5 * TIME_STEP) * rate
        acc_ref[n] = accum_ref[n] + (TIME_STEP / 3.0) * rate


def params(mib):
    return pltpu.CompilerParams(vmem_limit_bytes=mib << 20)


def in_hbm(array):
    return pltpu.with_memory_space_constraint(array, pltpu.HBM)


def local(positions, detuning, populations, base, section, accum):
    bf16, f32 = jnp.bfloat16, jnp.float32
    count = positions.shape[1]
    hbm, vmem = pl.BlockSpec(memory_space=pltpu.HBM), pl.BlockSpec(memory_space=pltpu.VMEM)
    anywhere = pl.BlockSpec(memory_space=pl.ANY)
    unit = pltpu.VMEM((2 * LANES, 16 * LANES), bf16)
    token = pltpu.VMEM((8, LANES), f32)
    rows = pltpu.VMEM((3, 2 * LANES, LANES), f32)

    def call(kernel, name, out_shape, in_specs, flops, scratch=()):
        return pl.pallas_call(
            kernel,
            out_shape=out_shape,
            in_specs=in_specs,
            out_specs=[vmem] * len(out_shape),
            scratch_shapes=scratch,
            compiler_params=params(6),
            cost_estimate=pl.CostEstimate(flops=flops, bytes_accessed=1 << 20, transcendentals=0),
            name=name,
        )

    block, pos, det, early_high, early_low = call(
        pack_kernel,
        "pack_block",
        (pltpu.VMEM((PART, LANES), f32), pltpu.VMEM(positions.shape, f32), token, unit, unit),
        [hbm] * 4,
        1 << 16,
        [rows, pltpu.SemaphoreType.DMA((6,))],
    )(in_hbm(section), in_hbm(populations.reshape(1, LANES)), in_hbm(positions), in_hbm(detuning.reshape(1, count)))
    other = lax.ppermute(block, "zh", [(0, 1), (1, 0)])
    near = lax.ppermute(section, "zl", [(i, i ^ 1) for i in range(4)])
    high0, low0, high1, low1, row = call(
        near_kernel, "near_tiles", (unit, unit, unit, unit, rows), [vmem], 30 << 20
    )(pos)

    both, second = call(
        halves_kernel, "join_halves", (pltpu.VMEM((2, PART, LANES), f32), token), [vmem, vmem, anywhere], 1
    )(block, other, high1)
    along_y = [lax.ppermute(both, "y", [(i, (i + d) % 4) for i in range(4)]) for d in (2, 1, 3)]
    high2, low2 = call(
        functools.partial(far_kernel, 2), "far_tiles_a", (unit, unit), [vmem, vmem, anywhere], 15 << 20
    )(pos, row, second)

    lines, pair, third = call(
        lines_kernel,
        "join_lines",
        (pltpu.VMEM((4, 2, PART, LANES), f32), pltpu.VMEM((2, 2, 16, LANES), f32), token),
        [vmem] * 6 + [anywhere],
        1,
    )(both, along_y[1], along_y[0], along_y[2], section, near, high2)
    along_x = [lax.ppermute(lines, "x", [(i, (i + d) % 4) for i in range(4)]) for d in (2, 1, 3)]
    pair = lax.ppermute(pair, "zl", [(i, i ^ 2) for i in range(4)])
    high3, low3 = call(
        functools.partial(far_kernel, 3), "far_tiles_b", (unit, unit), [vmem, vmem, anywhere], 15 << 20
    )(pos, row, third)

    (keep,) = call(
        product_kernel,
        "tile_products",
        (pltpu.VMEM((2, PART, LANES), f32),),
        [vmem] * 14,
        1 << 30,
        [
            pltpu.VMEM((4, LANES, 8 * LANES), bf16),
            pltpu.VMEM((2 * LANES, LANES), f32),
            pltpu.VMEM((2 * LANES, LANES), f32),
        ],
    )(early_high, early_low, high0, low0, high1, low1, high2, low2, high3, low3, lines, along_x[1], along_x[0], along_x[2])
    core = lax.ppermute(keep[0], "c", [(0, 1), (1, 0)])
    rest = pl.pallas_call(
        term_kernel,
        out_shape=pltpu.VMEM((2, 16, LANES), f32),
        in_specs=[vmem] * 5,
        out_specs=vmem,
        scratch_shapes=[pltpu.VMEM((3, LANES, LANES), f32), pltpu.VMEM((2, 64, LANES), f32)],
        compiler_params=params(4),
        cost_estimate=pl.CostEstimate(flops=1 << 22, bytes_accessed=1 << 18, transcendentals=1 << 11),
        name="slab_term",
    )(pos, section, near, pair, det)

    return pl.pallas_call(
        finish_kernel,
        out_shape=(jax.ShapeDtypeStruct(base.shape, f32),) * 2,
        compiler_params=params(4),
        cost_estimate=pl.CostEstimate(flops=1 << 16, bytes_accessed=1 << 18, transcendentals=0),
        name="finish_rate",
    )(keep, core, rest, section, base, accum)


def solution(mesh):
    fine = Mesh(mesh.devices.reshape(4, 4, 2, 2, 4), ("y", "x", "zh", "c", "zl"))
    rows = ("y", "x", "zh", "c")
    slab = P(None, "zl", rows)
    return jax.shard_map(
        local,
        mesh=fine,
        in_specs=(P(), P(), P(rows), slab, slab, slab),
        out_specs=(slab, slab),
        check_vma=False,
    )
```

time: 38.9 us -> 38.6 us (level)
  Pallas kernels: 14.4 us -> 13.8 us
    ppermute x8, starting transfers between devices: 17.6 us -> 19.1 us  [the longest x1 5.42 us: local(): other = lax.ppermute(block, 'zh', [(0, 1), (1, 0)])]
    ppermute x1, starting transfers between devices: 3.83 us -> 2.93 us  [local(): pair = lax.ppermute(pair, 'zl', [(i, i ^ 2) for i in range(4)])]
    pallas_call x6 -> x7, Pallas kernels: 13.5 us -> 12.9 us  [the longest x1 3.43 us: local(): call(pack_kernel, 'pack_block', (pltpu.VMEM((PART, LANES), f32), pltpu.VM...]
    ppermute x1, starting transfers between devices: 1.64 us -> 1.23 us  [local(): near = lax.ppermute(section, 'zl', [(i, i ^ 1) for i in range(4)])]
  transfers between devices with their start and end apart: 10 -> 10, of which waited for: 1 -> 1; matrix products, arithmetic and copies ran while one was open for 0% -> 0% of each run, Pallas kernels for 33% -> 25%
where the time goes in v9:
time: 38.6 us; the launch traced here: 38.5 us
  starting transfers between devices  23.3 us (60%)
  Pallas kernels  13.8 us (36%)
  between operations  0.77 us (2%)
  waiting for transfers between devices  0.55 us (1%)
    ppermute x1, starting transfers between devices, local(): other = lax.ppermute(block, 'zh', [(0, 1), (1, 0)])  5.42 us
    ppermute x3, starting transfers between devices, local(): lax.ppermute(both, 'y', [(i, (i + d) % 4) for i in range(4)])  5.06 us
    ppermute x3, starting transfers between devices, local(): lax.ppermute(lines, 'x', [(i, (i + d) % 4) for i in range(4)])  4.89 us
    ppermute x1, starting transfers between devices, local(): core = lax.ppermute(keep[0], 'c', [(0, 1), (1, 0)])  3.77 us
    pallas_call x1, Pallas kernels, local(): call(pack_kernel, 'pack_block', (pltpu.VMEM((PART, LANES), f32), pltpu.VM...  3.43 us
    ppermute x1, starting transfers between devices, local(): pair = lax.ppermute(pair, 'zl', [(i, i ^ 2) for i in range(4)])  2.93 us
    pallas_call x1, Pallas kernels, local(): call(product_kernel, 'tile_products', (pltpu.VMEM((2, PART, LANES), f32),...  2.68 us
    pallas_call x1, Pallas kernels, local(): call(near_kernel, 'near_tiles', (unit, unit, unit, unit, rows), [vmem], 3...  2.34 us
  transfers between devices with their start and end apart: 10, of which 1 were waited for; matrix products, arithmetic and copies ran while one was open for 0% of the time, Pallas kernels for 25%

profile of v9, /device:TPU:1, one launch (start us, length us, event | category | flops | bytes accessed | tf_op | source)
XLA Modules:
  0.0 38.5 jit_solution(8993471781317950478)
XLA Ops:
  0.6 3.4 %pack_block.1 = (f32[40,128]{1,0:T(8,128)S(1)}, f32[3,8192]{1,0:T(4,128)S(1)}, f32[8,128]{1,0:T(8,128)S(1)}, bf16[256,2048]{1,0:T(8,128)(2,1)S(1)}, bf16[256,2048]{1,0:T(8,128)(2,1)S(1)}) custom-call(f32[2,16,128]{2,1,0:T(8,128)} %slab_ref.5, f32[1,128]{1,0:T(1,128)} %bitcast.5, f32[3,8192]{1,0:T(4,128)} %pos_ref.1, f32[1,8192]{1,0:T(1,128)} %bitcast.4), custom_call_target="tpu_custom_call" | custom-call | flops 65536 | bytes 1048576 | tf_op jit(solution)/shard_map/pack_block/pallas_call | solution.py:287
  4.1 5.4 %collective-permute-start = (f32[40,128]{1,0:T(8,128)S(1)}, f32[40,128]{1,0:T(8,128)S(1)}, u32[]{:S(2)}, u32[]{:S(2)}) collective-permute-start(f32[40,128]{1,0:T(8,128)S(1)} %get-tuple-element.29.own_ref), channel_id=1, source_target_pairs={{0,8},{8,0},{1,9},{9,1},{2,10},{10,2},{3,11},{11,3},{4,12},{12,4},... | collective-permute-start | bytes 61448 | tf_op jit(solution)/shard_map/ppermute | solution.py:295
  9.5 2.3 %near_tiles.1 = (bf16[256,2048]{1,0:T(8,128)(2,1)S(1)}, bf16[256,2048]{1,0:T(8,128)(2,1)S(1)}, bf16[256,2048]{1,0:T(8,128)(2,1)S(1)}, bf16[256,2048]{1,0:T(8,128)(2,1)S(1)}, f32[3,256,128]{2,1,0:T(8,128)S(1)}) custom-call(f32[3,8192]{1,0:T(4,128)S(1)} %get-tuple-element.23.pos_ref), custom_call_target="tpu_custom_call" | custom-call | flops 31457280 | bytes 1048576 | tf_op jit(solution)/shard_map/near_tiles/pallas_call | solution.py:297
  11.8 0.0 collective-permute-done.other_ref
  11.8 0.0 copy-start
  11.9 1.4 %collective-permute-start.1 = (f32[2,40,128]{2,1,0:T(8,128)S(1)}, f32[2,40,128]{2,1,0:T(8,128)S(1)}, u32[]{:S(2)}, u32[]{:S(2)}) collective-permute-start(f32[2,40,128]{2,1,0:T(8,128)S(1)} %get-tuple-element.33.zero_ref), channel_id=1, source_target_pairs={{0,64},{64,128},{128,192},{192,0},{1,65},{65,129},{129,193},{193,1... | collective-permute-start | bytes 122888 | tf_op jit(solution)/shard_map/ppermute | solution.py:304
  13.2 2.6 %collective-permute-start.2 = (f32[2,40,128]{2,1,0:T(8,128)S(1)}, f32[2,40,128]{2,1,0:T(8,128)S(1)}, u32[]{:S(2)}, u32[]{:S(2)}) collective-permute-start(f32[2,40,128]{2,1,0:T(8,128)S(1)} %get-tuple-element.33.zero_ref), channel_id=1, source_target_pairs={{0,128},{64,192},{128,0},{192,64},{1,129},{65,193},{129,1},{193,65... | collective-permute-start | bytes 122888 | tf_op jit(solution)/shard_map/ppermute | solution.py:304
  15.9 1.1 %collective-permute-start.3 = (f32[2,40,128]{2,1,0:T(8,128)S(1)}, f32[2,40,128]{2,1,0:T(8,128)S(1)}, u32[]{:S(2)}, u32[]{:S(2)}) collective-permute-start(f32[2,40,128]{2,1,0:T(8,128)S(1)} %get-tuple-element.33.zero_ref), channel_id=1, source_target_pairs={{0,192},{64,0},{128,64},{192,128},{1,193},{65,1},{129,65},{193,129... | collective-permute-start | bytes 122888 | tf_op jit(solution)/shard_map/ppermute | solution.py:304
  16.9 0.0 copy-done
  16.9 1.2 %collective-permute-start.4 = (f32[2,16,128]{2,1,0:T(8,128)S(1)}, f32[2,16,128]{2,1,0:T(8,128)S(1)}, u32[]{:S(2)}, u32[]{:S(2)}) collective-permute-start(f32[2,16,128]{2,1,0:T(8,128)S(1)} %copy-done), channel_id=1, source_target_pairs={{0,1},{1,0},{2,3},{3,2},{4,5},{5,4},{6,7},{7,6},{8,9},{9,8},{10,11... | collective-permute-start | bytes 49160 | tf_op jit(solution)/shard_map/ppermute | solution.py:296
  18.2 2.2 %far_tiles_a.1 = (bf16[256,2048]{1,0:T(8,128)(2,1)S(1)}, bf16[256,2048]{1,0:T(8,128)(2,1)S(1)}) custom-call(f32[3,8192]{1,0:T(4,128)S(1)} %get-tuple-element.23.pos_ref, f32[3,256,128]{2,1,0:T(8,128)S(1)} %get-tuple-element.28.row_ref, f32[8,128]{1,0:T(8,128)S(1)} %get-tuple-element.30.token_ref), custom_call_target="tpu_custom_call" | custom-call | flops 15728640 | bytes 1048576 | tf_op jit(solution)/shard_map/far_tiles_a/pallas_call | solution.py:305
  20.4 0.0 collective-permute-done.4.near_ref
  20.4 0.0 collective-permute-done.1.one_ref
  20.4 0.0 collective-permute-done.2.two_ref
  20.4 0.0 collective-permute-done.3.three_ref
  20.4 1.3 %collective-permute-start.5 = (f32[4,2,40,128]{3,2,1,0:T(8,128)S(1)}, f32[4,2,40,128]{3,2,1,0:T(8,128)S(1)}, u32[]{:S(2)}, u32[]{:S(2)}) collective-permute-start(f32[4,2,40,128]{3,2,1,0:T(8,128)S(1)} %get-tuple-element.37.all0), channel_id=1, source_target_pairs={{0,16},{16,32},{32,48},{48,0},{1,17},{17,33},{33,49},{49,1},{2,18}... | collective-permute-start | bytes 491528 | tf_op jit(solution)/shard_map/ppermute | solution.py:316
  21.7 2.5 %collective-permute-start.6 = (f32[4,2,40,128]{3,2,1,0:T(8,128)S(1)}, f32[4,2,40,128]{3,2,1,0:T(8,128)S(1)}, u32[]{:S(2)}, u32[]{:S(2)}) collective-permute-start(f32[4,2,40,128]{3,2,1,0:T(8,128)S(1)} %get-tuple-element.37.all0), channel_id=1, source_target_pairs={{0,32},{16,48},{32,0},{48,16},{1,33},{17,49},{33,1},{49,17},{2,34}... | collective-permute-start | bytes 491528 | tf_op jit(solution)/shard_map/ppermute | solution.py:316
  24.2 1.2 %collective-permute-start.7 = (f32[4,2,40,128]{3,2,1,0:T(8,128)S(1)}, f32[4,2,40,128]{3,2,1,0:T(8,128)S(1)}, u32[]{:S(2)}, u32[]{:S(2)}) collective-permute-start(f32[4,2,40,128]{3,2,1,0:T(8,128)S(1)} %get-tuple-element.37.all0), channel_id=1, source_target_pairs={{0,48},{16,0},{32,16},{48,32},{1,49},{17,1},{33,17},{49,33},{2,50}... | collective-permute-start | bytes 491528 | tf_op jit(solution)/shard_map/ppermute | solution.py:316
  25.3 2.9 %collective-permute-start.9 = (f32[2,2,16,128]{3,2,1,0:T(8,128)S(1)}, f32[2,2,16,128]{3,2,1,0:T(8,128)S(1)}, u32[]{:S(2)}, u32[]{:S(2)}) collective-permute-start(f32[2,2,16,128]{3,2,1,0:T(8,128)S(1)} %get-tuple-element.38), channel_id=1, source_target_pairs={{0,2},{1,3},{2,0},{3,1},{4,6},{5,7},{6,4},{7,5},{8,10},{9,11},{10,... | collective-permute-start | bytes 98312 | tf_op jit(solution)/shard_map/ppermute | solution.py:317
  28.3 2.2 %far_tiles_b.1 = (bf16[256,2048]{1,0:T(8,128)(2,1)S(1)}, bf16[256,2048]{1,0:T(8,128)(2,1)S(1)}) custom-call(f32[3,8192]{1,0:T(4,128)S(1)} %get-tuple-element.23.pos_ref, f32[3,256,128]{2,1,0:T(8,128)S(1)} %get-tuple-element.28.row_ref, f32[8,128]{1,0:T(8,128)S(1)} %get-tuple-element.34.token_ref), custom_call_target="tpu_custom_call" | custom-call | flops 15728640 | bytes 1048576 | tf_op jit(solution)/shard_map/far_tiles_b/pallas_call | solution.py:318
  30.5 0.0 collective-permute-done.5.all1
  30.5 0.0 collective-permute-done.6.all2
  30.5 0.0 collective-permute-done.7.all3
  30.5 2.7 %tile_products.1.keep_ref = f32[2,40,128]{2,1,0:T(8,128)S(1)} custom-call(bf16[256,2048]{1,0:T(8,128)(2,1)S(1)} %get-tuple-element.21.early_high, bf16[256,2048]{1,0:T(8,128)(2,1)S(1)} %get-tuple-element.22.early_low, bf16[256,2048]{1,0:T(8,128)(2,1)S(1)} %get-tuple-element.24.high0, bf16[256,2048]{1,0:T(8,128)(2,1)S(1)} %get-tuple-element.25.low0, ...), custom_call_target="tpu_custom_call" | custom-call | flops 1073741824 | bytes 1048576 | tf_op jit(solution)/shard_map/tile_products/pallas_call | solution.py:322
  33.2 3.8 %collective-permute-start.8 = (f32[40,128]{1,0:T(8,128)S(1)}, f32[40,128]{1,0:T(8,128)S(1)}, u32[]{:S(2)}, u32[]{:S(2)}) collective-permute-start(f32[40,128]{1,0:T(8,128)S(1)} %slice_bitcast_fusion), channel_id=1, source_target_pairs={{0,4},{4,0},{1,5},{5,1},{2,6},{6,2},{3,7},{7,3},{8,12},{12,8},{9,1... | collective-permute-start | bytes 61448 | tf_op jit(solution)/shard_map/ppermute | solution.py:334
  37.0 0.0 collective-permute-done.9.pair_ref
  37.0 0.0 copy-start.1
  37.0 0.0 copy-start.2
  37.0 0.3 slab_term.1.rest_ref
  37.3 0.5 %collective-permute-done.8.core_ref = f32[40,128]{1,0:T(8,128)S(1)} collective-permute-done((f32[40,128]{1,0:T(8,128)S(1)}, f32[40,128]{1,0:T(8,128)S(1)}, u32[]{:S(2)}, u32[]{:S(2)}) %collective-permute-start.8) | collective-permute-done | bytes 20512 | tf_op jit(solution)/shard_map/ppermute | solution.py:334
  37.8 0.0 copy-done.1
  37.8 0.0 copy-done.2
  37.8 0.6 %finish_rate.1 = (f32[2,16,128]{2,1,0:T(8,128)}, f32[2,16,128]{2,1,0:T(8,128)}) custom-call(f32[2,40,128]{2,1,0:T(8,128)S(1)} %tile_products.1.keep_ref, f32[40,128]{1,0:T(8,128)S(1)} %collective-permute-done.8.core_ref, f32[2,16,128]{2,1,0:T(8,128)S(1)} %slab_term.1.rest_ref, f32[2,16,128]{2,1,0:T(8,128)S(1)} %copy-done, f32[2,16,128]{2,1,0:T(8,128)S(1)} %copy-done.1, ...), custom_call_target="tpu_custom_call" | custom-call | flops 65536 | bytes 262144 | tf_op jit(solution)/shard_map/finish_rate/pallas_call | solution.py:346
  (3 shorter events, 0.0 us)
Async XLA Ops:
  4.1 7.8 %collective-permute-start = (f32[40,128]{1,0:T(8,128)S(1)}, f32[40,128]{1,0:T(8,128)S(1)}, u32[]{:S(2)}, u32[]{:S(2)}) collective-permute-start(f32[40,128]{1,0:T(8,128)S(1)} %get-tuple-element.29.own_ref), channel_id=1, source_target_pairs={{0,8},{8,0},{1,9},{9,1},{2,10},{10,2},{3,11},{11,3},{4,12},{12,4},... | collective-permute-start | bytes 61448 | tf_op jit(solution)/shard_map/ppermute | solution.py:295
  11.8 5.1 %copy-start = (f32[2,16,128]{2,1,0:T(8,128)S(1)}, f32[2,16,128]{2,1,0:T(8,128)}, u32[]{:S(2)}) copy-start(f32[2,16,128]{2,1,0:T(8,128)} %slab_ref.5) | copy-start | bytes 49156
  11.9 8.5 %collective-permute-start.1 = (f32[2,40,128]{2,1,0:T(8,128)S(1)}, f32[2,40,128]{2,1,0:T(8,128)S(1)}, u32[]{:S(2)}, u32[]{:S(2)}) collective-permute-start(f32[2,40,128]{2,1,0:T(8,128)S(1)} %get-tuple-element.33.zero_ref), channel_id=1, source_target_pairs={{0,64},{64,128},{128,192},{192,0},{1,65},{65,129},{129,193},{193,1... | collective-permute-start | bytes 122888 | tf_op jit(solution)/shard_map/ppermute | solution.py:304
  13.2 7.1 %collective-permute-start.2 = (f32[2,40,128]{2,1,0:T(8,128)S(1)}, f32[2,40,128]{2,1,0:T(8,128)S(1)}, u32[]{:S(2)}, u32[]{:S(2)}) collective-permute-start(f32[2,40,128]{2,1,0:T(8,128)S(1)} %get-tuple-element.33.zero_ref), channel_id=1, source_target_pairs={{0,128},{64,192},{128,0},{192,64},{1,129},{65,193},{129,1},{193,65... | collective-permute-start | bytes 122888 | tf_op jit(solution)/shard_map/ppermute | solution.py:304
  15.9 4.5 %collective-permute-start.3 = (f32[2,40,128]{2,1,0:T(8,128)S(1)}, f32[2,40,128]{2,1,0:T(8,128)S(1)}, u32[]{:S(2)}, u32[]{:S(2)}) collective-permute-start(f32[2,40,128]{2,1,0:T(8,128)S(1)} %get-tuple-element.33.zero_ref), channel_id=1, source_target_pairs={{0,192},{64,0},{128,64},{192,128},{1,193},{65,1},{129,65},{193,129... | collective-permute-start | bytes 122888 | tf_op jit(solution)/shard_map/ppermute | solution.py:304
  16.9 3.4 %collective-permute-start.4 = (f32[2,16,128]{2,1,0:T(8,128)S(1)}, f32[2,16,128]{2,1,0:T(8,128)S(1)}, u32[]{:S(2)}, u32[]{:S(2)}) collective-permute-start(f32[2,16,128]{2,1,0:T(8,128)S(1)} %copy-done), channel_id=1, source_target_pairs={{0,1},{1,0},{2,3},{3,2},{4,5},{5,4},{6,7},{7,6},{8,9},{9,8},{10,11... | collective-permute-start | bytes 49160 | tf_op jit(solution)/shard_map/ppermute | solution.py:296
  20.4 10.1 %collective-permute-start.5 = (f32[4,2,40,128]{3,2,1,0:T(8,128)S(1)}, f32[4,2,40,128]{3,2,1,0:T(8,128)S(1)}, u32[]{:S(2)}, u32[]{:S(2)}) collective-permute-start(f32[4,2,40,128]{3,2,1,0:T(8,128)S(1)} %get-tuple-element.37.all0), channel_id=1, source_target_pairs={{0,16},{16,32},{32,48},{48,0},{1,17},{17,33},{33,49},{49,1},{2,18}... | collective-permute-start | bytes 491528 | tf_op jit(solution)/shard_map/ppermute | solution.py:316
  21.7 8.8 %collective-permute-start.6 = (f32[4,2,40,128]{3,2,1,0:T(8,128)S(1)}, f32[4,2,40,128]{3,2,1,0:T(8,128)S(1)}, u32[]{:S(2)}, u32[]{:S(2)}) collective-permute-start(f32[4,2,40,128]{3,2,1,0:T(8,128)S(1)} %get-tuple-element.37.all0), channel_id=1, source_target_pairs={{0,32},{16,48},{32,0},{48,16},{1,33},{17,49},{33,1},{49,17},{2,34}... | collective-permute-start | bytes 491528 | tf_op jit(solution)/shard_map/ppermute | solution.py:316
  24.2 6.3 %collective-permute-start.7 = (f32[4,2,40,128]{3,2,1,0:T(8,128)S(1)}, f32[4,2,40,128]{3,2,1,0:T(8,128)S(1)}, u32[]{:S(2)}, u32[]{:S(2)}) collective-permute-start(f32[4,2,40,128]{3,2,1,0:T(8,128)S(1)} %get-tuple-element.37.all0), channel_id=1, source_target_pairs={{0,48},{16,0},{32,16},{48,32},{1,49},{17,1},{33,17},{49,33},{2,50}... | collective-permute-start | bytes 491528 | tf_op jit(solution)/shard_map/ppermute | solution.py:316
  25.3 11.7 %collective-permute-start.9 = (f32[2,2,16,128]{3,2,1,0:T(8,128)S(1)}, f32[2,2,16,128]{3,2,1,0:T(8,128)S(1)}, u32[]{:S(2)}, u32[]{:S(2)}) collective-permute-start(f32[2,2,16,128]{3,2,1,0:T(8,128)S(1)} %get-tuple-element.38), channel_id=1, source_target_pairs={{0,2},{1,3},{2,0},{3,1},{4,6},{5,7},{6,4},{7,5},{8,10},{9,11},{10,... | collective-permute-start | bytes 98312 | tf_op jit(solution)/shard_map/ppermute | solution.py:317
  33.2 4.6 %collective-permute-start.8 = (f32[40,128]{1,0:T(8,128)S(1)}, f32[40,128]{1,0:T(8,128)S(1)}, u32[]{:S(2)}, u32[]{:S(2)}) collective-permute-start(f32[40,128]{1,0:T(8,128)S(1)} %slice_bitcast_fusion), channel_id=1, source_target_pairs={{0,4},{4,0},{1,5},{5,1},{2,6},{6,2},{3,7},{7,3},{8,12},{12,8},{9,1... | collective-permute-start | bytes 61448 | tf_op jit(solution)/shard_map/ppermute | solution.py:334
  37.0 0.8 %copy-start.1 = (f32[2,16,128]{2,1,0:T(8,128)S(1)}, f32[2,16,128]{2,1,0:T(8,128)}, u32[]{:S(2)}) copy-start(f32[2,16,128]{2,1,0:T(8,128)} %base_ref.1) | copy-start | bytes 49156
  37.0 0.8 %copy-start.2 = (f32[2,16,128]{2,1,0:T(8,128)S(1)}, f32[2,16,128]{2,1,0:T(8,128)}, u32[]{:S(2)}) copy-start(f32[2,16,128]{2,1,0:T(8,128)} %accum_ref.1) | copy-start | bytes 49156

commit v10 on v8

--- a/solution.py
+++ b/solution.py
@@ -1,3 +1,4 @@
+import functools
 import math
 
 import jax
@@ -53,8 +54,9 @@
 
 
 def place_of(step):
-    y = lax.rem(lax.axis_index("y") + 4 - lax.rem(step, 4), 4)
-    x = lax.rem(lax.axis_index("x") + 4 - lax.div(step, 4), 4)
+    down, across = lax.rem(step, 4), lax.div(step, 4)
+    y = lax.axis_index("y") ^ down ^ lax.div(down, 2)
+    x = lax.axis_index("x") ^ across ^ lax.div(across, 2)
     return y * 4 + x
 
 
@@ -80,10 +82,18 @@
     block_ref[32:PART, :] = jnp.where(top, 2.0 * block_ref[32:PART, :] - 1.0, 0.0)
 
 
-def merge_kernel(block_ref, one_ref, two_ref, three_ref, pos_ref, first_ref, all_ref, pos_out):
-    for n, ref in enumerate((block_ref, one_ref, two_ref, three_ref)):
-        all_ref[n] = ref[...]
-    pos_out[...] = pos_ref[...]
+def pair_kernel(block_ref, one_ref, after_ref, both_ref, token_ref):
+    both_ref[0] = block_ref[...]
+    both_ref[1] = one_ref[...]
+    token_ref[...] = block_ref[0:8, :]
+
+
+def line_kernel(both_ref, two_ref, slab_ref, near_ref, after_ref, all_ref, pair_ref, token_ref):
+    all_ref[0:2] = both_ref[...]
+    all_ref[2:4] = two_ref[...]
+    pair_ref[0] = slab_ref[...]
+    pair_ref[1] = near_ref[...]
+    token_ref[...] = both_ref[0, 0:8, :]
 
 
 def turned(pos_ref, k, index):
@@ -144,10 +154,6 @@
     rest_ref[1] = v_real - line * y_real - 0.5 * y_imag
 
 
-def early_own():
-    return (1 - lax.axis_index("zh")) * (lax.axis_index("zl") < 2).astype(jnp.int32)
-
-
 def fill_own(pos_ref, row_ref, high_ref, low_ref):
     tiles = pos_ref.shape[1] // (4 * LANES)
     quad = lax.axis_index("zh") * 2 + lax.axis_index("c")
@@ -159,15 +165,10 @@
             ref[:, lanes] = jnp.where(eye, 0.0, ref[:, lanes].astype(jnp.float32)).astype(jnp.bfloat16)
 
 
-def first_kernel(pos_ref, high_ref, low_ref, row_ref):
+def block_kernel(far, pos_ref, token_ref, high_ref, low_ref, row_ref):
     half, core = lax.axis_index("zh"), lax.axis_index("c")
-    fill_tiles(pos_ref, row_ref, high_ref, low_ref, ((1 - half) * 2 + 1 - core,), 0, LANES)
-
-
-def second_kernel(pos_ref, high_ref, low_ref, row_ref):
-    half, core = lax.axis_index("zh"), lax.axis_index("c")
-    quads = ((1 - half) * 2 + core, half * 2 + 1 - core)
-    fill_tiles(pos_ref, row_ref, high_ref, low_ref, quads, 0, 2 * LANES)
+    quad = ((1 - half) * 2 + 1 - core, (1 - half) * 2 + core, half * 2 + 1 - core)[far]
+    fill_tiles(pos_ref, row_ref, high_ref, low_ref, (quad,), 0, LANES)
 
 
 def fill_slab(refs, y_ref):
@@ -205,31 +206,18 @@
     return by_real, by_imag
 
 
-def send_kernel(pos_ref, high0, low0, high1, low1, all0, all1, all2, all3, out_ref, y_ref, own_high, own_low, row_ref):
+def send_kernel(high0, low0, high1, low1, all0, all1, all2, all3, out_ref, y_ref):
     fill_slab((all0, all1, all2, all3), y_ref)
     y = y_ref[...]
     store_products(*products(high0, low0, y), out_ref, 0)
-    store_products(*products(high1.at[pl.ds(0, LANES)], low1.at[pl.ds(0, LANES)], y), out_ref, 1)
-
-    @pl.when(early_own() == 1)
-    def _():
-        fill_own(pos_ref, row_ref, own_high, own_low)
-
-
-def keep_kernel(pos_ref, y_ref, high1, low1, done_high, done_low, slab_ref, near_ref, out_ref, pair_ref, row_ref, high_ref, low_ref):
-    pair_ref[0] = slab_ref[...]
-    pair_ref[1] = near_ref[...]
+    store_products(*products(high1, low1, y), out_ref, 1)
+
+
+def keep_kernel(pos_ref, y_ref, high2, low2, out_ref, row_ref, high_ref, low_ref):
+    fill_own(pos_ref, row_ref, high_ref, low_ref)
     y = y_ref[...]
-    store_products(*products(high1.at[pl.ds(LANES, LANES)], low1.at[pl.ds(LANES, LANES)], y), out_ref, 0)
-
-    @pl.when(early_own() == 1)
-    def _():
-        store_products(*products(done_high, done_low, y), out_ref, 1)
-
-    @pl.when(early_own() == 0)
-    def _():
-        fill_own(pos_ref, row_ref, high_ref, low_ref)
-        store_products(*products(high_ref, low_ref, y), out_ref, 1)
+    store_products(*products(high2, low2, y), out_ref, 0)
+    store_products(*products(high_ref, low_ref, y), out_ref, 1)
 
 
 def finish_kernel(keep_ref, half_ref, core_ref, rest_ref, slab_ref, base_ref, accum_ref, next_ref, acc_ref):
@@ -256,85 +244,72 @@
     tiles = count // (4 * LANES)
     deep = 2 * tiles * LANES
     hbm, vmem = pl.BlockSpec(memory_space=pltpu.HBM), pl.BlockSpec(memory_space=pltpu.VMEM)
-
-    block, pos, det = pl.pallas_call(
+    anywhere = pl.BlockSpec(memory_space=pl.ANY)
+    tile = pltpu.VMEM((LANES, deep), bf16)
+    token = pltpu.VMEM((8, LANES), f32)
+    rows = pltpu.VMEM((3, LANES, LANES), f32)
+
+    def call(kernel, name, out_shape, in_specs, flops, scratch=()):
+        return pl.pallas_call(
+            kernel,
+            out_shape=out_shape,
+            in_specs=in_specs,
+            out_specs=[vmem] * len(out_shape),
+            scratch_shapes=scratch,
+            compiler_params=params(6),
+            cost_estimate=pl.CostEstimate(flops=flops, bytes_accessed=1 << 20, transcendentals=0),
+            name=name,
+        )
+
+    def swap(array, axis, mask):
+        size = lax.axis_size(axis)
+        return lax.ppermute(array, axis, [(i, i ^ mask) for i in range(size)])
+
+    def far_block(n, after):
+        kernel = functools.partial(block_kernel, n)
+        return call(kernel, "far_block_" + "abc"[n], (tile, tile), [vmem, anywhere], 1 << 24, [rows])(pos, after)
+
+    block, pos, det = call(
         pack_kernel,
-        out_shape=(pltpu.VMEM((PART, LANES), f32), pltpu.VMEM(positions.shape, f32), pltpu.VMEM((8, LANES), f32)),
-        in_specs=[hbm] * 4,
-        out_specs=[vmem] * 3,
-        scratch_shapes=[pltpu.SemaphoreType.DMA((6,))],
-        compiler_params=params(4),
-        cost_estimate=pl.CostEstimate(flops=1 << 16, bytes_accessed=1 << 19, transcendentals=0),
-        name="pack_block",
+        "pack_block",
+        (pltpu.VMEM((PART, LANES), f32), pltpu.VMEM(positions.shape, f32), token),
+        [hbm] * 4,
+        1 << 16,
+        [pltpu.SemaphoreType.DMA((6,))],
     )(in_hbm(section), in_hbm(populations.reshape(1, LANES)), in_hbm(positions), in_hbm(detuning.reshape(1, count)))
-    along_y = [lax.ppermute(block, "y", [(i, (i + d) % 4) for i in range(4)]) for d in (1, 2, 3)]
-
-    high0, low0 = pl.pallas_call(
-        first_kernel,
-        out_shape=(pltpu.VMEM((LANES, deep), bf16),) * 2,
-        in_specs=[vmem],
-        out_specs=[vmem] * 2,
-        scratch_shapes=[pltpu.VMEM((3, LANES, LANES), f32)],
-        compiler_params=params(4),
-        cost_estimate=pl.CostEstimate(flops=15 << 20, bytes_accessed=2 << 20, transcendentals=1 << 20),
-        name="first_tiles",
-    )(pos)
-
-    merged, pos_again = pl.pallas_call(
-        merge_kernel,
-        out_shape=(pltpu.VMEM((4, PART, LANES), f32), pltpu.VMEM(positions.shape, f32)),
-        in_specs=[vmem] * 5 + [pl.BlockSpec(memory_space=pl.ANY)],
-        out_specs=[vmem] * 2,
-        compiler_params=params(2),
-        cost_estimate=pl.CostEstimate(flops=1, bytes_accessed=1 << 18, transcendentals=0),
-        name="merge_blocks",
-    )(block, *along_y, pos, high0)
-    along_x = [lax.ppermute(merged, "x", [(i, (i + d) % 4) for i in range(4)]) for d in (1, 2, 3)]
-    near = lax.ppermute(section, "zl", [(i, i ^ 1) for i in range(4)])
-
-    high1, low1 = pl.pallas_call(
-        second_kernel,
-        out_shape=(pltpu.VMEM((2 * LANES, deep), bf16),) * 2,
-        in_specs=[vmem],
-        out_specs=[vmem] * 2,
-        scratch_shapes=[pltpu.VMEM((3, 2 * LANES, LANES), f32)],
-        compiler_params=params(4),
-        cost_estimate=pl.CostEstimate(flops=30 << 20, bytes_accessed=4 << 20, transcendentals=1 << 20),
-        name="second_tiles",
-    )(pos_again)
-
-    sent, y, own_high, own_low = pl.pallas_call(
+    one = swap(block, "y", 1)
+    near = swap(section, "zl", 1)
+    high0, low0 = far_block(0, det)
+
+    both, second = call(
+        pair_kernel, "join_pair", (pltpu.VMEM((2, PART, LANES), f32), token), [vmem, vmem, anywhere], 1
+    )(block, one, high0)
+    two = swap(both, "y", 3)
+    high1, low1 = far_block(1, second)
+
+    line, pair, third = call(
+        line_kernel,
+        "join_line",
+        (pltpu.VMEM((4, PART, LANES), f32), pltpu.VMEM((2, 2, 16, LANES), f32), token),
+        [vmem] * 4 + [anywhere],
+        1,
+    )(both, two, section, near, high1)
+    across = [swap(line, "x", mask) for mask in (1, 3, 2)]
+    pair = swap(pair, "zl", 2)
+    high2, low2 = far_block(2, third)
+
+    sent, y = call(
         send_kernel,
-        out_shape=(
-            pltpu.VMEM((2, PART, LANES), f32),
-            pltpu.VMEM((LANES, deep // 2), bf16),
-            pltpu.VMEM((LANES, deep), bf16),
-            pltpu.VMEM((LANES, deep), bf16),
-        ),
-        in_specs=[vmem] * 9,
-        out_specs=[vmem] * 4,
-        scratch_shapes=[pltpu.VMEM((3, LANES, LANES), f32)],
-        compiler_params=params(8),
-        cost_estimate=pl.CostEstimate(flops=1 << 29, bytes_accessed=4 << 20, transcendentals=0),
-        name="send_products",
-    )(pos, high0, low0, high1, low1, merged, *along_x)
-    half = lax.ppermute(sent, "zh", [(0, 1), (1, 0)])
-
-    keep, pair = pl.pallas_call(
-        keep_kernel,
-        out_shape=(pltpu.VMEM((2, PART, LANES), f32), pltpu.VMEM((2, 2, 16, LANES), f32)),
-        in_specs=[vmem] * 8,
-        out_specs=[vmem] * 2,
-        scratch_shapes=[
-            pltpu.VMEM((3, LANES, LANES), f32),
-            pltpu.VMEM((LANES, deep), bf16),
-            pltpu.VMEM((LANES, deep), bf16),
-        ],
-        compiler_params=params(8),
-        cost_estimate=pl.CostEstimate(flops=1 << 29, bytes_accessed=4 << 20, transcendentals=1 << 20),
-        name="keep_products",
-    )(pos, y, high1, low1, own_high, own_low, section, near)
-    pair = lax.ppermute(pair, "zl", [(i, i ^ 2) for i in range(4)])
+        "send_products",
+        (pltpu.VMEM((2, PART, LANES), f32), pltpu.VMEM((LANES, deep // 2), bf16)),
+        [vmem] * 8,
+        1 << 29,
+    )(high0, low0, high1, low1, line, *across)
+    half = swap(sent, "zh", 1)
+
+    (keep,) = call(
+        keep_kernel, "keep_products", (pltpu.VMEM((2, PART, LANES), f32),), [vmem] * 4, 1 << 29, [rows, tile, tile]
+    )(pos, y, high2, low2)
     core = lax.ppermute(keep[0] + half[0], "c", [(0, 1), (1, 0)])
     rest = pl.pallas_call(
         term_kernel,

time: 38.9 us -> 36.9 us (0.949)
  starting transfers between devices: 23.1 us -> 20.6 us
    ppermute x9 -> x8, starting transfers between devices: 19.8 us -> 17.6 us  [swap(): return lax.ppermute(array, axis, [(i, i ^ mask) for i in range(size)])]
    pallas_call x6 -> x8, Pallas kernels: 13.5 us -> 13.7 us  [the longest x3 7.51 us: far_block(): call(kernel, 'far_block_' + 'abc'[n], (tile, tile), [vmem, anywhere], 1 <...]
  transfers between devices with their start and end apart: 10 -> 9, of which waited for: 1 -> 1; matrix products, arithmetic and copies ran while one was open for 0% -> 0% of each run, Pallas kernels for 33% -> 35%
where the time goes in v10:
time: 36.9 us; the launch traced here: 36.6 us
  starting transfers between devices  20.6 us (56%)
  Pallas kernels  14.6 us (40%)
  between operations  0.78 us (2%)
  waiting for transfers between devices  0.55 us (1%)
    ppermute x8, starting transfers between devices, swap(): return lax.ppermute(array, axis, [(i, i ^ mask) for i in range(size)])  17.6 us
    pallas_call x3, Pallas kernels, far_block(): call(kernel, 'far_block_' + 'abc'[n], (tile, tile), [vmem, anywhere], 1 <...  7.51 us
    pallas_call x1, Pallas kernels, local(): call(keep_kernel, 'keep_products', (pltpu.VMEM((2, PART, LANES), f32),),...  3.82 us
    ppermute x1, starting transfers between devices, local(): core = lax.ppermute(keep[0] + half[0], 'c', [(0, 1), (1, 0)])  3.03 us
    pallas_call x1, Pallas kernels, local(): call(send_kernel, 'send_products', (pltpu.VMEM((2, PART, LANES), f32), pl...  1.35 us
    pallas_call x1, Pallas kernels, local(): call(pack_kernel, 'pack_block', (pltpu.VMEM((PART, LANES), f32), pltpu.VM...  1.02 us
  transfers between devices with their start and end apart: 9, of which 1 were waited for; matrix products, arithmetic and copies ran while one was open for 0% of the time, Pallas kernels for 35%

profile of v10, /device:TPU:1, one launch (start us, length us, event | category | flops | bytes accessed | tf_op | source)
XLA Modules:
  0.0 36.6 jit_solution(5821096247721079561)
XLA Ops:
  0.6 1.0 %pack_block.1 = (f32[40,128]{1,0:T(8,128)S(1)}, f32[3,8192]{1,0:T(4,128)S(1)}, f32[8,128]{1,0:T(8,128)S(1)}) custom-call(f32[2,16,128]{2,1,0:T(8,128)} %slab_ref.5, f32[1,128]{1,0:T(1,128)} %bitcast.5, f32[3,8192]{1,0:T(4,128)} %pos_ref.1, f32[1,8192]{1,0:T(1,128)} %bitcast.4), custom_call_target="tpu_custom_call" | custom-call | flops 65536 | bytes 1048576 | tf_op jit(solution)/shard_map/pack_block/pallas_call | solution.py:272
  1.7 2.2 %collective-permute-start = (f32[40,128]{1,0:T(8,128)S(1)}, f32[40,128]{1,0:T(8,128)S(1)}, u32[]{:S(2)}, u32[]{:S(2)}) collective-permute-start(f32[40,128]{1,0:T(8,128)S(1)} %get-tuple-element.22.block_ref), channel_id=1, source_target_pairs={{0,64},{64,0},{128,192},{192,128},{1,65},{65,1},{129,193},{193,129... | collective-permute-start | bytes 61448 | tf_op jit(solution)/shard_map/ppermute | solution.py:266
  3.9 2.5 %far_block_a.1 = (bf16[128,4096]{1,0:T(8,128)(2,1)S(1)}, bf16[128,4096]{1,0:T(8,128)(2,1)S(1)}) custom-call(f32[3,8192]{1,0:T(4,128)S(1)} %get-tuple-element.18.pos_ref, f32[8,128]{1,0:T(8,128)S(1)} %get-tuple-element.19.token_ref.det_ref), custom_call_target="tpu_custom_call" | custom-call | flops 16777216 | bytes 1048576 | tf_op jit(solution)/shard_map/far_block_a/pallas_call | solution.py:270
  6.4 0.0 collective-permute-done.one_ref
  6.4 0.0 copy-start
  6.4 2.0 %collective-permute-start.1 = (f32[2,40,128]{2,1,0:T(8,128)S(1)}, f32[2,40,128]{2,1,0:T(8,128)S(1)}, u32[]{:S(2)}, u32[]{:S(2)}) collective-permute-start(f32[2,40,128]{2,1,0:T(8,128)S(1)} %get-tuple-element.26.both_ref), channel_id=1, source_target_pairs={{0,192},{64,128},{128,64},{192,0},{1,193},{65,129},{129,65},{193,1... | collective-permute-start | bytes 122888 | tf_op jit(solution)/shard_map/ppermute | solution.py:266
  8.4 0.0 copy-done
  8.4 1.6 %collective-permute-start.2 = (f32[2,16,128]{2,1,0:T(8,128)S(1)}, f32[2,16,128]{2,1,0:T(8,128)S(1)}, u32[]{:S(2)}, u32[]{:S(2)}) collective-permute-start(f32[2,16,128]{2,1,0:T(8,128)S(1)} %copy-done), channel_id=1, source_target_pairs={{0,1},{1,0},{2,3},{3,2},{4,5},{5,4},{6,7},{7,6},{8,9},{9,8},{10,11... | collective-permute-start | bytes 49160 | tf_op jit(solution)/shard_map/ppermute | solution.py:266
  10.0 2.5 %far_block_b.1 = (bf16[128,4096]{1,0:T(8,128)(2,1)S(1)}, bf16[128,4096]{1,0:T(8,128)(2,1)S(1)}) custom-call(f32[3,8192]{1,0:T(4,128)S(1)} %get-tuple-element.18.pos_ref, f32[8,128]{1,0:T(8,128)S(1)} %get-tuple-element.23.token_ref), custom_call_target="tpu_custom_call" | custom-call | flops 16777216 | bytes 1048576 | tf_op jit(solution)/shard_map/far_block_b/pallas_call | solution.py:270
  12.6 0.0 collective-permute-done.2.near_ref
  12.6 0.0 collective-permute-done.1.two_ref
  12.6 2.8 %collective-permute-start.5 = (f32[4,40,128]{2,1,0:T(8,128)S(1)}, f32[4,40,128]{2,1,0:T(8,128)S(1)}, u32[]{:S(2)}, u32[]{:S(2)}) collective-permute-start(f32[4,40,128]{2,1,0:T(8,128)S(1)} %get-tuple-element.27.all0), channel_id=1, source_target_pairs={{0,32},{16,48},{32,0},{48,16},{1,33},{17,49},{33,1},{49,17},{2,34}... | collective-permute-start | bytes 245768 | tf_op jit(solution)/shard_map/ppermute | solution.py:266
  15.4 0.9 %collective-permute-start.4 = (f32[4,40,128]{2,1,0:T(8,128)S(1)}, f32[4,40,128]{2,1,0:T(8,128)S(1)}, u32[]{:S(2)}, u32[]{:S(2)}) collective-permute-start(f32[4,40,128]{2,1,0:T(8,128)S(1)} %get-tuple-element.27.all0), channel_id=1, source_target_pairs={{0,48},{16,32},{32,16},{48,0},{1,49},{17,33},{33,17},{49,1},{2,50}... | collective-permute-start | bytes 245768 | tf_op jit(solution)/shard_map/ppermute | solution.py:266
  16.3 0.0 collective-permute-start.3
  16.3 3.0 %collective-permute-start.8 = (f32[2,2,16,128]{3,2,1,0:T(8,128)S(1)}, f32[2,2,16,128]{3,2,1,0:T(8,128)S(1)}, u32[]{:S(2)}, u32[]{:S(2)}) collective-permute-start(f32[2,2,16,128]{3,2,1,0:T(8,128)S(1)} %get-tuple-element.33), channel_id=1, source_target_pairs={{0,2},{1,3},{2,0},{3,1},{4,6},{5,7},{6,4},{7,5},{8,10},{9,11},{10,... | collective-permute-start | bytes 98312 | tf_op jit(solution)/shard_map/ppermute | solution.py:266
  19.3 2.5 %far_block_c.1 = (bf16[128,4096]{1,0:T(8,128)(2,1)S(1)}, bf16[128,4096]{1,0:T(8,128)(2,1)S(1)}) custom-call(f32[3,8192]{1,0:T(4,128)S(1)} %get-tuple-element.18.pos_ref, f32[8,128]{1,0:T(8,128)S(1)} %get-tuple-element.29.token_ref), custom_call_target="tpu_custom_call" | custom-call | flops 16777216 | bytes 1048576 | tf_op jit(solution)/shard_map/far_block_c/pallas_call | solution.py:270
  21.8 0.0 collective-permute-done.5.all3
  21.8 0.0 collective-permute-done.4.all2
  21.8 0.0 collective-permute-done.3.all1
  21.8 1.3 %send_products.1 = (f32[2,40,128]{2,1,0:T(8,128)S(1)}, bf16[128,2048]{1,0:T(8,128)(2,1)S(1)}) custom-call(bf16[128,4096]{1,0:T(8,128)(2,1)S(1)} %get-tuple-element.20.after_ref.high0, bf16[128,4096]{1,0:T(8,128)(2,1)S(1)} %get-tuple-element.21.low0, bf16[128,4096]{1,0:T(8,128)(2,1)S(1)} %get-tuple-element.24.after_ref.high1, ...), custom_call_target="tpu_custom_call" | custom-call | flops 536870912 | bytes 1048576 | tf_op jit(solution)/shard_map/send_products/pallas_call | solution.py:301
  23.2 5.1 %collective-permute-start.6 = (f32[2,40,128]{2,1,0:T(8,128)S(1)}, f32[2,40,128]{2,1,0:T(8,128)S(1)}, u32[]{:S(2)}, u32[]{:S(2)}) collective-permute-start(f32[2,40,128]{2,1,0:T(8,128)S(1)} %get-tuple-element.32), channel_id=1, source_target_pairs={{0,8},{8,0},{1,9},{9,1},{2,10},{10,2},{3,11},{11,3},{4,12},{12,4},... | collective-permute-start | bytes 122888 | tf_op jit(solution)/shard_map/ppermute | solution.py:266
  28.3 3.8 %keep_products.1.keep_ref = f32[2,40,128]{2,1,0:T(8,128)S(1)} custom-call(f32[3,8192]{1,0:T(4,128)S(1)} %get-tuple-element.18.pos_ref, bf16[128,2048]{1,0:T(8,128)(2,1)S(1)} %get-tuple-element.28.y_ref, bf16[128,4096]{1,0:T(8,128)(2,1)S(1)} %get-tuple-element.30.high2, bf16[128,4096]{1,0:T(8,128)(2,1)S(1)} %get-tuple-element.31.low2), custom_call_target="tpu_custom_call" | custom-call | flops 536870912 | bytes 1048576 | tf_op jit(solution)/shard_map/keep_products/pallas_call | solution.py:310
  32.1 0.0 collective-permute-done.6.half_ref
  32.1 0.0 copy-start.1
  32.1 0.0 copy-start.2
  32.1 3.0 %collective-permute-start.7 = (f32[40,128]{1,0:T(8,128)S(1)}, f32[40,128]{1,0:T(8,128)S(1)}, u32[]{:S(2)}, u32[]{:S(2)}) collective-permute-start(f32[40,128]{1,0:T(8,128)S(1)} %fusion), channel_id=1, source_target_pairs={{0,4},{4,0},{1,5},{5,1},{2,6},{6,2},{3,7},{7,3},{8,12},{12,8},{9,1... | collective-permute-start | bytes 61448 | tf_op jit(solution)/shard_map/ppermute | solution.py:313
  35.2 0.0 collective-permute-done.8.pair_ref
  35.2 0.3 slab_term.1.rest_ref
  35.5 0.5 %collective-permute-done.7.core_ref = f32[40,128]{1,0:T(8,128)S(1)} collective-permute-done((f32[40,128]{1,0:T(8,128)S(1)}, f32[40,128]{1,0:T(8,128)S(1)}, u32[]{:S(2)}, u32[]{:S(2)}) %collective-permute-start.7) | collective-permute-done | bytes 20512 | tf_op jit(solution)/shard_map/ppermute | solution.py:313
  36.0 0.0 copy-done.1
  36.0 0.0 copy-done.2
  36.0 0.6 %finish_rate.1 = (f32[2,16,128]{2,1,0:T(8,128)}, f32[2,16,128]{2,1,0:T(8,128)}) custom-call(f32[2,40,128]{2,1,0:T(8,128)S(1)} %keep_products.1.keep_ref, f32[2,40,128]{2,1,0:T(8,128)S(1)} %collective-permute-done.6.half_ref, f32[40,128]{1,0:T(8,128)S(1)} %collective-permute-done.7.core_ref, f32[2,16,128]{2,1,0:T(8,128)S(1)} %slab_term.1.rest_ref, ...), custom_call_target="tpu_custom_call" | custom-call | flops 65536 | bytes 262144 | tf_op jit(solution)/shard_map/finish_rate/pallas_call | solution.py:325
  (3 shorter events, 0.0 us)
Async XLA Ops:
  1.7 4.7 %collective-permute-start = (f32[40,128]{1,0:T(8,128)S(1)}, f32[40,128]{1,0:T(8,128)S(1)}, u32[]{:S(2)}, u32[]{:S(2)}) collective-permute-start(f32[40,128]{1,0:T(8,128)S(1)} %get-tuple-element.22.block_ref), channel_id=1, source_target_pairs={{0,64},{64,0},{128,192},{192,128},{1,65},{65,1},{129,193},{193,129... | collective-permute-start | bytes 61448 | tf_op jit(solution)/shard_map/ppermute | solution.py:266
  6.4 2.0 %copy-start = (f32[2,16,128]{2,1,0:T(8,128)S(1)}, f32[2,16,128]{2,1,0:T(8,128)}, u32[]{:S(2)}) copy-start(f32[2,16,128]{2,1,0:T(8,128)} %slab_ref.5) | copy-start | bytes 49156
  6.4 6.2 %collective-permute-start.1 = (f32[2,40,128]{2,1,0:T(8,128)S(1)}, f32[2,40,128]{2,1,0:T(8,128)S(1)}, u32[]{:S(2)}, u32[]{:S(2)}) collective-permute-start(f32[2,40,128]{2,1,0:T(8,128)S(1)} %get-tuple-element.26.both_ref), channel_id=1, source_target_pairs={{0,192},{64,128},{128,64},{192,0},{1,193},{65,129},{129,65},{193,1... | collective-permute-start | bytes 122888 | tf_op jit(solution)/shard_map/ppermute | solution.py:266
  8.4 4.1 %collective-permute-start.2 = (f32[2,16,128]{2,1,0:T(8,128)S(1)}, f32[2,16,128]{2,1,0:T(8,128)S(1)}, u32[]{:S(2)}, u32[]{:S(2)}) collective-permute-start(f32[2,16,128]{2,1,0:T(8,128)S(1)} %copy-done), channel_id=1, source_target_pairs={{0,1},{1,0},{2,3},{3,2},{4,5},{5,4},{6,7},{7,6},{8,9},{9,8},{10,11... | collective-permute-start | bytes 49160 | tf_op jit(solution)/shard_map/ppermute | solution.py:266
  12.6 9.2 %collective-permute-start.5 = (f32[4,40,128]{2,1,0:T(8,128)S(1)}, f32[4,40,128]{2,1,0:T(8,128)S(1)}, u32[]{:S(2)}, u32[]{:S(2)}) collective-permute-start(f32[4,40,128]{2,1,0:T(8,128)S(1)} %get-tuple-element.27.all0), channel_id=1, source_target_pairs={{0,32},{16,48},{32,0},{48,16},{1,33},{17,49},{33,1},{49,17},{2,34}... | collective-permute-start | bytes 245768 | tf_op jit(solution)/shard_map/ppermute | solution.py:266
  15.4 6.4 %collective-permute-start.4 = (f32[4,40,128]{2,1,0:T(8,128)S(1)}, f32[4,40,128]{2,1,0:T(8,128)S(1)}, u32[]{:S(2)}, u32[]{:S(2)}) collective-permute-start(f32[4,40,128]{2,1,0:T(8,128)S(1)} %get-tuple-element.27.all0), channel_id=1, source_target_pairs={{0,48},{16,32},{32,16},{48,0},{1,49},{17,33},{33,17},{49,1},{2,50}... | collective-permute-start | bytes 245768 | tf_op jit(solution)/shard_map/ppermute | solution.py:266
  16.3 5.5 %collective-permute-start.3 = (f32[4,40,128]{2,1,0:T(8,128)S(1)}, f32[4,40,128]{2,1,0:T(8,128)S(1)}, u32[]{:S(2)}, u32[]{:S(2)}) collective-permute-start(f32[4,40,128]{2,1,0:T(8,128)S(1)} %get-tuple-element.27.all0), channel_id=1, source_target_pairs={{0,16},{16,0},{32,48},{48,32},{1,17},{17,1},{33,49},{49,33},{2,18}... | collective-permute-start | bytes 245768 | tf_op jit(solution)/shard_map/ppermute | solution.py:266
  16.3 18.9 %collective-permute-start.8 = (f32[2,2,16,128]{3,2,1,0:T(8,128)S(1)}, f32[2,2,16,128]{3,2,1,0:T(8,128)S(1)}, u32[]{:S(2)}, u32[]{:S(2)}) collective-permute-start(f32[2,2,16,128]{3,2,1,0:T(8,128)S(1)} %get-tuple-element.33), channel_id=1, source_target_pairs={{0,2},{1,3},{2,0},{3,1},{4,6},{5,7},{6,4},{7,5},{8,10},{9,11},{10,... | collective-permute-start | bytes 98312 | tf_op jit(solution)/shard_map/ppermute | solution.py:266
  23.2 8.9 %collective-permute-start.6 = (f32[2,40,128]{2,1,0:T(8,128)S(1)}, f32[2,40,128]{2,1,0:T(8,128)S(1)}, u32[]{:S(2)}, u32[]{:S(2)}) collective-permute-start(f32[2,40,128]{2,1,0:T(8,128)S(1)} %get-tuple-element.32), channel_id=1, source_target_pairs={{0,8},{8,0},{1,9},{9,1},{2,10},{10,2},{3,11},{11,3},{4,12},{12,4},... | collective-permute-start | bytes 122888 | tf_op jit(solution)/shard_map/ppermute | solution.py:266
  32.1 3.9 %copy-start.1 = (f32[2,16,128]{2,1,0:T(8,128)S(1)}, f32[2,16,128]{2,1,0:T(8,128)}, u32[]{:S(2)}) copy-start(f32[2,16,128]{2,1,0:T(8,128)} %base_ref.1) | copy-start | bytes 49156
  32.1 3.9 %copy-start.2 = (f32[2,16,128]{2,1,0:T(8,128)S(1)}, f32[2,16,128]{2,1,0:T(8,128)}, u32[]{:S(2)}) copy-start(f32[2,16,128]{2,1,0:T(8,128)} %accum_ref.1) | copy-start | bytes 49156
  32.1 3.9 %collective-permute-start.7 = (f32[40,128]{1,0:T(8,128)S(1)}, f32[40,128]{1,0:T(8,128)S(1)}, u32[]{:S(2)}, u32[]{:S(2)}) collective-permute-start(f32[40,128]{1,0:T(8,128)S(1)} %fusion), channel_id=1, source_target_pairs={{0,4},{4,0},{1,5},{5,1},{2,6},{6,2},{3,7},{7,3},{8,12},{12,8},{9,1... | collective-permute-start | bytes 61448 | tf_op jit(solution)/shard_map/ppermute | solution.py:313

commit v11 on v10

--- a/solution.py
+++ b/solution.py
@@ -82,16 +82,18 @@
     block_ref[32:PART, :] = jnp.where(top, 2.0 * block_ref[32:PART, :] - 1.0, 0.0)
 
 
-def pair_kernel(block_ref, one_ref, after_ref, both_ref, token_ref):
+def pair_kernel(block_ref, one_ref, slab_ref, even_ref, after_ref, both_ref, cores_ref, token_ref):
     both_ref[0] = block_ref[...]
     both_ref[1] = one_ref[...]
+    cores_ref[0] = even_ref[...]
+    cores_ref[1] = slab_ref[...]
     token_ref[...] = block_ref[0:8, :]
 
 
-def line_kernel(both_ref, two_ref, slab_ref, near_ref, after_ref, all_ref, pair_ref, token_ref):
+def line_kernel(both_ref, two_ref, cores_ref, near_ref, after_ref, all_ref, pair_ref, token_ref):
     all_ref[0:2] = both_ref[...]
     all_ref[2:4] = two_ref[...]
-    pair_ref[0] = slab_ref[...]
+    pair_ref[0] = cores_ref[...]
     pair_ref[1] = near_ref[...]
     token_ref[...] = both_ref[0, 0:8, :]
 
@@ -125,7 +127,7 @@
     lax.fori_loop(0, tiles, tile, 0)
 
 
-def term_kernel(pos_ref, slab_ref, near_ref, pair_ref, det_ref, rest_ref, row_ref, full_ref):
+def take_slab_term(pos_ref, pair_ref, far_ref, det_ref, out_ref, row_ref, full_ref):
     own = lax.axis_index("zl")
     start = pl.multiple_of(own * 16, 16)
     offsets = []
@@ -136,22 +138,22 @@
     eye = (lax.broadcasted_iota(jnp.int32, (16, LANES), 0) + start) == lax.broadcasted_iota(jnp.int32, (16, LANES), 1)
     w_real = jnp.where(eye, det_ref[1:2, :], w_real)[:, 0:64]
     w_imag = jnp.where(eye, -0.5, w_imag)[:, 0:64]
-    for n, ref in enumerate((slab_ref, near_ref, pair_ref.at[0], pair_ref.at[1])):
-        place = own + (n % 2) * (1 - 2 * (own % 2))
-        place = place + (n // 2) * (2 - 4 * (own // 2))
-        there = pl.ds(pl.multiple_of(place * 16, 16), 16)
-        full_ref[0, there, :] = ref[0]
-        full_ref[1, there, :] = ref[1]
+    for n in range(4):
+        there = pl.ds(pl.multiple_of((own ^ n) * 16, 16), 16)
+        source = (pair_ref, far_ref)[n // 2]
+        for core in range(2):
+            for part in range(2):
+                full_ref[part, there, core * LANES : (core + 1) * LANES] = source[n % 2, core, part]
 
     def mul(a, b):
         return jnp.dot(a, b, precision=lax.Precision.HIGHEST, preferred_element_type=jnp.float32)
 
     v_real = mul(w_real, full_ref[0]) + mul(w_imag, full_ref[1])
     v_imag = mul(w_real, full_ref[1]) - mul(w_imag, full_ref[0])
-    y_real, y_imag = slab_ref[0], slab_ref[1]
-    line = det_ref[0:1, :]
-    rest_ref[0] = line * y_imag - 0.5 * y_real - v_imag
-    rest_ref[1] = v_real - line * y_real - 0.5 * y_imag
+    for core in range(2):
+        lanes = slice(core * LANES, (core + 1) * LANES)
+        out_ref[core, 0:16, :] -= v_real[:, lanes]
+        out_ref[core, 16:32, :] -= v_imag[:, lanes]
 
 
 def fill_own(pos_ref, row_ref, high_ref, low_ref):
@@ -213,18 +215,23 @@
     store_products(*products(high1, low1, y), out_ref, 1)
 
 
-def keep_kernel(pos_ref, y_ref, high2, low2, out_ref, row_ref, high_ref, low_ref):
+def keep_kernel(pos_ref, y_ref, high2, low2, pair_ref, far_ref, det_ref, out_ref, row_ref, high_ref, low_ref, full_ref):
     fill_own(pos_ref, row_ref, high_ref, low_ref)
     y = y_ref[...]
     store_products(*products(high2, low2, y), out_ref, 0)
     store_products(*products(high_ref, low_ref, y), out_ref, 1)
 
-
-def finish_kernel(keep_ref, half_ref, core_ref, rest_ref, slab_ref, base_ref, accum_ref, next_ref, acc_ref):
+    @pl.when(lax.axis_index("c") == 1)
+    def _():
+        take_slab_term(pos_ref, pair_ref, far_ref, det_ref, out_ref, row_ref, full_ref)
+
+
+def finish_kernel(keep_ref, half_ref, core_ref, det_ref, slab_ref, base_ref, accum_ref, next_ref, acc_ref):
     z = keep_ref[1] + half_ref[1] + core_ref[...]
-    shift = z[32:33]
-    rate_real = z[16:32] + shift * slab_ref[1] + rest_ref[0]
-    rate_imag = rest_ref[1] - z[0:16] - shift * slab_ref[0]
+    y_real, y_imag = slab_ref[0], slab_ref[1]
+    level = det_ref[0:1, :] + z[32:33]
+    rate_real = z[16:32] + level * y_imag - 0.5 * y_real
+    rate_imag = -z[0:16] - level * y_real - 0.5 * y_imag
     for n, rate in enumerate((rate_real, rate_imag)):
         next_ref[n] = base_ref[n] + (0.5 * TIME_STEP) * rate
         acc_ref[n] = accum_ref[n] + (TIME_STEP / 3.0) * rate
@@ -265,6 +272,9 @@
         size = lax.axis_size(axis)
         return lax.ppermute(array, axis, [(i, i ^ mask) for i in range(size)])
 
+    def odd_swap(array, mask):
+        return lax.ppermute(array, ("c", "zl"), [(4 + i, 4 + (i ^ mask)) for i in range(4)])
+
     def far_block(n, after):
         kernel = functools.partial(block_kernel, n)
         return call(kernel, "far_block_" + "abc"[n], (tile, tile), [vmem, anywhere], 1 << 24, [rows])(pos, after)
@@ -278,24 +288,29 @@
         [pltpu.SemaphoreType.DMA((6,))],
     )(in_hbm(section), in_hbm(populations.reshape(1, LANES)), in_hbm(positions), in_hbm(detuning.reshape(1, count)))
     one = swap(block, "y", 1)
-    near = swap(section, "zl", 1)
+    even = lax.ppermute(section, "c", [(0, 1)])
     high0, low0 = far_block(0, det)
 
-    both, second = call(
-        pair_kernel, "join_pair", (pltpu.VMEM((2, PART, LANES), f32), token), [vmem, vmem, anywhere], 1
-    )(block, one, high0)
+    both, cores, second = call(
+        pair_kernel,
+        "join_pair",
+        (pltpu.VMEM((2, PART, LANES), f32), pltpu.VMEM((2, 2, 16, LANES), f32), token),
+        [vmem] * 4 + [anywhere],
+        1,
+    )(block, one, section, even, high0)
     two = swap(both, "y", 3)
+    near = odd_swap(cores, 1)
     high1, low1 = far_block(1, second)
 
     line, pair, third = call(
         line_kernel,
         "join_line",
-        (pltpu.VMEM((4, PART, LANES), f32), pltpu.VMEM((2, 2, 16, LANES), f32), token),
+        (pltpu.VMEM((4, PART, LANES), f32), pltpu.VMEM((2, 2, 2, 16, LANES), f32), token),
         [vmem] * 4 + [anywhere],
         1,
-    )(both, two, section, near, high1)
+    )(both, two, cores, near, high1)
     across = [swap(line, "x", mask) for mask in (1, 3, 2)]
-    pair = swap(pair, "zl", 2)
+    distant = odd_swap(pair, 2)
     high2, low2 = far_block(2, third)
 
     sent, y = call(
@@ -308,27 +323,21 @@
     half = swap(sent, "zh", 1)
 
     (keep,) = call(
-        keep_kernel, "keep_products", (pltpu.VMEM((2, PART, LANES), f32),), [vmem] * 4, 1 << 29, [rows, tile, tile]
-    )(pos, y, high2, low2)
+        keep_kernel,
+        "keep_products",
+        (pltpu.VMEM((2, PART, LANES), f32),),
+        [vmem] * 7,
+        1 << 29,
+        [rows, tile, tile, pltpu.VMEM((2, 64, 2 * LANES), f32)],
+    )(pos, y, high2, low2, pair, distant, det)
     core = lax.ppermute(keep[0] + half[0], "c", [(0, 1), (1, 0)])
-    rest = pl.pallas_call(
-        term_kernel,
-        out_shape=pltpu.VMEM((2, 16, LANES), f32),
-        in_specs=[vmem] * 5,
-        out_specs=vmem,
-        scratch_shapes=[pltpu.VMEM((3, LANES, LANES), f32), pltpu.VMEM((2, 64, LANES), f32)],
-        compiler_params=params(4),
-        cost_estimate=pl.CostEstimate(flops=1 << 22, bytes_accessed=1 << 18, transcendentals=1 << 11),
-        name="slab_term",
-    )(pos, section, near, pair, det)
-
     return pl.pallas_call(
         finish_kernel,
         out_shape=(jax.ShapeDtypeStruct(base.shape, f32),) * 2,
         compiler_params=params(4),
         cost_estimate=pl.CostEstimate(flops=1 << 16, bytes_accessed=1 << 18, transcendentals=0),
         name="finish_rate",
-    )(keep, half, core, rest, section, base, accum)
+    )(keep, half, core, det, section, base, accum)
 
 
 def solution(mesh):

time: 36.9 us -> 39 us (1.057)
  starting transfers between devices: 20.6 us -> 22 us
  waiting for transfers between devices: 0.55 us -> 1.2 us
    ppermute x0 -> x3, starting transfers between devices: none -> 9.7 us  [the longest x2 8.42 us: odd_swap(): lax.ppermute(array, ('c', 'zl'), [(4 + i, 4 + (i ^ mask)) for i in range(...]
    ppermute x8 -> x6, starting transfers between devices: 17.6 us -> 12.2 us  [swap(): return lax.ppermute(array, axis, [(i, i ^ mask) for i in range(size)])]
    ppermute x1, starting transfers between devices: 3.03 us -> 0.09 us  [local(): core = lax.ppermute(keep[0] + half[0], 'c', [(0, 1), (1, 0)])]
    ppermute x1, waiting for transfers between devices: 0.53 us -> 1.18 us  [local(): core = lax.ppermute(keep[0] + half[0], 'c', [(0, 1), (1, 0)])]
  transfers between devices with their start and end apart: 9 -> 10, of which waited for: 1 -> 1; matrix products, arithmetic and copies ran while one was open for 0% -> 0% of each run, Pallas kernels for 35% -> 34%
where the time goes in v11:
time: 39 us; the launch traced here: 38.9 us
  starting transfers between devices  22 us (56%)
  Pallas kernels  14.8 us (38%)
  waiting for transfers between devices  1.2 us (3%)
  between operations  0.81 us (2%)
    ppermute x6, starting transfers between devices, swap(): return lax.ppermute(array, axis, [(i, i ^ mask) for i in range(size)])  12.2 us
    ppermute x2, starting transfers between devices, odd_swap(): lax.ppermute(array, ('c', 'zl'), [(4 + i, 4 + (i ^ mask)) for i in range(...  8.42 us
    pallas_call x3, Pallas kernels, far_block(): call(kernel, 'far_block_' + 'abc'[n], (tile, tile), [vmem, anywhere], 1 <...  7.58 us
    pallas_call x1, Pallas kernels, local(): call(keep_kernel, 'keep_products', (pltpu.VMEM((2, PART, LANES), f32),),...  4.16 us
    pallas_call x1, Pallas kernels, local(): call(send_kernel, 'send_products', (pltpu.VMEM((2, PART, LANES), f32), pl...  1.36 us
    ppermute x1, starting transfers between devices, local(): even = lax.ppermute(section, 'c', [(0, 1)])  1.28 us
    ppermute x1, waiting for transfers between devices, local(): core = lax.ppermute(keep[0] + half[0], 'c', [(0, 1), (1, 0)])  1.18 us
    pallas_call x1, Pallas kernels, local(): call(pack_kernel, 'pack_block', (pltpu.VMEM((PART, LANES), f32), pltpu.VM...  1.02 us
  transfers between devices with their start and end apart: 10, of which 1 were waited for; matrix products, arithmetic and copies ran while one was open for 0% of the time, Pallas kernels for 34%

profile of v11, /device:TPU:1, one launch (start us, length us, event | category | flops | bytes accessed | tf_op | source)
XLA Modules:
  0.0 38.9 jit_solution(8239689305647733100)
XLA Ops:
  0.6 0.0 copy-start
  0.6 1.0 %pack_block.1 = (f32[40,128]{1,0:T(8,128)S(1)}, f32[3,8192]{1,0:T(4,128)S(1)}, f32[8,128]{1,0:T(8,128)S(1)}) custom-call(f32[2,16,128]{2,1,0:T(8,128)} %slab_ref.3, f32[1,128]{1,0:T(1,128)} %bitcast.5, f32[3,8192]{1,0:T(4,128)} %pos_ref.1, f32[1,8192]{1,0:T(1,128)} %bitcast.4), custom_call_target="tpu_custom_call" | custom-call | flops 65536 | bytes 1048576 | tf_op jit(solution)/shard_map/pack_block/pallas_call | solution.py:282
  1.7 2.2 %collective-permute-start = (f32[40,128]{1,0:T(8,128)S(1)}, f32[40,128]{1,0:T(8,128)S(1)}, u32[]{:S(2)}, u32[]{:S(2)}) collective-permute-start(f32[40,128]{1,0:T(8,128)S(1)} %get-tuple-element.23.block_ref), channel_id=1, source_target_pairs={{0,64},{64,0},{128,192},{192,128},{1,65},{65,1},{129,193},{193,129... | collective-permute-start | bytes 61448 | tf_op jit(solution)/shard_map/ppermute | solution.py:273
  3.9 0.0 copy-done
  3.9 1.3 %collective-permute-start.1 = (f32[2,16,128]{2,1,0:T(8,128)S(1)}, f32[2,16,128]{2,1,0:T(8,128)S(1)}, u32[]{:S(2)}, u32[]{:S(2)}) collective-permute-start(f32[2,16,128]{2,1,0:T(8,128)S(1)} %copy-done), channel_id=1, source_target_pairs={{0,4},{1,5},{2,6},{3,7},{8,12},{9,13},{10,14},{11,15},{16,20},{17,... | collective-permute-start | bytes 49160 | tf_op jit(solution)/shard_map/ppermute | solution.py:291
  5.2 2.5 %far_block_a.1 = (bf16[128,4096]{1,0:T(8,128)(2,1)S(1)}, bf16[128,4096]{1,0:T(8,128)(2,1)S(1)}) custom-call(f32[3,8192]{1,0:T(4,128)S(1)} %get-tuple-element.19.pos_ref, f32[8,128]{1,0:T(8,128)S(1)} %get-tuple-element.20.token_ref.det_ref), custom_call_target="tpu_custom_call" | custom-call | flops 16777216 | bytes 1048576 | tf_op jit(solution)/shard_map/far_block_a/pallas_call | solution.py:280
  7.7 0.0 collective-permute-done.1.even_ref
  7.7 0.0 collective-permute-done.one_ref
  7.7 2.0 %collective-permute-start.2 = (f32[2,40,128]{2,1,0:T(8,128)S(1)}, f32[2,40,128]{2,1,0:T(8,128)S(1)}, u32[]{:S(2)}, u32[]{:S(2)}) collective-permute-start(f32[2,40,128]{2,1,0:T(8,128)S(1)} %get-tuple-element.27.both_ref), channel_id=1, source_target_pairs={{0,192},{64,128},{128,64},{192,0},{1,193},{65,129},{129,65},{193,1... | collective-permute-start | bytes 122888 | tf_op jit(solution)/shard_map/ppermute | solution.py:273
  9.7 3.5 %collective-permute-start.3 = (f32[2,2,16,128]{3,2,1,0:T(8,128)S(1)}, f32[2,2,16,128]{3,2,1,0:T(8,128)S(1)}, u32[]{:S(2)}, u32[]{:S(2)}) collective-permute-start(f32[2,2,16,128]{3,2,1,0:T(8,128)S(1)} %get-tuple-element.28.cores_ref), channel_id=1, source_target_pairs={{4,5},{5,4},{6,7},{7,6},{12,13},{13,12},{14,15},{15,14},{20,21},{2... | collective-permute-start | bytes 98312 | tf_op jit(solution)/shard_map/ppermute | solution.py:276
  13.3 2.5 %far_block_b.1 = (bf16[128,4096]{1,0:T(8,128)(2,1)S(1)}, bf16[128,4096]{1,0:T(8,128)(2,1)S(1)}) custom-call(f32[3,8192]{1,0:T(4,128)S(1)} %get-tuple-element.19.pos_ref, f32[8,128]{1,0:T(8,128)S(1)} %get-tuple-element.24.token_ref), custom_call_target="tpu_custom_call" | custom-call | flops 16777216 | bytes 1048576 | tf_op jit(solution)/shard_map/far_block_b/pallas_call | solution.py:280
  15.8 0.0 collective-permute-done.3.near_ref
  15.8 0.0 collective-permute-done.2.two_ref
  15.8 1.3 %collective-permute-start.4 = (f32[4,40,128]{2,1,0:T(8,128)S(1)}, f32[4,40,128]{2,1,0:T(8,128)S(1)}, u32[]{:S(2)}, u32[]{:S(2)}) collective-permute-start(f32[4,40,128]{2,1,0:T(8,128)S(1)} %get-tuple-element.29.all0), channel_id=1, source_target_pairs={{0,16},{16,0},{32,48},{48,32},{1,17},{17,1},{33,49},{49,33},{2,18}... | collective-permute-start | bytes 245768 | tf_op jit(solution)/shard_map/ppermute | solution.py:273
  17.1 1.8 %collective-permute-start.5 = (f32[4,40,128]{2,1,0:T(8,128)S(1)}, f32[4,40,128]{2,1,0:T(8,128)S(1)}, u32[]{:S(2)}, u32[]{:S(2)}) collective-permute-start(f32[4,40,128]{2,1,0:T(8,128)S(1)} %get-tuple-element.29.all0), channel_id=1, source_target_pairs={{0,48},{16,32},{32,16},{48,0},{1,49},{17,33},{33,17},{49,1},{2,50}... | collective-permute-start | bytes 245768 | tf_op jit(solution)/shard_map/ppermute | solution.py:273
  19.0 0.6 %collective-permute-start.6 = (f32[4,40,128]{2,1,0:T(8,128)S(1)}, f32[4,40,128]{2,1,0:T(8,128)S(1)}, u32[]{:S(2)}, u32[]{:S(2)}) collective-permute-start(f32[4,40,128]{2,1,0:T(8,128)S(1)} %get-tuple-element.29.all0), channel_id=1, source_target_pairs={{0,32},{16,48},{32,0},{48,16},{1,33},{17,49},{33,1},{49,17},{2,34}... | collective-permute-start | bytes 245768 | tf_op jit(solution)/shard_map/ppermute | solution.py:273
  19.6 4.9 %collective-permute-start.7 = (f32[2,2,2,16,128]{4,3,2,1,0:T(8,128)S(1)}, f32[2,2,2,16,128]{4,3,2,1,0:T(8,128)S(1)}, u32[]{:S(2)}, u32[]{:S(2)}) collective-permute-start(f32[2,2,2,16,128]{4,3,2,1,0:T(8,128)S(1)} %get-tuple-element.34.pair_ref), channel_id=1, source_target_pairs={{4,6},{5,7},{6,4},{7,5},{12,14},{13,15},{14,12},{15,13},{20,22},{2... | collective-permute-start | bytes 196616 | tf_op jit(solution)/shard_map/ppermute | solution.py:276
  24.5 2.5 %far_block_c.1 = (bf16[128,4096]{1,0:T(8,128)(2,1)S(1)}, bf16[128,4096]{1,0:T(8,128)(2,1)S(1)}) custom-call(f32[3,8192]{1,0:T(4,128)S(1)} %get-tuple-element.19.pos_ref, f32[8,128]{1,0:T(8,128)S(1)} %get-tuple-element.31.token_ref), custom_call_target="tpu_custom_call" | custom-call | flops 16777216 | bytes 1048576 | tf_op jit(solution)/shard_map/far_block_c/pallas_call | solution.py:280
  27.0 0.0 collective-permute-done.4.all1
  27.0 0.0 collective-permute-done.5.all2
  27.0 0.0 collective-permute-done.6.all3
  27.1 1.4 %send_products.1 = (f32[2,40,128]{2,1,0:T(8,128)S(1)}, bf16[128,2048]{1,0:T(8,128)(2,1)S(1)}) custom-call(bf16[128,4096]{1,0:T(8,128)(2,1)S(1)} %get-tuple-element.21.after_ref.high0, bf16[128,4096]{1,0:T(8,128)(2,1)S(1)} %get-tuple-element.22.low0, bf16[128,4096]{1,0:T(8,128)(2,1)S(1)} %get-tuple-element.25.after_ref.high1, ...), custom_call_target="tpu_custom_call" | custom-call | flops 536870912 | bytes 1048576 | tf_op jit(solution)/shard_map/send_products/pallas_call | solution.py:316
  28.4 4.3 %collective-permute-start.8 = (f32[2,40,128]{2,1,0:T(8,128)S(1)}, f32[2,40,128]{2,1,0:T(8,128)S(1)}, u32[]{:S(2)}, u32[]{:S(2)}) collective-permute-start(f32[2,40,128]{2,1,0:T(8,128)S(1)} %get-tuple-element.35), channel_id=1, source_target_pairs={{0,8},{8,0},{1,9},{9,1},{2,10},{10,2},{3,11},{11,3},{4,12},{12,4},... | collective-permute-start | bytes 122888 | tf_op jit(solution)/shard_map/ppermute | solution.py:273
  32.7 0.0 collective-permute-done.7.far_ref
  32.7 4.2 %keep_products.1.keep_ref = f32[2,40,128]{2,1,0:T(8,128)S(1)} custom-call(f32[3,8192]{1,0:T(4,128)S(1)} %get-tuple-element.19.pos_ref, bf16[128,2048]{1,0:T(8,128)(2,1)S(1)} %get-tuple-element.30.y_ref, bf16[128,4096]{1,0:T(8,128)(2,1)S(1)} %get-tuple-element.32.high2, bf16[128,4096]{1,0:T(8,128)(2,1)S(1)} %get-tuple-element.33.low2, ...), custom_call_target="tpu_custom_call" | custom-call | flops 536870912 | bytes 1048576 | tf_op jit(solution)/shard_map/keep_products/pallas_call | solution.py:325
  36.9 0.0 copy-start.1
  36.9 0.0 copy-start.2
  37.0 0.0 collective-permute-done.8.half_ref
  37.0 0.1 collective-permute-start.9
  37.1 1.2 %collective-permute-done.9.core_ref = f32[40,128]{1,0:T(8,128)S(1)} collective-permute-done((f32[40,128]{1,0:T(8,128)S(1)}, f32[40,128]{1,0:T(8,128)S(1)}, u32[]{:S(2)}, u32[]{:S(2)}) %collective-permute-start.9) | collective-permute-done | bytes 20512 | tf_op jit(solution)/shard_map/ppermute | solution.py:333
  38.3 0.0 copy-done.1
  38.3 0.0 copy-done.2
  38.3 0.6 %finish_rate.1 = (f32[2,16,128]{2,1,0:T(8,128)}, f32[2,16,128]{2,1,0:T(8,128)}) custom-call(f32[2,40,128]{2,1,0:T(8,128)S(1)} %keep_products.1.keep_ref, f32[2,40,128]{2,1,0:T(8,128)S(1)} %collective-permute-done.8.half_ref, f32[40,128]{1,0:T(8,128)S(1)} %collective-permute-done.9.core_ref, f32[8,128]{1,0:T(8,128)S(1)} %get-tuple-element.20.token_ref.det_ref, ...), custom_call_target="tpu_custom_call" | custom-call | flops 65536 | bytes 262144 | tf_op jit(solution)/shard_map/finish_rate/pallas_call | solution.py:334
  (3 shorter events, 0.0 us)
Async XLA Ops:
  0.6 3.3 %copy-start = (f32[2,16,128]{2,1,0:T(8,128)S(1)}, f32[2,16,128]{2,1,0:T(8,128)}, u32[]{:S(2)}) copy-start(f32[2,16,128]{2,1,0:T(8,128)} %slab_ref.3) | copy-start | bytes 49156
  1.7 6.0 %collective-permute-start = (f32[40,128]{1,0:T(8,128)S(1)}, f32[40,128]{1,0:T(8,128)S(1)}, u32[]{:S(2)}, u32[]{:S(2)}) collective-permute-start(f32[40,128]{1,0:T(8,128)S(1)} %get-tuple-element.23.block_ref), channel_id=1, source_target_pairs={{0,64},{64,0},{128,192},{192,128},{1,65},{65,1},{129,193},{193,129... | collective-permute-start | bytes 61448 | tf_op jit(solution)/shard_map/ppermute | solution.py:273
  3.9 3.8 %collective-permute-start.1 = (f32[2,16,128]{2,1,0:T(8,128)S(1)}, f32[2,16,128]{2,1,0:T(8,128)S(1)}, u32[]{:S(2)}, u32[]{:S(2)}) collective-permute-start(f32[2,16,128]{2,1,0:T(8,128)S(1)} %copy-done), channel_id=1, source_target_pairs={{0,4},{1,5},{2,6},{3,7},{8,12},{9,13},{10,14},{11,15},{16,20},{17,... | collective-permute-start | bytes 49160 | tf_op jit(solution)/shard_map/ppermute | solution.py:291
  7.7 8.1 %collective-permute-start.2 = (f32[2,40,128]{2,1,0:T(8,128)S(1)}, f32[2,40,128]{2,1,0:T(8,128)S(1)}, u32[]{:S(2)}, u32[]{:S(2)}) collective-permute-start(f32[2,40,128]{2,1,0:T(8,128)S(1)} %get-tuple-element.27.both_ref), channel_id=1, source_target_pairs={{0,192},{64,128},{128,64},{192,0},{1,193},{65,129},{129,65},{193,1... | collective-permute-start | bytes 122888 | tf_op jit(solution)/shard_map/ppermute | solution.py:273
  9.7 6.1 %collective-permute-start.3 = (f32[2,2,16,128]{3,2,1,0:T(8,128)S(1)}, f32[2,2,16,128]{3,2,1,0:T(8,128)S(1)}, u32[]{:S(2)}, u32[]{:S(2)}) collective-permute-start(f32[2,2,16,128]{3,2,1,0:T(8,128)S(1)} %get-tuple-element.28.cores_ref), channel_id=1, source_target_pairs={{4,5},{5,4},{6,7},{7,6},{12,13},{13,12},{14,15},{15,14},{20,21},{2... | collective-permute-start | bytes 98312 | tf_op jit(solution)/shard_map/ppermute | solution.py:276
  15.8 11.2 %collective-permute-start.4 = (f32[4,40,128]{2,1,0:T(8,128)S(1)}, f32[4,40,128]{2,1,0:T(8,128)S(1)}, u32[]{:S(2)}, u32[]{:S(2)}) collective-permute-start(f32[4,40,128]{2,1,0:T(8,128)S(1)} %get-tuple-element.29.all0), channel_id=1, source_target_pairs={{0,16},{16,0},{32,48},{48,32},{1,17},{17,1},{33,49},{49,33},{2,18}... | collective-permute-start | bytes 245768 | tf_op jit(solution)/shard_map/ppermute | solution.py:273
  17.1 9.9 %collective-permute-start.5 = (f32[4,40,128]{2,1,0:T(8,128)S(1)}, f32[4,40,128]{2,1,0:T(8,128)S(1)}, u32[]{:S(2)}, u32[]{:S(2)}) collective-permute-start(f32[4,40,128]{2,1,0:T(8,128)S(1)} %get-tuple-element.29.all0), channel_id=1, source_target_pairs={{0,48},{16,32},{32,16},{48,0},{1,49},{17,33},{33,17},{49,1},{2,50}... | collective-permute-start | bytes 245768 | tf_op jit(solution)/shard_map/ppermute | solution.py:273
  19.0 8.1 %collective-permute-start.6 = (f32[4,40,128]{2,1,0:T(8,128)S(1)}, f32[4,40,128]{2,1,0:T(8,128)S(1)}, u32[]{:S(2)}, u32[]{:S(2)}) collective-permute-start(f32[4,40,128]{2,1,0:T(8,128)S(1)} %get-tuple-element.29.all0), channel_id=1, source_target_pairs={{0,32},{16,48},{32,0},{48,16},{1,33},{17,49},{33,1},{49,17},{2,34}... | collective-permute-start | bytes 245768 | tf_op jit(solution)/shard_map/ppermute | solution.py:273
  19.6 13.1 %collective-permute-start.7 = (f32[2,2,2,16,128]{4,3,2,1,0:T(8,128)S(1)}, f32[2,2,2,16,128]{4,3,2,1,0:T(8,128)S(1)}, u32[]{:S(2)}, u32[]{:S(2)}) collective-permute-start(f32[2,2,2,16,128]{4,3,2,1,0:T(8,128)S(1)} %get-tuple-element.34.pair_ref), channel_id=1, source_target_pairs={{4,6},{5,7},{6,4},{7,5},{12,14},{13,15},{14,12},{15,13},{20,22},{2... | collective-permute-start | bytes 196616 | tf_op jit(solution)/shard_map/ppermute | solution.py:276
  28.4 8.5 %collective-permute-start.8 = (f32[2,40,128]{2,1,0:T(8,128)S(1)}, f32[2,40,128]{2,1,0:T(8,128)S(1)}, u32[]{:S(2)}, u32[]{:S(2)}) collective-permute-start(f32[2,40,128]{2,1,0:T(8,128)S(1)} %get-tuple-element.35), channel_id=1, source_target_pairs={{0,8},{8,0},{1,9},{9,1},{2,10},{10,2},{3,11},{11,3},{4,12},{12,4},... | collective-permute-start | bytes 122888 | tf_op jit(solution)/shard_map/ppermute | solution.py:273
  36.9 1.4 %copy-start.1 = (f32[2,16,128]{2,1,0:T(8,128)S(1)}, f32[2,16,128]{2,1,0:T(8,128)}, u32[]{:S(2)}) copy-start(f32[2,16,128]{2,1,0:T(8,128)} %base_ref.1) | copy-start | bytes 49156
  36.9 1.4 %copy-start.2 = (f32[2,16,128]{2,1,0:T(8,128)S(1)}, f32[2,16,128]{2,1,0:T(8,128)}, u32[]{:S(2)}) copy-start(f32[2,16,128]{2,1,0:T(8,128)} %accum_ref.1) | copy-start | bytes 49156
  37.0 1.3 %collective-permute-start.9 = (f32[40,128]{1,0:T(8,128)S(1)}, f32[40,128]{1,0:T(8,128)S(1)}, u32[]{:S(2)}, u32[]{:S(2)}) collective-permute-start(f32[40,128]{1,0:T(8,128)S(1)} %fusion), channel_id=1, source_target_pairs={{0,4},{4,0},{1,5},{5,1},{2,6},{6,2},{3,7},{7,3},{8,12},{12,8},{9,1... | collective-permute-start | bytes 61448 | tf_op jit(solution)/shard_map/ppermute | solution.py:333

commit v12 on v10

--- a/solution.py
+++ b/solution.py
@@ -154,21 +154,31 @@
     rest_ref[1] = v_real - line * y_real - 0.5 * y_imag
 
 
-def fill_own(pos_ref, row_ref, high_ref, low_ref):
-    tiles = pos_ref.shape[1] // (4 * LANES)
-    quad = lax.axis_index("zh") * 2 + lax.axis_index("c")
-    fill_tiles(pos_ref, row_ref, high_ref, low_ref, (quad,), 0, LANES)
+def clear_own(high_ref, low_ref, first):
     eye = lax.broadcasted_iota(jnp.int32, (LANES, LANES), 0) == lax.broadcasted_iota(jnp.int32, (LANES, LANES), 1)
+    half = high_ref.shape[1] // 2
     for part in range(2):
-        lanes = pl.ds(part * tiles * LANES, LANES)
+        lanes = pl.ds(part * half, LANES)
         for ref in (high_ref, low_ref):
-            ref[:, lanes] = jnp.where(eye, 0.0, ref[:, lanes].astype(jnp.float32)).astype(jnp.bfloat16)
+            own = ref[first : first + LANES, lanes].astype(jnp.float32)
+            ref[first : first + LANES, lanes] = jnp.where(eye, 0.0, own).astype(jnp.bfloat16)
+
+
+def own_quads():
+    half, core = lax.axis_index("zh"), lax.axis_index("c")
+    return half * 2 + 1 - core, half * 2 + core
 
 
 def block_kernel(far, pos_ref, token_ref, high_ref, low_ref, row_ref):
     half, core = lax.axis_index("zh"), lax.axis_index("c")
-    quad = ((1 - half) * 2 + 1 - core, (1 - half) * 2 + core, half * 2 + 1 - core)[far]
+    quad = (1 - half) * 2 + (core if far else 1 - core)
     fill_tiles(pos_ref, row_ref, high_ref, low_ref, (quad,), 0, LANES)
+
+
+def early_kernel(pos_ref, token_ref, high_ref, low_ref, row_ref):
+    @pl.when(lax.axis_index("zh") == 0)
+    def _():
+        fill_tiles(pos_ref, row_ref, high_ref, low_ref, own_quads()[:1], 0, LANES)
 
 
 def fill_slab(refs, y_ref):
@@ -206,18 +216,31 @@
     return by_real, by_imag
 
 
-def send_kernel(high0, low0, high1, low1, all0, all1, all2, all3, out_ref, y_ref):
+def send_kernel(pos_ref, high0, low0, high1, low1, all0, all1, all2, all3, out_ref, y_ref, own_high, own_low, row_ref):
     fill_slab((all0, all1, all2, all3), y_ref)
     y = y_ref[...]
     store_products(*products(high0, low0, y), out_ref, 0)
     store_products(*products(high1, low1, y), out_ref, 1)
 
-
-def keep_kernel(pos_ref, y_ref, high2, low2, out_ref, row_ref, high_ref, low_ref):
-    fill_own(pos_ref, row_ref, high_ref, low_ref)
+    @pl.when(lax.axis_index("zh") == 0)
+    def _():
+        fill_tiles(pos_ref, row_ref, own_high, own_low, own_quads()[1:], 0, LANES)
+        clear_own(own_high, own_low, 0)
+
+
+def keep_kernel(pos_ref, y_ref, high2, low2, own_high, own_low, out_ref, row_ref, high_ref, low_ref):
     y = y_ref[...]
-    store_products(*products(high2, low2, y), out_ref, 0)
-    store_products(*products(high_ref, low_ref, y), out_ref, 1)
+
+    @pl.when(lax.axis_index("zh") == 0)
+    def _():
+        store_products(*products(high2, low2, y), out_ref, 0)
+        store_products(*products(own_high, own_low, y), out_ref, 1)
+
+    @pl.when(lax.axis_index("zh") == 1)
+    def _():
+        fill_tiles(pos_ref, row_ref, high_ref, low_ref, own_quads(), 0, 2 * LANES)
+        clear_own(high_ref, low_ref, LANES)
+        store_products(*products(high_ref, low_ref, y), out_ref, 0)
 
 
 def finish_kernel(keep_ref, half_ref, core_ref, rest_ref, slab_ref, base_ref, accum_ref, next_ref, acc_ref):
@@ -267,7 +290,7 @@
 
     def far_block(n, after):
         kernel = functools.partial(block_kernel, n)
-        return call(kernel, "far_block_" + "abc"[n], (tile, tile), [vmem, anywhere], 1 << 24, [rows])(pos, after)
+        return call(kernel, "far_block_" + "ab"[n], (tile, tile), [vmem, anywhere], 1 << 24, [rows])(pos, after)
 
     block, pos, det = call(
         pack_kernel,
@@ -296,20 +319,29 @@
     )(both, two, section, near, high1)
     across = [swap(line, "x", mask) for mask in (1, 3, 2)]
     pair = swap(pair, "zl", 2)
-    high2, low2 = far_block(2, third)
-
-    sent, y = call(
+    high2, low2 = call(
+        early_kernel, "early_block", (tile, tile), [vmem, anywhere], 1 << 24, [rows]
+    )(pos, third)
+
+    sent, y, own_high, own_low = call(
         send_kernel,
         "send_products",
-        (pltpu.VMEM((2, PART, LANES), f32), pltpu.VMEM((LANES, deep // 2), bf16)),
-        [vmem] * 8,
+        (pltpu.VMEM((2, PART, LANES), f32), pltpu.VMEM((LANES, deep // 2), bf16), tile, tile),
+        [vmem] * 9,
         1 << 29,
-    )(high0, low0, high1, low1, line, *across)
+        [rows],
+    )(pos, high0, low0, high1, low1, line, *across)
     half = swap(sent, "zh", 1)
 
+    wide = pltpu.VMEM((2 * LANES, deep), bf16)
     (keep,) = call(
-        keep_kernel, "keep_products", (pltpu.VMEM((2, PART, LANES), f32),), [vmem] * 4, 1 << 29, [rows, tile, tile]
-    )(pos, y, high2, low2)
+        keep_kernel,
+        "keep_products",
+        (pltpu.VMEM((2, PART, LANES), f32),),
+        [vmem] * 6,
+        1 << 29,
+        [pltpu.VMEM((3, 2 * LANES, LANES), f32), wide, wide],
+    )(pos, y, high2, low2, own_high, own_low)
     core = lax.ppermute(keep[0] + half[0], "c", [(0, 1), (1, 0)])
     rest = pl.pallas_call(
         term_kernel,

time: 36.9 us -> 38.3 us (1.038)
  waiting for transfers between devices: 0.55 us -> 3.62 us
  starting transfers between devices: 20.6 us -> 19 us
    ppermute x8, waiting for transfers between devices: 0.02 us -> 3.09 us  [swap(): return lax.ppermute(array, axis, [(i, i ^ mask) for i in range(size)])]
    pallas_call x1, Pallas kernels: 1.35 us -> 3.9 us  [local(): call(send_kernel, 'send_products', (pltpu.VMEM((2, PART, LANES), f32), pl...]
    ppermute x8, starting transfers between devices: 17.6 us -> 15 us  [swap(): return lax.ppermute(array, axis, [(i, i ^ mask) for i in range(size)])]
    pallas_call x1, Pallas kernels: 3.82 us -> 1.34 us  [local(): call(keep_kernel, 'keep_products', (pltpu.VMEM((2, PART, LANES), f32),),...]
    ppermute x1, starting transfers between devices: 3.03 us -> 3.95 us  [local(): core = lax.ppermute(keep[0] + half[0], 'c', [(0, 1), (1, 0)])]
  transfers between devices with their start and end apart: 9 -> 9, of which waited for: 1 -> 2; matrix products, arithmetic and copies ran while one was open for 0% -> 0% of each run, Pallas kernels for 35% -> 34%
where the time goes in v12:
time: 38.3 us; the launch traced here: 38.1 us
  starting transfers between devices  19 us (50%)
  Pallas kernels  14.7 us (38%)
  waiting for transfers between devices  3.62 us (9%)
  between operations  0.76 us (2%)
    ppermute x8, starting transfers between devices, swap(): return lax.ppermute(array, axis, [(i, i ^ mask) for i in range(size)])  15 us
    pallas_call x2, Pallas kernels, far_block(): call(kernel, 'far_block_' + 'ab'[n], (tile, tile), [vmem, anywhere], 1 <<...  5.01 us
    ppermute x1, starting transfers between devices, local(): core = lax.ppermute(keep[0] + half[0], 'c', [(0, 1), (1, 0)])  3.95 us
    pallas_call x1, Pallas kernels, local(): call(send_kernel, 'send_products', (pltpu.VMEM((2, PART, LANES), f32), pl...  3.9 us
    ppermute x8, waiting for transfers between devices, swap(): return lax.ppermute(array, axis, [(i, i ^ mask) for i in range(size)])  3.09 us
    pallas_call x1, Pallas kernels, local(): call(early_kernel, 'early_block', (tile, tile), [vmem, anywhere], 1 << 24...  2.5 us
    pallas_call x1, Pallas kernels, local(): call(keep_kernel, 'keep_products', (pltpu.VMEM((2, PART, LANES), f32),),...  1.34 us
    pallas_call x1, Pallas kernels, local(): call(pack_kernel, 'pack_block', (pltpu.VMEM((PART, LANES), f32), pltpu.VM...  1.02 us
  transfers between devices with their start and end apart: 9, of which 2 were waited for; matrix products, arithmetic and copies ran while one was open for 0% of the time, Pallas kernels for 34%

profile of v12, /device:TPU:1, one launch (start us, length us, event | category | flops | bytes accessed | tf_op | source)
XLA Modules:
  0.0 38.1 jit_solution(9909056700402224792)
XLA Ops:
  0.6 1.0 %pack_block.1 = (f32[40,128]{1,0:T(8,128)S(1)}, f32[3,8192]{1,0:T(4,128)S(1)}, f32[8,128]{1,0:T(8,128)S(1)}) custom-call(f32[2,16,128]{2,1,0:T(8,128)} %slab_ref.5, f32[1,128]{1,0:T(1,128)} %bitcast.5, f32[3,8192]{1,0:T(4,128)} %pos_ref.1, f32[1,8192]{1,0:T(1,128)} %bitcast.4), custom_call_target="tpu_custom_call" | custom-call | flops 65536 | bytes 1048576 | tf_op jit(solution)/shard_map/pack_block/pallas_call | solution.py:295
  1.7 2.2 %collective-permute-start = (f32[40,128]{1,0:T(8,128)S(1)}, f32[40,128]{1,0:T(8,128)S(1)}, u32[]{:S(2)}, u32[]{:S(2)}) collective-permute-start(f32[40,128]{1,0:T(8,128)S(1)} %get-tuple-element.24.block_ref), channel_id=1, source_target_pairs={{0,64},{64,0},{128,192},{192,128},{1,65},{65,1},{129,193},{193,129... | collective-permute-start | bytes 61448 | tf_op jit(solution)/shard_map/ppermute | solution.py:289
  3.9 2.5 %far_block_a.1 = (bf16[128,4096]{1,0:T(8,128)(2,1)S(1)}, bf16[128,4096]{1,0:T(8,128)(2,1)S(1)}) custom-call(f32[3,8192]{1,0:T(4,128)S(1)} %get-tuple-element.20.pos_ref, f32[8,128]{1,0:T(8,128)S(1)} %get-tuple-element.21.token_ref.det_ref), custom_call_target="tpu_custom_call" | custom-call | flops 16777216 | bytes 1048576 | tf_op jit(solution)/shard_map/far_block_a/pallas_call | solution.py:293
  6.4 0.0 collective-permute-done.one_ref
  6.4 0.0 copy-start
  6.4 2.0 %collective-permute-start.1 = (f32[2,40,128]{2,1,0:T(8,128)S(1)}, f32[2,40,128]{2,1,0:T(8,128)S(1)}, u32[]{:S(2)}, u32[]{:S(2)}) collective-permute-start(f32[2,40,128]{2,1,0:T(8,128)S(1)} %get-tuple-element.28.both_ref), channel_id=1, source_target_pairs={{0,192},{64,128},{128,64},{192,0},{1,193},{65,129},{129,65},{193,1... | collective-permute-start | bytes 122888 | tf_op jit(solution)/shard_map/ppermute | solution.py:289
  8.4 0.0 copy-done
  8.4 1.6 %collective-permute-start.2 = (f32[2,16,128]{2,1,0:T(8,128)S(1)}, f32[2,16,128]{2,1,0:T(8,128)S(1)}, u32[]{:S(2)}, u32[]{:S(2)}) collective-permute-start(f32[2,16,128]{2,1,0:T(8,128)S(1)} %copy-done), channel_id=1, source_target_pairs={{0,1},{1,0},{2,3},{3,2},{4,5},{5,4},{6,7},{7,6},{8,9},{9,8},{10,11... | collective-permute-start | bytes 49160 | tf_op jit(solution)/shard_map/ppermute | solution.py:289
  10.0 2.5 %far_block_b.1 = (bf16[128,4096]{1,0:T(8,128)(2,1)S(1)}, bf16[128,4096]{1,0:T(8,128)(2,1)S(1)}) custom-call(f32[3,8192]{1,0:T(4,128)S(1)} %get-tuple-element.20.pos_ref, f32[8,128]{1,0:T(8,128)S(1)} %get-tuple-element.25.token_ref), custom_call_target="tpu_custom_call" | custom-call | flops 16777216 | bytes 1048576 | tf_op jit(solution)/shard_map/far_block_b/pallas_call | solution.py:293
  12.6 0.0 collective-permute-done.2.near_ref
  12.6 0.0 collective-permute-done.1.two_ref
  12.6 2.8 %collective-permute-start.5 = (f32[4,40,128]{2,1,0:T(8,128)S(1)}, f32[4,40,128]{2,1,0:T(8,128)S(1)}, u32[]{:S(2)}, u32[]{:S(2)}) collective-permute-start(f32[4,40,128]{2,1,0:T(8,128)S(1)} %get-tuple-element.29.all0), channel_id=1, source_target_pairs={{0,32},{16,48},{32,0},{48,16},{1,33},{17,49},{33,1},{49,17},{2,34}... | collective-permute-start | bytes 245768 | tf_op jit(solution)/shard_map/ppermute | solution.py:289
  15.4 0.9 %collective-permute-start.4 = (f32[4,40,128]{2,1,0:T(8,128)S(1)}, f32[4,40,128]{2,1,0:T(8,128)S(1)}, u32[]{:S(2)}, u32[]{:S(2)}) collective-permute-start(f32[4,40,128]{2,1,0:T(8,128)S(1)} %get-tuple-element.29.all0), channel_id=1, source_target_pairs={{0,48},{16,32},{32,16},{48,0},{1,49},{17,33},{33,17},{49,1},{2,50}... | collective-permute-start | bytes 245768 | tf_op jit(solution)/shard_map/ppermute | solution.py:289
  16.3 0.0 collective-permute-start.3
  16.3 3.0 %collective-permute-start.8 = (f32[2,2,16,128]{3,2,1,0:T(8,128)S(1)}, f32[2,2,16,128]{3,2,1,0:T(8,128)S(1)}, u32[]{:S(2)}, u32[]{:S(2)}) collective-permute-start(f32[2,2,16,128]{3,2,1,0:T(8,128)S(1)} %get-tuple-element.37), channel_id=1, source_target_pairs={{0,2},{1,3},{2,0},{3,1},{4,6},{5,7},{6,4},{7,5},{8,10},{9,11},{10,... | collective-permute-start | bytes 98312 | tf_op jit(solution)/shard_map/ppermute | solution.py:289
  19.3 2.5 %early_block.1 = (bf16[128,4096]{1,0:T(8,128)(2,1)S(1)}, bf16[128,4096]{1,0:T(8,128)(2,1)S(1)}) custom-call(f32[3,8192]{1,0:T(4,128)S(1)} %get-tuple-element.20.pos_ref, f32[8,128]{1,0:T(8,128)S(1)} %get-tuple-element.31.token_ref), custom_call_target="tpu_custom_call" | custom-call | flops 16777216 | bytes 1048576 | tf_op jit(solution)/shard_map/early_block/pallas_call | solution.py:322
  21.8 0.0 collective-permute-done.5.all3
  21.8 0.0 collective-permute-done.4.all2
  21.8 0.0 collective-permute-done.3.all1
  21.8 3.9 %send_products.1 = (f32[2,40,128]{2,1,0:T(8,128)S(1)}, bf16[128,2048]{1,0:T(8,128)(2,1)S(1)}, bf16[128,4096]{1,0:T(8,128)(2,1)S(1)}, bf16[128,4096]{1,0:T(8,128)(2,1)S(1)}) custom-call(f32[3,8192]{1,0:T(4,128)S(1)} %get-tuple-element.20.pos_ref, bf16[128,4096]{1,0:T(8,128)(2,1)S(1)} %get-tuple-element.22.after_ref.high0, ...), custom_call_target="tpu_custom_call" | custom-call | flops 536870912 | bytes 1048576 | tf_op jit(solution)/shard_map/send_products/pallas_call | solution.py:326
  25.7 2.5 %collective-permute-start.6 = (f32[2,40,128]{2,1,0:T(8,128)S(1)}, f32[2,40,128]{2,1,0:T(8,128)S(1)}, u32[]{:S(2)}, u32[]{:S(2)}) collective-permute-start(f32[2,40,128]{2,1,0:T(8,128)S(1)} %get-tuple-element.36), channel_id=1, source_target_pairs={{0,8},{8,0},{1,9},{9,1},{2,10},{10,2},{3,11},{11,3},{4,12},{12,4},... | collective-permute-start | bytes 122888 | tf_op jit(solution)/shard_map/ppermute | solution.py:289
  28.3 1.3 %keep_products.1.keep_ref = f32[2,40,128]{2,1,0:T(8,128)S(1)} custom-call(f32[3,8192]{1,0:T(4,128)S(1)} %get-tuple-element.20.pos_ref, bf16[128,2048]{1,0:T(8,128)(2,1)S(1)} %get-tuple-element.30.y_ref, bf16[128,4096]{1,0:T(8,128)(2,1)S(1)} %get-tuple-element.32.high2, bf16[128,4096]{1,0:T(8,128)(2,1)S(1)} %get-tuple-element.33.low2, ...), custom_call_target="tpu_custom_call" | custom-call | flops 536870912 | bytes 1048576 | tf_op jit(solution)/shard_map/keep_products/pallas_call | solution.py:337
  29.6 3.1 %collective-permute-done.6.half_ref = f32[2,40,128]{2,1,0:T(8,128)S(1)} collective-permute-done((f32[2,40,128]{2,1,0:T(8,128)S(1)}, f32[2,40,128]{2,1,0:T(8,128)S(1)}, u32[]{:S(2)}, u32[]{:S(2)}) %collective-permute-start.6) | collective-permute-done | bytes 40992 | tf_op jit(solution)/shard_map/ppermute | solution.py:289
  32.7 0.0 copy-start.1
  32.7 0.0 copy-start.2
  32.7 3.9 %collective-permute-start.7 = (f32[40,128]{1,0:T(8,128)S(1)}, f32[40,128]{1,0:T(8,128)S(1)}, u32[]{:S(2)}, u32[]{:S(2)}) collective-permute-start(f32[40,128]{1,0:T(8,128)S(1)} %fusion), channel_id=1, source_target_pairs={{0,4},{4,0},{1,5},{5,1},{2,6},{6,2},{3,7},{7,3},{8,12},{12,8},{9,1... | collective-permute-start | bytes 61448 | tf_op jit(solution)/shard_map/ppermute | solution.py:345
  36.6 0.0 collective-permute-done.8.pair_ref
  36.6 0.3 slab_term.1.rest_ref
  37.0 0.5 %collective-permute-done.7.core_ref = f32[40,128]{1,0:T(8,128)S(1)} collective-permute-done((f32[40,128]{1,0:T(8,128)S(1)}, f32[40,128]{1,0:T(8,128)S(1)}, u32[]{:S(2)}, u32[]{:S(2)}) %collective-permute-start.7) | collective-permute-done | bytes 20512 | tf_op jit(solution)/shard_map/ppermute | solution.py:345
  37.5 0.0 copy-done.1
  37.5 0.0 copy-done.2
  37.5 0.6 %finish_rate.1 = (f32[2,16,128]{2,1,0:T(8,128)}, f32[2,16,128]{2,1,0:T(8,128)}) custom-call(f32[2,40,128]{2,1,0:T(8,128)S(1)} %keep_products.1.keep_ref, f32[2,40,128]{2,1,0:T(8,128)S(1)} %collective-permute-done.6.half_ref, f32[40,128]{1,0:T(8,128)S(1)} %collective-permute-done.7.core_ref, f32[2,16,128]{2,1,0:T(8,128)S(1)} %slab_term.1.rest_ref, ...), custom_call_target="tpu_custom_call" | custom-call | flops 65536 | bytes 262144 | tf_op jit(solution)/shard_map/finish_rate/pallas_call | solution.py:357
  (3 shorter events, 0.0 us)
Async XLA Ops:
  1.7 4.7 %collective-permute-start = (f32[40,128]{1,0:T(8,128)S(1)}, f32[40,128]{1,0:T(8,128)S(1)}, u32[]{:S(2)}, u32[]{:S(2)}) collective-permute-start(f32[40,128]{1,0:T(8,128)S(1)} %get-tuple-element.24.block_ref), channel_id=1, source_target_pairs={{0,64},{64,0},{128,192},{192,128},{1,65},{65,1},{129,193},{193,129... | collective-permute-start | bytes 61448 | tf_op jit(solution)/shard_map/ppermute | solution.py:289
  6.4 2.0 %copy-start = (f32[2,16,128]{2,1,0:T(8,128)S(1)}, f32[2,16,128]{2,1,0:T(8,128)}, u32[]{:S(2)}) copy-start(f32[2,16,128]{2,1,0:T(8,128)} %slab_ref.5) | copy-start | bytes 49156
  6.4 6.2 %collective-permute-start.1 = (f32[2,40,128]{2,1,0:T(8,128)S(1)}, f32[2,40,128]{2,1,0:T(8,128)S(1)}, u32[]{:S(2)}, u32[]{:S(2)}) collective-permute-start(f32[2,40,128]{2,1,0:T(8,128)S(1)} %get-tuple-element.28.both_ref), channel_id=1, source_target_pairs={{0,192},{64,128},{128,64},{192,0},{1,193},{65,129},{129,65},{193,1... | collective-permute-start | bytes 122888 | tf_op jit(solution)/shard_map/ppermute | solution.py:289
  8.4 4.1 %collective-permute-start.2 = (f32[2,16,128]{2,1,0:T(8,128)S(1)}, f32[2,16,128]{2,1,0:T(8,128)S(1)}, u32[]{:S(2)}, u32[]{:S(2)}) collective-permute-start(f32[2,16,128]{2,1,0:T(8,128)S(1)} %copy-done), channel_id=1, source_target_pairs={{0,1},{1,0},{2,3},{3,2},{4,5},{5,4},{6,7},{7,6},{8,9},{9,8},{10,11... | collective-permute-start | bytes 49160 | tf_op jit(solution)/shard_map/ppermute | solution.py:289
  12.6 9.2 %collective-permute-start.5 = (f32[4,40,128]{2,1,0:T(8,128)S(1)}, f32[4,40,128]{2,1,0:T(8,128)S(1)}, u32[]{:S(2)}, u32[]{:S(2)}) collective-permute-start(f32[4,40,128]{2,1,0:T(8,128)S(1)} %get-tuple-element.29.all0), channel_id=1, source_target_pairs={{0,32},{16,48},{32,0},{48,16},{1,33},{17,49},{33,1},{49,17},{2,34}... | collective-permute-start | bytes 245768 | tf_op jit(solution)/shard_map/ppermute | solution.py:289
  15.4 6.4 %collective-permute-start.4 = (f32[4,40,128]{2,1,0:T(8,128)S(1)}, f32[4,40,128]{2,1,0:T(8,128)S(1)}, u32[]{:S(2)}, u32[]{:S(2)}) collective-permute-start(f32[4,40,128]{2,1,0:T(8,128)S(1)} %get-tuple-element.29.all0), channel_id=1, source_target_pairs={{0,48},{16,32},{32,16},{48,0},{1,49},{17,33},{33,17},{49,1},{2,50}... | collective-permute-start | bytes 245768 | tf_op jit(solution)/shard_map/ppermute | solution.py:289
  16.3 5.5 %collective-permute-start.3 = (f32[4,40,128]{2,1,0:T(8,128)S(1)}, f32[4,40,128]{2,1,0:T(8,128)S(1)}, u32[]{:S(2)}, u32[]{:S(2)}) collective-permute-start(f32[4,40,128]{2,1,0:T(8,128)S(1)} %get-tuple-element.29.all0), channel_id=1, source_target_pairs={{0,16},{16,0},{32,48},{48,32},{1,17},{17,1},{33,49},{49,33},{2,18}... | collective-permute-start | bytes 245768 | tf_op jit(solution)/shard_map/ppermute | solution.py:289
  16.3 20.4 %collective-permute-start.8 = (f32[2,2,16,128]{3,2,1,0:T(8,128)S(1)}, f32[2,2,16,128]{3,2,1,0:T(8,128)S(1)}, u32[]{:S(2)}, u32[]{:S(2)}) collective-permute-start(f32[2,2,16,128]{3,2,1,0:T(8,128)S(1)} %get-tuple-element.37), channel_id=1, source_target_pairs={{0,2},{1,3},{2,0},{3,1},{4,6},{5,7},{6,4},{7,5},{8,10},{9,11},{10,... | collective-permute-start | bytes 98312 | tf_op jit(solution)/shard_map/ppermute | solution.py:289
  25.7 7.0 %collective-permute-start.6 = (f32[2,40,128]{2,1,0:T(8,128)S(1)}, f32[2,40,128]{2,1,0:T(8,128)S(1)}, u32[]{:S(2)}, u32[]{:S(2)}) collective-permute-start(f32[2,40,128]{2,1,0:T(8,128)S(1)} %get-tuple-element.36), channel_id=1, source_target_pairs={{0,8},{8,0},{1,9},{9,1},{2,10},{10,2},{3,11},{11,3},{4,12},{12,4},... | collective-permute-start | bytes 122888 | tf_op jit(solution)/shard_map/ppermute | solution.py:289
  32.7 4.8 %copy-start.1 = (f32[2,16,128]{2,1,0:T(8,128)S(1)}, f32[2,16,128]{2,1,0:T(8,128)}, u32[]{:S(2)}) copy-start(f32[2,16,128]{2,1,0:T(8,128)} %base_ref.1) | copy-start | bytes 49156
  32.7 4.8 %copy-start.2 = (f32[2,16,128]{2,1,0:T(8,128)S(1)}, f32[2,16,128]{2,1,0:T(8,128)}, u32[]{:S(2)}) copy-start(f32[2,16,128]{2,1,0:T(8,128)} %accum_ref.1) | copy-start | bytes 49156
  32.7 4.8 %collective-permute-start.7 = (f32[40,128]{1,0:T(8,128)S(1)}, f32[40,128]{1,0:T(8,128)S(1)}, u32[]{:S(2)}, u32[]{:S(2)}) collective-permute-start(f32[40,128]{1,0:T(8,128)S(1)} %fusion), channel_id=1, source_target_pairs={{0,4},{4,0},{1,5},{5,1},{2,6},{6,2},{3,7},{7,3},{8,12},{12,8},{9,1... | collective-permute-start | bytes 61448 | tf_op jit(solution)/shard_map/ppermute | solution.py:345

commit v13 on v12

--- a/solution.py
+++ b/solution.py
@@ -216,25 +216,23 @@
     return by_real, by_imag
 
 
-def send_kernel(pos_ref, high0, low0, high1, low1, all0, all1, all2, all3, out_ref, y_ref, own_high, own_low, row_ref):
+def send_kernel(high0, low0, high1, low1, all0, all1, all2, all3, out_ref, y_ref):
     fill_slab((all0, all1, all2, all3), y_ref)
     y = y_ref[...]
     store_products(*products(high0, low0, y), out_ref, 0)
     store_products(*products(high1, low1, y), out_ref, 1)
 
+
+def keep_kernel(pos_ref, y_ref, high2, low2, out_ref, row_ref, high_ref, low_ref):
+    y = y_ref[...]
+
     @pl.when(lax.axis_index("zh") == 0)
     def _():
-        fill_tiles(pos_ref, row_ref, own_high, own_low, own_quads()[1:], 0, LANES)
-        clear_own(own_high, own_low, 0)
-
-
-def keep_kernel(pos_ref, y_ref, high2, low2, own_high, own_low, out_ref, row_ref, high_ref, low_ref):
-    y = y_ref[...]
-
-    @pl.when(lax.axis_index("zh") == 0)
-    def _():
+        high, low = high_ref.at[pl.ds(0, LANES)], low_ref.at[pl.ds(0, LANES)]
+        fill_tiles(pos_ref, row_ref, high, low, own_quads()[1:], 0, LANES)
+        clear_own(high, low, 0)
         store_products(*products(high2, low2, y), out_ref, 0)
-        store_products(*products(own_high, own_low, y), out_ref, 1)
+        store_products(*products(high, low, y), out_ref, 1)
 
     @pl.when(lax.axis_index("zh") == 1)
     def _():
@@ -323,14 +321,13 @@
         early_kernel, "early_block", (tile, tile), [vmem, anywhere], 1 << 24, [rows]
     )(pos, third)
 
-    sent, y, own_high, own_low = call(
+    sent, y = call(
         send_kernel,
         "send_products",
-        (pltpu.VMEM((2, PART, LANES), f32), pltpu.VMEM((LANES, deep // 2), bf16), tile, tile),
-        [vmem] * 9,
+        (pltpu.VMEM((2, PART, LANES), f32), pltpu.VMEM((LANES, deep // 2), bf16)),
+        [vmem] * 8,
         1 << 29,
-        [rows],
-    )(pos, high0, low0, high1, low1, line, *across)
+    )(high0, low0, high1, low1, line, *across)
     half = swap(sent, "zh", 1)
 
     wide = pltpu.VMEM((2 * LANES, deep), bf16)
@@ -338,10 +335,10 @@
         keep_kernel,
         "keep_products",
         (pltpu.VMEM((2, PART, LANES), f32),),
-        [vmem] * 6,
+        [vmem] * 4,
         1 << 29,
         [pltpu.VMEM((3, 2 * LANES, LANES), f32), wide, wide],
-    )(pos, y, high2, low2, own_high, own_low)
+    )(pos, y, high2, low2)
     core = lax.ppermute(keep[0] + half[0], "c", [(0, 1), (1, 0)])
     rest = pl.pallas_call(
         term_kernel,

time: 38.3 us -> 36.9 us (0.963)
  waiting for transfers between devices: 3.62 us -> 0.55 us
  starting transfers between devices: 19 us -> 20.6 us
    ppermute x8, waiting for transfers between devices: 3.09 us -> 0.02 us  [swap(): return lax.ppermute(array, axis, [(i, i ^ mask) for i in range(size)])]
    pallas_call x1, Pallas kernels: 3.9 us -> 1.35 us  [local(): call(send_kernel, 'send_products', (pltpu.VMEM((2, PART, LANES), f32), pl...]
    ppermute x8, starting transfers between devices: 15 us -> 17.6 us  [swap(): return lax.ppermute(array, axis, [(i, i ^ mask) for i in range(size)])]
    pallas_call x1, Pallas kernels: 1.34 us -> 3.87 us  [local(): call(keep_kernel, 'keep_products', (pltpu.VMEM((2, PART, LANES), f32),),...]
    ppermute x1, starting transfers between devices: 3.95 us -> 3.03 us  [local(): core = lax.ppermute(keep[0] + half[0], 'c', [(0, 1), (1, 0)])]
  transfers between devices with their start and end apart: 9 -> 9, of which waited for: 2 -> 1; matrix products, arithmetic and copies ran while one was open for 0% -> 0% of each run, Pallas kernels for 34% -> 36%
where the time goes in v13:
time: 36.9 us; the launch traced here: 36.7 us
  starting transfers between devices  20.6 us (56%)
  Pallas kernels  14.7 us (40%)
  between operations  0.78 us (2%)
  waiting for transfers between devices  0.55 us (1%)
    ppermute x8, starting transfers between devices, swap(): return lax.ppermute(array, axis, [(i, i ^ mask) for i in range(size)])  17.6 us
    pallas_call x2, Pallas kernels, far_block(): call(kernel, 'far_block_' + 'ab'[n], (tile, tile), [vmem, anywhere], 1 <<...  5.01 us
    pallas_call x1, Pallas kernels, local(): call(keep_kernel, 'keep_products', (pltpu.VMEM((2, PART, LANES), f32),),...  3.87 us
    ppermute x1, starting transfers between devices, local(): core = lax.ppermute(keep[0] + half[0], 'c', [(0, 1), (1, 0)])  3.03 us
    pallas_call x1, Pallas kernels, local(): call(early_kernel, 'early_block', (tile, tile), [vmem, anywhere], 1 << 24...  2.5 us
    pallas_call x1, Pallas kernels, local(): call(send_kernel, 'send_products', (pltpu.VMEM((2, PART, LANES), f32), pl...  1.35 us
    pallas_call x1, Pallas kernels, local(): call(pack_kernel, 'pack_block', (pltpu.VMEM((PART, LANES), f32), pltpu.VM...  1.02 us
  transfers between devices with their start and end apart: 9, of which 1 were waited for; matrix products, arithmetic and copies ran while one was open for 0% of the time, Pallas kernels for 36%

profile of v13, /device:TPU:1, one launch (start us, length us, event | category | flops | bytes accessed | tf_op | source)
XLA Modules:
  0.0 36.7 jit_solution(397867029565770993)
XLA Ops:
  0.6 1.0 %pack_block.1 = (f32[40,128]{1,0:T(8,128)S(1)}, f32[3,8192]{1,0:T(4,128)S(1)}, f32[8,128]{1,0:T(8,128)S(1)}) custom-call(f32[2,16,128]{2,1,0:T(8,128)} %slab_ref.5, f32[1,128]{1,0:T(1,128)} %bitcast.5, f32[3,8192]{1,0:T(4,128)} %pos_ref.1, f32[1,8192]{1,0:T(1,128)} %bitcast.4), custom_call_target="tpu_custom_call" | custom-call | flops 65536 | bytes 1048576 | tf_op jit(solution)/shard_map/pack_block/pallas_call | solution.py:293
  1.7 2.2 %collective-permute-start = (f32[40,128]{1,0:T(8,128)S(1)}, f32[40,128]{1,0:T(8,128)S(1)}, u32[]{:S(2)}, u32[]{:S(2)}) collective-permute-start(f32[40,128]{1,0:T(8,128)S(1)} %get-tuple-element.22.block_ref), channel_id=1, source_target_pairs={{0,64},{64,0},{128,192},{192,128},{1,65},{65,1},{129,193},{193,129... | collective-permute-start | bytes 61448 | tf_op jit(solution)/shard_map/ppermute | solution.py:287
  3.9 2.5 %far_block_a.1 = (bf16[128,4096]{1,0:T(8,128)(2,1)S(1)}, bf16[128,4096]{1,0:T(8,128)(2,1)S(1)}) custom-call(f32[3,8192]{1,0:T(4,128)S(1)} %get-tuple-element.18.pos_ref, f32[8,128]{1,0:T(8,128)S(1)} %get-tuple-element.19.token_ref.det_ref), custom_call_target="tpu_custom_call" | custom-call | flops 16777216 | bytes 1048576 | tf_op jit(solution)/shard_map/far_block_a/pallas_call | solution.py:291
  6.4 0.0 collective-permute-done.one_ref
  6.4 0.0 copy-start
  6.4 2.0 %collective-permute-start.1 = (f32[2,40,128]{2,1,0:T(8,128)S(1)}, f32[2,40,128]{2,1,0:T(8,128)S(1)}, u32[]{:S(2)}, u32[]{:S(2)}) collective-permute-start(f32[2,40,128]{2,1,0:T(8,128)S(1)} %get-tuple-element.26.both_ref), channel_id=1, source_target_pairs={{0,192},{64,128},{128,64},{192,0},{1,193},{65,129},{129,65},{193,1... | collective-permute-start | bytes 122888 | tf_op jit(solution)/shard_map/ppermute | solution.py:287
  8.4 0.0 copy-done
  8.4 1.6 %collective-permute-start.2 = (f32[2,16,128]{2,1,0:T(8,128)S(1)}, f32[2,16,128]{2,1,0:T(8,128)S(1)}, u32[]{:S(2)}, u32[]{:S(2)}) collective-permute-start(f32[2,16,128]{2,1,0:T(8,128)S(1)} %copy-done), channel_id=1, source_target_pairs={{0,1},{1,0},{2,3},{3,2},{4,5},{5,4},{6,7},{7,6},{8,9},{9,8},{10,11... | collective-permute-start | bytes 49160 | tf_op jit(solution)/shard_map/ppermute | solution.py:287
  10.0 2.5 %far_block_b.1 = (bf16[128,4096]{1,0:T(8,128)(2,1)S(1)}, bf16[128,4096]{1,0:T(8,128)(2,1)S(1)}) custom-call(f32[3,8192]{1,0:T(4,128)S(1)} %get-tuple-element.18.pos_ref, f32[8,128]{1,0:T(8,128)S(1)} %get-tuple-element.23.token_ref), custom_call_target="tpu_custom_call" | custom-call | flops 16777216 | bytes 1048576 | tf_op jit(solution)/shard_map/far_block_b/pallas_call | solution.py:291
  12.6 0.0 collective-permute-done.2.near_ref
  12.6 0.0 collective-permute-done.1.two_ref
  12.6 2.8 %collective-permute-start.5 = (f32[4,40,128]{2,1,0:T(8,128)S(1)}, f32[4,40,128]{2,1,0:T(8,128)S(1)}, u32[]{:S(2)}, u32[]{:S(2)}) collective-permute-start(f32[4,40,128]{2,1,0:T(8,128)S(1)} %get-tuple-element.27.all0), channel_id=1, source_target_pairs={{0,32},{16,48},{32,0},{48,16},{1,33},{17,49},{33,1},{49,17},{2,34}... | collective-permute-start | bytes 245768 | tf_op jit(solution)/shard_map/ppermute | solution.py:287
  15.4 0.9 %collective-permute-start.4 = (f32[4,40,128]{2,1,0:T(8,128)S(1)}, f32[4,40,128]{2,1,0:T(8,128)S(1)}, u32[]{:S(2)}, u32[]{:S(2)}) collective-permute-start(f32[4,40,128]{2,1,0:T(8,128)S(1)} %get-tuple-element.27.all0), channel_id=1, source_target_pairs={{0,48},{16,32},{32,16},{48,0},{1,49},{17,33},{33,17},{49,1},{2,50}... | collective-permute-start | bytes 245768 | tf_op jit(solution)/shard_map/ppermute | solution.py:287
  16.3 0.0 collective-permute-start.3
  16.3 3.0 %collective-permute-start.8 = (f32[2,2,16,128]{3,2,1,0:T(8,128)S(1)}, f32[2,2,16,128]{3,2,1,0:T(8,128)S(1)}, u32[]{:S(2)}, u32[]{:S(2)}) collective-permute-start(f32[2,2,16,128]{3,2,1,0:T(8,128)S(1)} %get-tuple-element.33), channel_id=1, source_target_pairs={{0,2},{1,3},{2,0},{3,1},{4,6},{5,7},{6,4},{7,5},{8,10},{9,11},{10,... | collective-permute-start | bytes 98312 | tf_op jit(solution)/shard_map/ppermute | solution.py:287
  19.3 2.5 %early_block.1 = (bf16[128,4096]{1,0:T(8,128)(2,1)S(1)}, bf16[128,4096]{1,0:T(8,128)(2,1)S(1)}) custom-call(f32[3,8192]{1,0:T(4,128)S(1)} %get-tuple-element.18.pos_ref, f32[8,128]{1,0:T(8,128)S(1)} %get-tuple-element.29.token_ref), custom_call_target="tpu_custom_call" | custom-call | flops 16777216 | bytes 1048576 | tf_op jit(solution)/shard_map/early_block/pallas_call | solution.py:320
  21.8 0.0 collective-permute-done.5.all3
  21.8 0.0 collective-permute-done.4.all2
  21.8 0.0 collective-permute-done.3.all1
  21.8 1.3 %send_products.1 = (f32[2,40,128]{2,1,0:T(8,128)S(1)}, bf16[128,2048]{1,0:T(8,128)(2,1)S(1)}) custom-call(bf16[128,4096]{1,0:T(8,128)(2,1)S(1)} %get-tuple-element.20.after_ref.high0, bf16[128,4096]{1,0:T(8,128)(2,1)S(1)} %get-tuple-element.21.low0, bf16[128,4096]{1,0:T(8,128)(2,1)S(1)} %get-tuple-element.24.after_ref.high1, ...), custom_call_target="tpu_custom_call" | custom-call | flops 536870912 | bytes 1048576 | tf_op jit(solution)/shard_map/send_products/pallas_call | solution.py:324
  23.2 5.1 %collective-permute-start.6 = (f32[2,40,128]{2,1,0:T(8,128)S(1)}, f32[2,40,128]{2,1,0:T(8,128)S(1)}, u32[]{:S(2)}, u32[]{:S(2)}) collective-permute-start(f32[2,40,128]{2,1,0:T(8,128)S(1)} %get-tuple-element.32), channel_id=1, source_target_pairs={{0,8},{8,0},{1,9},{9,1},{2,10},{10,2},{3,11},{11,3},{4,12},{12,4},... | collective-permute-start | bytes 122888 | tf_op jit(solution)/shard_map/ppermute | solution.py:287
  28.3 3.9 %keep_products.1.keep_ref = f32[2,40,128]{2,1,0:T(8,128)S(1)} custom-call(f32[3,8192]{1,0:T(4,128)S(1)} %get-tuple-element.18.pos_ref, bf16[128,2048]{1,0:T(8,128)(2,1)S(1)} %get-tuple-element.28.y_ref, bf16[128,4096]{1,0:T(8,128)(2,1)S(1)} %get-tuple-element.30.high2, bf16[128,4096]{1,0:T(8,128)(2,1)S(1)} %get-tuple-element.31.low2), custom_call_target="tpu_custom_call" | custom-call | flops 536870912 | bytes 1048576 | tf_op jit(solution)/shard_map/keep_products/pallas_call | solution.py:334
  32.1 0.0 collective-permute-done.6.half_ref
  32.2 0.0 copy-start.1
  32.2 0.0 copy-start.2
  32.2 3.0 %collective-permute-start.7 = (f32[40,128]{1,0:T(8,128)S(1)}, f32[40,128]{1,0:T(8,128)S(1)}, u32[]{:S(2)}, u32[]{:S(2)}) collective-permute-start(f32[40,128]{1,0:T(8,128)S(1)} %fusion), channel_id=1, source_target_pairs={{0,4},{4,0},{1,5},{5,1},{2,6},{6,2},{3,7},{7,3},{8,12},{12,8},{9,1... | collective-permute-start | bytes 61448 | tf_op jit(solution)/shard_map/ppermute | solution.py:342
  35.2 0.0 collective-permute-done.8.pair_ref
  35.2 0.3 slab_term.1.rest_ref
  35.5 0.5 %collective-permute-done.7.core_ref = f32[40,128]{1,0:T(8,128)S(1)} collective-permute-done((f32[40,128]{1,0:T(8,128)S(1)}, f32[40,128]{1,0:T(8,128)S(1)}, u32[]{:S(2)}, u32[]{:S(2)}) %collective-permute-start.7) | collective-permute-done | bytes 20512 | tf_op jit(solution)/shard_map/ppermute | solution.py:342
  36.1 0.0 copy-done.1
  36.1 0.0 copy-done.2
  36.1 0.6 %finish_rate.1 = (f32[2,16,128]{2,1,0:T(8,128)}, f32[2,16,128]{2,1,0:T(8,128)}) custom-call(f32[2,40,128]{2,1,0:T(8,128)S(1)} %keep_products.1.keep_ref, f32[2,40,128]{2,1,0:T(8,128)S(1)} %collective-permute-done.6.half_ref, f32[40,128]{1,0:T(8,128)S(1)} %collective-permute-done.7.core_ref, f32[2,16,128]{2,1,0:T(8,128)S(1)} %slab_term.1.rest_ref, ...), custom_call_target="tpu_custom_call" | custom-call | flops 65536 | bytes 262144 | tf_op jit(solution)/shard_map/finish_rate/pallas_call | solution.py:354
  (3 shorter events, 0.0 us)
Async XLA Ops:
  1.7 4.7 %collective-permute-start = (f32[40,128]{1,0:T(8,128)S(1)}, f32[40,128]{1,0:T(8,128)S(1)}, u32[]{:S(2)}, u32[]{:S(2)}) collective-permute-start(f32[40,128]{1,0:T(8,128)S(1)} %get-tuple-element.22.block_ref), channel_id=1, source_target_pairs={{0,64},{64,0},{128,192},{192,128},{1,65},{65,1},{129,193},{193,129... | collective-permute-start | bytes 61448 | tf_op jit(solution)/shard_map/ppermute | solution.py:287
  6.4 2.0 %copy-start = (f32[2,16,128]{2,1,0:T(8,128)S(1)}, f32[2,16,128]{2,1,0:T(8,128)}, u32[]{:S(2)}) copy-start(f32[2,16,128]{2,1,0:T(8,128)} %slab_ref.5) | copy-start | bytes 49156
  6.4 6.2 %collective-permute-start.1 = (f32[2,40,128]{2,1,0:T(8,128)S(1)}, f32[2,40,128]{2,1,0:T(8,128)S(1)}, u32[]{:S(2)}, u32[]{:S(2)}) collective-permute-start(f32[2,40,128]{2,1,0:T(8,128)S(1)} %get-tuple-element.26.both_ref), channel_id=1, source_target_pairs={{0,192},{64,128},{128,64},{192,0},{1,193},{65,129},{129,65},{193,1... | collective-permute-start | bytes 122888 | tf_op jit(solution)/shard_map/ppermute | solution.py:287
  8.4 4.1 %collective-permute-start.2 = (f32[2,16,128]{2,1,0:T(8,128)S(1)}, f32[2,16,128]{2,1,0:T(8,128)S(1)}, u32[]{:S(2)}, u32[]{:S(2)}) collective-permute-start(f32[2,16,128]{2,1,0:T(8,128)S(1)} %copy-done), channel_id=1, source_target_pairs={{0,1},{1,0},{2,3},{3,2},{4,5},{5,4},{6,7},{7,6},{8,9},{9,8},{10,11... | collective-permute-start | bytes 49160 | tf_op jit(solution)/shard_map/ppermute | solution.py:287
  12.6 9.2 %collective-permute-start.5 = (f32[4,40,128]{2,1,0:T(8,128)S(1)}, f32[4,40,128]{2,1,0:T(8,128)S(1)}, u32[]{:S(2)}, u32[]{:S(2)}) collective-permute-start(f32[4,40,128]{2,1,0:T(8,128)S(1)} %get-tuple-element.27.all0), channel_id=1, source_target_pairs={{0,32},{16,48},{32,0},{48,16},{1,33},{17,49},{33,1},{49,17},{2,34}... | collective-permute-start | bytes 245768 | tf_op jit(solution)/shard_map/ppermute | solution.py:287
  15.4 6.4 %collective-permute-start.4 = (f32[4,40,128]{2,1,0:T(8,128)S(1)}, f32[4,40,128]{2,1,0:T(8,128)S(1)}, u32[]{:S(2)}, u32[]{:S(2)}) collective-permute-start(f32[4,40,128]{2,1,0:T(8,128)S(1)} %get-tuple-element.27.all0), channel_id=1, source_target_pairs={{0,48},{16,32},{32,16},{48,0},{1,49},{17,33},{33,17},{49,1},{2,50}... | collective-permute-start | bytes 245768 | tf_op jit(solution)/shard_map/ppermute | solution.py:287
  16.3 5.5 %collective-permute-start.3 = (f32[4,40,128]{2,1,0:T(8,128)S(1)}, f32[4,40,128]{2,1,0:T(8,128)S(1)}, u32[]{:S(2)}, u32[]{:S(2)}) collective-permute-start(f32[4,40,128]{2,1,0:T(8,128)S(1)} %get-tuple-element.27.all0), channel_id=1, source_target_pairs={{0,16},{16,0},{32,48},{48,32},{1,17},{17,1},{33,49},{49,33},{2,18}... | collective-permute-start | bytes 245768 | tf_op jit(solution)/shard_map/ppermute | solution.py:287
  16.3 18.9 %collective-permute-start.8 = (f32[2,2,16,128]{3,2,1,0:T(8,128)S(1)}, f32[2,2,16,128]{3,2,1,0:T(8,128)S(1)}, u32[]{:S(2)}, u32[]{:S(2)}) collective-permute-start(f32[2,2,16,128]{3,2,1,0:T(8,128)S(1)} %get-tuple-element.33), channel_id=1, source_target_pairs={{0,2},{1,3},{2,0},{3,1},{4,6},{5,7},{6,4},{7,5},{8,10},{9,11},{10,... | collective-permute-start | bytes 98312 | tf_op jit(solution)/shard_map/ppermute | solution.py:287
  23.2 9.0 %collective-permute-start.6 = (f32[2,40,128]{2,1,0:T(8,128)S(1)}, f32[2,40,128]{2,1,0:T(8,128)S(1)}, u32[]{:S(2)}, u32[]{:S(2)}) collective-permute-start(f32[2,40,128]{2,1,0:T(8,128)S(1)} %get-tuple-element.32), channel_id=1, source_target_pairs={{0,8},{8,0},{1,9},{9,1},{2,10},{10,2},{3,11},{11,3},{4,12},{12,4},... | collective-permute-start | bytes 122888 | tf_op jit(solution)/shard_map/ppermute | solution.py:287
  32.2 3.9 %copy-start.1 = (f32[2,16,128]{2,1,0:T(8,128)S(1)}, f32[2,16,128]{2,1,0:T(8,128)}, u32[]{:S(2)}) copy-start(f32[2,16,128]{2,1,0:T(8,128)} %base_ref.1) | copy-start | bytes 49156
  32.2 3.9 %copy-start.2 = (f32[2,16,128]{2,1,0:T(8,128)S(1)}, f32[2,16,128]{2,1,0:T(8,128)}, u32[]{:S(2)}) copy-start(f32[2,16,128]{2,1,0:T(8,128)} %accum_ref.1) | copy-start | bytes 49156
  32.2 3.9 %collective-permute-start.7 = (f32[40,128]{1,0:T(8,128)S(1)}, f32[40,128]{1,0:T(8,128)S(1)}, u32[]{:S(2)}, u32[]{:S(2)}) collective-permute-start(f32[40,128]{1,0:T(8,128)S(1)} %fusion), channel_id=1, source_target_pairs={{0,4},{4,0},{1,5},{5,1},{2,6},{6,2},{3,7},{7,3},{8,12},{12,8},{9,1... | collective-permute-start | bytes 61448 | tf_op jit(solution)/shard_map/ppermute | solution.py:342

commit v14 on v13

--- a/solution.py
+++ b/solution.py
@@ -88,11 +88,9 @@
     token_ref[...] = block_ref[0:8, :]
 
 
-def line_kernel(both_ref, two_ref, slab_ref, near_ref, after_ref, all_ref, pair_ref, token_ref):
+def line_kernel(both_ref, two_ref, near_ref, after_ref, all_ref, token_ref):
     all_ref[0:2] = both_ref[...]
     all_ref[2:4] = two_ref[...]
-    pair_ref[0] = slab_ref[...]
-    pair_ref[1] = near_ref[...]
     token_ref[...] = both_ref[0, 0:8, :]
 
 
@@ -109,20 +107,22 @@
         for k in range(3):
             row_ref[k, n * LANES : (n + 1) * LANES, :] = turned(pos_ref, k, place * 4 + other)
 
-    def tile(step, carry):
-        at = lanes_at(place_of(step) * 4 + quad)
-        cols = [pos_ref[k : k + 1, at] for k in range(3)]
-        for n in range(0, count, 32):
-            size = min(32, count - n)
-            dx, dy, dz = [row_ref[k, first + n : first + n + size, :] - cols[k] for k in range(3)]
-            for part, value in enumerate(coupling(dx, dy, dz)):
-                high, low = split(value)
-                lanes = lanes_at(step + part * tiles)
-                high_ref[n : n + size, lanes] = high
-                low_ref[n : n + size, lanes] = low
+    together = 4 * LANES // count
+
+    def tile(group, carry):
+        for step in [group * together + n for n in range(together)]:
+            at = lanes_at(place_of(step) * 4 + quad)
+            cols = [pos_ref[k : k + 1, at] for k in range(3)]
+            for n in range(0, count, 32):
+                dx, dy, dz = [row_ref[k, first + n : first + n + 32, :] - cols[k] for k in range(3)]
+                for part, value in enumerate(coupling(dx, dy, dz)):
+                    high, low = split(value)
+                    lanes = lanes_at(step + part * tiles)
+                    high_ref[n : n + 32, lanes] = high
+                    low_ref[n : n + 32, lanes] = low
         return carry
 
-    lax.fori_loop(0, tiles, tile, 0)
+    lax.fori_loop(0, tiles // together, tile, 0)
 
 
 def term_kernel(pos_ref, slab_ref, near_ref, pair_ref, det_ref, rest_ref, row_ref, full_ref):
@@ -140,15 +140,15 @@
         place = own + (n % 2) * (1 - 2 * (own % 2))
         place = place + (n // 2) * (2 - 4 * (own // 2))
         there = pl.ds(pl.multiple_of(place * 16, 16), 16)
-        full_ref[0, there, :] = ref[0]
-        full_ref[1, there, :] = ref[1]
+        full_ref[0, there, :] = ref[0:16]
+        full_ref[1, there, :] = ref[16:32]
 
     def mul(a, b):
         return jnp.dot(a, b, precision=lax.Precision.HIGHEST, preferred_element_type=jnp.float32)
 
     v_real = mul(w_real, full_ref[0]) + mul(w_imag, full_ref[1])
     v_imag = mul(w_real, full_ref[1]) - mul(w_imag, full_ref[0])
-    y_real, y_imag = slab_ref[0], slab_ref[1]
+    y_real, y_imag = slab_ref[0:16], slab_ref[16:32]
     line = det_ref[0:1, :]
     rest_ref[0] = line * y_imag - 0.5 * y_real - v_imag
     rest_ref[1] = v_real - line * y_real - 0.5 * y_imag
@@ -175,8 +175,21 @@
     fill_tiles(pos_ref, row_ref, high_ref, low_ref, (quad,), 0, LANES)
 
 
+def ahead():
+    return (1 - lax.axis_index("zh")) * (lax.axis_index("zl") < 2).astype(jnp.int32)
+
+
+def ahead_kernel(pos_ref, slab_ref, near_ref, token_ref, high_ref, low_ref, pair_ref, row_ref):
+    pair_ref[0] = slab_ref[...]
+    pair_ref[1] = near_ref[...]
+
+    @pl.when(ahead() == 1)
+    def _():
+        fill_tiles(pos_ref, row_ref, high_ref, low_ref, own_quads()[:1], 0, LANES)
+
+
 def early_kernel(pos_ref, token_ref, high_ref, low_ref, row_ref):
-    @pl.when(lax.axis_index("zh") == 0)
+    @pl.when((1 - lax.axis_index("zh")) - ahead() == 1)
     def _():
         fill_tiles(pos_ref, row_ref, high_ref, low_ref, own_quads()[:1], 0, LANES)
 
@@ -216,14 +229,18 @@
     return by_real, by_imag
 
 
-def send_kernel(high0, low0, high1, low1, all0, all1, all2, all3, out_ref, y_ref):
+def send_kernel(high0, low0, high1, low1, high3, low3, all0, all1, all2, all3, out_ref, y_ref, first_ref):
     fill_slab((all0, all1, all2, all3), y_ref)
     y = y_ref[...]
     store_products(*products(high0, low0, y), out_ref, 0)
     store_products(*products(high1, low1, y), out_ref, 1)
 
-
-def keep_kernel(pos_ref, y_ref, high2, low2, out_ref, row_ref, high_ref, low_ref):
+    @pl.when(ahead() == 1)
+    def _():
+        store_products(*products(high3, low3, y), first_ref, 0)
+
+
+def keep_kernel(pos_ref, y_ref, high2, low2, first_ref, out_ref, row_ref, high_ref, low_ref):
     y = y_ref[...]
 
     @pl.when(lax.axis_index("zh") == 0)
@@ -231,8 +248,15 @@
         high, low = high_ref.at[pl.ds(0, LANES)], low_ref.at[pl.ds(0, LANES)]
         fill_tiles(pos_ref, row_ref, high, low, own_quads()[1:], 0, LANES)
         clear_own(high, low, 0)
+        store_products(*products(high, low, y), out_ref, 1)
+
+    @pl.when(ahead() == 1)
+    def _():
+        out_ref[0] = first_ref[0]
+
+    @pl.when((1 - lax.axis_index("zh")) - ahead() == 1)
+    def _():
         store_products(*products(high2, low2, y), out_ref, 0)
-        store_products(*products(high, low, y), out_ref, 1)
 
     @pl.when(lax.axis_index("zh") == 1)
     def _():
@@ -244,8 +268,8 @@
 def finish_kernel(keep_ref, half_ref, core_ref, rest_ref, slab_ref, base_ref, accum_ref, next_ref, acc_ref):
     z = keep_ref[1] + half_ref[1] + core_ref[...]
     shift = z[32:33]
-    rate_real = z[16:32] + shift * slab_ref[1] + rest_ref[0]
-    rate_imag = rest_ref[1] - z[0:16] - shift * slab_ref[0]
+    rate_real = z[16:32] + shift * slab_ref[16:32] + rest_ref[0]
+    rate_imag = rest_ref[1] - z[0:16] - shift * slab_ref[0:16]
     for n, rate in enumerate((rate_real, rate_imag)):
         next_ref[n] = base_ref[n] + (0.5 * TIME_STEP) * rate
         acc_ref[n] = accum_ref[n] + (TIME_STEP / 3.0) * rate
@@ -299,7 +323,7 @@
         [pltpu.SemaphoreType.DMA((6,))],
     )(in_hbm(section), in_hbm(populations.reshape(1, LANES)), in_hbm(positions), in_hbm(detuning.reshape(1, count)))
     one = swap(block, "y", 1)
-    near = swap(section, "zl", 1)
+    near = swap(block, "zl", 1)
     high0, low0 = far_block(0, det)
 
     both, second = call(
@@ -308,26 +332,34 @@
     two = swap(both, "y", 3)
     high1, low1 = far_block(1, second)
 
-    line, pair, third = call(
-        line_kernel,
-        "join_line",
-        (pltpu.VMEM((4, PART, LANES), f32), pltpu.VMEM((2, 2, 16, LANES), f32), token),
-        [vmem] * 4 + [anywhere],
-        1,
-    )(both, two, section, near, high1)
+    line, third = call(
+        line_kernel, "join_line", (pltpu.VMEM((4, PART, LANES), f32), token), [vmem] * 3 + [anywhere], 1
+    )(both, two, near, high1)
     across = [swap(line, "x", mask) for mask in (1, 3, 2)]
+    high3, low3, pair = call(
+        ahead_kernel,
+        "ahead_block",
+        (tile, tile, pltpu.VMEM((2, PART, LANES), f32)),
+        [vmem] * 3 + [anywhere],
+        1 << 24,
+        [rows],
+    )(pos, block, near, third)
     pair = swap(pair, "zl", 2)
     high2, low2 = call(
         early_kernel, "early_block", (tile, tile), [vmem, anywhere], 1 << 24, [rows]
-    )(pos, third)
-
-    sent, y = call(
+    )(pos, high3)
+
+    sent, y, first = call(
         send_kernel,
         "send_products",
-        (pltpu.VMEM((2, PART, LANES), f32), pltpu.VMEM((LANES, deep // 2), bf16)),
-        [vmem] * 8,
+        (
+            pltpu.VMEM((2, PART, LANES), f32),
+            pltpu.VMEM((LANES, deep // 2), bf16),
+            pltpu.VMEM((1, PART, LANES), f32),
+        ),
+        [vmem] * 10,
         1 << 29,
-    )(high0, low0, high1, low1, line, *across)
+    )(high0, low0, high1, low1, high3, low3, line, *across)
     half = swap(sent, "zh", 1)
 
     wide = pltpu.VMEM((2 * LANES, deep), bf16)
@@ -335,10 +367,10 @@
         keep_kernel,
         "keep_products",
         (pltpu.VMEM((2, PART, LANES), f32),),
-        [vmem] * 4,
+        [vmem] * 5,
         1 << 29,
         [pltpu.VMEM((3, 2 * LANES, LANES), f32), wide, wide],
-    )(pos, y, high2, low2)
+    )(pos, y, high2, low2, first)
     core = lax.ppermute(keep[0] + half[0], "c", [(0, 1), (1, 0)])
     rest = pl.pallas_call(
         term_kernel,
@@ -349,7 +381,7 @@
         compiler_params=params(4),
         cost_estimate=pl.CostEstimate(flops=1 << 22, bytes_accessed=1 << 18, transcendentals=1 << 11),
         name="slab_term",
-    )(pos, section, near, pair, det)
+    )(pos, block, near, pair, det)
 
     return pl.pallas_call(
         finish_kernel,
@@ -357,7 +389,7 @@
         compiler_params=params(4),
         cost_estimate=pl.CostEstimate(flops=1 << 16, bytes_accessed=1 << 18, transcendentals=0),
         name="finish_rate",
-    )(keep, half, core, rest, section, base, accum)
+    )(keep, half, core, rest, block, base, accum)
 
 
 def solution(mesh):

time: 36.9 us -> 36.3 us (0.984)
  starting transfers between devices: 20.6 us -> 18.8 us
  waiting for transfers between devices: 0.55 us -> 2.06 us
    pallas_call x1, Pallas kernels: 2.5 us -> 0.01 us  [local(): call(early_kernel, 'early_block', (tile, tile), [vmem, anywhere], 1 << 24...]
    pallas_call x1 -> x2, Pallas kernels: 0.01 us -> 2.39 us  [the longest x1 2.38 us: local(): call(ahead_kernel, 'ahead_block', (tile, tile, pltpu.VMEM((2, PART, LANES...]
    ppermute x8, starting transfers between devices: 17.6 us -> 15.5 us  [swap(): return lax.ppermute(array, axis, [(i, i ^ mask) for i in range(size)])]
    ppermute x8, waiting for transfers between devices: 0.02 us -> 1.54 us  [swap(): return lax.ppermute(array, axis, [(i, i ^ mask) for i in range(size)])]
    pallas_call x1, Pallas kernels: 1.35 us -> 2.07 us  [local(): call(send_kernel, 'send_products', (pltpu.VMEM((2, PART, LANES), f32), pl...]
    pallas_call x1, Pallas kernels: 3.87 us -> 3.28 us  [local(): call(keep_kernel, 'keep_products', (pltpu.VMEM((2, PART, LANES), f32),),...]
  transfers between devices with their start and end apart: 9 -> 9, of which waited for: 1 -> 2; matrix products, arithmetic and copies ran while one was open for 0% -> 0% of each run, Pallas kernels for 36% -> 36%
where the time goes in v14:
time: 36.3 us; the launch traced here: 36.1 us
  starting transfers between devices  18.8 us (52%)
  Pallas kernels  14.5 us (40%)
  waiting for transfers between devices  2.06 us (6%)
  between operations  0.76 us (2%)
    ppermute x8, starting transfers between devices, swap(): return lax.ppermute(array, axis, [(i, i ^ mask) for i in range(size)])  15.5 us
    pallas_call x2, Pallas kernels, far_block(): call(kernel, 'far_block_' + 'ab'[n], (tile, tile), [vmem, anywhere], 1 <<...  4.82 us
    pallas_call x1, Pallas kernels, local(): call(keep_kernel, 'keep_products', (pltpu.VMEM((2, PART, LANES), f32),),...  3.28 us
    ppermute x1, starting transfers between devices, local(): core = lax.ppermute(keep[0] + half[0], 'c', [(0, 1), (1, 0)])  3.28 us
    pallas_call x1, Pallas kernels, local(): call(ahead_kernel, 'ahead_block', (tile, tile, pltpu.VMEM((2, PART, LANES...  2.38 us
    pallas_call x1, Pallas kernels, local(): call(send_kernel, 'send_products', (pltpu.VMEM((2, PART, LANES), f32), pl...  2.07 us
    ppermute x8, waiting for transfers between devices, swap(): return lax.ppermute(array, axis, [(i, i ^ mask) for i in range(size)])  1.54 us
    pallas_call x1, Pallas kernels, local(): call(pack_kernel, 'pack_block', (pltpu.VMEM((PART, LANES), f32), pltpu.VM...  1.01 us
  transfers between devices with their start and end apart: 9, of which 2 were waited for; matrix products, arithmetic and copies ran while one was open for 0% of the time, Pallas kernels for 36%

profile of v14, /device:TPU:1, one launch (start us, length us, event | category | flops | bytes accessed | tf_op | source)
XLA Modules:
  0.0 36.1 jit_solution(6766070162401897611)
XLA Ops:
  0.6 1.0 %pack_block.1 = (f32[40,128]{1,0:T(8,128)S(1)}, f32[3,8192]{1,0:T(4,128)S(1)}, f32[8,128]{1,0:T(8,128)S(1)}) custom-call(f32[2,16,128]{2,1,0:T(8,128)} %section_ref.1, f32[1,128]{1,0:T(1,128)} %bitcast.5, f32[3,8192]{1,0:T(4,128)} %pos_ref.1, f32[1,8192]{1,0:T(1,128)} %bitcast.4), custom_call_target="tpu_custom_call" | custom-call | flops 65536 | bytes 1048576 | tf_op jit(solution)/shard_map/pack_block/pallas_call | solution.py:317
  1.7 2.2 %collective-permute-start = (f32[40,128]{1,0:T(8,128)S(1)}, f32[40,128]{1,0:T(8,128)S(1)}, u32[]{:S(2)}, u32[]{:S(2)}) collective-permute-start(f32[40,128]{1,0:T(8,128)S(1)} %get-tuple-element.25.block_ref.slab_ref), channel_id=1, source_target_pairs={{0,64},{64,0},{128,192},{192,128},{1,65},{65,1},{129,193},{193,129... | collective-permute-start | bytes 61448 | tf_op jit(solution)/shard_map/ppermute | solution.py:311
  3.9 2.4 %far_block_a.1 = (bf16[128,4096]{1,0:T(8,128)(2,1)S(1)}, bf16[128,4096]{1,0:T(8,128)(2,1)S(1)}) custom-call(f32[3,8192]{1,0:T(4,128)S(1)} %get-tuple-element.21.pos_ref, f32[8,128]{1,0:T(8,128)S(1)} %get-tuple-element.22.token_ref.det_ref), custom_call_target="tpu_custom_call" | custom-call | flops 16777216 | bytes 1048576 | tf_op jit(solution)/shard_map/far_block_a/pallas_call | solution.py:315
  6.3 0.0 collective-permute-done.one_ref
  6.3 2.0 %collective-permute-start.2 = (f32[2,40,128]{2,1,0:T(8,128)S(1)}, f32[2,40,128]{2,1,0:T(8,128)S(1)}, u32[]{:S(2)}, u32[]{:S(2)}) collective-permute-start(f32[2,40,128]{2,1,0:T(8,128)S(1)} %get-tuple-element.29.both_ref), channel_id=1, source_target_pairs={{0,192},{64,128},{128,64},{192,0},{1,193},{65,129},{129,65},{193,1... | collective-permute-start | bytes 122888 | tf_op jit(solution)/shard_map/ppermute | solution.py:311
  8.3 1.6 %collective-permute-start.1 = (f32[40,128]{1,0:T(8,128)S(1)}, f32[40,128]{1,0:T(8,128)S(1)}, u32[]{:S(2)}, u32[]{:S(2)}) collective-permute-start(f32[40,128]{1,0:T(8,128)S(1)} %get-tuple-element.25.block_ref.slab_ref), channel_id=1, source_target_pairs={{0,1},{1,0},{2,3},{3,2},{4,5},{5,4},{6,7},{7,6},{8,9},{9,8},{10,11... | collective-permute-start | bytes 61448 | tf_op jit(solution)/shard_map/ppermute | solution.py:311
  9.9 2.4 %far_block_b.1 = (bf16[128,4096]{1,0:T(8,128)(2,1)S(1)}, bf16[128,4096]{1,0:T(8,128)(2,1)S(1)}) custom-call(f32[3,8192]{1,0:T(4,128)S(1)} %get-tuple-element.21.pos_ref, f32[8,128]{1,0:T(8,128)S(1)} %get-tuple-element.26.token_ref), custom_call_target="tpu_custom_call" | custom-call | flops 16777216 | bytes 1048576 | tf_op jit(solution)/shard_map/far_block_b/pallas_call | solution.py:315
  12.4 0.0 collective-permute-done.1.near_ref
  12.4 0.0 collective-permute-done.2.two_ref
  12.4 2.8 %collective-permute-start.5 = (f32[4,40,128]{2,1,0:T(8,128)S(1)}, f32[4,40,128]{2,1,0:T(8,128)S(1)}, u32[]{:S(2)}, u32[]{:S(2)}) collective-permute-start(f32[4,40,128]{2,1,0:T(8,128)S(1)} %get-tuple-element.33.all0), channel_id=1, source_target_pairs={{0,32},{16,48},{32,0},{48,16},{1,33},{17,49},{33,1},{49,17},{2,34}... | collective-permute-start | bytes 245768 | tf_op jit(solution)/shard_map/ppermute | solution.py:311
  15.2 0.9 %collective-permute-start.4 = (f32[4,40,128]{2,1,0:T(8,128)S(1)}, f32[4,40,128]{2,1,0:T(8,128)S(1)}, u32[]{:S(2)}, u32[]{:S(2)}) collective-permute-start(f32[4,40,128]{2,1,0:T(8,128)S(1)} %get-tuple-element.33.all0), channel_id=1, source_target_pairs={{0,48},{16,32},{32,16},{48,0},{1,49},{17,33},{33,17},{49,1},{2,50}... | collective-permute-start | bytes 245768 | tf_op jit(solution)/shard_map/ppermute | solution.py:311
  16.1 0.0 collective-permute-start.3
  16.1 2.4 %ahead_block.1 = (bf16[128,4096]{1,0:T(8,128)(2,1)S(1)}, bf16[128,4096]{1,0:T(8,128)(2,1)S(1)}, f32[2,40,128]{2,1,0:T(8,128)S(1)}) custom-call(f32[3,8192]{1,0:T(4,128)S(1)} %get-tuple-element.21.pos_ref, f32[40,128]{1,0:T(8,128)S(1)} %get-tuple-element.25.block_ref.slab_ref, f32[40,128]{1,0:T(8,128)S(1)} %collective-permute-done.1.near_ref, ...), custom_call_target="tpu_custom_call" | custom-call | flops 16777216 | bytes 1048576 | tf_op jit(solution)/shard_map/ahead_block/pallas_call | solution.py:339
  18.5 0.6 %collective-permute-start.8 = (f32[2,40,128]{2,1,0:T(8,128)S(1)}, f32[2,40,128]{2,1,0:T(8,128)S(1)}, u32[]{:S(2)}, u32[]{:S(2)}) collective-permute-start(f32[2,40,128]{2,1,0:T(8,128)S(1)} %get-tuple-element.39), channel_id=1, source_target_pairs={{0,2},{1,3},{2,0},{3,1},{4,6},{5,7},{6,4},{7,5},{8,10},{9,11},{10,... | collective-permute-start | bytes 122888 | tf_op jit(solution)/shard_map/ppermute | solution.py:311
  19.1 0.0 collective-permute-done.5.all3
  19.1 1.5 %collective-permute-done.4.all2 = f32[4,40,128]{2,1,0:T(8,128)S(1)} collective-permute-done((f32[4,40,128]{2,1,0:T(8,128)S(1)}, f32[4,40,128]{2,1,0:T(8,128)S(1)}, u32[]{:S(2)}, u32[]{:S(2)}) %collective-permute-start.4) | collective-permute-done | bytes 81952 | tf_op jit(solution)/shard_map/ppermute | solution.py:311
  20.6 0.0 collective-permute-done.3.all1
  20.6 2.1 %send_products.1 = (f32[2,40,128]{2,1,0:T(8,128)S(1)}, bf16[128,2048]{1,0:T(8,128)(2,1)S(1)}, f32[1,40,128]{2,1,0:T(8,128)S(1)}) custom-call(bf16[128,4096]{1,0:T(8,128)(2,1)S(1)} %get-tuple-element.23.after_ref.high0, bf16[128,4096]{1,0:T(8,128)(2,1)S(1)} %get-tuple-element.24.low0, bf16[128,4096]{1,0:T(8,128)(2,1)S(1)} %get-tuple-element.27.after_ref.high1, ...), custom_call_target="tpu_custom_call" | custom-call | flops 536870912 | bytes 1048576 | tf_op jit(solution)/shard_map/send_products/pallas_call | solution.py:352
  22.7 5.4 %collective-permute-start.6 = (f32[2,40,128]{2,1,0:T(8,128)S(1)}, f32[2,40,128]{2,1,0:T(8,128)S(1)}, u32[]{:S(2)}, u32[]{:S(2)}) collective-permute-start(f32[2,40,128]{2,1,0:T(8,128)S(1)} %get-tuple-element.38), channel_id=1, source_target_pairs={{0,8},{8,0},{1,9},{9,1},{2,10},{10,2},{3,11},{11,3},{4,12},{12,4},... | collective-permute-start | bytes 122888 | tf_op jit(solution)/shard_map/ppermute | solution.py:311
  28.1 3.3 %keep_products.1.keep_ref = f32[2,40,128]{2,1,0:T(8,128)S(1)} custom-call(f32[3,8192]{1,0:T(4,128)S(1)} %get-tuple-element.21.pos_ref, bf16[128,2048]{1,0:T(8,128)(2,1)S(1)} %get-tuple-element.34.y_ref, bf16[128,4096]{1,0:T(8,128)(2,1)S(1)} %get-tuple-element.35.high2, bf16[128,4096]{1,0:T(8,128)(2,1)S(1)} %get-tuple-element.36.low2, ...), custom_call_target="tpu_custom_call" | custom-call | flops 536870912 | bytes 1048576 | tf_op jit(solution)/shard_map/keep_products/pallas_call | solution.py:366
  31.3 0.0 collective-permute-done.6.half_ref
  31.4 0.0 copy-start
  31.4 0.0 copy-start.1
  31.4 3.3 %collective-permute-start.7 = (f32[40,128]{1,0:T(8,128)S(1)}, f32[40,128]{1,0:T(8,128)S(1)}, u32[]{:S(2)}, u32[]{:S(2)}) collective-permute-start(f32[40,128]{1,0:T(8,128)S(1)} %fusion), channel_id=1, source_target_pairs={{0,4},{4,0},{1,5},{5,1},{2,6},{6,2},{3,7},{7,3},{8,12},{12,8},{9,1... | collective-permute-start | bytes 61448 | tf_op jit(solution)/shard_map/ppermute | solution.py:374
  34.7 0.0 collective-permute-done.8.pair_ref
  34.7 0.3 slab_term.1.rest_ref
  35.0 0.5 %collective-permute-done.7.core_ref = f32[40,128]{1,0:T(8,128)S(1)} collective-permute-done((f32[40,128]{1,0:T(8,128)S(1)}, f32[40,128]{1,0:T(8,128)S(1)}, u32[]{:S(2)}, u32[]{:S(2)}) %collective-permute-start.7) | collective-permute-done | bytes 20512 | tf_op jit(solution)/shard_map/ppermute | solution.py:374
  35.5 0.0 copy-done
  35.5 0.0 copy-done.1
  35.5 0.6 %finish_rate.1 = (f32[2,16,128]{2,1,0:T(8,128)}, f32[2,16,128]{2,1,0:T(8,128)}) custom-call(f32[2,40,128]{2,1,0:T(8,128)S(1)} %keep_products.1.keep_ref, f32[2,40,128]{2,1,0:T(8,128)S(1)} %collective-permute-done.6.half_ref, f32[40,128]{1,0:T(8,128)S(1)} %collective-permute-done.7.core_ref, f32[2,16,128]{2,1,0:T(8,128)S(1)} %slab_term.1.rest_ref, ...), custom_call_target="tpu_custom_call" | custom-call | flops 65536 | bytes 262144 | tf_op jit(solution)/shard_map/finish_rate/pallas_call | solution.py:386
  (4 shorter events, 0.0 us)
Async XLA Ops:
  1.7 4.6 %collective-permute-start = (f32[40,128]{1,0:T(8,128)S(1)}, f32[40,128]{1,0:T(8,128)S(1)}, u32[]{:S(2)}, u32[]{:S(2)}) collective-permute-start(f32[40,128]{1,0:T(8,128)S(1)} %get-tuple-element.25.block_ref.slab_ref), channel_id=1, source_target_pairs={{0,64},{64,0},{128,192},{192,128},{1,65},{65,1},{129,193},{193,129... | collective-permute-start | bytes 61448 | tf_op jit(solution)/shard_map/ppermute | solution.py:311
  6.3 6.1 %collective-permute-start.2 = (f32[2,40,128]{2,1,0:T(8,128)S(1)}, f32[2,40,128]{2,1,0:T(8,128)S(1)}, u32[]{:S(2)}, u32[]{:S(2)}) collective-permute-start(f32[2,40,128]{2,1,0:T(8,128)S(1)} %get-tuple-element.29.both_ref), channel_id=1, source_target_pairs={{0,192},{64,128},{128,64},{192,0},{1,193},{65,129},{129,65},{193,1... | collective-permute-start | bytes 122888 | tf_op jit(solution)/shard_map/ppermute | solution.py:311
  8.3 4.1 %collective-permute-start.1 = (f32[40,128]{1,0:T(8,128)S(1)}, f32[40,128]{1,0:T(8,128)S(1)}, u32[]{:S(2)}, u32[]{:S(2)}) collective-permute-start(f32[40,128]{1,0:T(8,128)S(1)} %get-tuple-element.25.block_ref.slab_ref), channel_id=1, source_target_pairs={{0,1},{1,0},{2,3},{3,2},{4,5},{5,4},{6,7},{7,6},{8,9},{9,8},{10,11... | collective-permute-start | bytes 61448 | tf_op jit(solution)/shard_map/ppermute | solution.py:311
  12.4 6.7 %collective-permute-start.5 = (f32[4,40,128]{2,1,0:T(8,128)S(1)}, f32[4,40,128]{2,1,0:T(8,128)S(1)}, u32[]{:S(2)}, u32[]{:S(2)}) collective-permute-start(f32[4,40,128]{2,1,0:T(8,128)S(1)} %get-tuple-element.33.all0), channel_id=1, source_target_pairs={{0,32},{16,48},{32,0},{48,16},{1,33},{17,49},{33,1},{49,17},{2,34}... | collective-permute-start | bytes 245768 | tf_op jit(solution)/shard_map/ppermute | solution.py:311
  15.2 5.4 %collective-permute-start.4 = (f32[4,40,128]{2,1,0:T(8,128)S(1)}, f32[4,40,128]{2,1,0:T(8,128)S(1)}, u32[]{:S(2)}, u32[]{:S(2)}) collective-permute-start(f32[4,40,128]{2,1,0:T(8,128)S(1)} %get-tuple-element.33.all0), channel_id=1, source_target_pairs={{0,48},{16,32},{32,16},{48,0},{1,49},{17,33},{33,17},{49,1},{2,50}... | collective-permute-start | bytes 245768 | tf_op jit(solution)/shard_map/ppermute | solution.py:311
  16.1 4.5 %collective-permute-start.3 = (f32[4,40,128]{2,1,0:T(8,128)S(1)}, f32[4,40,128]{2,1,0:T(8,128)S(1)}, u32[]{:S(2)}, u32[]{:S(2)}) collective-permute-start(f32[4,40,128]{2,1,0:T(8,128)S(1)} %get-tuple-element.33.all0), channel_id=1, source_target_pairs={{0,16},{16,0},{32,48},{48,32},{1,17},{17,1},{33,49},{49,33},{2,18}... | collective-permute-start | bytes 245768 | tf_op jit(solution)/shard_map/ppermute | solution.py:311
  18.5 16.2 %collective-permute-start.8 = (f32[2,40,128]{2,1,0:T(8,128)S(1)}, f32[2,40,128]{2,1,0:T(8,128)S(1)}, u32[]{:S(2)}, u32[]{:S(2)}) collective-permute-start(f32[2,40,128]{2,1,0:T(8,128)S(1)} %get-tuple-element.39), channel_id=1, source_target_pairs={{0,2},{1,3},{2,0},{3,1},{4,6},{5,7},{6,4},{7,5},{8,10},{9,11},{10,... | collective-permute-start | bytes 122888 | tf_op jit(solution)/shard_map/ppermute | solution.py:311
  22.7 8.7 %collective-permute-start.6 = (f32[2,40,128]{2,1,0:T(8,128)S(1)}, f32[2,40,128]{2,1,0:T(8,128)S(1)}, u32[]{:S(2)}, u32[]{:S(2)}) collective-permute-start(f32[2,40,128]{2,1,0:T(8,128)S(1)} %get-tuple-element.38), channel_id=1, source_target_pairs={{0,8},{8,0},{1,9},{9,1},{2,10},{10,2},{3,11},{11,3},{4,12},{12,4},... | collective-permute-start | bytes 122888 | tf_op jit(solution)/shard_map/ppermute | solution.py:311
  31.4 4.1 %copy-start = (f32[2,16,128]{2,1,0:T(8,128)S(1)}, f32[2,16,128]{2,1,0:T(8,128)}, u32[]{:S(2)}) copy-start(f32[2,16,128]{2,1,0:T(8,128)} %base_ref.1) | copy-start | bytes 49156
  31.4 4.1 %copy-start.1 = (f32[2,16,128]{2,1,0:T(8,128)S(1)}, f32[2,16,128]{2,1,0:T(8,128)}, u32[]{:S(2)}) copy-start(f32[2,16,128]{2,1,0:T(8,128)} %accum_ref.1) | copy-start | bytes 49156
  31.4 4.1 %collective-permute-start.7 = (f32[40,128]{1,0:T(8,128)S(1)}, f32[40,128]{1,0:T(8,128)S(1)}, u32[]{:S(2)}, u32[]{:S(2)}) collective-permute-start(f32[40,128]{1,0:T(8,128)S(1)} %fusion), channel_id=1, source_target_pairs={{0,4},{4,0},{1,5},{5,1},{2,6},{6,2},{3,7},{7,3},{8,12},{12,8},{9,1... | collective-permute-start | bytes 61448 | tf_op jit(solution)/shard_map/ppermute | solution.py:374

commit v15 on v14

--- a/solution.py
+++ b/solution.py
@@ -99,10 +99,9 @@
     return jnp.broadcast_to(line, (LANES, LANES)).T
 
 
-def fill_tiles(pos_ref, row_ref, high_ref, low_ref, quads, first, count):
+def fill_tiles(pos_ref, row_ref, high_ref, low_ref, quads, first, count, begin=0, end=16):
     quad = lax.axis_index("zh") * 2 + lax.axis_index("c")
     place = own_place()
-    tiles = pos_ref.shape[1] // (4 * LANES)
     for n, other in enumerate(quads):
         for k in range(3):
             row_ref[k, n * LANES : (n + 1) * LANES, :] = turned(pos_ref, k, place * 4 + other)
@@ -117,12 +116,12 @@
                 dx, dy, dz = [row_ref[k, first + n : first + n + 32, :] - cols[k] for k in range(3)]
                 for part, value in enumerate(coupling(dx, dy, dz)):
                     high, low = split(value)
-                    lanes = lanes_at(step + part * tiles)
+                    lanes = lanes_at(step - begin + part * (end - begin))
                     high_ref[n : n + 32, lanes] = high
                     low_ref[n : n + 32, lanes] = low
         return carry
 
-    lax.fori_loop(0, tiles // together, tile, 0)
+    lax.fori_loop(begin // together, end // together, tile, 0)
 
 
 def term_kernel(pos_ref, slab_ref, near_ref, pair_ref, det_ref, rest_ref, row_ref, full_ref):
@@ -229,7 +228,7 @@
     return by_real, by_imag
 
 
-def send_kernel(high0, low0, high1, low1, high3, low3, all0, all1, all2, all3, out_ref, y_ref, first_ref):
+def send_kernel(high0, low0, high1, low1, high3, low3, pos_ref, all0, all1, all2, all3, out_ref, y_ref, first_ref, row_ref, part_high, part_low):
     fill_slab((all0, all1, all2, all3), y_ref)
     y = y_ref[...]
     store_products(*products(high0, low0, y), out_ref, 0)
@@ -237,25 +236,30 @@
 
     @pl.when(ahead() == 1)
     def _():
+        fill_tiles(pos_ref, row_ref, part_high, part_low, own_quads()[1:], 0, LANES, 0, 4)
+        clear_own(part_high, part_low, 0)
         store_products(*products(high3, low3, y), first_ref, 0)
+        store_products(*products(part_high, part_low, y[:, 0 : 4 * LANES]), first_ref, 1)
 
 
 def keep_kernel(pos_ref, y_ref, high2, low2, first_ref, out_ref, row_ref, high_ref, low_ref):
     y = y_ref[...]
-
-    @pl.when(lax.axis_index("zh") == 0)
-    def _():
-        high, low = high_ref.at[pl.ds(0, LANES)], low_ref.at[pl.ds(0, LANES)]
+    rows = pl.ds(0, LANES)
+
+    @pl.when(ahead() == 1)
+    def _():
+        high, low = high_ref.at[rows, pl.ds(0, 24 * LANES)], low_ref.at[rows, pl.ds(0, 24 * LANES)]
+        fill_tiles(pos_ref, row_ref, high, low, own_quads()[1:], 0, LANES, 4, 16)
+        store_products(*products(high, low, y[:, 4 * LANES :]), out_ref, 1)
+        out_ref[0] = first_ref[0]
+        out_ref[1] += first_ref[1]
+
+    @pl.when((1 - lax.axis_index("zh")) - ahead() == 1)
+    def _():
+        high, low = high_ref.at[rows], low_ref.at[rows]
         fill_tiles(pos_ref, row_ref, high, low, own_quads()[1:], 0, LANES)
         clear_own(high, low, 0)
         store_products(*products(high, low, y), out_ref, 1)
-
-    @pl.when(ahead() == 1)
-    def _():
-        out_ref[0] = first_ref[0]
-
-    @pl.when((1 - lax.axis_index("zh")) - ahead() == 1)
-    def _():
         store_products(*products(high2, low2, y), out_ref, 0)
 
     @pl.when(lax.axis_index("zh") == 1)
@@ -355,11 +359,12 @@
         (
             pltpu.VMEM((2, PART, LANES), f32),
             pltpu.VMEM((LANES, deep // 2), bf16),
-            pltpu.VMEM((1, PART, LANES), f32),
+            pltpu.VMEM((2, PART, LANES), f32),
         ),
-        [vmem] * 10,
+        [vmem] * 11,
         1 << 29,
-    )(high0, low0, high1, low1, high3, low3, line, *across)
+        [rows, pltpu.VMEM((LANES, 8 * LANES), bf16), pltpu.VMEM((LANES, 8 * LANES), bf16)],
+    )(high0, low0, high1, low1, high3, low3, pos, line, *across)
     half = swap(sent, "zh", 1)
 
     wide = pltpu.VMEM((2 * LANES, deep), bf16)

time: 36.3 us -> 35.8 us (0.986)
  starting transfers between devices: 18.8 us -> 18.3 us
    pallas_call x1, Pallas kernels: 3.28 us -> 2.46 us  [local(): call(keep_kernel, 'keep_products', (pltpu.VMEM((2, PART, LANES), f32),),...]
    ppermute x8, starting transfers between devices: 15.5 us -> 14.8 us  [swap(): return lax.ppermute(array, axis, [(i, i ^ mask) for i in range(size)])]
    pallas_call x1, Pallas kernels: 2.07 us -> 2.76 us  [local(): call(send_kernel, 'send_products', (pltpu.VMEM((2, PART, LANES), f32), pl...]
where the time goes in v15:
time: 35.8 us; the launch traced here: 35.6 us
  starting transfers between devices  18.3 us (51%)
  Pallas kernels  14.5 us (41%)
  waiting for transfers between devices  2.06 us (6%)
  between operations  0.76 us (2%)
    ppermute x8, starting transfers between devices, swap(): return lax.ppermute(array, axis, [(i, i ^ mask) for i in range(size)])  14.8 us
    pallas_call x2, Pallas kernels, far_block(): call(kernel, 'far_block_' + 'ab'[n], (tile, tile), [vmem, anywhere], 1 <<...  4.87 us
    ppermute x1, starting transfers between devices, local(): core = lax.ppermute(keep[0] + half[0], 'c', [(0, 1), (1, 0)])  3.54 us
    pallas_call x1, Pallas kernels, local(): call(send_kernel, 'send_products', (pltpu.VMEM((2, PART, LANES), f32), pl...  2.76 us
    pallas_call x1, Pallas kernels, local(): call(keep_kernel, 'keep_products', (pltpu.VMEM((2, PART, LANES), f32),),...  2.46 us
    pallas_call x1, Pallas kernels, local(): call(ahead_kernel, 'ahead_block', (tile, tile, pltpu.VMEM((2, PART, LANES...  2.44 us
    ppermute x8, waiting for transfers between devices, swap(): return lax.ppermute(array, axis, [(i, i ^ mask) for i in range(size)])  1.54 us
    pallas_call x1, Pallas kernels, local(): call(pack_kernel, 'pack_block', (pltpu.VMEM((PART, LANES), f32), pltpu.VM...  1.01 us
  transfers between devices with their start and end apart: 9, of which 2 were waited for; matrix products, arithmetic and copies ran while one was open for 0% of the time, Pallas kernels for 36%

profile of v15, /device:TPU:1, one launch (start us, length us, event | category | flops | bytes accessed | tf_op | source)
XLA Modules:
  0.0 35.6 jit_solution(14014481336711968731)
XLA Ops:
  0.6 1.0 %pack_block.1 = (f32[40,128]{1,0:T(8,128)S(1)}, f32[3,8192]{1,0:T(4,128)S(1)}, f32[8,128]{1,0:T(8,128)S(1)}) custom-call(f32[2,16,128]{2,1,0:T(8,128)} %section_ref.1, f32[1,128]{1,0:T(1,128)} %bitcast.5, f32[3,8192]{1,0:T(4,128)} %pos_ref.1, f32[1,8192]{1,0:T(1,128)} %bitcast.4), custom_call_target="tpu_custom_call" | custom-call | flops 65536 | bytes 1048576 | tf_op jit(solution)/shard_map/pack_block/pallas_call | solution.py:321
  1.7 2.2 %collective-permute-start = (f32[40,128]{1,0:T(8,128)S(1)}, f32[40,128]{1,0:T(8,128)S(1)}, u32[]{:S(2)}, u32[]{:S(2)}) collective-permute-start(f32[40,128]{1,0:T(8,128)S(1)} %get-tuple-element.25.block_ref.slab_ref), channel_id=1, source_target_pairs={{0,64},{64,0},{128,192},{192,128},{1,65},{65,1},{129,193},{193,129... | collective-permute-start | bytes 61448 | tf_op jit(solution)/shard_map/ppermute | solution.py:315
  3.9 2.4 %far_block_a.1 = (bf16[128,4096]{1,0:T(8,128)(2,1)S(1)}, bf16[128,4096]{1,0:T(8,128)(2,1)S(1)}) custom-call(f32[3,8192]{1,0:T(4,128)S(1)} %get-tuple-element.21.pos_ref, f32[8,128]{1,0:T(8,128)S(1)} %get-tuple-element.22.token_ref.det_ref), custom_call_target="tpu_custom_call" | custom-call | flops 16777216 | bytes 1048576 | tf_op jit(solution)/shard_map/far_block_a/pallas_call | solution.py:319
  6.3 0.0 collective-permute-done.one_ref
  6.3 2.0 %collective-permute-start.2 = (f32[2,40,128]{2,1,0:T(8,128)S(1)}, f32[2,40,128]{2,1,0:T(8,128)S(1)}, u32[]{:S(2)}, u32[]{:S(2)}) collective-permute-start(f32[2,40,128]{2,1,0:T(8,128)S(1)} %get-tuple-element.29.both_ref), channel_id=1, source_target_pairs={{0,192},{64,128},{128,64},{192,0},{1,193},{65,129},{129,65},{193,1... | collective-permute-start | bytes 122888 | tf_op jit(solution)/shard_map/ppermute | solution.py:315
  8.3 1.6 %collective-permute-start.1 = (f32[40,128]{1,0:T(8,128)S(1)}, f32[40,128]{1,0:T(8,128)S(1)}, u32[]{:S(2)}, u32[]{:S(2)}) collective-permute-start(f32[40,128]{1,0:T(8,128)S(1)} %get-tuple-element.25.block_ref.slab_ref), channel_id=1, source_target_pairs={{0,1},{1,0},{2,3},{3,2},{4,5},{5,4},{6,7},{7,6},{8,9},{9,8},{10,11... | collective-permute-start | bytes 61448 | tf_op jit(solution)/shard_map/ppermute | solution.py:315
  10.0 2.4 %far_block_b.1 = (bf16[128,4096]{1,0:T(8,128)(2,1)S(1)}, bf16[128,4096]{1,0:T(8,128)(2,1)S(1)}) custom-call(f32[3,8192]{1,0:T(4,128)S(1)} %get-tuple-element.21.pos_ref, f32[8,128]{1,0:T(8,128)S(1)} %get-tuple-element.26.token_ref), custom_call_target="tpu_custom_call" | custom-call | flops 16777216 | bytes 1048576 | tf_op jit(solution)/shard_map/far_block_b/pallas_call | solution.py:319
  12.4 0.0 collective-permute-done.1.near_ref
  12.4 0.0 collective-permute-done.2.two_ref
  12.4 2.8 %collective-permute-start.5 = (f32[4,40,128]{2,1,0:T(8,128)S(1)}, f32[4,40,128]{2,1,0:T(8,128)S(1)}, u32[]{:S(2)}, u32[]{:S(2)}) collective-permute-start(f32[4,40,128]{2,1,0:T(8,128)S(1)} %get-tuple-element.33.all0), channel_id=1, source_target_pairs={{0,32},{16,48},{32,0},{48,16},{1,33},{17,49},{33,1},{49,17},{2,34}... | collective-permute-start | bytes 245768 | tf_op jit(solution)/shard_map/ppermute | solution.py:315
  15.3 0.9 %collective-permute-start.4 = (f32[4,40,128]{2,1,0:T(8,128)S(1)}, f32[4,40,128]{2,1,0:T(8,128)S(1)}, u32[]{:S(2)}, u32[]{:S(2)}) collective-permute-start(f32[4,40,128]{2,1,0:T(8,128)S(1)} %get-tuple-element.33.all0), channel_id=1, source_target_pairs={{0,48},{16,32},{32,16},{48,0},{1,49},{17,33},{33,17},{49,1},{2,50}... | collective-permute-start | bytes 245768 | tf_op jit(solution)/shard_map/ppermute | solution.py:315
  16.1 0.0 collective-permute-start.3
  16.1 2.4 %ahead_block.1 = (bf16[128,4096]{1,0:T(8,128)(2,1)S(1)}, bf16[128,4096]{1,0:T(8,128)(2,1)S(1)}, f32[2,40,128]{2,1,0:T(8,128)S(1)}) custom-call(f32[3,8192]{1,0:T(4,128)S(1)} %get-tuple-element.21.pos_ref, f32[40,128]{1,0:T(8,128)S(1)} %get-tuple-element.25.block_ref.slab_ref, f32[40,128]{1,0:T(8,128)S(1)} %collective-permute-done.1.near_ref, ...), custom_call_target="tpu_custom_call" | custom-call | flops 16777216 | bytes 1048576 | tf_op jit(solution)/shard_map/ahead_block/pallas_call | solution.py:343
  18.6 0.5 %collective-permute-start.8 = (f32[2,40,128]{2,1,0:T(8,128)S(1)}, f32[2,40,128]{2,1,0:T(8,128)S(1)}, u32[]{:S(2)}, u32[]{:S(2)}) collective-permute-start(f32[2,40,128]{2,1,0:T(8,128)S(1)} %get-tuple-element.39), channel_id=1, source_target_pairs={{0,2},{1,3},{2,0},{3,1},{4,6},{5,7},{6,4},{7,5},{8,10},{9,11},{10,... | collective-permute-start | bytes 122888 | tf_op jit(solution)/shard_map/ppermute | solution.py:315
  19.1 0.0 collective-permute-done.5.all3
  19.1 1.5 %collective-permute-done.4.all2 = f32[4,40,128]{2,1,0:T(8,128)S(1)} collective-permute-done((f32[4,40,128]{2,1,0:T(8,128)S(1)}, f32[4,40,128]{2,1,0:T(8,128)S(1)}, u32[]{:S(2)}, u32[]{:S(2)}) %collective-permute-start.4) | collective-permute-done | bytes 81952 | tf_op jit(solution)/shard_map/ppermute | solution.py:315
  20.7 0.0 collective-permute-done.3.all1
  20.7 2.8 %send_products.1 = (f32[2,40,128]{2,1,0:T(8,128)S(1)}, bf16[128,2048]{1,0:T(8,128)(2,1)S(1)}, f32[2,40,128]{2,1,0:T(8,128)S(1)}) custom-call(bf16[128,4096]{1,0:T(8,128)(2,1)S(1)} %get-tuple-element.23.after_ref.high0, bf16[128,4096]{1,0:T(8,128)(2,1)S(1)} %get-tuple-element.24.low0, bf16[128,4096]{1,0:T(8,128)(2,1)S(1)} %get-tuple-element.27.after_ref.high1, ...), custom_call_target="tpu_custom_call" | custom-call | flops 536870912 | bytes 1048576 | tf_op jit(solution)/shard_map/send_products/pallas_call | solution.py:356
  23.4 4.7 %collective-permute-start.6 = (f32[2,40,128]{2,1,0:T(8,128)S(1)}, f32[2,40,128]{2,1,0:T(8,128)S(1)}, u32[]{:S(2)}, u32[]{:S(2)}) collective-permute-start(f32[2,40,128]{2,1,0:T(8,128)S(1)} %get-tuple-element.38), channel_id=1, source_target_pairs={{0,8},{8,0},{1,9},{9,1},{2,10},{10,2},{3,11},{11,3},{4,12},{12,4},... | collective-permute-start | bytes 122888 | tf_op jit(solution)/shard_map/ppermute | solution.py:315
  28.1 2.5 %keep_products.1.keep_ref = f32[2,40,128]{2,1,0:T(8,128)S(1)} custom-call(f32[3,8192]{1,0:T(4,128)S(1)} %get-tuple-element.21.pos_ref, bf16[128,2048]{1,0:T(8,128)(2,1)S(1)} %get-tuple-element.34.y_ref, bf16[128,4096]{1,0:T(8,128)(2,1)S(1)} %get-tuple-element.35.high2, bf16[128,4096]{1,0:T(8,128)(2,1)S(1)} %get-tuple-element.36.low2, ...), custom_call_target="tpu_custom_call" | custom-call | flops 536870912 | bytes 1048576 | tf_op jit(solution)/shard_map/keep_products/pallas_call | solution.py:371
  30.6 0.0 collective-permute-done.6.half_ref
  30.6 0.0 copy-start
  30.6 0.0 copy-start.1
  30.6 3.5 %collective-permute-start.7 = (f32[40,128]{1,0:T(8,128)S(1)}, f32[40,128]{1,0:T(8,128)S(1)}, u32[]{:S(2)}, u32[]{:S(2)}) collective-permute-start(f32[40,128]{1,0:T(8,128)S(1)} %fusion), channel_id=1, source_target_pairs={{0,4},{4,0},{1,5},{5,1},{2,6},{6,2},{3,7},{7,3},{8,12},{12,8},{9,1... | collective-permute-start | bytes 61448 | tf_op jit(solution)/shard_map/ppermute | solution.py:379
  34.2 0.0 collective-permute-done.8.pair_ref
  34.2 0.3 slab_term.1.rest_ref
  34.5 0.5 %collective-permute-done.7.core_ref = f32[40,128]{1,0:T(8,128)S(1)} collective-permute-done((f32[40,128]{1,0:T(8,128)S(1)}, f32[40,128]{1,0:T(8,128)S(1)}, u32[]{:S(2)}, u32[]{:S(2)}) %collective-permute-start.7) | collective-permute-done | bytes 20512 | tf_op jit(solution)/shard_map/ppermute | solution.py:379
  35.0 0.0 copy-done
  35.0 0.0 copy-done.1
  35.0 0.6 %finish_rate.1 = (f32[2,16,128]{2,1,0:T(8,128)}, f32[2,16,128]{2,1,0:T(8,128)}) custom-call(f32[2,40,128]{2,1,0:T(8,128)S(1)} %keep_products.1.keep_ref, f32[2,40,128]{2,1,0:T(8,128)S(1)} %collective-permute-done.6.half_ref, f32[40,128]{1,0:T(8,128)S(1)} %collective-permute-done.7.core_ref, f32[2,16,128]{2,1,0:T(8,128)S(1)} %slab_term.1.rest_ref, ...), custom_call_target="tpu_custom_call" | custom-call | flops 65536 | bytes 262144 | tf_op jit(solution)/shard_map/finish_rate/pallas_call | solution.py:391
  (4 shorter events, 0.0 us)
Async XLA Ops:
  1.7 4.7 %collective-permute-start = (f32[40,128]{1,0:T(8,128)S(1)}, f32[40,128]{1,0:T(8,128)S(1)}, u32[]{:S(2)}, u32[]{:S(2)}) collective-permute-start(f32[40,128]{1,0:T(8,128)S(1)} %get-tuple-element.25.block_ref.slab_ref), channel_id=1, source_target_pairs={{0,64},{64,0},{128,192},{192,128},{1,65},{65,1},{129,193},{193,129... | collective-permute-start | bytes 61448 | tf_op jit(solution)/shard_map/ppermute | solution.py:315
  6.3 6.1 %collective-permute-start.2 = (f32[2,40,128]{2,1,0:T(8,128)S(1)}, f32[2,40,128]{2,1,0:T(8,128)S(1)}, u32[]{:S(2)}, u32[]{:S(2)}) collective-permute-start(f32[2,40,128]{2,1,0:T(8,128)S(1)} %get-tuple-element.29.both_ref), channel_id=1, source_target_pairs={{0,192},{64,128},{128,64},{192,0},{1,193},{65,129},{129,65},{193,1... | collective-permute-start | bytes 122888 | tf_op jit(solution)/shard_map/ppermute | solution.py:315
  8.3 4.1 %collective-permute-start.1 = (f32[40,128]{1,0:T(8,128)S(1)}, f32[40,128]{1,0:T(8,128)S(1)}, u32[]{:S(2)}, u32[]{:S(2)}) collective-permute-start(f32[40,128]{1,0:T(8,128)S(1)} %get-tuple-element.25.block_ref.slab_ref), channel_id=1, source_target_pairs={{0,1},{1,0},{2,3},{3,2},{4,5},{5,4},{6,7},{7,6},{8,9},{9,8},{10,11... | collective-permute-start | bytes 61448 | tf_op jit(solution)/shard_map/ppermute | solution.py:315
  12.4 6.7 %collective-permute-start.5 = (f32[4,40,128]{2,1,0:T(8,128)S(1)}, f32[4,40,128]{2,1,0:T(8,128)S(1)}, u32[]{:S(2)}, u32[]{:S(2)}) collective-permute-start(f32[4,40,128]{2,1,0:T(8,128)S(1)} %get-tuple-element.33.all0), channel_id=1, source_target_pairs={{0,32},{16,48},{32,0},{48,16},{1,33},{17,49},{33,1},{49,17},{2,34}... | collective-permute-start | bytes 245768 | tf_op jit(solution)/shard_map/ppermute | solution.py:315
  15.3 5.4 %collective-permute-start.4 = (f32[4,40,128]{2,1,0:T(8,128)S(1)}, f32[4,40,128]{2,1,0:T(8,128)S(1)}, u32[]{:S(2)}, u32[]{:S(2)}) collective-permute-start(f32[4,40,128]{2,1,0:T(8,128)S(1)} %get-tuple-element.33.all0), channel_id=1, source_target_pairs={{0,48},{16,32},{32,16},{48,0},{1,49},{17,33},{33,17},{49,1},{2,50}... | collective-permute-start | bytes 245768 | tf_op jit(solution)/shard_map/ppermute | solution.py:315
  16.1 4.5 %collective-permute-start.3 = (f32[4,40,128]{2,1,0:T(8,128)S(1)}, f32[4,40,128]{2,1,0:T(8,128)S(1)}, u32[]{:S(2)}, u32[]{:S(2)}) collective-permute-start(f32[4,40,128]{2,1,0:T(8,128)S(1)} %get-tuple-element.33.all0), channel_id=1, source_target_pairs={{0,16},{16,0},{32,48},{48,32},{1,17},{17,1},{33,49},{49,33},{2,18}... | collective-permute-start | bytes 245768 | tf_op jit(solution)/shard_map/ppermute | solution.py:315
  18.6 15.6 %collective-permute-start.8 = (f32[2,40,128]{2,1,0:T(8,128)S(1)}, f32[2,40,128]{2,1,0:T(8,128)S(1)}, u32[]{:S(2)}, u32[]{:S(2)}) collective-permute-start(f32[2,40,128]{2,1,0:T(8,128)S(1)} %get-tuple-element.39), channel_id=1, source_target_pairs={{0,2},{1,3},{2,0},{3,1},{4,6},{5,7},{6,4},{7,5},{8,10},{9,11},{10,... | collective-permute-start | bytes 122888 | tf_op jit(solution)/shard_map/ppermute | solution.py:315
  23.4 7.2 %collective-permute-start.6 = (f32[2,40,128]{2,1,0:T(8,128)S(1)}, f32[2,40,128]{2,1,0:T(8,128)S(1)}, u32[]{:S(2)}, u32[]{:S(2)}) collective-permute-start(f32[2,40,128]{2,1,0:T(8,128)S(1)} %get-tuple-element.38), channel_id=1, source_target_pairs={{0,8},{8,0},{1,9},{9,1},{2,10},{10,2},{3,11},{11,3},{4,12},{12,4},... | collective-permute-start | bytes 122888 | tf_op jit(solution)/shard_map/ppermute | solution.py:315
  30.6 4.4 %copy-start = (f32[2,16,128]{2,1,0:T(8,128)S(1)}, f32[2,16,128]{2,1,0:T(8,128)}, u32[]{:S(2)}) copy-start(f32[2,16,128]{2,1,0:T(8,128)} %base_ref.1) | copy-start | bytes 49156
  30.6 4.4 %copy-start.1 = (f32[2,16,128]{2,1,0:T(8,128)S(1)}, f32[2,16,128]{2,1,0:T(8,128)}, u32[]{:S(2)}) copy-start(f32[2,16,128]{2,1,0:T(8,128)} %accum_ref.1) | copy-start | bytes 49156
  30.6 4.4 %collective-permute-start.7 = (f32[40,128]{1,0:T(8,128)S(1)}, f32[40,128]{1,0:T(8,128)S(1)}, u32[]{:S(2)}, u32[]{:S(2)}) collective-permute-start(f32[40,128]{1,0:T(8,128)S(1)} %fusion), channel_id=1, source_target_pairs={{0,4},{4,0},{1,5},{5,1},{2,6},{6,2},{3,7},{7,3},{8,12},{12,8},{9,1... | collective-permute-start | bytes 61448 | tf_op jit(solution)/shard_map/ppermute | solution.py:379

commit v16 on v15

--- a/solution.py
+++ b/solution.py
@@ -190,7 +190,7 @@
 def early_kernel(pos_ref, token_ref, high_ref, low_ref, row_ref):
     @pl.when((1 - lax.axis_index("zh")) - ahead() == 1)
     def _():
-        fill_tiles(pos_ref, row_ref, high_ref, low_ref, own_quads()[:1], 0, LANES)
+        fill_tiles(pos_ref, row_ref, high_ref, low_ref, own_quads()[:1], 0, LANES, 0, 12)
 
 
 def fill_slab(refs, y_ref):
@@ -228,7 +228,7 @@
     return by_real, by_imag
 
 
-def send_kernel(high0, low0, high1, low1, high3, low3, pos_ref, all0, all1, all2, all3, out_ref, y_ref, first_ref, row_ref, part_high, part_low):
+def send_kernel(high0, low0, high1, low1, pos_ref, all0, all1, all2, all3, out_ref, y_ref, first_ref, row_ref, part_high, part_low):
     fill_slab((all0, all1, all2, all3), y_ref)
     y = y_ref[...]
     store_products(*products(high0, low0, y), out_ref, 0)
@@ -238,11 +238,10 @@
     def _():
         fill_tiles(pos_ref, row_ref, part_high, part_low, own_quads()[1:], 0, LANES, 0, 4)
         clear_own(part_high, part_low, 0)
-        store_products(*products(high3, low3, y), first_ref, 0)
-        store_products(*products(part_high, part_low, y[:, 0 : 4 * LANES]), first_ref, 1)
-
-
-def keep_kernel(pos_ref, y_ref, high2, low2, first_ref, out_ref, row_ref, high_ref, low_ref):
+        store_products(*products(part_high, part_low, y[:, 0 : 4 * LANES]), first_ref, 0)
+
+
+def keep_kernel(pos_ref, y_ref, high2, low2, high3, low3, first_ref, out_ref, row_ref, high_ref, low_ref):
     y = y_ref[...]
     rows = pl.ds(0, LANES)
 
@@ -251,8 +250,8 @@
         high, low = high_ref.at[rows, pl.ds(0, 24 * LANES)], low_ref.at[rows, pl.ds(0, 24 * LANES)]
         fill_tiles(pos_ref, row_ref, high, low, own_quads()[1:], 0, LANES, 4, 16)
         store_products(*products(high, low, y[:, 4 * LANES :]), out_ref, 1)
-        out_ref[0] = first_ref[0]
-        out_ref[1] += first_ref[1]
+        store_products(*products(high3, low3, y), out_ref, 0)
+        out_ref[1] += first_ref[0]
 
     @pl.when((1 - lax.axis_index("zh")) - ahead() == 1)
     def _():
@@ -260,7 +259,12 @@
         fill_tiles(pos_ref, row_ref, high, low, own_quads()[1:], 0, LANES)
         clear_own(high, low, 0)
         store_products(*products(high, low, y), out_ref, 1)
-        store_products(*products(high2, low2, y), out_ref, 0)
+        late_high = high_ref.at[pl.ds(LANES, LANES), pl.ds(0, 8 * LANES)]
+        late_low = low_ref.at[pl.ds(LANES, LANES), pl.ds(0, 8 * LANES)]
+        fill_tiles(pos_ref, row_ref, late_high, late_low, own_quads()[:1], 0, LANES, 12, 16)
+        most = products(high2, low2, y[:, 0 : 12 * LANES])
+        more = products(late_high, late_low, y[:, 12 * LANES :])
+        store_products(most[0] + more[0], most[1] + more[1], out_ref, 0)
 
     @pl.when(lax.axis_index("zh") == 1)
     def _():
@@ -305,7 +309,7 @@
             in_specs=in_specs,
             out_specs=[vmem] * len(out_shape),
             scratch_shapes=scratch,
-            compiler_params=params(6),
+            compiler_params=params(12),
             cost_estimate=pl.CostEstimate(flops=flops, bytes_accessed=1 << 20, transcendentals=0),
             name=name,
         )
@@ -349,8 +353,9 @@
         [rows],
     )(pos, block, near, third)
     pair = swap(pair, "zl", 2)
+    most = pltpu.VMEM((LANES, 24 * LANES), bf16)
     high2, low2 = call(
-        early_kernel, "early_block", (tile, tile), [vmem, anywhere], 1 << 24, [rows]
+        early_kernel, "early_block", (most, most), [vmem, anywhere], 1 << 24, [rows]
     )(pos, high3)
 
     sent, y, first = call(
@@ -359,12 +364,12 @@
         (
             pltpu.VMEM((2, PART, LANES), f32),
             pltpu.VMEM((LANES, deep // 2), bf16),
-            pltpu.VMEM((2, PART, LANES), f32),
+            pltpu.VMEM((1, PART, LANES), f32),
         ),
-        [vmem] * 11,
+        [vmem] * 9,
         1 << 29,
         [rows, pltpu.VMEM((LANES, 8 * LANES), bf16), pltpu.VMEM((LANES, 8 * LANES), bf16)],
-    )(high0, low0, high1, low1, high3, low3, pos, line, *across)
+    )(high0, low0, high1, low1, pos, line, *across)
     half = swap(sent, "zh", 1)
 
     wide = pltpu.VMEM((2 * LANES, deep), bf16)
@@ -372,10 +377,10 @@
         keep_kernel,
         "keep_products",
         (pltpu.VMEM((2, PART, LANES), f32),),
-        [vmem] * 5,
+        [vmem] * 7,
         1 << 29,
         [pltpu.VMEM((3, 2 * LANES, LANES), f32), wide, wide],
-    )(pos, y, high2, low2, first)
+    )(pos, y, high2, low2, high3, low3, first)
     core = lax.ppermute(keep[0] + half[0], "c", [(0, 1), (1, 0)])
     rest = pl.pallas_call(
         term_kernel,

time: 35.8 us -> 36.2 us (1.011)
    pallas_call x1, Pallas kernels: 2.46 us -> 3.21 us  [local(): call(keep_kernel, 'keep_products', (pltpu.VMEM((2, PART, LANES), f32),),...]
    pallas_call x1, Pallas kernels: 2.76 us -> 2.3 us  [local(): call(send_kernel, 'send_products', (pltpu.VMEM((2, PART, LANES), f32), pl...]
    ppermute x8, starting transfers between devices: 14.8 us -> 15.2 us  [swap(): return lax.ppermute(array, axis, [(i, i ^ mask) for i in range(size)])]
where the time goes in v16:
time: 36.2 us; the launch traced here: 36.1 us
  starting transfers between devices  18.5 us (51%)
  Pallas kernels  14.7 us (41%)
  waiting for transfers between devices  2.06 us (6%)
  between operations  0.76 us (2%)
    ppermute x8, starting transfers between devices, swap(): return lax.ppermute(array, axis, [(i, i ^ mask) for i in range(size)])  15.2 us
    pallas_call x2, Pallas kernels, far_block(): call(kernel, 'far_block_' + 'ab'[n], (tile, tile), [vmem, anywhere], 1 <<...  4.82 us
    ppermute x1, starting transfers between devices, local(): core = lax.ppermute(keep[0] + half[0], 'c', [(0, 1), (1, 0)])  3.26 us
    pallas_call x1, Pallas kernels, local(): call(keep_kernel, 'keep_products', (pltpu.VMEM((2, PART, LANES), f32),),...  3.21 us
    pallas_call x1, Pallas kernels, local(): call(ahead_kernel, 'ahead_block', (tile, tile, pltpu.VMEM((2, PART, LANES...  2.44 us
    pallas_call x1, Pallas kernels, local(): call(send_kernel, 'send_products', (pltpu.VMEM((2, PART, LANES), f32), pl...  2.3 us
    ppermute x8, waiting for transfers between devices, swap(): return lax.ppermute(array, axis, [(i, i ^ mask) for i in range(size)])  1.54 us
    pallas_call x1, Pallas kernels, local(): call(pack_kernel, 'pack_block', (pltpu.VMEM((PART, LANES), f32), pltpu.VM...  1.01 us
  transfers between devices with their start and end apart: 9, of which 2 were waited for; matrix products, arithmetic and copies ran while one was open for 0% of the time, Pallas kernels for 36%

profile of v16, /device:TPU:1, one launch (start us, length us, event | category | flops | bytes accessed | tf_op | source)
XLA Modules:
  0.0 36.1 jit_solution(10695548769203297846)
XLA Ops:
  0.6 1.0 %pack_block.1 = (f32[40,128]{1,0:T(8,128)S(1)}, f32[3,8192]{1,0:T(4,128)S(1)}, f32[8,128]{1,0:T(8,128)S(1)}) custom-call(f32[2,16,128]{2,1,0:T(8,128)} %section_ref.1, f32[1,128]{1,0:T(1,128)} %bitcast.5, f32[3,8192]{1,0:T(4,128)} %pos_ref.1, f32[1,8192]{1,0:T(1,128)} %bitcast.4), custom_call_target="tpu_custom_call" | custom-call | flops 65536 | bytes 1048576 | tf_op jit(solution)/shard_map/pack_block/pallas_call | solution.py:325
  1.7 2.2 %collective-permute-start = (f32[40,128]{1,0:T(8,128)S(1)}, f32[40,128]{1,0:T(8,128)S(1)}, u32[]{:S(2)}, u32[]{:S(2)}) collective-permute-start(f32[40,128]{1,0:T(8,128)S(1)} %get-tuple-element.25.block_ref.slab_ref), channel_id=1, source_target_pairs={{0,64},{64,0},{128,192},{192,128},{1,65},{65,1},{129,193},{193,129... | collective-permute-start | bytes 61448 | tf_op jit(solution)/shard_map/ppermute | solution.py:319
  3.9 2.4 %far_block_a.1 = (bf16[128,4096]{1,0:T(8,128)(2,1)S(1)}, bf16[128,4096]{1,0:T(8,128)(2,1)S(1)}) custom-call(f32[3,8192]{1,0:T(4,128)S(1)} %get-tuple-element.21.pos_ref, f32[8,128]{1,0:T(8,128)S(1)} %get-tuple-element.22.token_ref.det_ref), custom_call_target="tpu_custom_call" | custom-call | flops 16777216 | bytes 1048576 | tf_op jit(solution)/shard_map/far_block_a/pallas_call | solution.py:323
  6.3 0.0 collective-permute-done.one_ref
  6.3 2.0 %collective-permute-start.1 = (f32[2,40,128]{2,1,0:T(8,128)S(1)}, f32[2,40,128]{2,1,0:T(8,128)S(1)}, u32[]{:S(2)}, u32[]{:S(2)}) collective-permute-start(f32[2,40,128]{2,1,0:T(8,128)S(1)} %get-tuple-element.29.both_ref), channel_id=1, source_target_pairs={{0,192},{64,128},{128,64},{192,0},{1,193},{65,129},{129,65},{193,1... | collective-permute-start | bytes 122888 | tf_op jit(solution)/shard_map/ppermute | solution.py:319
  8.3 1.6 %collective-permute-start.2 = (f32[40,128]{1,0:T(8,128)S(1)}, f32[40,128]{1,0:T(8,128)S(1)}, u32[]{:S(2)}, u32[]{:S(2)}) collective-permute-start(f32[40,128]{1,0:T(8,128)S(1)} %get-tuple-element.25.block_ref.slab_ref), channel_id=1, source_target_pairs={{0,1},{1,0},{2,3},{3,2},{4,5},{5,4},{6,7},{7,6},{8,9},{9,8},{10,11... | collective-permute-start | bytes 61448 | tf_op jit(solution)/shard_map/ppermute | solution.py:319
  10.0 2.4 %far_block_b.1 = (bf16[128,4096]{1,0:T(8,128)(2,1)S(1)}, bf16[128,4096]{1,0:T(8,128)(2,1)S(1)}) custom-call(f32[3,8192]{1,0:T(4,128)S(1)} %get-tuple-element.21.pos_ref, f32[8,128]{1,0:T(8,128)S(1)} %get-tuple-element.26.token_ref), custom_call_target="tpu_custom_call" | custom-call | flops 16777216 | bytes 1048576 | tf_op jit(solution)/shard_map/far_block_b/pallas_call | solution.py:323
  12.4 0.0 collective-permute-done.2.near_ref
  12.4 0.0 collective-permute-done.1.two_ref
  12.4 2.8 %collective-permute-start.5 = (f32[4,40,128]{2,1,0:T(8,128)S(1)}, f32[4,40,128]{2,1,0:T(8,128)S(1)}, u32[]{:S(2)}, u32[]{:S(2)}) collective-permute-start(f32[4,40,128]{2,1,0:T(8,128)S(1)} %get-tuple-element.30.all0), channel_id=1, source_target_pairs={{0,32},{16,48},{32,0},{48,16},{1,33},{17,49},{33,1},{49,17},{2,34}... | collective-permute-start | bytes 245768 | tf_op jit(solution)/shard_map/ppermute | solution.py:319
  15.2 0.9 %collective-permute-start.4 = (f32[4,40,128]{2,1,0:T(8,128)S(1)}, f32[4,40,128]{2,1,0:T(8,128)S(1)}, u32[]{:S(2)}, u32[]{:S(2)}) collective-permute-start(f32[4,40,128]{2,1,0:T(8,128)S(1)} %get-tuple-element.30.all0), channel_id=1, source_target_pairs={{0,48},{16,32},{32,16},{48,0},{1,49},{17,33},{33,17},{49,1},{2,50}... | collective-permute-start | bytes 245768 | tf_op jit(solution)/shard_map/ppermute | solution.py:319
  16.1 0.0 collective-permute-start.3
  16.1 2.4 %ahead_block.1 = (bf16[128,4096]{1,0:T(8,128)(2,1)S(1)}, bf16[128,4096]{1,0:T(8,128)(2,1)S(1)}, f32[2,40,128]{2,1,0:T(8,128)S(1)}) custom-call(f32[3,8192]{1,0:T(4,128)S(1)} %get-tuple-element.21.pos_ref, f32[40,128]{1,0:T(8,128)S(1)} %get-tuple-element.25.block_ref.slab_ref, f32[40,128]{1,0:T(8,128)S(1)} %collective-permute-done.2.near_ref, ...), custom_call_target="tpu_custom_call" | custom-call | flops 16777216 | bytes 1048576 | tf_op jit(solution)/shard_map/ahead_block/pallas_call | solution.py:347
  18.5 0.5 %collective-permute-start.8 = (f32[2,40,128]{2,1,0:T(8,128)S(1)}, f32[2,40,128]{2,1,0:T(8,128)S(1)}, u32[]{:S(2)}, u32[]{:S(2)}) collective-permute-start(f32[2,40,128]{2,1,0:T(8,128)S(1)} %get-tuple-element.39), channel_id=1, source_target_pairs={{0,2},{1,3},{2,0},{3,1},{4,6},{5,7},{6,4},{7,5},{8,10},{9,11},{10,... | collective-permute-start | bytes 122888 | tf_op jit(solution)/shard_map/ppermute | solution.py:319
  19.1 0.0 collective-permute-done.5.all3
  19.1 1.5 %collective-permute-done.4.all2 = f32[4,40,128]{2,1,0:T(8,128)S(1)} collective-permute-done((f32[4,40,128]{2,1,0:T(8,128)S(1)}, f32[4,40,128]{2,1,0:T(8,128)S(1)}, u32[]{:S(2)}, u32[]{:S(2)}) %collective-permute-start.4) | collective-permute-done | bytes 81952 | tf_op jit(solution)/shard_map/ppermute | solution.py:319
  20.6 0.0 collective-permute-done.3.all1
  20.6 2.3 %send_products.1 = (f32[2,40,128]{2,1,0:T(8,128)S(1)}, bf16[128,2048]{1,0:T(8,128)(2,1)S(1)}, f32[1,40,128]{2,1,0:T(8,128)S(1)}) custom-call(bf16[128,4096]{1,0:T(8,128)(2,1)S(1)} %get-tuple-element.23.after_ref.high0, bf16[128,4096]{1,0:T(8,128)(2,1)S(1)} %get-tuple-element.24.low0, bf16[128,4096]{1,0:T(8,128)(2,1)S(1)} %get-tuple-element.27.after_ref.high1, ...), custom_call_target="tpu_custom_call" | custom-call | flops 536870912 | bytes 1048576 | tf_op jit(solution)/shard_map/send_products/pallas_call | solution.py:361
  22.9 5.1 %collective-permute-start.6 = (f32[2,40,128]{2,1,0:T(8,128)S(1)}, f32[2,40,128]{2,1,0:T(8,128)S(1)}, u32[]{:S(2)}, u32[]{:S(2)}) collective-permute-start(f32[2,40,128]{2,1,0:T(8,128)S(1)} %get-tuple-element.38), channel_id=1, source_target_pairs={{0,8},{8,0},{1,9},{9,1},{2,10},{10,2},{3,11},{11,3},{4,12},{12,4},... | collective-permute-start | bytes 122888 | tf_op jit(solution)/shard_map/ppermute | solution.py:319
  28.1 3.2 %keep_products.1.keep_ref = f32[2,40,128]{2,1,0:T(8,128)S(1)} custom-call(f32[3,8192]{1,0:T(4,128)S(1)} %get-tuple-element.21.pos_ref, bf16[128,2048]{1,0:T(8,128)(2,1)S(1)} %get-tuple-element.31.y_ref, bf16[128,3072]{1,0:T(8,128)(2,1)S(1)} %get-tuple-element.34.high2, bf16[128,3072]{1,0:T(8,128)(2,1)S(1)} %get-tuple-element.35.low2, ...), custom_call_target="tpu_custom_call" | custom-call | flops 536870912 | bytes 1048576 | tf_op jit(solution)/shard_map/keep_products/pallas_call | solution.py:376
  31.3 0.0 collective-permute-done.6.half_ref
  31.3 0.0 copy-start
  31.3 0.0 copy-start.1
  31.3 3.3 %collective-permute-start.7 = (f32[40,128]{1,0:T(8,128)S(1)}, f32[40,128]{1,0:T(8,128)S(1)}, u32[]{:S(2)}, u32[]{:S(2)}) collective-permute-start(f32[40,128]{1,0:T(8,128)S(1)} %fusion), channel_id=1, source_target_pairs={{0,4},{4,0},{1,5},{5,1},{2,6},{6,2},{3,7},{7,3},{8,12},{12,8},{9,1... | collective-permute-start | bytes 61448 | tf_op jit(solution)/shard_map/ppermute | solution.py:384
  34.6 0.0 collective-permute-done.8.pair_ref
  34.6 0.3 slab_term.1.rest_ref
  34.9 0.5 %collective-permute-done.7.core_ref = f32[40,128]{1,0:T(8,128)S(1)} collective-permute-done((f32[40,128]{1,0:T(8,128)S(1)}, f32[40,128]{1,0:T(8,128)S(1)}, u32[]{:S(2)}, u32[]{:S(2)}) %collective-permute-start.7) | collective-permute-done | bytes 20512 | tf_op jit(solution)/shard_map/ppermute | solution.py:384
  35.4 0.0 copy-done
  35.4 0.0 copy-done.1
  35.4 0.6 %finish_rate.1 = (f32[2,16,128]{2,1,0:T(8,128)}, f32[2,16,128]{2,1,0:T(8,128)}) custom-call(f32[2,40,128]{2,1,0:T(8,128)S(1)} %keep_products.1.keep_ref, f32[2,40,128]{2,1,0:T(8,128)S(1)} %collective-permute-done.6.half_ref, f32[40,128]{1,0:T(8,128)S(1)} %collective-permute-done.7.core_ref, f32[2,16,128]{2,1,0:T(8,128)S(1)} %slab_term.1.rest_ref, ...), custom_call_target="tpu_custom_call" | custom-call | flops 65536 | bytes 262144 | tf_op jit(solution)/shard_map/finish_rate/pallas_call | solution.py:396
  (4 shorter events, 0.0 us)
Async XLA Ops:
  1.7 4.7 %collective-permute-start = (f32[40,128]{1,0:T(8,128)S(1)}, f32[40,128]{1,0:T(8,128)S(1)}, u32[]{:S(2)}, u32[]{:S(2)}) collective-permute-start(f32[40,128]{1,0:T(8,128)S(1)} %get-tuple-element.25.block_ref.slab_ref), channel_id=1, source_target_pairs={{0,64},{64,0},{128,192},{192,128},{1,65},{65,1},{129,193},{193,129... | collective-permute-start | bytes 61448 | tf_op jit(solution)/shard_map/ppermute | solution.py:319
  6.3 6.0 %collective-permute-start.1 = (f32[2,40,128]{2,1,0:T(8,128)S(1)}, f32[2,40,128]{2,1,0:T(8,128)S(1)}, u32[]{:S(2)}, u32[]{:S(2)}) collective-permute-start(f32[2,40,128]{2,1,0:T(8,128)S(1)} %get-tuple-element.29.both_ref), channel_id=1, source_target_pairs={{0,192},{64,128},{128,64},{192,0},{1,193},{65,129},{129,65},{193,1... | collective-permute-start | bytes 122888 | tf_op jit(solution)/shard_map/ppermute | solution.py:319
  8.3 4.0 %collective-permute-start.2 = (f32[40,128]{1,0:T(8,128)S(1)}, f32[40,128]{1,0:T(8,128)S(1)}, u32[]{:S(2)}, u32[]{:S(2)}) collective-permute-start(f32[40,128]{1,0:T(8,128)S(1)} %get-tuple-element.25.block_ref.slab_ref), channel_id=1, source_target_pairs={{0,1},{1,0},{2,3},{3,2},{4,5},{5,4},{6,7},{7,6},{8,9},{9,8},{10,11... | collective-permute-start | bytes 61448 | tf_op jit(solution)/shard_map/ppermute | solution.py:319
  12.4 6.7 %collective-permute-start.5 = (f32[4,40,128]{2,1,0:T(8,128)S(1)}, f32[4,40,128]{2,1,0:T(8,128)S(1)}, u32[]{:S(2)}, u32[]{:S(2)}) collective-permute-start(f32[4,40,128]{2,1,0:T(8,128)S(1)} %get-tuple-element.30.all0), channel_id=1, source_target_pairs={{0,32},{16,48},{32,0},{48,16},{1,33},{17,49},{33,1},{49,17},{2,34}... | collective-permute-start | bytes 245768 | tf_op jit(solution)/shard_map/ppermute | solution.py:319
  15.2 5.4 %collective-permute-start.4 = (f32[4,40,128]{2,1,0:T(8,128)S(1)}, f32[4,40,128]{2,1,0:T(8,128)S(1)}, u32[]{:S(2)}, u32[]{:S(2)}) collective-permute-start(f32[4,40,128]{2,1,0:T(8,128)S(1)} %get-tuple-element.30.all0), channel_id=1, source_target_pairs={{0,48},{16,32},{32,16},{48,0},{1,49},{17,33},{33,17},{49,1},{2,50}... | collective-permute-start | bytes 245768 | tf_op jit(solution)/shard_map/ppermute | solution.py:319
  16.1 4.5 %collective-permute-start.3 = (f32[4,40,128]{2,1,0:T(8,128)S(1)}, f32[4,40,128]{2,1,0:T(8,128)S(1)}, u32[]{:S(2)}, u32[]{:S(2)}) collective-permute-start(f32[4,40,128]{2,1,0:T(8,128)S(1)} %get-tuple-element.30.all0), channel_id=1, source_target_pairs={{0,16},{16,0},{32,48},{48,32},{1,17},{17,1},{33,49},{49,33},{2,18}... | collective-permute-start | bytes 245768 | tf_op jit(solution)/shard_map/ppermute | solution.py:319
  18.5 16.0 %collective-permute-start.8 = (f32[2,40,128]{2,1,0:T(8,128)S(1)}, f32[2,40,128]{2,1,0:T(8,128)S(1)}, u32[]{:S(2)}, u32[]{:S(2)}) collective-permute-start(f32[2,40,128]{2,1,0:T(8,128)S(1)} %get-tuple-element.39), channel_id=1, source_target_pairs={{0,2},{1,3},{2,0},{3,1},{4,6},{5,7},{6,4},{7,5},{8,10},{9,11},{10,... | collective-permute-start | bytes 122888 | tf_op jit(solution)/shard_map/ppermute | solution.py:319
  22.9 8.4 %collective-permute-start.6 = (f32[2,40,128]{2,1,0:T(8,128)S(1)}, f32[2,40,128]{2,1,0:T(8,128)S(1)}, u32[]{:S(2)}, u32[]{:S(2)}) collective-permute-start(f32[2,40,128]{2,1,0:T(8,128)S(1)} %get-tuple-element.38), channel_id=1, source_target_pairs={{0,8},{8,0},{1,9},{9,1},{2,10},{10,2},{3,11},{11,3},{4,12},{12,4},... | collective-permute-start | bytes 122888 | tf_op jit(solution)/shard_map/ppermute | solution.py:319
  31.3 4.1 %copy-start = (f32[2,16,128]{2,1,0:T(8,128)S(1)}, f32[2,16,128]{2,1,0:T(8,128)}, u32[]{:S(2)}) copy-start(f32[2,16,128]{2,1,0:T(8,128)} %base_ref.1) | copy-start | bytes 49156
  31.3 4.1 %copy-start.1 = (f32[2,16,128]{2,1,0:T(8,128)S(1)}, f32[2,16,128]{2,1,0:T(8,128)}, u32[]{:S(2)}) copy-start(f32[2,16,128]{2,1,0:T(8,128)} %accum_ref.1) | copy-start | bytes 49156
  31.3 4.1 %collective-permute-start.7 = (f32[40,128]{1,0:T(8,128)S(1)}, f32[40,128]{1,0:T(8,128)S(1)}, u32[]{:S(2)}, u32[]{:S(2)}) collective-permute-start(f32[40,128]{1,0:T(8,128)S(1)} %fusion), channel_id=1, source_target_pairs={{0,4},{4,0},{1,5},{5,1},{2,6},{6,2},{3,7},{7,3},{8,12},{12,8},{9,1... | collective-permute-start | bytes 61448 | tf_op jit(solution)/shard_map/ppermute | solution.py:384

commit v17 on v15

--- a/solution.py
+++ b/solution.py
@@ -339,7 +339,8 @@
     line, third = call(
         line_kernel, "join_line", (pltpu.VMEM((4, PART, LANES), f32), token), [vmem] * 3 + [anywhere], 1
     )(both, two, near, high1)
-    across = [swap(line, "x", mask) for mask in (1, 3, 2)]
+    two_hops, three, next_to = [swap(line, "x", mask) for mask in (2, 3, 1)]
+    across = [next_to, three, two_hops]
     high3, low3, pair = call(
         ahead_kernel,
         "ahead_block",

time: 35.8 us -> 35.8 us (level)
  no operation moved by 1% of the time
where the time goes in v17:
time: 35.8 us; the launch traced here: 35.6 us
  starting transfers between devices  18.3 us (51%)
  Pallas kernels  14.5 us (41%)
  waiting for transfers between devices  2.06 us (6%)
  between operations  0.76 us (2%)
    ppermute x8, starting transfers between devices, swap(): return lax.ppermute(array, axis, [(i, i ^ mask) for i in range(size)])  14.8 us
    pallas_call x2, Pallas kernels, far_block(): call(kernel, 'far_block_' + 'ab'[n], (tile, tile), [vmem, anywhere], 1 <<...  4.87 us
    ppermute x1, starting transfers between devices, local(): core = lax.ppermute(keep[0] + half[0], 'c', [(0, 1), (1, 0)])  3.54 us
    pallas_call x1, Pallas kernels, local(): call(send_kernel, 'send_products', (pltpu.VMEM((2, PART, LANES), f32), pl...  2.76 us
    pallas_call x1, Pallas kernels, local(): call(keep_kernel, 'keep_products', (pltpu.VMEM((2, PART, LANES), f32),),...  2.46 us
    pallas_call x1, Pallas kernels, local(): call(ahead_kernel, 'ahead_block', (tile, tile, pltpu.VMEM((2, PART, LANES...  2.44 us
    ppermute x8, waiting for transfers between devices, swap(): return lax.ppermute(array, axis, [(i, i ^ mask) for i in range(size)])  1.54 us
    pallas_call x1, Pallas kernels, local(): call(pack_kernel, 'pack_block', (pltpu.VMEM((PART, LANES), f32), pltpu.VM...  1.01 us
  transfers between devices with their start and end apart: 9, of which 2 were waited for; matrix products, arithmetic and copies ran while one was open for 0% of the time, Pallas kernels for 36%

profile of v17, /device:TPU:1, one launch (start us, length us, event | category | flops | bytes accessed | tf_op | source)
XLA Modules:
  0.0 35.6 jit_solution(14014481336711968731)
XLA Ops:
  0.6 1.0 %pack_block.1 = (f32[40,128]{1,0:T(8,128)S(1)}, f32[3,8192]{1,0:T(4,128)S(1)}, f32[8,128]{1,0:T(8,128)S(1)}) custom-call(f32[2,16,128]{2,1,0:T(8,128)} %section_ref.1, f32[1,128]{1,0:T(1,128)} %bitcast.5, f32[3,8192]{1,0:T(4,128)} %pos_ref.1, f32[1,8192]{1,0:T(1,128)} %bitcast.4), custom_call_target="tpu_custom_call" | custom-call | flops 65536 | bytes 1048576 | tf_op jit(solution)/shard_map/pack_block/pallas_call | solution.py:321
  1.7 2.2 %collective-permute-start = (f32[40,128]{1,0:T(8,128)S(1)}, f32[40,128]{1,0:T(8,128)S(1)}, u32[]{:S(2)}, u32[]{:S(2)}) collective-permute-start(f32[40,128]{1,0:T(8,128)S(1)} %get-tuple-element.25.block_ref.slab_ref), channel_id=1, source_target_pairs={{0,64},{64,0},{128,192},{192,128},{1,65},{65,1},{129,193},{193,129... | collective-permute-start | bytes 61448 | tf_op jit(solution)/shard_map/ppermute | solution.py:315
  3.9 2.4 %far_block_a.1 = (bf16[128,4096]{1,0:T(8,128)(2,1)S(1)}, bf16[128,4096]{1,0:T(8,128)(2,1)S(1)}) custom-call(f32[3,8192]{1,0:T(4,128)S(1)} %get-tuple-element.21.pos_ref, f32[8,128]{1,0:T(8,128)S(1)} %get-tuple-element.22.token_ref.det_ref), custom_call_target="tpu_custom_call" | custom-call | flops 16777216 | bytes 1048576 | tf_op jit(solution)/shard_map/far_block_a/pallas_call | solution.py:319
  6.3 0.0 collective-permute-done.one_ref
  6.3 2.0 %collective-permute-start.2 = (f32[2,40,128]{2,1,0:T(8,128)S(1)}, f32[2,40,128]{2,1,0:T(8,128)S(1)}, u32[]{:S(2)}, u32[]{:S(2)}) collective-permute-start(f32[2,40,128]{2,1,0:T(8,128)S(1)} %get-tuple-element.29.both_ref), channel_id=1, source_target_pairs={{0,192},{64,128},{128,64},{192,0},{1,193},{65,129},{129,65},{193,1... | collective-permute-start | bytes 122888 | tf_op jit(solution)/shard_map/ppermute | solution.py:315
  8.3 1.6 %collective-permute-start.1 = (f32[40,128]{1,0:T(8,128)S(1)}, f32[40,128]{1,0:T(8,128)S(1)}, u32[]{:S(2)}, u32[]{:S(2)}) collective-permute-start(f32[40,128]{1,0:T(8,128)S(1)} %get-tuple-element.25.block_ref.slab_ref), channel_id=1, source_target_pairs={{0,1},{1,0},{2,3},{3,2},{4,5},{5,4},{6,7},{7,6},{8,9},{9,8},{10,11... | collective-permute-start | bytes 61448 | tf_op jit(solution)/shard_map/ppermute | solution.py:315
  10.0 2.4 %far_block_b.1 = (bf16[128,4096]{1,0:T(8,128)(2,1)S(1)}, bf16[128,4096]{1,0:T(8,128)(2,1)S(1)}) custom-call(f32[3,8192]{1,0:T(4,128)S(1)} %get-tuple-element.21.pos_ref, f32[8,128]{1,0:T(8,128)S(1)} %get-tuple-element.26.token_ref), custom_call_target="tpu_custom_call" | custom-call | flops 16777216 | bytes 1048576 | tf_op jit(solution)/shard_map/far_block_b/pallas_call | solution.py:319
  12.4 0.0 collective-permute-done.1.near_ref
  12.4 0.0 collective-permute-done.2.two_ref
  12.4 2.8 %collective-permute-start.5 = (f32[4,40,128]{2,1,0:T(8,128)S(1)}, f32[4,40,128]{2,1,0:T(8,128)S(1)}, u32[]{:S(2)}, u32[]{:S(2)}) collective-permute-start(f32[4,40,128]{2,1,0:T(8,128)S(1)} %get-tuple-element.33.all0), channel_id=1, source_target_pairs={{0,32},{16,48},{32,0},{48,16},{1,33},{17,49},{33,1},{49,17},{2,34}... | collective-permute-start | bytes 245768 | tf_op jit(solution)/shard_map/ppermute | solution.py:315
  15.3 0.9 %collective-permute-start.4 = (f32[4,40,128]{2,1,0:T(8,128)S(1)}, f32[4,40,128]{2,1,0:T(8,128)S(1)}, u32[]{:S(2)}, u32[]{:S(2)}) collective-permute-start(f32[4,40,128]{2,1,0:T(8,128)S(1)} %get-tuple-element.33.all0), channel_id=1, source_target_pairs={{0,48},{16,32},{32,16},{48,0},{1,49},{17,33},{33,17},{49,1},{2,50}... | collective-permute-start | bytes 245768 | tf_op jit(solution)/shard_map/ppermute | solution.py:315
  16.1 0.0 collective-permute-start.3
  16.1 2.4 %ahead_block.1 = (bf16[128,4096]{1,0:T(8,128)(2,1)S(1)}, bf16[128,4096]{1,0:T(8,128)(2,1)S(1)}, f32[2,40,128]{2,1,0:T(8,128)S(1)}) custom-call(f32[3,8192]{1,0:T(4,128)S(1)} %get-tuple-element.21.pos_ref, f32[40,128]{1,0:T(8,128)S(1)} %get-tuple-element.25.block_ref.slab_ref, f32[40,128]{1,0:T(8,128)S(1)} %collective-permute-done.1.near_ref, ...), custom_call_target="tpu_custom_call" | custom-call | flops 16777216 | bytes 1048576 | tf_op jit(solution)/shard_map/ahead_block/pallas_call | solution.py:344
  18.6 0.5 %collective-permute-start.8 = (f32[2,40,128]{2,1,0:T(8,128)S(1)}, f32[2,40,128]{2,1,0:T(8,128)S(1)}, u32[]{:S(2)}, u32[]{:S(2)}) collective-permute-start(f32[2,40,128]{2,1,0:T(8,128)S(1)} %get-tuple-element.39), channel_id=1, source_target_pairs={{0,2},{1,3},{2,0},{3,1},{4,6},{5,7},{6,4},{7,5},{8,10},{9,11},{10,... | collective-permute-start | bytes 122888 | tf_op jit(solution)/shard_map/ppermute | solution.py:315
  19.1 0.0 collective-permute-done.5.all3
  19.1 1.5 %collective-permute-done.4.all2 = f32[4,40,128]{2,1,0:T(8,128)S(1)} collective-permute-done((f32[4,40,128]{2,1,0:T(8,128)S(1)}, f32[4,40,128]{2,1,0:T(8,128)S(1)}, u32[]{:S(2)}, u32[]{:S(2)}) %collective-permute-start.4) | collective-permute-done | bytes 81952 | tf_op jit(solution)/shard_map/ppermute | solution.py:315
  20.7 0.0 collective-permute-done.3.all1
  20.7 2.8 %send_products.1 = (f32[2,40,128]{2,1,0:T(8,128)S(1)}, bf16[128,2048]{1,0:T(8,128)(2,1)S(1)}, f32[2,40,128]{2,1,0:T(8,128)S(1)}) custom-call(bf16[128,4096]{1,0:T(8,128)(2,1)S(1)} %get-tuple-element.23.after_ref.high0, bf16[128,4096]{1,0:T(8,128)(2,1)S(1)} %get-tuple-element.24.low0, bf16[128,4096]{1,0:T(8,128)(2,1)S(1)} %get-tuple-element.27.after_ref.high1, ...), custom_call_target="tpu_custom_call" | custom-call | flops 536870912 | bytes 1048576 | tf_op jit(solution)/shard_map/send_products/pallas_call | solution.py:357
  23.4 4.7 %collective-permute-start.6 = (f32[2,40,128]{2,1,0:T(8,128)S(1)}, f32[2,40,128]{2,1,0:T(8,128)S(1)}, u32[]{:S(2)}, u32[]{:S(2)}) collective-permute-start(f32[2,40,128]{2,1,0:T(8,128)S(1)} %get-tuple-element.38), channel_id=1, source_target_pairs={{0,8},{8,0},{1,9},{9,1},{2,10},{10,2},{3,11},{11,3},{4,12},{12,4},... | collective-permute-start | bytes 122888 | tf_op jit(solution)/shard_map/ppermute | solution.py:315
  28.1 2.5 %keep_products.1.keep_ref = f32[2,40,128]{2,1,0:T(8,128)S(1)} custom-call(f32[3,8192]{1,0:T(4,128)S(1)} %get-tuple-element.21.pos_ref, bf16[128,2048]{1,0:T(8,128)(2,1)S(1)} %get-tuple-element.34.y_ref, bf16[128,4096]{1,0:T(8,128)(2,1)S(1)} %get-tuple-element.35.high2, bf16[128,4096]{1,0:T(8,128)(2,1)S(1)} %get-tuple-element.36.low2, ...), custom_call_target="tpu_custom_call" | custom-call | flops 536870912 | bytes 1048576 | tf_op jit(solution)/shard_map/keep_products/pallas_call | solution.py:372
  30.6 0.0 collective-permute-done.6.half_ref
  30.6 0.0 copy-start
  30.6 0.0 copy-start.1
  30.6 3.5 %collective-permute-start.7 = (f32[40,128]{1,0:T(8,128)S(1)}, f32[40,128]{1,0:T(8,128)S(1)}, u32[]{:S(2)}, u32[]{:S(2)}) collective-permute-start(f32[40,128]{1,0:T(8,128)S(1)} %fusion), channel_id=1, source_target_pairs={{0,4},{4,0},{1,5},{5,1},{2,6},{6,2},{3,7},{7,3},{8,12},{12,8},{9,1... | collective-permute-start | bytes 61448 | tf_op jit(solution)/shard_map/ppermute | solution.py:380
  34.2 0.0 collective-permute-done.8.pair_ref
  34.2 0.3 slab_term.1.rest_ref
  34.5 0.5 %collective-permute-done.7.core_ref = f32[40,128]{1,0:T(8,128)S(1)} collective-permute-done((f32[40,128]{1,0:T(8,128)S(1)}, f32[40,128]{1,0:T(8,128)S(1)}, u32[]{:S(2)}, u32[]{:S(2)}) %collective-permute-start.7) | collective-permute-done | bytes 20512 | tf_op jit(solution)/shard_map/ppermute | solution.py:380
  35.0 0.0 copy-done
  35.0 0.0 copy-done.1
  35.0 0.6 %finish_rate.1 = (f32[2,16,128]{2,1,0:T(8,128)}, f32[2,16,128]{2,1,0:T(8,128)}) custom-call(f32[2,40,128]{2,1,0:T(8,128)S(1)} %keep_products.1.keep_ref, f32[2,40,128]{2,1,0:T(8,128)S(1)} %collective-permute-done.6.half_ref, f32[40,128]{1,0:T(8,128)S(1)} %collective-permute-done.7.core_ref, f32[2,16,128]{2,1,0:T(8,128)S(1)} %slab_term.1.rest_ref, ...), custom_call_target="tpu_custom_call" | custom-call | flops 65536 | bytes 262144 | tf_op jit(solution)/shard_map/finish_rate/pallas_call | solution.py:392
  (4 shorter events, 0.0 us)
Async XLA Ops:
  1.7 4.7 %collective-permute-start = (f32[40,128]{1,0:T(8,128)S(1)}, f32[40,128]{1,0:T(8,128)S(1)}, u32[]{:S(2)}, u32[]{:S(2)}) collective-permute-start(f32[40,128]{1,0:T(8,128)S(1)} %get-tuple-element.25.block_ref.slab_ref), channel_id=1, source_target_pairs={{0,64},{64,0},{128,192},{192,128},{1,65},{65,1},{129,193},{193,129... | collective-permute-start | bytes 61448 | tf_op jit(solution)/shard_map/ppermute | solution.py:315
  6.3 6.1 %collective-permute-start.2 = (f32[2,40,128]{2,1,0:T(8,128)S(1)}, f32[2,40,128]{2,1,0:T(8,128)S(1)}, u32[]{:S(2)}, u32[]{:S(2)}) collective-permute-start(f32[2,40,128]{2,1,0:T(8,128)S(1)} %get-tuple-element.29.both_ref), channel_id=1, source_target_pairs={{0,192},{64,128},{128,64},{192,0},{1,193},{65,129},{129,65},{193,1... | collective-permute-start | bytes 122888 | tf_op jit(solution)/shard_map/ppermute | solution.py:315
  8.3 4.1 %collective-permute-start.1 = (f32[40,128]{1,0:T(8,128)S(1)}, f32[40,128]{1,0:T(8,128)S(1)}, u32[]{:S(2)}, u32[]{:S(2)}) collective-permute-start(f32[40,128]{1,0:T(8,128)S(1)} %get-tuple-element.25.block_ref.slab_ref), channel_id=1, source_target_pairs={{0,1},{1,0},{2,3},{3,2},{4,5},{5,4},{6,7},{7,6},{8,9},{9,8},{10,11... | collective-permute-start | bytes 61448 | tf_op jit(solution)/shard_map/ppermute | solution.py:315
  12.4 6.7 %collective-permute-start.5 = (f32[4,40,128]{2,1,0:T(8,128)S(1)}, f32[4,40,128]{2,1,0:T(8,128)S(1)}, u32[]{:S(2)}, u32[]{:S(2)}) collective-permute-start(f32[4,40,128]{2,1,0:T(8,128)S(1)} %get-tuple-element.33.all0), channel_id=1, source_target_pairs={{0,32},{16,48},{32,0},{48,16},{1,33},{17,49},{33,1},{49,17},{2,34}... | collective-permute-start | bytes 245768 | tf_op jit(solution)/shard_map/ppermute | solution.py:315
  15.3 5.4 %collective-permute-start.4 = (f32[4,40,128]{2,1,0:T(8,128)S(1)}, f32[4,40,128]{2,1,0:T(8,128)S(1)}, u32[]{:S(2)}, u32[]{:S(2)}) collective-permute-start(f32[4,40,128]{2,1,0:T(8,128)S(1)} %get-tuple-element.33.all0), channel_id=1, source_target_pairs={{0,48},{16,32},{32,16},{48,0},{1,49},{17,33},{33,17},{49,1},{2,50}... | collective-permute-start | bytes 245768 | tf_op jit(solution)/shard_map/ppermute | solution.py:315
  16.1 4.5 %collective-permute-start.3 = (f32[4,40,128]{2,1,0:T(8,128)S(1)}, f32[4,40,128]{2,1,0:T(8,128)S(1)}, u32[]{:S(2)}, u32[]{:S(2)}) collective-permute-start(f32[4,40,128]{2,1,0:T(8,128)S(1)} %get-tuple-element.33.all0), channel_id=1, source_target_pairs={{0,16},{16,0},{32,48},{48,32},{1,17},{17,1},{33,49},{49,33},{2,18}... | collective-permute-start | bytes 245768 | tf_op jit(solution)/shard_map/ppermute | solution.py:315
  18.6 15.6 %collective-permute-start.8 = (f32[2,40,128]{2,1,0:T(8,128)S(1)}, f32[2,40,128]{2,1,0:T(8,128)S(1)}, u32[]{:S(2)}, u32[]{:S(2)}) collective-permute-start(f32[2,40,128]{2,1,0:T(8,128)S(1)} %get-tuple-element.39), channel_id=1, source_target_pairs={{0,2},{1,3},{2,0},{3,1},{4,6},{5,7},{6,4},{7,5},{8,10},{9,11},{10,... | collective-permute-start | bytes 122888 | tf_op jit(solution)/shard_map/ppermute | solution.py:315
  23.4 7.2 %collective-permute-start.6 = (f32[2,40,128]{2,1,0:T(8,128)S(1)}, f32[2,40,128]{2,1,0:T(8,128)S(1)}, u32[]{:S(2)}, u32[]{:S(2)}) collective-permute-start(f32[2,40,128]{2,1,0:T(8,128)S(1)} %get-tuple-element.38), channel_id=1, source_target_pairs={{0,8},{8,0},{1,9},{9,1},{2,10},{10,2},{3,11},{11,3},{4,12},{12,4},... | collective-permute-start | bytes 122888 | tf_op jit(solution)/shard_map/ppermute | solution.py:315
  30.6 4.4 %copy-start = (f32[2,16,128]{2,1,0:T(8,128)S(1)}, f32[2,16,128]{2,1,0:T(8,128)}, u32[]{:S(2)}) copy-start(f32[2,16,128]{2,1,0:T(8,128)} %base_ref.1) | copy-start | bytes 49156
  30.6 4.4 %copy-start.1 = (f32[2,16,128]{2,1,0:T(8,128)S(1)}, f32[2,16,128]{2,1,0:T(8,128)}, u32[]{:S(2)}) copy-start(f32[2,16,128]{2,1,0:T(8,128)} %accum_ref.1) | copy-start | bytes 49156
  30.6 4.4 %collective-permute-start.7 = (f32[40,128]{1,0:T(8,128)S(1)}, f32[40,128]{1,0:T(8,128)S(1)}, u32[]{:S(2)}, u32[]{:S(2)}) collective-permute-start(f32[40,128]{1,0:T(8,128)S(1)} %fusion), channel_id=1, source_target_pairs={{0,4},{4,0},{1,5},{5,1},{2,6},{6,2},{3,7},{7,3},{8,12},{12,8},{9,1... | collective-permute-start | bytes 61448 | tf_op jit(solution)/shard_map/ppermute | solution.py:380

commit v18 on v17

--- a/solution.py
+++ b/solution.py
@@ -228,7 +228,7 @@
     return by_real, by_imag
 
 
-def send_kernel(high0, low0, high1, low1, high3, low3, pos_ref, all0, all1, all2, all3, out_ref, y_ref, first_ref, row_ref, part_high, part_low):
+def send_kernel(high0, low0, high1, low1, high3, low3, pos_ref, all0, all3, all2, all1, out_ref, y_ref, first_ref, row_ref, part_high, part_low):
     fill_slab((all0, all1, all2, all3), y_ref)
     y = y_ref[...]
     store_products(*products(high0, low0, y), out_ref, 0)
@@ -340,7 +340,7 @@
         line_kernel, "join_line", (pltpu.VMEM((4, PART, LANES), f32), token), [vmem] * 3 + [anywhere], 1
     )(both, two, near, high1)
     two_hops, three, next_to = [swap(line, "x", mask) for mask in (2, 3, 1)]
-    across = [next_to, three, two_hops]
+    across = [two_hops, three, next_to]
     high3, low3, pair = call(
         ahead_kernel,
         "ahead_block",

time: 35.8 us -> 36.8 us (1.028)
  starting transfers between devices: 18.3 us -> 18.9 us
  waiting for transfers between devices: 2.06 us -> 2.45 us
    ppermute x1, starting transfers between devices: 3.54 us -> 4.31 us  [local(): core = lax.ppermute(keep[0] + half[0], 'c', [(0, 1), (1, 0)])]
    ppermute x8, waiting for transfers between devices: 1.54 us -> 1.92 us  [swap(): return lax.ppermute(array, axis, [(i, i ^ mask) for i in range(size)])]
  transfers between devices with their start and end apart: 9 -> 9, of which waited for: 2 -> 2; matrix products, arithmetic and copies ran while one was open for 0% -> 0% of each run, Pallas kernels for 36% -> 35%
where the time goes in v18:
time: 36.8 us; the launch traced here: 36.7 us
  starting transfers between devices  18.9 us (51%)
  Pallas kernels  14.5 us (39%)
  waiting for transfers between devices  2.45 us (7%)
  between operations  0.76 us (2%)
    ppermute x8, starting transfers between devices, swap(): return lax.ppermute(array, axis, [(i, i ^ mask) for i in range(size)])  14.6 us
    pallas_call x2, Pallas kernels, far_block(): call(kernel, 'far_block_' + 'ab'[n], (tile, tile), [vmem, anywhere], 1 <<...  4.87 us
    ppermute x1, starting transfers between devices, local(): core = lax.ppermute(keep[0] + half[0], 'c', [(0, 1), (1, 0)])  4.31 us
    pallas_call x1, Pallas kernels, local(): call(send_kernel, 'send_products', (pltpu.VMEM((2, PART, LANES), f32), pl...  2.75 us
    pallas_call x1, Pallas kernels, local(): call(keep_kernel, 'keep_products', (pltpu.VMEM((2, PART, LANES), f32),),...  2.45 us
    pallas_call x1, Pallas kernels, local(): call(ahead_kernel, 'ahead_block', (tile, tile, pltpu.VMEM((2, PART, LANES...  2.44 us
    ppermute x8, waiting for transfers between devices, swap(): return lax.ppermute(array, axis, [(i, i ^ mask) for i in range(size)])  1.92 us
    pallas_call x1, Pallas kernels, local(): call(pack_kernel, 'pack_block', (pltpu.VMEM((PART, LANES), f32), pltpu.VM...  1.01 us
  transfers between devices with their start and end apart: 9, of which 2 were waited for; matrix products, arithmetic and copies ran while one was open for 0% of the time, Pallas kernels for 35%

profile of v18, /device:TPU:1, one launch (start us, length us, event | category | flops | bytes accessed | tf_op | source)
XLA Modules:
  0.0 36.7 jit_solution(10198169037852352031)
XLA Ops:
  0.6 1.0 %pack_block.1 = (f32[40,128]{1,0:T(8,128)S(1)}, f32[3,8192]{1,0:T(4,128)S(1)}, f32[8,128]{1,0:T(8,128)S(1)}) custom-call(f32[2,16,128]{2,1,0:T(8,128)} %section_ref.1, f32[1,128]{1,0:T(1,128)} %bitcast.5, f32[3,8192]{1,0:T(4,128)} %pos_ref.1, f32[1,8192]{1,0:T(1,128)} %bitcast.4), custom_call_target="tpu_custom_call" | custom-call | flops 65536 | bytes 1048576 | tf_op jit(solution)/shard_map/pack_block/pallas_call | solution.py:321
  1.7 2.2 %collective-permute-start = (f32[40,128]{1,0:T(8,128)S(1)}, f32[40,128]{1,0:T(8,128)S(1)}, u32[]{:S(2)}, u32[]{:S(2)}) collective-permute-start(f32[40,128]{1,0:T(8,128)S(1)} %get-tuple-element.25.block_ref.slab_ref), channel_id=1, source_target_pairs={{0,64},{64,0},{128,192},{192,128},{1,65},{65,1},{129,193},{193,129... | collective-permute-start | bytes 61448 | tf_op jit(solution)/shard_map/ppermute | solution.py:315
  3.9 2.4 %far_block_a.1 = (bf16[128,4096]{1,0:T(8,128)(2,1)S(1)}, bf16[128,4096]{1,0:T(8,128)(2,1)S(1)}) custom-call(f32[3,8192]{1,0:T(4,128)S(1)} %get-tuple-element.21.pos_ref, f32[8,128]{1,0:T(8,128)S(1)} %get-tuple-element.22.token_ref.det_ref), custom_call_target="tpu_custom_call" | custom-call | flops 16777216 | bytes 1048576 | tf_op jit(solution)/shard_map/far_block_a/pallas_call | solution.py:319
  6.3 0.0 collective-permute-done.one_ref
  6.3 2.0 %collective-permute-start.2 = (f32[2,40,128]{2,1,0:T(8,128)S(1)}, f32[2,40,128]{2,1,0:T(8,128)S(1)}, u32[]{:S(2)}, u32[]{:S(2)}) collective-permute-start(f32[2,40,128]{2,1,0:T(8,128)S(1)} %get-tuple-element.29.both_ref), channel_id=1, source_target_pairs={{0,192},{64,128},{128,64},{192,0},{1,193},{65,129},{129,65},{193,1... | collective-permute-start | bytes 122888 | tf_op jit(solution)/shard_map/ppermute | solution.py:315
  8.3 1.6 %collective-permute-start.1 = (f32[40,128]{1,0:T(8,128)S(1)}, f32[40,128]{1,0:T(8,128)S(1)}, u32[]{:S(2)}, u32[]{:S(2)}) collective-permute-start(f32[40,128]{1,0:T(8,128)S(1)} %get-tuple-element.25.block_ref.slab_ref), channel_id=1, source_target_pairs={{0,1},{1,0},{2,3},{3,2},{4,5},{5,4},{6,7},{7,6},{8,9},{9,8},{10,11... | collective-permute-start | bytes 61448 | tf_op jit(solution)/shard_map/ppermute | solution.py:315
  10.0 2.4 %far_block_b.1 = (bf16[128,4096]{1,0:T(8,128)(2,1)S(1)}, bf16[128,4096]{1,0:T(8,128)(2,1)S(1)}) custom-call(f32[3,8192]{1,0:T(4,128)S(1)} %get-tuple-element.21.pos_ref, f32[8,128]{1,0:T(8,128)S(1)} %get-tuple-element.26.token_ref), custom_call_target="tpu_custom_call" | custom-call | flops 16777216 | bytes 1048576 | tf_op jit(solution)/shard_map/far_block_b/pallas_call | solution.py:319
  12.4 0.0 collective-permute-done.1.near_ref
  12.4 0.0 collective-permute-done.2.two_ref
  12.4 1.3 %collective-permute-start.5 = (f32[4,40,128]{2,1,0:T(8,128)S(1)}, f32[4,40,128]{2,1,0:T(8,128)S(1)}, u32[]{:S(2)}, u32[]{:S(2)}) collective-permute-start(f32[4,40,128]{2,1,0:T(8,128)S(1)} %get-tuple-element.33.all0), channel_id=1, source_target_pairs={{0,16},{16,0},{32,48},{48,32},{1,17},{17,1},{33,49},{49,33},{2,18}... | collective-permute-start | bytes 245768 | tf_op jit(solution)/shard_map/ppermute | solution.py:315
  13.7 1.8 %collective-permute-start.4 = (f32[4,40,128]{2,1,0:T(8,128)S(1)}, f32[4,40,128]{2,1,0:T(8,128)S(1)}, u32[]{:S(2)}, u32[]{:S(2)}) collective-permute-start(f32[4,40,128]{2,1,0:T(8,128)S(1)} %get-tuple-element.33.all0), channel_id=1, source_target_pairs={{0,48},{16,32},{32,16},{48,0},{1,49},{17,33},{33,17},{49,1},{2,50}... | collective-permute-start | bytes 245768 | tf_op jit(solution)/shard_map/ppermute | solution.py:315
  15.6 0.6 %collective-permute-start.3 = (f32[4,40,128]{2,1,0:T(8,128)S(1)}, f32[4,40,128]{2,1,0:T(8,128)S(1)}, u32[]{:S(2)}, u32[]{:S(2)}) collective-permute-start(f32[4,40,128]{2,1,0:T(8,128)S(1)} %get-tuple-element.33.all0), channel_id=1, source_target_pairs={{0,32},{16,48},{32,0},{48,16},{1,33},{17,49},{33,1},{49,17},{2,34}... | collective-permute-start | bytes 245768 | tf_op jit(solution)/shard_map/ppermute | solution.py:315
  16.2 2.4 %ahead_block.1 = (bf16[128,4096]{1,0:T(8,128)(2,1)S(1)}, bf16[128,4096]{1,0:T(8,128)(2,1)S(1)}, f32[2,40,128]{2,1,0:T(8,128)S(1)}) custom-call(f32[3,8192]{1,0:T(4,128)S(1)} %get-tuple-element.21.pos_ref, f32[40,128]{1,0:T(8,128)S(1)} %get-tuple-element.25.block_ref.slab_ref, f32[40,128]{1,0:T(8,128)S(1)} %collective-permute-done.1.near_ref, ...), custom_call_target="tpu_custom_call" | custom-call | flops 16777216 | bytes 1048576 | tf_op jit(solution)/shard_map/ahead_block/pallas_call | solution.py:344
  18.6 0.5 %collective-permute-start.8 = (f32[2,40,128]{2,1,0:T(8,128)S(1)}, f32[2,40,128]{2,1,0:T(8,128)S(1)}, u32[]{:S(2)}, u32[]{:S(2)}) collective-permute-start(f32[2,40,128]{2,1,0:T(8,128)S(1)} %get-tuple-element.39), channel_id=1, source_target_pairs={{0,2},{1,3},{2,0},{3,1},{4,6},{5,7},{6,4},{7,5},{8,10},{9,11},{10,... | collective-permute-start | bytes 122888 | tf_op jit(solution)/shard_map/ppermute | solution.py:315
  19.2 0.0 collective-permute-done.5.all1
  19.2 0.0 collective-permute-done.4.all2
  19.2 1.9 %collective-permute-done.3.all3 = f32[4,40,128]{2,1,0:T(8,128)S(1)} collective-permute-done((f32[4,40,128]{2,1,0:T(8,128)S(1)}, f32[4,40,128]{2,1,0:T(8,128)S(1)}, u32[]{:S(2)}, u32[]{:S(2)}) %collective-permute-start.3) | collective-permute-done | bytes 81952 | tf_op jit(solution)/shard_map/ppermute | solution.py:315
  21.1 2.8 %send_products.1 = (f32[2,40,128]{2,1,0:T(8,128)S(1)}, bf16[128,2048]{1,0:T(8,128)(2,1)S(1)}, f32[2,40,128]{2,1,0:T(8,128)S(1)}) custom-call(bf16[128,4096]{1,0:T(8,128)(2,1)S(1)} %get-tuple-element.23.after_ref.high0, bf16[128,4096]{1,0:T(8,128)(2,1)S(1)} %get-tuple-element.24.low0, bf16[128,4096]{1,0:T(8,128)(2,1)S(1)} %get-tuple-element.27.after_ref.high1, ...), custom_call_target="tpu_custom_call" | custom-call | flops 536870912 | bytes 1048576 | tf_op jit(solution)/shard_map/send_products/pallas_call | solution.py:357
  23.9 4.5 %collective-permute-start.6 = (f32[2,40,128]{2,1,0:T(8,128)S(1)}, f32[2,40,128]{2,1,0:T(8,128)S(1)}, u32[]{:S(2)}, u32[]{:S(2)}) collective-permute-start(f32[2,40,128]{2,1,0:T(8,128)S(1)} %get-tuple-element.38), channel_id=1, source_target_pairs={{0,8},{8,0},{1,9},{9,1},{2,10},{10,2},{3,11},{11,3},{4,12},{12,4},... | collective-permute-start | bytes 122888 | tf_op jit(solution)/shard_map/ppermute | solution.py:315
  28.4 2.5 %keep_products.1.keep_ref = f32[2,40,128]{2,1,0:T(8,128)S(1)} custom-call(f32[3,8192]{1,0:T(4,128)S(1)} %get-tuple-element.21.pos_ref, bf16[128,2048]{1,0:T(8,128)(2,1)S(1)} %get-tuple-element.34.y_ref, bf16[128,4096]{1,0:T(8,128)(2,1)S(1)} %get-tuple-element.35.high2, bf16[128,4096]{1,0:T(8,128)(2,1)S(1)} %get-tuple-element.36.low2, ...), custom_call_target="tpu_custom_call" | custom-call | flops 536870912 | bytes 1048576 | tf_op jit(solution)/shard_map/keep_products/pallas_call | solution.py:372
  30.8 0.0 collective-permute-done.6.half_ref
  30.8 0.0 copy-start
  30.9 0.0 copy-start.1
  30.9 4.3 %collective-permute-start.7 = (f32[40,128]{1,0:T(8,128)S(1)}, f32[40,128]{1,0:T(8,128)S(1)}, u32[]{:S(2)}, u32[]{:S(2)}) collective-permute-start(f32[40,128]{1,0:T(8,128)S(1)} %fusion), channel_id=1, source_target_pairs={{0,4},{4,0},{1,5},{5,1},{2,6},{6,2},{3,7},{7,3},{8,12},{12,8},{9,1... | collective-permute-start | bytes 61448 | tf_op jit(solution)/shard_map/ppermute | solution.py:380
  35.2 0.0 collective-permute-done.8.pair_ref
  35.2 0.3 slab_term.1.rest_ref
  35.5 0.5 %collective-permute-done.7.core_ref = f32[40,128]{1,0:T(8,128)S(1)} collective-permute-done((f32[40,128]{1,0:T(8,128)S(1)}, f32[40,128]{1,0:T(8,128)S(1)}, u32[]{:S(2)}, u32[]{:S(2)}) %collective-permute-start.7) | collective-permute-done | bytes 20512 | tf_op jit(solution)/shard_map/ppermute | solution.py:380
  36.0 0.0 copy-done
  36.0 0.0 copy-done.1
  36.0 0.6 %finish_rate.1 = (f32[2,16,128]{2,1,0:T(8,128)}, f32[2,16,128]{2,1,0:T(8,128)}) custom-call(f32[2,40,128]{2,1,0:T(8,128)S(1)} %keep_products.1.keep_ref, f32[2,40,128]{2,1,0:T(8,128)S(1)} %collective-permute-done.6.half_ref, f32[40,128]{1,0:T(8,128)S(1)} %collective-permute-done.7.core_ref, f32[2,16,128]{2,1,0:T(8,128)S(1)} %slab_term.1.rest_ref, ...), custom_call_target="tpu_custom_call" | custom-call | flops 65536 | bytes 262144 | tf_op jit(solution)/shard_map/finish_rate/pallas_call | solution.py:392
  (4 shorter events, 0.0 us)
Async XLA Ops:
  1.7 4.7 %collective-permute-start = (f32[40,128]{1,0:T(8,128)S(1)}, f32[40,128]{1,0:T(8,128)S(1)}, u32[]{:S(2)}, u32[]{:S(2)}) collective-permute-start(f32[40,128]{1,0:T(8,128)S(1)} %get-tuple-element.25.block_ref.slab_ref), channel_id=1, source_target_pairs={{0,64},{64,0},{128,192},{192,128},{1,65},{65,1},{129,193},{193,129... | collective-permute-start | bytes 61448 | tf_op jit(solution)/shard_map/ppermute | solution.py:315
  6.3 6.1 %collective-permute-start.2 = (f32[2,40,128]{2,1,0:T(8,128)S(1)}, f32[2,40,128]{2,1,0:T(8,128)S(1)}, u32[]{:S(2)}, u32[]{:S(2)}) collective-permute-start(f32[2,40,128]{2,1,0:T(8,128)S(1)} %get-tuple-element.29.both_ref), channel_id=1, source_target_pairs={{0,192},{64,128},{128,64},{192,0},{1,193},{65,129},{129,65},{193,1... | collective-permute-start | bytes 122888 | tf_op jit(solution)/shard_map/ppermute | solution.py:315
  8.3 4.1 %collective-permute-start.1 = (f32[40,128]{1,0:T(8,128)S(1)}, f32[40,128]{1,0:T(8,128)S(1)}, u32[]{:S(2)}, u32[]{:S(2)}) collective-permute-start(f32[40,128]{1,0:T(8,128)S(1)} %get-tuple-element.25.block_ref.slab_ref), channel_id=1, source_target_pairs={{0,1},{1,0},{2,3},{3,2},{4,5},{5,4},{6,7},{7,6},{8,9},{9,8},{10,11... | collective-permute-start | bytes 61448 | tf_op jit(solution)/shard_map/ppermute | solution.py:315
  12.4 6.8 %collective-permute-start.5 = (f32[4,40,128]{2,1,0:T(8,128)S(1)}, f32[4,40,128]{2,1,0:T(8,128)S(1)}, u32[]{:S(2)}, u32[]{:S(2)}) collective-permute-start(f32[4,40,128]{2,1,0:T(8,128)S(1)} %get-tuple-element.33.all0), channel_id=1, source_target_pairs={{0,16},{16,0},{32,48},{48,32},{1,17},{17,1},{33,49},{49,33},{2,18}... | collective-permute-start | bytes 245768 | tf_op jit(solution)/shard_map/ppermute | solution.py:315
  13.7 5.5 %collective-permute-start.4 = (f32[4,40,128]{2,1,0:T(8,128)S(1)}, f32[4,40,128]{2,1,0:T(8,128)S(1)}, u32[]{:S(2)}, u32[]{:S(2)}) collective-permute-start(f32[4,40,128]{2,1,0:T(8,128)S(1)} %get-tuple-element.33.all0), channel_id=1, source_target_pairs={{0,48},{16,32},{32,16},{48,0},{1,49},{17,33},{33,17},{49,1},{2,50}... | collective-permute-start | bytes 245768 | tf_op jit(solution)/shard_map/ppermute | solution.py:315
  15.6 5.5 %collective-permute-start.3 = (f32[4,40,128]{2,1,0:T(8,128)S(1)}, f32[4,40,128]{2,1,0:T(8,128)S(1)}, u32[]{:S(2)}, u32[]{:S(2)}) collective-permute-start(f32[4,40,128]{2,1,0:T(8,128)S(1)} %get-tuple-element.33.all0), channel_id=1, source_target_pairs={{0,32},{16,48},{32,0},{48,16},{1,33},{17,49},{33,1},{49,17},{2,34}... | collective-permute-start | bytes 245768 | tf_op jit(solution)/shard_map/ppermute | solution.py:315
  18.6 16.5 %collective-permute-start.8 = (f32[2,40,128]{2,1,0:T(8,128)S(1)}, f32[2,40,128]{2,1,0:T(8,128)S(1)}, u32[]{:S(2)}, u32[]{:S(2)}) collective-permute-start(f32[2,40,128]{2,1,0:T(8,128)S(1)} %get-tuple-element.39), channel_id=1, source_target_pairs={{0,2},{1,3},{2,0},{3,1},{4,6},{5,7},{6,4},{7,5},{8,10},{9,11},{10,... | collective-permute-start | bytes 122888 | tf_op jit(solution)/shard_map/ppermute | solution.py:315
  23.9 7.0 %collective-permute-start.6 = (f32[2,40,128]{2,1,0:T(8,128)S(1)}, f32[2,40,128]{2,1,0:T(8,128)S(1)}, u32[]{:S(2)}, u32[]{:S(2)}) collective-permute-start(f32[2,40,128]{2,1,0:T(8,128)S(1)} %get-tuple-element.38), channel_id=1, source_target_pairs={{0,8},{8,0},{1,9},{9,1},{2,10},{10,2},{3,11},{11,3},{4,12},{12,4},... | collective-permute-start | bytes 122888 | tf_op jit(solution)/shard_map/ppermute | solution.py:315
  30.8 5.2 %copy-start = (f32[2,16,128]{2,1,0:T(8,128)S(1)}, f32[2,16,128]{2,1,0:T(8,128)}, u32[]{:S(2)}) copy-start(f32[2,16,128]{2,1,0:T(8,128)} %base_ref.1) | copy-start | bytes 49156
  30.9 5.2 %copy-start.1 = (f32[2,16,128]{2,1,0:T(8,128)S(1)}, f32[2,16,128]{2,1,0:T(8,128)}, u32[]{:S(2)}) copy-start(f32[2,16,128]{2,1,0:T(8,128)} %accum_ref.1) | copy-start | bytes 49156
  30.9 5.2 %collective-permute-start.7 = (f32[40,128]{1,0:T(8,128)S(1)}, f32[40,128]{1,0:T(8,128)S(1)}, u32[]{:S(2)}, u32[]{:S(2)}) collective-permute-start(f32[40,128]{1,0:T(8,128)S(1)} %fusion), channel_id=1, source_target_pairs={{0,4},{4,0},{1,5},{5,1},{2,6},{6,2},{3,7},{7,3},{8,12},{12,8},{9,1... | collective-permute-start | bytes 61448 | tf_op jit(solution)/shard_map/ppermute | solution.py:380
